TPU v7x, 32 devices: a whole 2x2x4 slice. The times are simulated.
32 devices in a mesh: psg: 8 (over z, y), qry: 4 (over x, core).
Axes of the slice: x: 2, y: 2, z: 4, core: 2. Of those that a mesh axis runs over, the one named last changes fastest.
Arguments:
- queries: bfloat16 [128, 32, 128], P(('psg', 'qry')), may hold values from -6 to 6
- passages: bfloat16 [256, 256, 128], P('psg'), may hold values from -6 to 6
- candidates: int32 [128, 32], P(('psg', 'qry')), may hold values from 0 to 255, as said below
- teacher: float32 [128, 32], P(('psg', 'qry')), may hold values from -8 to 8
Outputs:
- pair_loss: float32 [128], P(('psg', 'qry'))
- grad_queries: bfloat16 [128, 32, 128], P(('psg', 'qry'))
- grad_passages: bfloat16 [256, 256, 128], P('psg', 'qry')
Inputs may be any that keep to these rules, and one draw needn't show every extreme that they name: Passage p lies in block p // 32. Among the 4 x 32 candidates of one device's queries (aligned blocks of 4 rows), at most 40 lie in one passage block; one passage block, the same for all devices, holds exactly 40 of every device's candidates. Candidate ids of one query may repeat.
All inputs are finite; a program needn't handle non-finite values.
Results may differ from a plain program's by a relative error of at most 0.019.
Values may be sent and summed in bfloat16 or wider, within the bound.
No kernel may reach another device: no remote copies, remote signals or barrier semaphores. Data moves between devices by JAX's collectives and lax.ppermute only.
A program may use at most 64 MiB of HBM per device.

v0:
```python
import math

import jax
import jax.numpy as jnp
from jax import lax
from jax.sharding import PartitionSpec as P

epsilon = 1e-06
softness_scale = 0.05


def normalize(values):
    widened = values.astype(jnp.float32)
    inverse_norm = lax.rsqrt(jnp.sum(widened * widened, -1, keepdims=True) + epsilon)
    return (widened * inverse_norm, inverse_norm)


def select_rows(row_ids, table):
    row_total = table.shape[0]
    picker = (row_ids[:, None] == lax.iota(jnp.int32, row_total)[None, :]).astype(jnp.bfloat16)
    flat_table = table.reshape(row_total, -1)
    chosen = jnp.dot(picker, flat_table, preferred_element_type=jnp.float32).astype(jnp.bfloat16)
    return chosen.reshape((row_ids.shape[0],) + table.shape[1:])


def add_rows(accum, row_ids, delta):
    row_total = accum.shape[0]
    placer = (row_ids[:, None] == lax.iota(jnp.int32, row_total)[None, :]).astype(jnp.float32)
    flat_delta = delta.reshape(row_ids.shape[0], -1)
    added = jnp.einsum("sr,sx->rx", placer, flat_delta, precision=lax.Precision.HIGHEST)
    return accum + added.reshape(accum.shape)


def shards(queries, passages, candidates, teacher):
    query_count, query_tokens, feature_count = queries.shape
    pass_count, passage_tokens, _ = passages.shape
    cand_count = candidates.shape[1]
    owner_count = lax.axis_size("psg")
    capacity = max(2, (5 * query_count * cand_count + 2 * owner_count - 1) // (2 * owner_count))
    slot_count = owner_count * capacity
    pair_count = query_count * cand_count
    query_unit, query_inverse = normalize(queries)
    passage_unit, passage_inverse = normalize(passages)
    query_norm = query_unit.astype(jnp.bfloat16)
    passage_norm = passage_unit.astype(jnp.bfloat16)
    owner_ids = (candidates // pass_count).reshape(-1)
    local_ids = (candidates % pass_count).reshape(-1)
    onehot = (owner_ids[:, None] == lax.iota(jnp.int32, owner_count)[None, :]).astype(jnp.int32)
    before = jnp.cumsum(onehot, 0) - onehot
    rank_in_owner = jnp.sum(before * onehot, 1)
    slot_ids = owner_ids * capacity + rank_in_owner
    query_local = lax.iota(jnp.int32, pair_count) // cand_count
    slot_code = (
        jnp.zeros((slot_count,), jnp.int32)
        .at[slot_ids]
        .set(query_local * pass_count + local_ids + 1)
    )
    send_code = slot_code.reshape(owner_count, capacity)
    sender = lax.iota(jnp.int32, slot_count) // capacity
    received_label = lax.all_to_all(send_code, "psg", split_axis=0, concat_axis=0, tiled=True)
    query_rows = lax.all_gather(query_norm, "psg", axis=0, tiled=True)
    flat_peek = received_label.reshape(-1)
    fetch_rows = sender * query_count + jnp.where(flat_peek > 0, (flat_peek - 1) // pass_count, 0)
    flat_code = received_label.reshape(-1)
    live = flat_code > 0
    pass_index = jnp.where(live, (flat_code - 1) % pass_count, 0)
    target_rows = sender * query_count + jnp.where(live, (flat_code - 1) // pass_count, 0)
    block_len = math.gcd(slot_count, 64)
    block_total = slot_count // block_len

    def block_terms(offset):
        row_ids = lax.dynamic_slice_in_dim(fetch_rows, offset, block_len)
        passage_ids = lax.dynamic_slice_in_dim(pass_index, offset, block_len)
        query_tile = select_rows(row_ids, query_rows)
        passage_tile = select_rows(passage_ids, passage_norm)
        token_products = jnp.einsum(
            "sqe,spe->sqp", query_tile, passage_tile, preferred_element_type=jnp.float32
        )
        power_value = jnp.exp(token_products / softness_scale)
        return (query_tile, passage_tile, passage_ids, power_value, jnp.sum(power_value, -1))

    def forward_block(offset):
        reduced_sum = block_terms(offset)[4]
        return jnp.sum(softness_scale * jnp.log(reduced_sum), -1)

    offsets = lax.iota(jnp.int32, block_total) * block_len
    slot_scores = lax.map(forward_block, offsets).reshape(owner_count, capacity)
    scores_home = lax.all_to_all(slot_scores, "psg", split_axis=0, concat_axis=0, tiled=True)
    scores = scores_home.reshape(-1)[slot_ids].reshape(query_count, cand_count)
    teacher_exp = jnp.exp(teacher)
    mentor_score_sum = jnp.sum(teacher_exp, -1, keepdims=True)
    target = teacher_exp / mentor_score_sum
    log_target = teacher - jnp.log(mentor_score_sum)
    score_exp = jnp.exp(scores)
    score_total = jnp.sum(score_exp, -1, keepdims=True)
    likelihood = score_exp / score_total
    pair_loss = jnp.sum(target * (log_target - scores), -1) + jnp.log(score_total[:, 0])
    score_grad = likelihood - target
    send_grad = jnp.zeros((slot_count,), jnp.float32).at[slot_ids].set(score_grad.reshape(-1))
    recv_grad = lax.all_to_all(
        send_grad.reshape(owner_count, capacity), "psg", split_axis=0, concat_axis=0, tiled=True
    )
    flat_grad = recv_grad.reshape(-1)

    def backward(step_index, running):
        query_accum, passage_accum = running
        offset = step_index * block_len
        query_tile, passage_tile, passage_ids, power_value, reduced_sum = block_terms(offset)
        slot_grad = lax.dynamic_slice_in_dim(flat_grad, offset, block_len)
        weights = (slot_grad[:, None, None] * power_value / reduced_sum[:, :, None]).astype(
            jnp.bfloat16
        )
        query_delta = jnp.einsum(
            "sqp,spe->sqe", weights, passage_tile, preferred_element_type=jnp.float32
        )
        passage_delta = jnp.einsum(
            "sqp,sqe->spe", weights, query_tile, preferred_element_type=jnp.float32
        )
        home_rows = lax.dynamic_slice_in_dim(target_rows, offset, block_len)
        return (
            add_rows(query_accum, home_rows, query_delta),
            add_rows(passage_accum, passage_ids, passage_delta),
        )

    start_state = (
        jnp.zeros((owner_count * query_count, query_tokens, feature_count), jnp.float32),
        jnp.zeros((pass_count, passage_tokens, feature_count), jnp.float32),
    )
    query_accum, passage_accum = lax.fori_loop(0, block_total, backward, start_state)
    result_output = lax.all_to_all(
        query_accum.reshape(owner_count, query_count, query_tokens, feature_count).astype(
            jnp.bfloat16
        ),
        "psg",
        split_axis=0,
        concat_axis=0,
        tiled=True,
    ).astype(jnp.float32)
    unit_query_grad = jnp.sum(result_output, 0)
    unit_passage_grad = lax.psum_scatter(
        passage_accum.astype(jnp.bfloat16), "qry", scatter_dimension=1, tiled=True
    ).astype(jnp.float32)
    token_share = unit_passage_grad.shape[1]
    shard_start = lax.axis_index("qry") * token_share
    unit_slice = lax.dynamic_slice_in_dim(passage_unit, shard_start, token_share, 1)
    inverse_slice = lax.dynamic_slice_in_dim(passage_inverse, shard_start, token_share, 1)
    grad_queries = query_inverse * (
        unit_query_grad - query_unit * jnp.sum(query_unit * unit_query_grad, -1, keepdims=True)
    )
    grad_passages = inverse_slice * (
        unit_passage_grad - unit_slice * jnp.sum(unit_slice * unit_passage_grad, -1, keepdims=True)
    )
    return (pair_loss, grad_queries.astype(jnp.bfloat16), grad_passages.astype(jnp.bfloat16))


def solution(mesh):
    placed = (
        P(("psg", "qry"), None, None),
        P("psg", None, None),
        P(("psg", "qry"), None),
        P(("psg", "qry"), None),
    )
    return jax.shard_map(
        shards,
        mesh=mesh,
        in_specs=placed,
        out_specs=(P(("psg", "qry")), P(("psg", "qry"), None, None), P("psg", "qry", None)),
        check_vma=False,
    )
```

profile of v0, /device:TPU:0, one launch (start us, length us, event | category | flops | bytes accessed | tf_op | source)
XLA Modules:
  0.0 281.0 jit_solution(4697915038884723669)
XLA Ops:
  10.2 7.3 %all-to-all-start = ((s32[8,1,40]{2,1,0:T(1,128)}), s32[8,1,40]{2,1,0:T(1,128)S(1)}, u32[]{:S(2)}, u32[]{:S(2)}) async-start(s32[8,1,40]{2,1,0:T(1,128)} %all_to_all.21), calls=%async_computation | async-start | bytes 8192 | tf_op jit(solution)/shard_map/all_to_all | solution.py:60
  19.3 2.7 fusion.34
  22.1 31.3 %all_gather.3 = bf16[32,32,128]{2,1,0:T(8,128)(2,1)S(1)} all-gather(bf16[4,32,128]{2,1,0:T(8,128)(2,1)S(1)} %copy.50), channel_id=1, replica_groups=mesh['psg'=8,'qry'=4] {'psg'}, dimensions={0}, use_global_device_ids=true | all-gather | bytes 294912 | tf_op jit(solution)/shard_map/all_gather | solution.py:61
  53.4 3.8 %convert_multiply_fusion = (f32[32,256,128]{2,1,0:T(8,128)}, bf16[32,256,128]{2,1,0:T(8,128)(2,1)S(1)}) fusion(bf16[32,256,128]{2,1,0:T(8,128)(2,1)} %param.9, f32[32,256]{1,0:T(8,128)S(1)} %add_rsqrt_fusion), kind=kLoop, calls=%fused_computation.49 | loop fusion | flops 3145728 | bytes 8421376 | tf_op jit(solution)/shard_map/mul | solution.py:15
  57.4 38.0 %while.27 = (s32[]{:T(128)}, f32[5,64]{1,0:T(8,128)S(1)}, s32[5]{0:T(128)S(1)}, s32[320]{0:T(512)S(1)}, bf16[32,32,128]{2,1,0:T(8,128)(2,1)S(1)}, /*index=5*/s32...) while((s32[]{:T(128)}, f32[5,64]{1,0:T(8,128)S(1)}, s32[5]{0:T(128)S(1)}, ...), condition=%wide.region_9.10_spmd, body=%wide.region_6.9_spmd.sunk | while | flops 288626624 | bytes 21268904 | solution.py:87
  96.1 5.4 %all-to-all-start.1 = ((f32[8,1,40]{2,1,0:T(1,128)}), f32[8,1,40]{2,1,0:T(1,128)S(1)}, u32[]{:S(2)}, u32[]{:S(2)}) async-start(f32[8,1,40]{2,1,0:T(1,128)} %all_to_all.23), calls=%async_computation.1 | async-start | bytes 8192 | tf_op jit(solution)/shard_map/all_to_all | solution.py:88
  101.7 6.3 %all-to-all-done.1 = f32[8,1,40]{2,1,0:T(1,128)S(1)} async-done(((f32[8,1,40]{2,1,0:T(1,128)}), f32[8,1,40]{2,1,0:T(1,128)S(1)}, u32[]{:S(2)}, u32[]{:S(2)}) %all-to-all-start.1) | async-done | bytes 1312 | tf_op jit(solution)/shard_map/all_to_all | solution.py:88
  112.6 3.3 %all-to-all-start.2 = ((f32[8,1,40]{2,1,0:T(1,128)}), f32[8,1,40]{2,1,0:T(1,128)S(1)}, u32[]{:S(2)}, u32[]{:S(2)}) async-start(f32[8,1,40]{2,1,0:T(1,128)} %all_to_all.25), calls=%async_computation.2 | async-start | bytes 8192 | tf_op jit(solution)/shard_map/all_to_all | solution.py:100
  116.0 6.3 %all-to-all-done.2 = f32[8,1,40]{2,1,0:T(1,128)S(1)} async-done(((f32[8,1,40]{2,1,0:T(1,128)}), f32[8,1,40]{2,1,0:T(1,128)S(1)}, u32[]{:S(2)}, u32[]{:S(2)}) %all-to-all-start.2) | async-done | bytes 1312 | tf_op jit(solution)/shard_map/all_to_all | solution.py:100
  123.0 109.9 %while.28 = (s32[]{:T(128)}, f32[32,32,128]{2,0,1:T(8,128)S(1)}, f32[32,256,128]{2,0,1:T(8,128)}, s32[320]{0:T(512)S(1)}, f32[320]{0:T(512)S(1)}, /*index=5*/bf1...) while((s32[]{:T(128)}, f32[32,32,128]{2,0,1:T(8,128)S(1)}, ...), condition=%wide.region_15.16_spmd.clone, body=%wide.region_13.15_spmd.clone.sunk | while | flops 1469585408 | bytes 94137584 | solution.py:129
  132.5 10.6 %select_add_fusion.2 = f32[32,256,128]{2,0,1:T(8,128)S(1)} fusion(f32[32,256,128]{2,0,1:T(8,128)S(1)} %copy-done, pred[]{:T(512)S(6)} %compare.11, s32[64]{0:T(128)S(1)} %dynamic_slice.59, f32[8,8,256,128]{3,2,1,0:T(8,128)S(1)} %bitcast.147), kind=kOutput, calls=%fused_computation.23.clone.1 | convolution fusion | flops 807405568 | bytes 16777472 | tf_op jit(solution)/shard_map/while/body/eval_jaxpr/sr,sx->rx/dot_general | solution.py:30
  143.1 2.0 copy-done.1
  154.4 10.6 %select_add_fusion.2 = f32[32,256,128]{2,0,1:T(8,128)S(1)} fusion(f32[32,256,128]{2,0,1:T(8,128)S(1)} %copy-done, pred[]{:T(512)S(6)} %compare.11, s32[64]{0:T(128)S(1)} %dynamic_slice.59, f32[8,8,256,128]{3,2,1,0:T(8,128)S(1)} %bitcast.147), kind=kOutput, calls=%fused_computation.23.clone.1 | convolution fusion | flops 807405568 | bytes 16777472 | tf_op jit(solution)/shard_map/while/body/eval_jaxpr/sr,sx->rx/dot_general | solution.py:30
  165.1 2.0 copy-done.1
  176.4 10.6 %select_add_fusion.2 = f32[32,256,128]{2,0,1:T(8,128)S(1)} fusion(f32[32,256,128]{2,0,1:T(8,128)S(1)} %copy-done, pred[]{:T(512)S(6)} %compare.11, s32[64]{0:T(128)S(1)} %dynamic_slice.59, f32[8,8,256,128]{3,2,1,0:T(8,128)S(1)} %bitcast.147), kind=kOutput, calls=%fused_computation.23.clone.1 | convolution fusion | flops 807405568 | bytes 16777472 | tf_op jit(solution)/shard_map/while/body/eval_jaxpr/sr,sx->rx/dot_general | solution.py:30
  198.3 10.6 %select_add_fusion.2 = f32[32,256,128]{2,0,1:T(8,128)S(1)} fusion(f32[32,256,128]{2,0,1:T(8,128)S(1)} %copy-done, pred[]{:T(512)S(6)} %compare.11, s32[64]{0:T(128)S(1)} %dynamic_slice.59, f32[8,8,256,128]{3,2,1,0:T(8,128)S(1)} %bitcast.147), kind=kOutput, calls=%fused_computation.23.clone.1 | convolution fusion | flops 807405568 | bytes 16777472 | tf_op jit(solution)/shard_map/while/body/eval_jaxpr/sr,sx->rx/dot_general | solution.py:30
  209.0 2.0 copy-done.1
  220.3 10.6 %select_add_fusion.2 = f32[32,256,128]{2,0,1:T(8,128)S(1)} fusion(f32[32,256,128]{2,0,1:T(8,128)S(1)} %copy-done, pred[]{:T(512)S(6)} %compare.11, s32[64]{0:T(128)S(1)} %dynamic_slice.59, f32[8,8,256,128]{3,2,1,0:T(8,128)S(1)} %bitcast.147), kind=kOutput, calls=%fused_computation.23.clone.1 | convolution fusion | flops 807405568 | bytes 16777472 | tf_op jit(solution)/shard_map/while/body/eval_jaxpr/sr,sx->rx/dot_general | solution.py:30
  230.9 2.0 copy-done.1
  232.9 6.0 %copy.113 = bf16[32,256,128]{2,1,0:T(8,128)(2,1)} copy(f32[32,256,128]{2,0,1:T(8,128)} %get-tuple-element.206) | data formatting | bytes 6291456 | tf_op jit(solution)/shard_map/while | solution.py:129
  240.1 3.4 %all-to-all-start.3 = ((bf16[8,4,32,128]{3,1,2,0:T(4,128)(2,1)}), bf16[8,4,32,128]{3,1,2,0:T(4,128)(2,1)S(1)}, u32[]{:S(2)}, u32[]{:S(2)}) async-start(bf16[8,4,32,128]{3,1,2,0:T(4,128)(2,1)} %copy.52), calls=%async_computation.3 | async-start | bytes 524288 | tf_op jit(solution)/shard_map/all_to_all | solution.py:130
  244.1 7.6 %all-to-all-done.3 = bf16[8,4,32,128]{3,1,2,0:T(4,128)(2,1)S(1)} async-done(((bf16[8,4,32,128]{3,1,2,0:T(4,128)(2,1)}), bf16[8,4,32,128]{3,1,2,0:T(4,128)(2,1)S(1)}, u32[]{:S(2)}, u32[]{:S(2)}) %all-to-all-start.3) | async-done | bytes 262176 | tf_op jit(solution)/shard_map/all_to_all | solution.py:130
  253.5 14.3 %reduce-scatter.2.cloned.1.call-done = bf16[32,64,128]{2,1,0:T(8,128)(2,1)} async-done(((bf16[32,256,128]{2,1,0:T(8,128)(2,1)}), bf16[32,64,128]{2,1,0:T(8,128)(2,1)}) %reduce-scatter.2.cloned.1.call-update) | async-done | bytes 524304 | tf_op jit(solution)/shard_map/reduce_scatter | solution.py:140
  267.8 6.3 %fusion.39 = bf16[32,64,128]{2,1,0:T(8,128)(2,1)} fusion(bf16[32,64,128]{2,1,0:T(8,128)(2,1)} %reduce-scatter.2.cloned.1.call-done, f32[32,256,128]{2,1,0:T(8,128)} %get-tuple-element.285, s32[]{:T(128)S(6)} %select_n.80, f32[32,64]{1,0:T(8,128)S(1)} %constant_dynamic-slice_fusion), kind=kOutput, calls=%fused_computation.58 | output fusion | flops 1837183 | bytes 3679232 | tf_op jit(solution)/shard_map/mul | solution.py:151
  (181 shorter events, 91.3 us)
Async XLA Ops:
  10.2 46.9 %all-to-all-start = ((s32[8,1,40]{2,1,0:T(1,128)}), s32[8,1,40]{2,1,0:T(1,128)S(1)}, u32[]{:S(2)}, u32[]{:S(2)}) async-start(s32[8,1,40]{2,1,0:T(1,128)} %all_to_all.21), calls=%async_computation | async-start | bytes 8192 | tf_op jit(solution)/shard_map/all_to_all | solution.py:60
  57.4 44.2 %copy-start.3 = (f32[4,32]{1,0:T(4,128)S(1)}, f32[4,32]{1,0:T(4,128)}, u32[]{:S(2)}) copy-start(f32[4,32]{1,0:T(4,128)} %param.11) | copy-start | bytes 1540
  96.1 11.8 %all-to-all-start.1 = ((f32[8,1,40]{2,1,0:T(1,128)}), f32[8,1,40]{2,1,0:T(1,128)S(1)}, u32[]{:S(2)}, u32[]{:S(2)}) async-start(f32[8,1,40]{2,1,0:T(1,128)} %all_to_all.23), calls=%async_computation.1 | async-start | bytes 8192 | tf_op jit(solution)/shard_map/all_to_all | solution.py:88
  112.6 9.6 %all-to-all-start.2 = ((f32[8,1,40]{2,1,0:T(1,128)}), f32[8,1,40]{2,1,0:T(1,128)S(1)}, u32[]{:S(2)}, u32[]{:S(2)}) async-start(f32[8,1,40]{2,1,0:T(1,128)} %all_to_all.25), calls=%async_computation.2 | async-start | bytes 8192 | tf_op jit(solution)/shard_map/all_to_all | solution.py:100
  115.9 151.9 %reduce-scatter.2.cloned.1.call-start = ((), (), s32[]{:S(2)}) async-start(), calls=%async_computation.5 | async-start | bytes 2621440 | tf_op jit(solution)/shard_map/reduce_scatter | solution.py:140
  130.3 2.2 copy-start
  143.1 2.0 copy-start.1
  152.2 2.2 copy-start
  165.1 2.0 copy-start.1
  174.2 2.2 copy-start
  187.0 2.0 copy-start.1
  196.1 2.2 copy-start
  208.9 2.0 copy-start.1
  218.1 2.2 copy-start
  230.9 2.0 copy-start.1
  232.9 18.8 %copy-start.2 = (bf16[4,32,128]{2,1,0:T(8,128)(2,1)S(1)}, bf16[4,32,128]{2,1,0:T(8,128)(2,1)}, u32[]{:S(2)}) copy-start(bf16[4,32,128]{2,1,0:T(8,128)(2,1)} %param.8) | copy-start | bytes 98308
  240.1 11.6 %all-to-all-start.3 = ((bf16[8,4,32,128]{3,1,2,0:T(4,128)(2,1)}), bf16[8,4,32,128]{3,1,2,0:T(4,128)(2,1)S(1)}, u32[]{:S(2)}, u32[]{:S(2)}) async-start(bf16[8,4,32,128]{3,1,2,0:T(4,128)(2,1)} %copy.52), calls=%async_computation.3 | async-start | bytes 524288 | tf_op jit(solution)/shard_map/all_to_all | solution.py:130
Sparse Core Ops, SparseCore 0:
  239.0 28.7 reduce-scatter.1
where the time goes:
time: 282 us; the launch traced here: 281 us
  matrix products  108 us (38%)
  local copies, waits for them, and re-layouts  43.7 us (15%)
  waiting for transfers between devices  34.4 us (12%)
  blocking collectives  31.3 us (11%)
  starting transfers between devices  19.5 us (7%)
  other arithmetic  19.4 us (7%)
  between operations  14.2 us (5%)
  loops' own time  10.5 us (4%)
    dot_general x10, matrix products, add_rows(): jnp.einsum('sr,sx->rx', placer, flat_delta, precision=lax.Precision.HIGHEST)  59.3 us
    all_gather x1, blocking collectives, shards(): query_rows = lax.all_gather(query_norm, 'psg', axis=0, tiled=True)  31.3 us
    while x40, local copies, waits for them, and re-layouts  23.9 us
    dot_general x20, matrix products, select_rows(): jnp.dot(picker, flat_table, preferred_element_type=jnp.float32)  18.6 us
    dot_general x10, matrix products, block_terms(): jnp.einsum('sqe,spe->sqp', query_tile, passage_tile, preferred_element_ty...  16.2 us
    reduce_scatter x1, waiting for transfers between devices, shards(): lax.psum_scatter(passage_accum.astype(jnp.bfloat16), 'qry', scatter_dimen...  14.3 us
    another operation x1, loops' own time, shards(): slot_scores = lax.map(forward_block, offsets).reshape(owner_count, capacity)  9.97 us
    dot_general x5, matrix products, backward(): jnp.einsum('sqp,sqe->spe', weights, query_tile, preferred_element_type=jn...  9.23 us
  transfers between devices with their start and end apart: 5, of which 4 were waited for; matrix products, arithmetic and copies ran while one was open for 4% of the time, Pallas kernels for 0%

commit v1 on v0

v1 whole, which is shorter than its diff:
```python
import math

import jax
import jax.numpy as jnp
from jax import lax
from jax.experimental import pallas as pl
from jax.experimental.pallas import tpu as pltpu
from jax.sharding import PartitionSpec as P

epsilon = 1e-06
softness_scale = 0.05
block_pairs = 16
vmem_bytes = 20 << 20
row_pad = 8

VMEM = pl.BlockSpec(memory_space=pltpu.VMEM)


def params():
    return pltpu.CompilerParams(vmem_limit_bytes=vmem_bytes)


def unit_rows(values):
    widened = values.astype(jnp.float32)
    inverse = lax.rsqrt(jnp.sum(widened * widened, -1, keepdims=True) + epsilon)
    return widened * inverse, inverse


def lane_ids(shape):
    return lax.broadcasted_iota(jnp.int32, shape, len(shape) - 1)


def tangent(raw, grad):
    unit, inverse = unit_rows(raw)
    return inverse * (grad - unit * jnp.sum(unit * grad, -1, keepdims=True))


def passages_kernel(slices, in_ref, norm_ref, flip_ref, own_ref):
    count, tokens, _ = in_ref.shape
    share = tokens // slices
    me = lax.axis_index("qry")
    base = pl.program_id(0) * count
    for item in range(count):
        for place in range(slices):
            start = pl.multiple_of((me ^ place) * share, share)
            raw = in_ref[item, pl.ds(start, share), :]
            if place == 0:
                own_ref[base + item] = raw
            norm_ref[base + item, pl.ds(place * share, share), :] = unit_rows(raw)[0].astype(
                jnp.bfloat16
            )
        flip_ref[base + item] = jnp.transpose(norm_ref[base + item], (1, 0))


def prepare_passages(passages, slices):
    count, tokens, width = passages.shape
    step = math.gcd(count, 8)
    share = tokens // slices
    return pl.pallas_call(
        lambda *refs: passages_kernel(slices, *refs),
        grid=(count // step,),
        in_specs=[pl.BlockSpec((step, tokens, width), lambda i: (i, 0, 0))],
        out_specs=[VMEM, VMEM, VMEM],
        out_shape=[
            pltpu.VMEM((count, tokens, width), jnp.bfloat16),
            pltpu.VMEM((count, width, tokens), jnp.bfloat16),
            pltpu.VMEM((count, share, width), jnp.bfloat16),
        ],
        compiler_params=params(),
        cost_estimate=pl.CostEstimate(flops=1 << 24, bytes_accessed=6 << 20, transcendentals=0),
        name="prepare_passages",
    )(passages)


def each_extra(pass_count, list_smem, count_row, visit):
    def passage_step(p, used):
        pairs = list_smem[count_row, p]
        blocks = (pairs + block_pairs - 1) // block_pairs
        extra = jnp.maximum(blocks - 1, 0)

        def step(b, carry):
            visit(p, (b + 1) * block_pairs, pass_count + used + b)
            return carry

        lax.fori_loop(0, extra, step, 0)
        return used + extra

    lax.fori_loop(0, pass_count, passage_step, jnp.int32(0))


def forward_kernel(
    cand_count,
    query_count,
    query_tokens,
    recv_ref,
    norm_ref,
    soft_ref,
    qn_ref,
    score_ref,
    many_ref,
    target_ref,
    list_ref,
    zw_ref,
    ext_ref,
    low_ref,
    sums_ref,
    list_smem,
    sem,
):
    sources = recv_ref.shape[0]
    pass_count, tokens, width = norm_ref.shape
    group = sources * query_count
    rows = query_count * query_tokens
    stride = group + row_pad
    count_row = list_ref.shape[0] - row_pad
    owner = lax.axis_index("psg").astype(jnp.float32)
    for s in range(sources):
        packed = recv_ref[s, rows : rows + 16, :].astype(jnp.float32)
        ext_ref[s * query_count : (s + 1) * query_count, :] = packed[:query_count]
        low_ref[s * query_count : (s + 1) * query_count, :] = packed[8 : 8 + query_count]
        qn_ref[s * rows : (s + 1) * rows, :] = unit_rows(recv_ref[s, :rows, :])[0].astype(
            jnp.bfloat16
        )
    qn_ref[sources * rows :, :] = jnp.zeros((query_tokens, width), jnp.bfloat16)

    main = ext_ref[...]
    lanes = lane_ids(main.shape)
    lanes_float = lanes.astype(jnp.float32)
    live = lanes < cand_count
    local = pltpu.roll(main, 128 - cand_count, 1)
    logits = (
        pltpu.roll(main, 128 - 2 * cand_count, 1)
        + pltpu.roll(main, 128 - 3 * cand_count, 1)
        + low_ref[...]
    )
    raised = jnp.where(live, jnp.exp(logits), 0.0)
    target = raised / jnp.sum(raised, -1, keepdims=True)
    local = jnp.where(main == owner, local, -1.0)
    many = jnp.zeros(main.shape, jnp.float32)
    wanted = jnp.zeros(main.shape, jnp.float32)
    for c in range(cand_count):
        same = local[:, c : c + 1] == lanes_float
        many = many + jnp.where(same, 1.0, 0.0)
        wanted = wanted + jnp.where(same, target[:, c : c + 1], 0.0)
    many_ref[...] = many
    target_ref[...] = wanted
    active = many > 0.0
    lower = (
        lax.broadcasted_iota(jnp.int32, (group, group), 0)
        > lax.broadcasted_iota(jnp.int32, (group, group), 1)
    ).astype(jnp.bfloat16)
    active_value = jnp.where(active, 1.0, 0.0)
    rank = jnp.dot(lower, active_value.astype(jnp.bfloat16), preferred_element_type=jnp.float32)
    rank = jnp.where(active, rank, -1.0)
    less = lax.broadcasted_iota(jnp.int32, main.shape, 0).astype(jnp.float32) - group
    for k in range(count_row):
        found = jnp.sum(jnp.where(rank == k, less, 0.0), 0, keepdims=True) + group
        list_ref[k : k + 1, :] = found.astype(jnp.int32)
    total = jnp.sum(active_value, 0, keepdims=True).astype(jnp.int32)
    list_ref[count_row:, :] = jnp.broadcast_to(total, (row_pad, 128))
    copy = pltpu.make_async_copy(list_ref, list_smem, sem)
    copy.start()
    copy.wait()

    half = block_pairs // 2

    def block(p, first, slot):
        passage = norm_ref[p]
        for h in range(2):
            ids = [list_smem[first + h * half + r, p] for r in range(half)]
            tile = jnp.concatenate(
                [
                    qn_ref[pl.ds(pl.multiple_of(n * query_tokens, query_tokens), query_tokens), :]
                    for n in ids
                ],
                0,
            )
            dots = lax.dot_general(
                passage, tile, (((1,), (1,)), ((), ())), preferred_element_type=jnp.float32
            )
            power = jnp.exp(dots * (1.0 / softness_scale))
            sums = jnp.sum(power, 0, keepdims=True)
            span = half * query_tokens
            soft_ref[slot, :, h * span : (h + 1) * span] = (power * (1.0 / sums)).astype(
                jnp.bfloat16
            )
            for r in range(half):
                sums_ref[pl.ds(p * stride + ids[r], 1), :query_tokens] = sums[
                    :, r * query_tokens : (r + 1) * query_tokens
                ]

    def step(p, carry):
        block(2 * p, 0, 2 * p)
        block(2 * p + 1, 0, 2 * p + 1)
        return carry

    lax.fori_loop(0, pass_count // 2, step, 0)
    each_extra(pass_count, list_smem, count_row, block)

    scores = jnp.zeros(main.shape, jnp.float32)
    for p in range(pass_count):
        logs = jnp.log(sums_ref[p * stride : p * stride + group, :])
        value = softness_scale * jnp.sum(
            jnp.where(lanes < query_tokens, logs, 0.0), -1, keepdims=True
        )
        scores = jnp.where(lanes == p, value, scores)
    scores = jnp.where(active, scores, 0.0)
    score_ref[...] = scores
    mass = jnp.sum(many * jnp.exp(scores), -1, keepdims=True)
    agreed = jnp.sum(wanted * scores, -1, keepdims=True)
    message = jnp.where(lanes == 0, mass, jnp.where(lanes == 1, agreed, 0.0))
    for s in range(sources):
        zw_ref[s] = message


def forward(received, norm, cand_count, query_count, query_tokens):
    sources = received.shape[0]
    pass_count, tokens, width = norm.shape
    group = sources * query_count
    capacity = max(2, -(-5 * query_count * cand_count // (2 * sources)))
    blocks = pass_count + sources * capacity // block_pairs
    list_rows = -(-group // block_pairs) * block_pairs + row_pad
    rows = query_count * query_tokens
    flops = 2 * pass_count * block_pairs * query_tokens * tokens * width
    return pl.pallas_call(
        lambda *refs: forward_kernel(cand_count, query_count, query_tokens, *refs),
        in_specs=[VMEM, VMEM],
        out_specs=[VMEM] * 7,
        out_shape=[
            pltpu.VMEM((blocks, tokens, block_pairs * query_tokens), jnp.bfloat16),
            pltpu.VMEM((sources * rows + query_tokens, width), jnp.bfloat16),
            pltpu.VMEM((group, 128), jnp.float32),
            pltpu.VMEM((group, 128), jnp.float32),
            pltpu.VMEM((group, 128), jnp.float32),
            pltpu.VMEM((list_rows, 128), jnp.int32),
            jax.ShapeDtypeStruct((sources, group, 128), jnp.float32),
        ],
        scratch_shapes=[
            pltpu.VMEM((group, 128), jnp.float32),
            pltpu.VMEM((group, 128), jnp.float32),
            pltpu.VMEM((pass_count * (group + row_pad), 128), jnp.float32),
            pltpu.SMEM((list_rows, 128), jnp.int32),
            pltpu.SemaphoreType.DMA,
        ],
        compiler_params=params(),
        cost_estimate=pl.CostEstimate(flops=flops, bytes_accessed=12 << 20, transcendentals=1 << 22),
        name="forward",
    )(received, norm)


def attend_kernel(flip_ref, soft_ref, list_ref, out_ref, list_smem, sem):
    pass_count = flip_ref.shape[0]
    copy = pltpu.make_async_copy(list_ref, list_smem, sem)
    copy.start()

    def block(p, first, slot):
        mixed = jnp.dot(flip_ref[p], soft_ref[slot], preferred_element_type=jnp.float32)
        out_ref[slot] = jnp.transpose(mixed, (1, 0)).astype(jnp.bfloat16)

    def step(p, carry):
        block(2 * p, 0, 2 * p)
        block(2 * p + 1, 0, 2 * p + 1)
        return carry

    lax.fori_loop(0, pass_count // 2, step, 0)
    copy.wait()
    each_extra(pass_count, list_smem, list_ref.shape[0] - row_pad, block)


def attend(flip, soft, ids):
    blocks, tokens, columns = soft.shape
    width = flip.shape[1]
    flops = 2 * flip.shape[0] * columns * tokens * width
    return pl.pallas_call(
        attend_kernel,
        in_specs=[VMEM] * 3,
        out_specs=VMEM,
        out_shape=pltpu.VMEM((blocks, columns, width), jnp.bfloat16),
        scratch_shapes=[pltpu.SMEM(ids.shape, jnp.int32), pltpu.SemaphoreType.DMA],
        compiler_params=params(),
        cost_estimate=pl.CostEstimate(flops=flops, bytes_accessed=12 << 20, transcendentals=0),
        name="attend",
    )(flip, soft, ids)


def backward_kernel(
    query_tokens,
    zw_ref,
    score_ref,
    many_ref,
    target_ref,
    list_ref,
    qn_ref,
    soft_ref,
    mixed_ref,
    query_ref,
    own_ref,
    core_ref,
    far_ref,
    cross_ref,
    grad_ref,
    accum_ref,
    list_smem,
    sem,
):
    copy = pltpu.make_async_copy(list_ref, list_smem, sem)
    copy.start()
    sources, group, _ = zw_ref.shape
    pass_count, share, width = own_ref.shape
    stride = group + row_pad
    count_row = list_ref.shape[0] - row_pad
    sums = zw_ref[0]
    for s in range(1, sources):
        sums = sums + zw_ref[s]
    many = many_ref[...]
    grads = many * jnp.exp(score_ref[...]) / sums[:, :1] - target_ref[...]
    for p in range(pass_count):
        grad_ref[p * stride : p * stride + group, :] = jnp.broadcast_to(
            grads[:, p : p + 1], (group, 128)
        )
        grad_ref[p * stride + group : (p + 1) * stride, :] = jnp.zeros((row_pad, 128), jnp.float32)
    accum_ref[...] = jnp.zeros(accum_ref.shape, jnp.float32)
    copy.wait()

    def query_rows(n):
        return pl.ds(pl.multiple_of(n * query_tokens, query_tokens), query_tokens)

    def pair_block(p, first, slot):
        ids = [list_smem[first + r, p] for r in range(block_pairs)]
        scales = [grad_ref[pl.ds(p * stride + n, 1), :] for n in ids]
        tile = jnp.concatenate(
            [
                (qn_ref[query_rows(n), :].astype(jnp.float32) * scale).astype(jnp.bfloat16)
                for n, scale in zip(ids, scales)
            ],
            0,
        )
        added = [
            accum_ref[query_rows(n), :]
            + mixed_ref[slot, r * query_tokens : (r + 1) * query_tokens, :].astype(jnp.float32)
            * scales[r]
            for r, n in enumerate(ids)
        ]
        for n, value in zip(ids, added):
            accum_ref[query_rows(n), :] = value
        return jnp.dot(soft_ref[slot], tile, preferred_element_type=jnp.float32)

    outs = (own_ref, core_ref, far_ref, cross_ref)

    def block(p):
        value = pair_block(p, 0, p).astype(jnp.bfloat16)
        for place, ref in enumerate(outs):
            ref[p] = value[place * share : (place + 1) * share]

    def extra(p, first, slot):
        value = pair_block(p, first, slot)
        for place, ref in enumerate(outs):
            piece = value[place * share : (place + 1) * share]
            ref[p] = (ref[p].astype(jnp.float32) + piece).astype(jnp.bfloat16)

    def step(p, carry):
        block(2 * p)
        block(2 * p + 1)
        return carry

    lax.fori_loop(0, pass_count // 2, step, 0)
    each_extra(pass_count, list_smem, count_row, extra)
    query_ref[...] = accum_ref[: group * query_tokens, :].astype(jnp.bfloat16)


def backward(zw, score, many, target, ids, qn, soft, mixed, pass_count, query_tokens, slices):
    sources, group, _ = zw.shape
    tokens = soft.shape[1]
    width = qn.shape[1]
    piece = jax.ShapeDtypeStruct((pass_count, tokens // slices, width), jnp.bfloat16)
    flops = 2 * pass_count * soft.shape[2] * tokens * width
    return pl.pallas_call(
        lambda *refs: backward_kernel(query_tokens, *refs),
        in_specs=[VMEM] * 8,
        out_specs=[VMEM] * 5,
        out_shape=[
            jax.ShapeDtypeStruct((group * query_tokens, width), jnp.bfloat16),
            piece,
            piece,
            piece,
            piece,
        ],
        scratch_shapes=[
            pltpu.VMEM((pass_count * (group + row_pad), 128), jnp.float32),
            pltpu.VMEM(((group + 1) * query_tokens, width), jnp.float32),
            pltpu.SMEM(ids.shape, jnp.int32),
            pltpu.SemaphoreType.DMA,
        ],
        compiler_params=params(),
        cost_estimate=pl.CostEstimate(flops=flops, bytes_accessed=16 << 20, transcendentals=0),
        name="backward",
    )(zw, score, many, target, ids, qn, soft, mixed)


def finish_kernel(raw_ref, *refs):
    out_ref = refs[-1]
    grad = refs[0][...].astype(jnp.float32)
    for ref in refs[1:-1]:
        grad = grad + ref[...].astype(jnp.float32)
    out_ref[...] = tangent(raw_ref[...], grad).astype(jnp.bfloat16)


def finish(raw, parts):
    shape = raw.shape
    step = math.gcd(shape[0], 8)
    spec = pl.BlockSpec((step,) + shape[1:], lambda i: (i, 0, 0))
    return pl.pallas_call(
        finish_kernel,
        grid=(shape[0] // step,),
        in_specs=[spec] * (1 + len(parts)),
        out_specs=spec,
        out_shape=jax.ShapeDtypeStruct(shape, jnp.bfloat16),
        compiler_params=params(),
        name="finish",
    )(raw, *parts)


def finish_queries_kernel(raw_ref, parts_ref, out_ref):
    grad = parts_ref[0].astype(jnp.float32)
    for s in range(1, parts_ref.shape[0]):
        grad = grad + parts_ref[s].astype(jnp.float32)
    out_ref[...] = tangent(raw_ref[...], grad).astype(jnp.bfloat16)


def finish_queries(raw, parts):
    return pl.pallas_call(
        finish_queries_kernel,
        in_specs=[VMEM, VMEM],
        out_specs=VMEM,
        out_shape=jax.ShapeDtypeStruct(raw.shape, jnp.bfloat16),
        compiler_params=params(),
        name="finish_queries",
    )(raw, parts)


def three_parts(values):
    high = lax.reduce_precision(values, 8, 7)
    rest = values - high
    middle = lax.reduce_precision(rest, 8, 7)
    return high, middle, rest - middle


def shards(queries, passages, candidates, teacher):
    query_count, query_tokens, width = queries.shape
    pass_count = passages.shape[0]
    cand_count = candidates.shape[1]
    sources = lax.axis_size("psg")
    slices = lax.axis_size("qry")
    rows = query_count * query_tokens

    high, middle, low = three_parts(teacher)
    main = jnp.concatenate(
        [
            (candidates // pass_count).astype(jnp.float32),
            (candidates % pass_count).astype(jnp.float32),
            high,
            middle,
        ],
        1,
    )
    low = jnp.pad(low, ((0, 8 - query_count), (0, 128 - cand_count)))
    main = jnp.pad(main, ((0, 8 - query_count), (0, 0)))
    packed = jnp.concatenate(
        [queries.reshape(rows, width), main.astype(jnp.bfloat16), low.astype(jnp.bfloat16)], 0
    )
    received = lax.all_to_all(
        jnp.broadcast_to(packed[None], (sources,) + packed.shape),
        "psg",
        split_axis=0,
        concat_axis=0,
        tiled=True,
    )
    norm, flip, own_raw = prepare_passages(passages, slices)
    soft, qn, score, many, target, ids, zw = forward(
        received, norm, cand_count, query_count, query_tokens
    )
    zw = lax.all_to_all(zw, "psg", split_axis=0, concat_axis=0, tiled=True)
    mixed = attend(flip, soft, ids)
    query_parts, own, core, far, cross = backward(
        zw, score, many, target, ids, qn, soft, mixed, pass_count, query_tokens, slices
    )

    near = [(k, k ^ 1) for k in range(slices)]
    away = [(k, k ^ 2) for k in range(slices)]
    cross = lax.ppermute(cross, "qry", near)
    far = (far.astype(jnp.float32) + cross.astype(jnp.float32)).astype(jnp.bfloat16)
    far = lax.ppermute(far, "qry", away)
    core = lax.ppermute(core, "qry", near)
    query_parts = lax.all_to_all(
        query_parts.reshape(sources, rows, width), "psg", split_axis=0, concat_axis=0, tiled=True
    )
    grad_queries = finish_queries(queries.reshape(rows, width), query_parts)
    grad_passages = finish(own_raw, [own, core, far])

    raised = jnp.exp(teacher)
    raised_sum = jnp.sum(raised, -1, keepdims=True)
    log_target = teacher - jnp.log(raised_sum)
    known = jnp.sum(raised / raised_sum * log_target, -1)
    mine = lax.dynamic_slice_in_dim(
        zw[:, :, :2], lax.axis_index("psg") * query_count, query_count, 1
    )
    mine = jnp.sum(mine, 0)
    pair_loss = known - mine[:, 1] + jnp.log(mine[:, 0])
    return (pair_loss, grad_queries.reshape(queries.shape), grad_passages)


def solution(mesh):
    placed = (
        P(("psg", "qry"), None, None),
        P("psg", None, None),
        P(("psg", "qry"), None),
        P(("psg", "qry"), None),
    )
    return jax.shard_map(
        shards,
        mesh=mesh,
        in_specs=placed,
        out_specs=(P(("psg", "qry")), P(("psg", "qry"), None, None), P("psg", "qry", None)),
        check_vma=False,
    )
```

time: 282 us -> 93.9 us (0.33)
  matrix products: 108 us -> 0 us
  blocking collectives: 31.3 us -> 0 us
  Pallas kernels: 0 us -> 29.5 us
  waiting for transfers between devices: 34.4 us -> 14.2 us
  local copies, waits for them, and re-layouts: 43.7 us -> 25.8 us
  other arithmetic: 19.4 us -> 3.95 us
  between operations: 14.2 us -> 0.73 us
  loops' own time: 10.5 us -> 0 us
    dot_general x50 -> x0, matrix products: 108 us -> none  [the longest x10 59.3 us: add_rows(): jnp.einsum('sr,sx->rx', placer, flat_delta, precision=lax.Precision.HIGHEST)]
    all_gather x1 -> x0, blocking collectives: 31.3 us -> none  [shards(): query_rows = lax.all_gather(query_norm, 'psg', axis=0, tiled=True)]
    while x42 -> x0, local copies, waits for them, and re-layouts: 30.2 us -> none
    pallas_call x0 -> x6, Pallas kernels: none -> 29.5 us  [the longest x1 10.6 us: forward(): pl.pallas_call(lambda *refs: forward_kernel(cand_count, query_count, quer...]
    unnamed x5 -> x18, local copies, waits for them, and re-layouts: 0.64 us -> 24.8 us
    reduce_scatter x1 -> x0, waiting for transfers between devices: 14.3 us -> none  [shards(): lax.psum_scatter(passage_accum.astype(jnp.bfloat16), 'qry', scatter_dimen...]
    mul x5 -> x0, other arithmetic: 12 us -> none  [the longest x1 6.32 us: shards(): unit_slice * jnp.sum(unit_slice * unit_passage_grad, -1, keepdims=True)]
    another operation x2 -> x0, loops' own time: 10.5 us -> none  [the longest x1 9.97 us: shards(): slot_scores = lax.map(forward_block, offsets).reshape(owner_count, capacity)]
  transfers between devices with their start and end apart: 5 -> 6, of which waited for: 4 -> 3; matrix products, arithmetic and copies ran while one was open for 4% -> 1% of each run, Pallas kernels for 0% -> 9%
where the time goes in v1:
time: 93.9 us; the launch traced here: 93.2 us
  Pallas kernels  29.5 us (31%)
  local copies, waits for them, and re-layouts  25.8 us (27%)
  starting transfers between devices  19 us (20%)
  waiting for transfers between devices  14.2 us (15%)
  other arithmetic  3.95 us (4%)
    unnamed x18, local copies, waits for them, and re-layouts  24.8 us
    pallas_call x1, Pallas kernels, forward(): pl.pallas_call(lambda *refs: forward_kernel(cand_count, query_count, quer...  10.6 us
    pallas_call x1, Pallas kernels, backward(): pl.pallas_call(lambda *refs: backward_kernel(query_tokens, *refs), in_spe...  8.45 us
    all_to_all x1, waiting for transfers between devices, shards(): lax.all_to_all(query_parts.reshape(sources, rows, width), 'psg', split_ax...  8.21 us
    all_to_all x1, starting transfers between devices, shards(): lax.all_to_all(jnp.broadcast_to(packed[None], (sources,) + packed.shape),...  7.28 us
    all_to_all x1, starting transfers between devices, shards(): lax.all_to_all(query_parts.reshape(sources, rows, width), 'psg', split_ax...  6.02 us
    pallas_call x1, Pallas kernels, attend(): pl.pallas_call(attend_kernel, in_specs=[VMEM] * 3, out_specs=VMEM, out_sh...  5.65 us
    all_to_all x1, waiting for transfers between devices, shards(): lax.all_to_all(jnp.broadcast_to(packed[None], (sources,) + packed.shape),...  4.63 us
  transfers between devices with their start and end apart: 6, of which 3 were waited for; matrix products, arithmetic and copies ran while one was open for 1% of the time, Pallas kernels for 9%

profile of v1, /device:TPU:0, one launch (start us, length us, event | category | flops | bytes accessed | tf_op | source)
XLA Modules:
  0.0 93.2 jit_solution(16443367124678313759)
XLA Ops:
  0.6 0.8 exponential_reduce_fusion
  2.1 0.9 fusion.15
  3.1 0.8 fusion.1
  4.6 7.3 %all-to-all-start = ((bf16[8,144,128]{2,1,0:T(8,128)(2,1)}), bf16[8,144,128]{2,1,0:T(8,128)(2,1)S(1)}, u32[]{:S(2)}, u32[]{:S(2)}) async-start(bf16[8,144,128]{2,1,0:T(8,128)(2,1)} %broadcast_in_dim.2), calls=%async_computation | async-start | bytes 589824 | tf_op jit(solution)/shard_map/all_to_all | solution.py:471
  11.9 1.6 %copy-done.5 = bf16[32,256,128]{2,1,0:T(8,128)(2,1)S(1)} copy-done((bf16[32,256,128]{2,1,0:T(8,128)(2,1)S(1)}, bf16[32,256,128]{2,1,0:T(8,128)(2,1)}, u32[]{:S(2)}) %copy-start.5) | copy-done | bytes 2097176
  13.5 2.1 %prepare_passages.1 = (bf16[32,256,128]{2,1,0:T(8,128)(2,1)S(1)}, bf16[32,128,256]{2,1,0:T(8,128)(2,1)S(1)}, bf16[32,64,128]{2,1,0:T(8,128)(2,1)S(1)}) custom-call(bf16[32,256,128]{2,1,0:T(8,128)(2,1)S(1)} %copy-done.5), custom_call_target="tpu_custom_call" | custom-call | flops 16777216 | bytes 6291456 | tf_op jit(solution)/shard_map/prepare_passages/pallas_call | solution.py:59
  15.6 1.3 %copy-done.7 = bf16[32,256,128]{2,1,0:T(8,128)(2,1)} copy-done((bf16[32,256,128]{2,1,0:T(8,128)(2,1)}, bf16[32,256,128]{2,1,0:T(8,128)(2,1)S(1)}, u32[]{:S(2)}) %copy-start.7) | copy-done | bytes 2097176
  16.9 4.6 %all-to-all-done.refs_0_ = bf16[8,144,128]{2,1,0:T(8,128)(2,1)S(1)} async-done(((bf16[8,144,128]{2,1,0:T(8,128)(2,1)}), bf16[8,144,128]{2,1,0:T(8,128)(2,1)S(1)}, u32[]{:S(2)}, u32[]{:S(2)}) %all-to-all-start) | async-done | bytes 294944 | tf_op jit(solution)/shard_map/all_to_all | solution.py:471
  21.5 1.6 %copy-done.8 = bf16[32,256,128]{2,1,0:T(8,128)(2,1)S(1)} copy-done((bf16[32,256,128]{2,1,0:T(8,128)(2,1)S(1)}, bf16[32,256,128]{2,1,0:T(8,128)(2,1)}, u32[]{:S(2)}) %copy-start.8) | copy-done | bytes 2097176
  23.1 10.6 %forward.1 = (bf16[52,256,512]{2,1,0:T(8,128)(2,1)S(1)}, bf16[1056,128]{1,0:T(8,128)(2,1)S(1)}, f32[32,128]{1,0:T(8,128)S(1)}, f32[32,128]{1,0:T(8,128)S(1)}, f3...) custom-call(bf16[8,144,128]{2,1,0:T(8,128)(2,1)S(1)} %all-to-all-done.refs_0_, ...), custom_call_target="tpu_custom_call" | custom-call | flops 1073741824 | bytes 12582912 | tf_op jit(solution)/shard_map/forward/pallas_call | solution.py:225
  33.7 4.9 %copy-done = bf16[52,256,512]{2,1,0:T(8,128)(2,1)} copy-done((bf16[52,256,512]{2,1,0:T(8,128)(2,1)}, bf16[52,256,512]{2,1,0:T(8,128)(2,1)S(1)}, u32[]{:S(2)}) %copy-start) | copy-done | bytes 13631512
  38.6 3.6 %all-to-all-start.1 = ((f32[8,32,128]{2,1,0:T(8,128)}), f32[8,32,128]{2,1,0:T(8,128)S(1)}, u32[]{:S(2)}, u32[]{:S(2)}) async-start(f32[8,32,128]{2,1,0:T(8,128)} %get-tuple-element.19), calls=%async_computation.1 | async-start | bytes 262144 | tf_op jit(solution)/shard_map/all_to_all | solution.py:482
  42.2 4.9 %copy-done.1 = bf16[52,256,512]{2,1,0:T(8,128)(2,1)S(1)} copy-done((bf16[52,256,512]{2,1,0:T(8,128)(2,1)S(1)}, bf16[52,256,512]{2,1,0:T(8,128)(2,1)}, u32[]{:S(2)}) %copy-start.1) | copy-done | bytes 13631512
  47.0 5.7 %attend.1.refs_7_ = bf16[52,512,128]{2,1,0:T(8,128)(2,1)S(1)} custom-call(bf16[32,128,256]{2,1,0:T(8,128)(2,1)S(1)} %get-tuple-element.26.flip_ref, bf16[52,256,512]{2,1,0:T(8,128)(2,1)S(1)} %copy-done.1, s32[40,128]{1,0:T(8,128)S(1)} %get-tuple-element.23.list_ref.refs_4_), custom_call_target="tpu_custom_call" | custom-call | flops 1073741824 | bytes 12582912 | tf_op jit(solution)/shard_map/attend/pallas_call | solution.py:274
  52.7 2.7 %copy-done.3 = bf16[52,512,128]{2,1,0:T(8,128)(2,1)} copy-done((bf16[52,512,128]{2,1,0:T(8,128)(2,1)}, bf16[52,512,128]{2,1,0:T(8,128)(2,1)S(1)}, u32[]{:S(2)}) %copy-start.3) | copy-done | bytes 6815768
  55.4 4.9 %copy-done.2 = bf16[52,256,512]{2,1,0:T(8,128)(2,1)S(1)} copy-done((bf16[52,256,512]{2,1,0:T(8,128)(2,1)S(1)}, bf16[52,256,512]{2,1,0:T(8,128)(2,1)}, u32[]{:S(2)}) %copy-start.2) | copy-done | bytes 13631512
  60.3 2.9 %copy-done.4 = bf16[52,512,128]{2,1,0:T(8,128)(2,1)S(1)} copy-done((bf16[52,512,128]{2,1,0:T(8,128)(2,1)S(1)}, bf16[52,512,128]{2,1,0:T(8,128)(2,1)}, u32[]{:S(2)}) %copy-start.4) | copy-done | bytes 6815768
  63.3 8.4 %backward.1 = (bf16[1024,128]{1,0:T(8,128)(2,1)}, bf16[32,64,128]{2,1,0:T(8,128)(2,1)S(1)}, bf16[32,64,128]{2,1,0:T(8,128)(2,1)}, bf16[32,64,128]{2,1,0:T(8,128)(2,1)S(1)}, bf16[32,64,128]{2,1,0:T(8,128)(2,1)S(1)}) custom-call(f32[8,32,128]{2,1,0:T(8,128)S(1)} %all-to-all-done.1.refs_0_, f32[32,128]{1,0:T(8,128)S(1)} %get-tuple-element.20.refs_1_, ...), custom_call_target="tpu_custom_call" | custom-call | flops 1073741824 | bytes 16777216 | tf_op jit(solution)/shard_map/backward/pallas_call | solution.py:377
  72.3 1.4 %collective-permute-done.1 = bf16[32,64,128]{2,1,0:T(8,128)(2,1)S(1)} collective-permute-done((bf16[32,64,128]{2,1,0:T(8,128)(2,1)S(1)}, bf16[32,64,128]{2,1,0:T(8,128)(2,1)S(1)}, u32[]{:S(2)}, u32[]{:S(2)}) %collective-permute-start.1) | collective-permute-done | bytes 524320 | tf_op jit(solution)/shard_map/ppermute | solution.py:490
  73.9 1.5 %collective-permute-start.2 = (bf16[32,64,128]{2,1,0:T(8,128)(2,1)S(1)}, bf16[32,64,128]{2,1,0:T(8,128)(2,1)S(1)}, u32[]{:S(2)}, u32[]{:S(2)}) collective-permute-start(bf16[32,64,128]{2,1,0:T(8,128)(2,1)S(1)} %add_convert_fusion), channel_id=1, source_target_pairs={{0,2},{1,3},{2,0},{3,1},{4,6},{5,7},{6,4},{7,5},{8,10},{9,11},{10,... | collective-permute-start | bytes 1572872 | tf_op jit(solution)/shard_map/ppermute | solution.py:492
  75.4 6.0 %all-to-all-start.2 = ((bf16[8,128,128]{2,1,0:T(8,128)(2,1)}), bf16[8,128,128]{2,1,0:T(8,128)(2,1)S(1)}, u32[]{:S(2)}, u32[]{:S(2)}) async-start(bf16[8,128,128]{2,1,0:T(8,128)(2,1)} %bitcast.1), calls=%async_computation.2 | async-start | bytes 524288 | tf_op jit(solution)/shard_map/all_to_all | solution.py:494
  82.2 8.2 %all-to-all-done.2.parts_ref = bf16[8,128,128]{2,1,0:T(8,128)(2,1)S(1)} async-done(((bf16[8,128,128]{2,1,0:T(8,128)(2,1)}), bf16[8,128,128]{2,1,0:T(8,128)(2,1)S(1)}, u32[]{:S(2)}, u32[]{:S(2)}) %all-to-all-start.2) | async-done | bytes 262176 | tf_op jit(solution)/shard_map/all_to_all | solution.py:494
  90.4 0.8 finish_queries.1
  91.2 2.0 %finish.1 = bf16[32,64,128]{2,1,0:T(8,128)(2,1)} custom-call(bf16[32,64,128]{2,1,0:T(8,128)(2,1)S(1)} %get-tuple-element.28.raw_ref, bf16[32,64,128]{2,1,0:T(8,128)(2,1)S(1)} %get-tuple-element.29.refs_0_, bf16[32,64,128]{2,1,0:T(8,128)(2,1)S(1)} %collective-permute-done.refs_1_, bf16[32,64,128]{2,1,0:T(8,128)(2,1)S(1)} %collective-permute-done.2.refs_2_), custom_call_target="tpu_custom_call" | custom-call | tf_op jit(solution)/shard_map/finish/pallas_call | solution.py:412
  (23 shorter events, 3.0 us)
Async XLA Ops:
  4.6 16.9 %all-to-all-start = ((bf16[8,144,128]{2,1,0:T(8,128)(2,1)}), bf16[8,144,128]{2,1,0:T(8,128)(2,1)S(1)}, u32[]{:S(2)}, u32[]{:S(2)}) async-start(bf16[8,144,128]{2,1,0:T(8,128)(2,1)} %broadcast_in_dim.2), calls=%async_computation | async-start | bytes 589824 | tf_op jit(solution)/shard_map/all_to_all | solution.py:471
  11.9 1.6 %copy-start.5 = (bf16[32,256,128]{2,1,0:T(8,128)(2,1)S(1)}, bf16[32,256,128]{2,1,0:T(8,128)(2,1)}, u32[]{:S(2)}) copy-start(bf16[32,256,128]{2,1,0:T(8,128)(2,1)} %refs_0_.1) | copy-start | bytes 6291460
  15.5 1.3 %copy-start.7 = (bf16[32,256,128]{2,1,0:T(8,128)(2,1)}, bf16[32,256,128]{2,1,0:T(8,128)(2,1)S(1)}, u32[]{:S(2)}) copy-start(bf16[32,256,128]{2,1,0:T(8,128)(2,1)S(1)} %get-tuple-element.18.refs_1_) | copy-start | bytes 6291460
  21.5 1.6 %copy-start.8 = (bf16[32,256,128]{2,1,0:T(8,128)(2,1)S(1)}, bf16[32,256,128]{2,1,0:T(8,128)(2,1)}, u32[]{:S(2)}) copy-start(bf16[32,256,128]{2,1,0:T(8,128)(2,1)} %copy-done.7) | copy-start | bytes 6291460
  33.7 4.9 %copy-start = (bf16[52,256,512]{2,1,0:T(8,128)(2,1)}, bf16[52,256,512]{2,1,0:T(8,128)(2,1)S(1)}, u32[]{:S(2)}) copy-start(bf16[52,256,512]{2,1,0:T(8,128)(2,1)S(1)} %get-tuple-element.25.soft_ref.refs_6_) | copy-start | bytes 40894468
  38.6 16.9 %all-to-all-start.1 = ((f32[8,32,128]{2,1,0:T(8,128)}), f32[8,32,128]{2,1,0:T(8,128)S(1)}, u32[]{:S(2)}, u32[]{:S(2)}) async-start(f32[8,32,128]{2,1,0:T(8,128)} %get-tuple-element.19), calls=%async_computation.1 | async-start | bytes 262144 | tf_op jit(solution)/shard_map/all_to_all | solution.py:482
  42.2 4.9 %copy-start.1 = (bf16[52,256,512]{2,1,0:T(8,128)(2,1)S(1)}, bf16[52,256,512]{2,1,0:T(8,128)(2,1)}, u32[]{:S(2)}) copy-start(bf16[52,256,512]{2,1,0:T(8,128)(2,1)} %copy-done) | copy-start | bytes 40894468
  52.7 2.7 %copy-start.3 = (bf16[52,512,128]{2,1,0:T(8,128)(2,1)}, bf16[52,512,128]{2,1,0:T(8,128)(2,1)S(1)}, u32[]{:S(2)}) copy-start(bf16[52,512,128]{2,1,0:T(8,128)(2,1)S(1)} %attend.1.refs_7_) | copy-start | bytes 20447236
  55.4 4.9 %copy-start.2 = (bf16[52,256,512]{2,1,0:T(8,128)(2,1)S(1)}, bf16[52,256,512]{2,1,0:T(8,128)(2,1)}, u32[]{:S(2)}) copy-start(bf16[52,256,512]{2,1,0:T(8,128)(2,1)} %copy-done) | copy-start | bytes 40894468
  60.3 2.9 %copy-start.4 = (bf16[52,512,128]{2,1,0:T(8,128)(2,1)S(1)}, bf16[52,512,128]{2,1,0:T(8,128)(2,1)}, u32[]{:S(2)}) copy-start(bf16[52,512,128]{2,1,0:T(8,128)(2,1)} %copy-done.3) | copy-start | bytes 20447236
  71.7 18.7 %copy-start.6 = (bf16[4,32,128]{2,1,0:T(8,128)(2,1)S(1)}, bf16[4,32,128]{2,1,0:T(8,128)(2,1)}, u32[]{:S(2)}) copy-start(bf16[4,32,128]{2,1,0:T(8,128)(2,1)} %param.4) | copy-start | bytes 98308
  71.7 2.0 %collective-permute-start.1 = (bf16[32,64,128]{2,1,0:T(8,128)(2,1)S(1)}, bf16[32,64,128]{2,1,0:T(8,128)(2,1)S(1)}, u32[]{:S(2)}, u32[]{:S(2)}) collective-permute-start(bf16[32,64,128]{2,1,0:T(8,128)(2,1)S(1)} %get-tuple-element.32), channel_id=1, source_target_pairs={{0,1},{1,0},{2,3},{3,2},{4,5},{5,4},{6,7},{7,6},{8,9},{9,8},{10,11... | collective-permute-start | bytes 1572872 | tf_op jit(solution)/shard_map/ppermute | solution.py:490
  71.8 19.4 %collective-permute-start = (bf16[32,64,128]{2,1,0:T(8,128)(2,1)}, bf16[32,64,128]{2,1,0:T(8,128)(2,1)S(1)}, u32[]{:S(2)}, u32[]{:S(2)}) collective-permute-start(bf16[32,64,128]{2,1,0:T(8,128)(2,1)} %get-tuple-element.30), channel_id=1, source_target_pairs={{0,1},{1,0},{2,3},{3,2},{4,5},{5,4},{6,7},{7,6},{8,9},{9,8},{10,11... | collective-permute-start | bytes 1572872 | tf_op jit(solution)/shard_map/ppermute | solution.py:493
  73.9 17.3 %collective-permute-start.2 = (bf16[32,64,128]{2,1,0:T(8,128)(2,1)S(1)}, bf16[32,64,128]{2,1,0:T(8,128)(2,1)S(1)}, u32[]{:S(2)}, u32[]{:S(2)}) collective-permute-start(bf16[32,64,128]{2,1,0:T(8,128)(2,1)S(1)} %add_convert_fusion), channel_id=1, source_target_pairs={{0,2},{1,3},{2,0},{3,1},{4,6},{5,7},{6,4},{7,5},{8,10},{9,11},{10,... | collective-permute-start | bytes 1572872 | tf_op jit(solution)/shard_map/ppermute | solution.py:492
  75.4 15.0 %all-to-all-start.2 = ((bf16[8,128,128]{2,1,0:T(8,128)(2,1)}), bf16[8,128,128]{2,1,0:T(8,128)(2,1)S(1)}, u32[]{:S(2)}, u32[]{:S(2)}) async-start(bf16[8,128,128]{2,1,0:T(8,128)(2,1)} %bitcast.1), calls=%async_computation.2 | async-start | bytes 524288 | tf_op jit(solution)/shard_map/all_to_all | solution.py:494

commit v2 on v1

v2 whole, which is shorter than its diff:
```python
import math

import jax
import jax.numpy as jnp
from jax import lax
from jax.experimental import pallas as pl
from jax.experimental.pallas import tpu as pltpu
from jax.sharding import PartitionSpec as P

epsilon = 1e-06
softness_scale = 0.05
block_pairs = 16
vmem_bytes = 44 << 20
row_pad = 8

VMEM = pl.BlockSpec(memory_space=pltpu.VMEM)
HBM = pl.BlockSpec(memory_space=pltpu.HBM)
unroll = 4


def in_hbm(array):
    return pltpu.with_memory_space_constraint(array, pltpu.HBM)


def params():
    return pltpu.CompilerParams(vmem_limit_bytes=vmem_bytes)


def unit_rows(values):
    widened = values.astype(jnp.float32)
    inverse = lax.rsqrt(jnp.sum(widened * widened, -1, keepdims=True) + epsilon)
    return widened * inverse, inverse


def round_bf16(values):
    return values.astype(jnp.bfloat16).astype(jnp.float32)


def pack_kernel(pass_count, *refs):
    sources, targets, out_ref, sems = refs[:3], refs[4:7], refs[3], refs[7]
    copies = [
        pltpu.make_async_copy(source, target, sems.at[i])
        for i, (source, target) in enumerate(zip(sources, targets))
    ]
    for copy in copies:
        copy.start()
    for copy in copies:
        copy.wait()
    queries_ref, candidates_ref, teacher_ref = targets
    query_count, cand_count = teacher_ref.shape
    ids = candidates_ref[...].astype(jnp.float32)
    owner = jnp.floor((ids + 0.5) * (1.0 / pass_count))
    values = teacher_ref[...]
    high = round_bf16(values)
    middle = round_bf16(values - high)
    low = values - high - middle
    main = jnp.concatenate([owner, ids - owner * pass_count, high, middle], 1)
    blank = jnp.zeros((8 - query_count, 128), jnp.float32)
    low = jnp.concatenate([low, jnp.zeros((query_count, 128 - cand_count), jnp.float32)], 1)
    extra = jnp.concatenate([main, blank, low, blank], 0).astype(jnp.bfloat16)
    rows = queries_ref.shape[0]
    for d in range(out_ref.shape[0]):
        out_ref[d, :rows, :] = queries_ref[...]
        out_ref[d, rows:, :] = extra


def pack(queries, candidates, teacher, sources, pass_count):
    rows, width = queries.shape
    return pl.pallas_call(
        lambda *refs: pack_kernel(pass_count, *refs),
        in_specs=[HBM] * 3,
        out_specs=VMEM,
        out_shape=jax.ShapeDtypeStruct((sources, rows + 16, width), jnp.bfloat16),
        scratch_shapes=[
            pltpu.VMEM(queries.shape, queries.dtype),
            pltpu.VMEM(candidates.shape, candidates.dtype),
            pltpu.VMEM(teacher.shape, teacher.dtype),
            pltpu.SemaphoreType.DMA((3,)),
        ],
        compiler_params=params(),
        name="pack",
    )(in_hbm(queries), in_hbm(candidates), in_hbm(teacher))


def lane_ids(shape):
    return lax.broadcasted_iota(jnp.int32, shape, len(shape) - 1)


def tangent(raw, grad):
    unit, inverse = unit_rows(raw)
    return inverse * (grad - unit * jnp.sum(unit * grad, -1, keepdims=True))


def passages_kernel(slices, in_ref, norm_ref, flip_ref, own_ref):
    count, tokens, _ = in_ref.shape
    share = tokens // slices
    me = lax.axis_index("qry")
    for item in range(count):
        for place in range(slices):
            start = pl.multiple_of((me ^ place) * share, share)
            raw = in_ref[item, pl.ds(start, share), :]
            if place == 0:
                own_ref[item] = raw
            norm_ref[item, pl.ds(place * share, share), :] = unit_rows(raw)[0].astype(
                jnp.bfloat16
            )
        flip_ref[item] = jnp.transpose(norm_ref[item], (1, 0))


def prepare_passages(passages, slices):
    count, tokens, width = passages.shape
    step = math.gcd(count, 8)
    share = tokens // slices
    return pl.pallas_call(
        lambda *refs: passages_kernel(slices, *refs),
        grid=(count // step,),
        in_specs=[pl.BlockSpec((step, tokens, width), lambda i: (i, 0, 0))],
        out_specs=[
            pl.BlockSpec((step, tokens, width), lambda i: (i, 0, 0)),
            pl.BlockSpec((step, width, tokens), lambda i: (i, 0, 0)),
            pl.BlockSpec((step, share, width), lambda i: (i, 0, 0)),
        ],
        out_shape=[
            jax.ShapeDtypeStruct((count, tokens, width), jnp.bfloat16),
            jax.ShapeDtypeStruct((count, width, tokens), jnp.bfloat16),
            jax.ShapeDtypeStruct((count, share, width), jnp.bfloat16),
        ],
        compiler_params=params(),
        cost_estimate=pl.CostEstimate(flops=1 << 24, bytes_accessed=6 << 20, transcendentals=0),
        name="prepare_passages",
    )(in_hbm(passages))


def each_extra(pass_count, list_smem, count_row, visit):
    def passage_step(p, used):
        pairs = list_smem[count_row, p]
        blocks = (pairs + block_pairs - 1) // block_pairs
        extra = jnp.maximum(blocks - 1, 0)

        def step(b, carry):
            visit(p, (b + 1) * block_pairs, pass_count + used + b)
            return carry

        lax.fori_loop(0, extra, step, 0)
        return used + extra

    return lax.fori_loop(0, pass_count, passage_step, jnp.int32(0))


def forward_kernel(
    cand_count,
    query_count,
    query_tokens,
    recv_ref,
    norm_hbm,
    soft_hbm,
    qn_ref,
    score_ref,
    many_ref,
    target_ref,
    list_ref,
    zw_ref,
    norm_ref,
    soft_ref,
    ext_ref,
    low_ref,
    sums_ref,
    list_smem,
    sem,
    norm_sem,
    soft_sems,
):
    norm_copy = pltpu.make_async_copy(norm_hbm, norm_ref, norm_sem)
    norm_copy.start()
    sources = recv_ref.shape[0]
    pass_count, tokens, width = norm_ref.shape
    group = sources * query_count
    rows = query_count * query_tokens
    stride = group + row_pad
    count_row = list_ref.shape[0] - row_pad
    owner = lax.axis_index("psg").astype(jnp.float32)
    for s in range(sources):
        packed = recv_ref[s, rows : rows + 16, :].astype(jnp.float32)
        ext_ref[s * query_count : (s + 1) * query_count, :] = packed[:query_count]
        low_ref[s * query_count : (s + 1) * query_count, :] = packed[8 : 8 + query_count]
        qn_ref[s * rows : (s + 1) * rows, :] = unit_rows(recv_ref[s, :rows, :])[0].astype(
            jnp.bfloat16
        )
    qn_ref[sources * rows :, :] = jnp.zeros((query_tokens, width), jnp.bfloat16)

    main = ext_ref[...]
    lanes = lane_ids(main.shape)
    lanes_float = lanes.astype(jnp.float32)
    live = lanes < cand_count
    local = pltpu.roll(main, 128 - cand_count, 1)
    logits = (
        pltpu.roll(main, 128 - 2 * cand_count, 1)
        + pltpu.roll(main, 128 - 3 * cand_count, 1)
        + low_ref[...]
    )
    raised = jnp.where(live, jnp.exp(logits), 0.0)
    target = raised / jnp.sum(raised, -1, keepdims=True)
    local = jnp.where(main == owner, local, -1.0)
    many = jnp.zeros(main.shape, jnp.float32)
    wanted = jnp.zeros(main.shape, jnp.float32)
    for c in range(cand_count):
        same = local[:, c : c + 1] == lanes_float
        many = many + jnp.where(same, 1.0, 0.0)
        wanted = wanted + jnp.where(same, target[:, c : c + 1], 0.0)
    many_ref[...] = many
    target_ref[...] = wanted
    active = many > 0.0
    lower = (
        lax.broadcasted_iota(jnp.int32, (group, group), 0)
        > lax.broadcasted_iota(jnp.int32, (group, group), 1)
    ).astype(jnp.bfloat16)
    active_value = jnp.where(active, 1.0, 0.0)
    rank = jnp.dot(lower, active_value.astype(jnp.bfloat16), preferred_element_type=jnp.float32)
    rank = jnp.where(active, rank, -1.0)
    less = lax.broadcasted_iota(jnp.int32, main.shape, 0).astype(jnp.float32) - group
    for k in range(count_row):
        found = jnp.sum(jnp.where(rank == k, less, 0.0), 0, keepdims=True) + group
        list_ref[k : k + 1, :] = found.astype(jnp.int32)
    total = jnp.sum(active_value, 0, keepdims=True).astype(jnp.int32)
    list_ref[count_row:, :] = jnp.broadcast_to(total, (row_pad, 128))
    copy = pltpu.make_async_copy(list_ref, list_smem, sem)
    copy.start()
    norm_copy.wait()
    copy.wait()

    half = block_pairs // 2

    def soft_copy(slot):
        return pltpu.make_async_copy(soft_ref.at[slot], soft_hbm.at[slot], soft_sems.at[slot])

    def block(p, first, slot):
        passage = norm_ref[p]
        for h in range(2):
            ids = [list_smem[first + h * half + r, p] for r in range(half)]
            tile = jnp.concatenate(
                [
                    qn_ref[pl.ds(pl.multiple_of(n * query_tokens, query_tokens), query_tokens), :]
                    for n in ids
                ],
                0,
            )
            dots = lax.dot_general(
                passage, tile, (((1,), (1,)), ((), ())), preferred_element_type=jnp.float32
            )
            power = jnp.exp2(dots * (math.log2(math.e) / softness_scale))
            sums = jnp.sum(power, 0, keepdims=True)
            span = half * query_tokens
            soft_ref[slot, :, h * span : (h + 1) * span] = (power * (1.0 / sums)).astype(
                jnp.bfloat16
            )
            for r in range(half):
                sums_ref[pl.ds(p * stride + ids[r], 1), :query_tokens] = sums[
                    :, r * query_tokens : (r + 1) * query_tokens
                ]

    def step(p, carry):
        for u in range(unroll):
            block(unroll * p + u, 0, unroll * p + u)
        for u in range(unroll):
            soft_copy(unroll * p + u).start()
        return carry

    def extra(p, first, slot):
        block(p, first, slot)
        soft_copy(slot).start()

    lax.fori_loop(0, pass_count // unroll, step, 0)
    used = each_extra(pass_count, list_smem, count_row, extra)

    scores = jnp.zeros(main.shape, jnp.float32)
    for p in range(pass_count):
        logs = jnp.log(sums_ref[p * stride : p * stride + group, :])
        value = softness_scale * jnp.sum(
            jnp.where(lanes < query_tokens, logs, 0.0), -1, keepdims=True
        )
        scores = jnp.where(lanes == p, value, scores)
    scores = jnp.where(active, scores, 0.0)
    score_ref[...] = scores
    mass = jnp.sum(many * jnp.exp(scores), -1, keepdims=True)
    agreed = jnp.sum(wanted * scores, -1, keepdims=True)
    message = jnp.where(lanes == 0, mass, jnp.where(lanes == 1, agreed, 0.0))
    for s in range(sources):
        zw_ref[s] = message

    def drain(slot, carry):
        soft_copy(slot).wait()
        return carry

    lax.fori_loop(0, pass_count + used, drain, 0)


def forward(received, norm, cand_count, query_count, query_tokens):
    sources = received.shape[0]
    pass_count, tokens, width = norm.shape
    group = sources * query_count
    capacity = max(2, -(-5 * query_count * cand_count // (2 * sources)))
    blocks = pass_count + sources * capacity // block_pairs
    list_rows = -(-group // block_pairs) * block_pairs + row_pad
    rows = query_count * query_tokens
    soft_shape = (blocks, tokens, block_pairs * query_tokens)
    flops = 2 * pass_count * block_pairs * query_tokens * tokens * width
    return pl.pallas_call(
        lambda *refs: forward_kernel(cand_count, query_count, query_tokens, *refs),
        in_specs=[VMEM, HBM],
        out_specs=[HBM] + [VMEM] * 6,
        out_shape=[
            pltpu.HBM(soft_shape, jnp.bfloat16),
            jax.ShapeDtypeStruct((sources * rows + query_tokens, width), jnp.bfloat16),
            jax.ShapeDtypeStruct((group, 128), jnp.float32),
            jax.ShapeDtypeStruct((group, 128), jnp.float32),
            jax.ShapeDtypeStruct((group, 128), jnp.float32),
            jax.ShapeDtypeStruct((list_rows, 128), jnp.int32),
            jax.ShapeDtypeStruct((sources, group, 128), jnp.float32),
        ],
        scratch_shapes=[
            pltpu.VMEM(norm.shape, jnp.bfloat16),
            pltpu.VMEM(soft_shape, jnp.bfloat16),
            pltpu.VMEM((group, 128), jnp.float32),
            pltpu.VMEM((group, 128), jnp.float32),
            pltpu.VMEM((pass_count * (group + row_pad), 128), jnp.float32),
            pltpu.SMEM((list_rows, 128), jnp.int32),
            pltpu.SemaphoreType.DMA,
            pltpu.SemaphoreType.DMA,
            pltpu.SemaphoreType.DMA((blocks,)),
        ],
        compiler_params=params(),
        cost_estimate=pl.CostEstimate(flops=flops, bytes_accessed=12 << 20, transcendentals=1 << 22),
        name="forward",
    )(received, in_hbm(norm))


def spread(ref, values, pass_count, stride):
    group = values.shape[0]
    for p in range(pass_count):
        ref[p * stride : p * stride + group, :] = jnp.broadcast_to(
            values[:, p : p + 1], (group, 128)
        )
        ref[p * stride + group : (p + 1) * stride, :] = jnp.zeros((stride - group, 128), jnp.float32)


def attend_kernel(
    query_tokens,
    flip_hbm,
    soft_hbm,
    list_ref,
    score_ref,
    many_ref,
    target_ref,
    raised_ref,
    wanted_ref,
    flip_ref,
    soft_ref,
    raised_rows,
    wanted_rows,
    raised_sum,
    wanted_sum,
    list_smem,
    sem,
    flip_sem,
    soft_sems,
):
    pass_count = flip_ref.shape[0]
    group = score_ref.shape[0]
    stride = group + row_pad
    list_copy = pltpu.make_async_copy(list_ref, list_smem, sem)
    list_copy.start()
    flip_copy = pltpu.make_async_copy(flip_hbm, flip_ref, flip_sem)
    flip_copy.start()

    def soft_copy(slot):
        return pltpu.make_async_copy(soft_hbm.at[slot], soft_ref.at[slot], soft_sems.at[slot])

    def fetch(slot, carry):
        soft_copy(slot).start()
        return carry

    lax.fori_loop(0, pass_count, fetch, 0)
    spread(raised_rows, many_ref[...] * jnp.exp(score_ref[...]), pass_count, stride)
    spread(wanted_rows, target_ref[...], pass_count, stride)
    raised_sum[...] = jnp.zeros(raised_sum.shape, jnp.float32)
    wanted_sum[...] = jnp.zeros(wanted_sum.shape, jnp.float32)
    list_copy.wait()
    flip_copy.wait()

    def block(p, first, slot):
        mixed = jnp.dot(flip_ref[p], soft_ref[slot], preferred_element_type=jnp.float32)
        mixed = jnp.transpose(mixed, (1, 0))
        ids = [list_smem[first + r, p] for r in range(block_pairs)]
        places = [pl.ds(pl.multiple_of(n * query_tokens, query_tokens), query_tokens) for n in ids]
        for total, rows in ((raised_sum, raised_rows), (wanted_sum, wanted_rows)):
            added = [
                total[place, :]
                + mixed[r * query_tokens : (r + 1) * query_tokens]
                * rows[pl.ds(p * stride + ids[r], 1), :]
                for r, place in enumerate(places)
            ]
            for place, value in zip(places, added):
                total[place, :] = value

    def step(p, carry):
        for u in range(unroll):
            soft_copy(unroll * p + u).wait()
        for u in range(unroll):
            block(unroll * p + u, 0, unroll * p + u)
        return carry

    def extra(p, first, slot):
        soft_copy(slot).start()
        soft_copy(slot).wait()
        block(p, first, slot)

    lax.fori_loop(0, pass_count // unroll, step, 0)
    each_extra(pass_count, list_smem, list_ref.shape[0] - row_pad, extra)
    raised_ref[...] = raised_sum[: group * query_tokens, :]
    wanted_ref[...] = wanted_sum[: group * query_tokens, :]


def attend(flip, soft, ids, score, many, target, query_tokens):
    blocks, tokens, columns = soft.shape
    pass_count, width, _ = flip.shape
    group = score.shape[0]
    flops = 2 * pass_count * columns * tokens * width
    total = jax.ShapeDtypeStruct((group * query_tokens, width), jnp.float32)
    rows = pltpu.VMEM((pass_count * (group + row_pad), 128), jnp.float32)
    padded = pltpu.VMEM(((group + 1) * query_tokens, width), jnp.float32)
    return pl.pallas_call(
        lambda *refs: attend_kernel(query_tokens, *refs),
        in_specs=[HBM, HBM] + [VMEM] * 4,
        out_specs=[VMEM] * 2,
        out_shape=[total, total],
        scratch_shapes=[
            pltpu.VMEM(flip.shape, jnp.bfloat16),
            pltpu.VMEM(soft.shape, jnp.bfloat16),
            rows,
            rows,
            padded,
            padded,
            pltpu.SMEM(ids.shape, jnp.int32),
            pltpu.SemaphoreType.DMA,
            pltpu.SemaphoreType.DMA,
            pltpu.SemaphoreType.DMA((blocks,)),
        ],
        compiler_params=params(),
        cost_estimate=pl.CostEstimate(flops=flops, bytes_accessed=12 << 20, transcendentals=0),
        name="attend",
    )(in_hbm(flip), in_hbm(soft), ids, score, many, target)


def halving_order(count):
    order = [0]
    bit = count // 2
    while bit:
        order = order + [x | bit for x in order]
        bit //= 2
    return order


def query_kernel(
    query_tokens,
    zw_ref,
    score_ref,
    many_ref,
    target_ref,
    raised_ref,
    wanted_ref,
    keep_ref,
    send_ref,
    grads_ref,
    scale_ref,
    query_ref,
):
    sources, group, _ = zw_ref.shape
    sums = zw_ref[0]
    for s in range(1, sources):
        sums = sums + zw_ref[s]
    inverse = 1.0 / sums[:, :1]
    grads_ref[...] = many_ref[...] * jnp.exp(score_ref[...]) * inverse - target_ref[...]
    scale_ref[...] = jnp.broadcast_to(inverse, scale_ref.shape)
    for n in range(group):
        place = pl.ds(n * query_tokens, query_tokens)
        query_ref[place, :] = (
            raised_ref[place, :] * scale_ref[n : n + 1, :] - wanted_ref[place, :]
        ).astype(jnp.bfloat16)
    me = lax.axis_index("psg")
    rows = group // sources * query_tokens
    half = keep_ref.shape[0]
    for place, d in enumerate(halving_order(sources)):
        start = pl.multiple_of((me ^ d) * rows, rows)
        value = query_ref[pl.ds(start, rows), :]
        if place < half:
            keep_ref[place] = value
        else:
            send_ref[place - half] = value


def query_backward(zw, score, many, target, raised, wanted):
    sources, group, _ = zw.shape
    rows, width = raised.shape
    part = jax.ShapeDtypeStruct((sources // 2, rows // sources, width), jnp.bfloat16)
    return pl.pallas_call(
        lambda *refs: query_kernel(rows // group, *refs),
        in_specs=[VMEM] * 6,
        out_specs=[VMEM] * 3,
        out_shape=[part, part, jax.ShapeDtypeStruct((group, 128), jnp.float32)],
        scratch_shapes=[
            pltpu.VMEM((group, 128), jnp.float32),
            pltpu.VMEM((rows, width), jnp.bfloat16),
        ],
        compiler_params=params(),
        name="query_backward",
    )(zw, score, many, target, raised, wanted)


def passage_kernel(
    query_tokens,
    list_ref,
    grads_ref,
    qn_ref,
    soft_hbm,
    own_ref,
    core_ref,
    far_ref,
    cross_ref,
    soft_ref,
    grad_ref,
    list_smem,
    sem,
    soft_sems,
):
    list_copy = pltpu.make_async_copy(list_ref, list_smem, sem)
    list_copy.start()
    pass_count, share, width = own_ref.shape
    stride = grads_ref.shape[0] + row_pad
    count_row = list_ref.shape[0] - row_pad

    def soft_copy(slot):
        return pltpu.make_async_copy(soft_hbm.at[slot], soft_ref.at[slot], soft_sems.at[slot])

    def fetch(slot, carry):
        soft_copy(slot).start()
        return carry

    lax.fori_loop(0, pass_count, fetch, 0)
    spread(grad_ref, grads_ref[...], pass_count, stride)
    list_copy.wait()

    def product(p, first, slot):
        ids = [list_smem[first + r, p] for r in range(block_pairs)]
        tile = jnp.concatenate(
            [
                (
                    qn_ref[
                        pl.ds(pl.multiple_of(n * query_tokens, query_tokens), query_tokens), :
                    ].astype(jnp.float32)
                    * grad_ref[pl.ds(p * stride + n, 1), :]
                ).astype(jnp.bfloat16)
                for n in ids
            ],
            0,
        )
        return jnp.dot(soft_ref[slot], tile, preferred_element_type=jnp.float32)

    outs = (own_ref, core_ref, far_ref, cross_ref)

    def step(p, carry):
        for u in range(unroll):
            soft_copy(unroll * p + u).wait()
        for u in range(unroll):
            value = product(unroll * p + u, 0, unroll * p + u).astype(jnp.bfloat16)
            for place, ref in enumerate(outs):
                ref[unroll * p + u] = value[place * share : (place + 1) * share]
        return carry

    def extra(p, first, slot):
        soft_copy(slot).start()
        soft_copy(slot).wait()
        value = product(p, first, slot)
        for place, ref in enumerate(outs):
            piece = value[place * share : (place + 1) * share]
            ref[p] = (ref[p].astype(jnp.float32) + piece).astype(jnp.bfloat16)

    lax.fori_loop(0, pass_count // unroll, step, 0)
    each_extra(pass_count, list_smem, count_row, extra)


def passage_backward(ids, grads, qn, soft, pass_count, query_tokens, slices):
    tokens = soft.shape[1]
    width = qn.shape[1]
    piece = jax.ShapeDtypeStruct((pass_count, tokens // slices, width), jnp.bfloat16)
    flops = 2 * pass_count * soft.shape[2] * tokens * width
    return pl.pallas_call(
        lambda *refs: passage_kernel(query_tokens, *refs),
        in_specs=[VMEM] * 3 + [HBM],
        out_specs=[VMEM] * 4,
        out_shape=[piece] * 4,
        scratch_shapes=[
            pltpu.VMEM(soft.shape, jnp.bfloat16),
            pltpu.VMEM((pass_count * (grads.shape[0] + row_pad), 128), jnp.float32),
            pltpu.SMEM(ids.shape, jnp.int32),
            pltpu.SemaphoreType.DMA,
            pltpu.SemaphoreType.DMA((soft.shape[0],)),
        ],
        compiler_params=params(),
        cost_estimate=pl.CostEstimate(flops=flops, bytes_accessed=12 << 20, transcendentals=0),
        name="passage_backward",
    )(ids, grads, qn, in_hbm(soft))


def finish_kernel(raw_ref, *refs):
    out_ref = refs[-1]
    grad = refs[0][...].astype(jnp.float32)
    for ref in refs[1:-1]:
        grad = grad + ref[...].astype(jnp.float32)
    out_ref[...] = tangent(raw_ref[...], grad).astype(jnp.bfloat16)


def finish(raw, parts):
    shape = raw.shape
    step = math.gcd(shape[0], 8)
    spec = pl.BlockSpec((step,) + shape[1:], lambda i: (i, 0, 0))
    return pl.pallas_call(
        finish_kernel,
        grid=(shape[0] // step,),
        in_specs=[spec] * (1 + len(parts)),
        out_specs=spec,
        out_shape=jax.ShapeDtypeStruct(shape, jnp.bfloat16),
        compiler_params=params(),
        name="finish",
    )(raw, *parts)


def finish_queries(raw, parts):
    return pl.pallas_call(
        finish_kernel,
        in_specs=[VMEM] * (1 + len(parts)),
        out_specs=VMEM,
        out_shape=jax.ShapeDtypeStruct(raw.shape, jnp.bfloat16),
        compiler_params=params(),
        name="finish_queries",
    )(raw, *parts)


def shards(queries, passages, candidates, teacher):
    query_count, query_tokens, width = queries.shape
    pass_count = passages.shape[0]
    cand_count = candidates.shape[1]
    sources = lax.axis_size("psg")
    slices = lax.axis_size("qry")
    rows = query_count * query_tokens

    received = lax.all_to_all(
        pack(queries.reshape(rows, width), candidates, teacher, sources, pass_count),
        "psg",
        split_axis=0,
        concat_axis=0,
        tiled=True,
    )
    norm, flip, own_raw = prepare_passages(passages, slices)
    soft, qn, score, many, target, ids, zw = forward(
        received, norm, cand_count, query_count, query_tokens
    )
    zw = lax.all_to_all(zw, "psg", split_axis=0, concat_axis=0, tiled=True)
    raised_sum, wanted_sum = attend(flip, soft, ids, score, many, target, query_tokens)
    keep, send, grads = query_backward(zw, score, many, target, raised_sum, wanted_sum)
    bit = 1
    while bit < sources:
        swap = [(i, i ^ bit) for i in range(sources)]
        send = lax.ppermute(send, "psg", swap)
        if bit * 2 < sources:
            total = keep.astype(jnp.float32) + send.astype(jnp.float32)
            half = total.shape[0] // 2
            keep, send = total[:half], total[half:].astype(jnp.bfloat16)
        bit *= 2
    grad_queries = finish_queries(queries.reshape(rows, width), [keep[0], send[0]])

    own, core, far, cross = passage_backward(
        ids, grads, qn, soft, pass_count, query_tokens, slices
    )
    near = [(k, k ^ 1) for k in range(slices)]
    away = [(k, k ^ 2) for k in range(slices)]
    cross = lax.ppermute(cross, "qry", near)
    far = (far.astype(jnp.float32) + cross.astype(jnp.float32)).astype(jnp.bfloat16)
    far = lax.ppermute(far, "qry", away)
    core = lax.ppermute(core, "qry", near)
    grad_passages = finish(own_raw, [own, core, far])

    raised = jnp.exp(teacher)
    raised_sum = jnp.sum(raised, -1, keepdims=True)
    log_target = teacher - jnp.log(raised_sum)
    known = jnp.sum(raised / raised_sum * log_target, -1)
    mine = lax.dynamic_slice_in_dim(
        zw[:, :, :2], lax.axis_index("psg") * query_count, query_count, 1
    )
    mine = jnp.sum(mine, 0)
    pair_loss = known - mine[:, 1] + jnp.log(mine[:, 0])
    return (pair_loss, grad_queries.reshape(queries.shape), grad_passages)


def solution(mesh):
    placed = (
        P(("psg", "qry"), None, None),
        P("psg", None, None),
        P(("psg", "qry"), None),
        P(("psg", "qry"), None),
    )
    return jax.shard_map(
        shards,
        mesh=mesh,
        in_specs=placed,
        out_specs=(P(("psg", "qry")), P(("psg", "qry"), None, None), P("psg", "qry", None)),
        check_vma=False,
    )
```

time: 93.9 us -> 72.7 us (0.77)
  local copies, waits for them, and re-layouts: 25.8 us -> 2.83 us
  Pallas kernels: 29.5 us -> 32.6 us
  other arithmetic: 3.95 us -> 2.1 us
    unnamed x18 -> x8, local copies, waits for them, and re-layouts: 24.8 us -> 2.62 us
    all_to_all x2 -> x1, waiting for transfers between devices: 12.8 us -> 3.33 us  [shards(): lax.all_to_all(pack(queries.reshape(rows, width), candidates, teacher, so...]
    ppermute x0 -> x3, starting transfers between devices: none -> 6.29 us  [shards(): send = lax.ppermute(send, 'psg', swap)]
    all_to_all x2 -> x1, starting transfers between devices: 13.3 us -> 7.29 us  [shards(): lax.all_to_all(pack(queries.reshape(rows, width), candidates, teacher, so...]
    ppermute x0 -> x3, waiting for transfers between devices: none -> 5.93 us  [shards(): send = lax.ppermute(send, 'psg', swap)]
    ppermute x1, waiting for transfers between devices: 0.01 us -> 5.53 us  [shards(): far = lax.ppermute(far, 'qry', away)]
    pallas_call x3 -> x5, Pallas kernels: 14.9 us -> 17.2 us  [the longest x1 8.44 us: attend(): pl.pallas_call(lambda *refs: attend_kernel(query_tokens, *refs), in_specs...]
    pallas_call x1, Pallas kernels: 2.05 us -> 3.67 us  [prepare_passages(): pl.pallas_call(lambda *refs: passages_kernel(slices, *refs), grid=(count...]
  transfers between devices with their start and end apart: 6 -> 8, of which waited for: 3 -> 4; matrix products, arithmetic and copies ran while one was open for 1% -> 3% of each run, Pallas kernels for 9% -> 18%
where the time goes in v2:
time: 72.7 us; the launch traced here: 72.2 us
  Pallas kernels  32.6 us (45%)
  starting transfers between devices  19.1 us (26%)
  waiting for transfers between devices  14.8 us (20%)
  local copies, waits for them, and re-layouts  2.83 us (4%)
  other arithmetic  2.1 us (3%)
  between operations  0.77 us (1%)
    pallas_call x1, Pallas kernels, forward(): pl.pallas_call(lambda *refs: forward_kernel(cand_count, query_count, quer...  9.73 us
    pallas_call x1, Pallas kernels, attend(): pl.pallas_call(lambda *refs: attend_kernel(query_tokens, *refs), in_specs...  8.44 us
    all_to_all x1, starting transfers between devices, shards(): lax.all_to_all(pack(queries.reshape(rows, width), candidates, teacher, so...  7.29 us
    ppermute x3, starting transfers between devices, shards(): send = lax.ppermute(send, 'psg', swap)  6.29 us
    pallas_call x1, Pallas kernels, passage_backward(): pl.pallas_call(lambda *refs: passage_kernel(query_tokens, *refs), in_spec...  6.17 us
    ppermute x3, waiting for transfers between devices, shards(): send = lax.ppermute(send, 'psg', swap)  5.93 us
    ppermute x1, waiting for transfers between devices, shards(): far = lax.ppermute(far, 'qry', away)  5.53 us
    pallas_call x1, Pallas kernels, prepare_passages(): pl.pallas_call(lambda *refs: passages_kernel(slices, *refs), grid=(count...  3.67 us
  transfers between devices with their start and end apart: 8, of which 4 were waited for; matrix products, arithmetic and copies ran while one was open for 3% of the time, Pallas kernels for 18%

profile of v2, /device:TPU:0, one launch (start us, length us, event | category | flops | bytes accessed | tf_op | source)
XLA Modules:
  0.0 72.2 jit_solution(4595506223313000929)
XLA Ops:
  0.6 1.6 %pack.1 = bf16[8,144,128]{2,1,0:T(8,128)(2,1)} custom-call(bf16[128,128]{1,0:T(8,128)(2,1)} %bitcast.7, s32[4,32]{1,0:T(4,128)} %refs_1_.1, f32[4,32]{1,0:T(4,128)} %refs_2_.1), custom_call_target="tpu_custom_call" | custom-call | tf_op jit(solution)/shard_map/pack/pallas_call | solution.py:69
  2.2 7.3 %all-to-all-start = ((bf16[8,144,128]{2,1,0:T(8,128)(2,1)}), bf16[8,144,128]{2,1,0:T(8,128)(2,1)S(1)}, u32[]{:S(2)}, u32[]{:S(2)}) async-start(bf16[8,144,128]{2,1,0:T(8,128)(2,1)} %pack.1), calls=%async_computation | async-start | bytes 589824 | tf_op jit(solution)/shard_map/all_to_all | solution.py:656
  9.5 3.7 %prepare_passages.1 = (bf16[32,256,128]{2,1,0:T(8,128)(2,1)S(1)}, bf16[32,128,256]{2,1,0:T(8,128)(2,1)S(1)}, bf16[32,64,128]{2,1,0:T(8,128)(2,1)S(1)}) custom-call(bf16[32,256,128]{2,1,0:T(8,128)(2,1)} %refs_0_.1), custom_call_target="tpu_custom_call" | custom-call | flops 16777216 | bytes 6291456 | tf_op jit(solution)/shard_map/prepare_passages/pallas_call | solution.py:114
  13.2 1.3 %copy-done = bf16[32,128,256]{2,1,0:T(8,128)(2,1)} copy-done((bf16[32,128,256]{2,1,0:T(8,128)(2,1)}, bf16[32,128,256]{2,1,0:T(8,128)(2,1)S(1)}, u32[]{:S(2)}) %copy-start) | copy-done | bytes 2097176
  14.5 1.3 %copy-done.2 = bf16[32,256,128]{2,1,0:T(8,128)(2,1)} copy-done((bf16[32,256,128]{2,1,0:T(8,128)(2,1)}, bf16[32,256,128]{2,1,0:T(8,128)(2,1)S(1)}, u32[]{:S(2)}) %copy-start.2) | copy-done | bytes 2097176
  15.8 3.3 %all-to-all-done.refs_0_ = bf16[8,144,128]{2,1,0:T(8,128)(2,1)S(1)} async-done(((bf16[8,144,128]{2,1,0:T(8,128)(2,1)}), bf16[8,144,128]{2,1,0:T(8,128)(2,1)S(1)}, u32[]{:S(2)}, u32[]{:S(2)}) %all-to-all-start) | async-done | bytes 294944 | tf_op jit(solution)/shard_map/all_to_all | solution.py:656
  19.1 9.7 %forward.1 = (bf16[52,256,512]{2,1,0:T(8,128)(2,1)}, bf16[1056,128]{1,0:T(8,128)(2,1)S(1)}, f32[32,128]{1,0:T(8,128)S(1)}, f32[32,128]{1,0:T(8,128)S(1)}, f32[32...) custom-call(bf16[8,144,128]{2,1,0:T(8,128)(2,1)S(1)} %all-to-all-done.refs_0_, ...), custom_call_target="tpu_custom_call" | custom-call | flops 1073741824 | bytes 12582912 | tf_op jit(solution)/shard_map/forward/pallas_call | solution.py:307
  28.9 3.6 %all-to-all-start.1 = ((f32[8,32,128]{2,1,0:T(8,128)}), f32[8,32,128]{2,1,0:T(8,128)S(1)}, u32[]{:S(2)}, u32[]{:S(2)}) async-start(f32[8,32,128]{2,1,0:T(8,128)} %get-tuple-element.23), calls=%async_computation.1 | async-start | bytes 262144 | tf_op jit(solution)/shard_map/all_to_all | solution.py:667
  32.5 8.4 %attend.1 = (f32[1024,128]{1,0:T(8,128)S(1)}, f32[1024,128]{1,0:T(8,128)S(1)}) custom-call(bf16[32,128,256]{2,1,0:T(8,128)(2,1)} %copy-done, bf16[52,256,512]{2,1,0:T(8,128)(2,1)} %get-tuple-element.28.refs_1_.refs_3_, s32[40,128]{1,0:T(8,128)S(1)} %get-tuple-element.29.refs_2_.refs_0_, f32[32,128]{1,0:T(8,128)S(1)} %get-tuple-element.24.refs_3_.refs_1_, ...), custom_call_target="tpu_custom_call" | custom-call | flops 1073741824 | bytes 12582912 | tf_op jit(solution)/shard_map/attend/pallas_call | solution.py:431
  41.1 6.2 %passage_backward.1 = (bf16[32,64,128]{2,1,0:T(8,128)(2,1)S(1)}, bf16[32,64,128]{2,1,0:T(8,128)(2,1)S(1)}, bf16[32,64,128]{2,1,0:T(8,128)(2,1)S(1)}, bf16[32,64,128]{2,1,0:T(8,128)(2,1)S(1)}) custom-call(s32[40,128]{1,0:T(8,128)S(1)} %get-tuple-element.29.refs_2_.refs_0_, f32[32,128]{1,0:T(8,128)S(1)} %get-tuple-element.35.refs_1_, ...), custom_call_target="tpu_custom_call" | custom-call | flops 1073741824 | bytes 12582912 | tf_op jit(solution)/shard_map/passage_backward/pallas_call | solution.py:596
  47.5 2.1 %collective-permute-start = (bf16[4,128,128]{2,1,0:T(8,128)(2,1)S(1)}, bf16[4,128,128]{2,1,0:T(8,128)(2,1)S(1)}, u32[]{:S(2)}, u32[]{:S(2)}) collective-permute-start(bf16[4,128,128]{2,1,0:T(8,128)(2,1)S(1)} %get-tuple-element.33), channel_id=1, source_target_pairs={{0,4},{4,0},{8,12},{12,8},{16,20},{20,16},{24,28},{28,24},{1,5},{5... | collective-permute-start | bytes 393224 | tf_op jit(solution)/shard_map/ppermute | solution.py:673
  49.6 0.2 fusion
  49.8 0.3 collective-permute-start.3
  50.1 0.2 slice_reduce_fusion
  50.2 3.5 %collective-permute-done = bf16[4,128,128]{2,1,0:T(8,128)(2,1)S(1)} collective-permute-done((bf16[4,128,128]{2,1,0:T(8,128)(2,1)S(1)}, bf16[4,128,128]{2,1,0:T(8,128)(2,1)S(1)}, u32[]{:S(2)}, u32[]{:S(2)}) %collective-permute-start) | collective-permute-done | bytes 131104 | tf_op jit(solution)/shard_map/ppermute | solution.py:673
  53.8 1.8 %collective-permute-start.1 = (bf16[2,128,128]{2,1,0:T(8,128)(2,1)S(1)}, bf16[2,128,128]{2,1,0:T(8,128)(2,1)S(1)}, u32[]{:S(2)}, u32[]{:S(2)}) collective-permute-start(bf16[2,128,128]{2,1,0:T(8,128)(2,1)S(1)} %slice.41), channel_id=1, source_target_pairs={{0,8},{4,12},{8,0},{12,4},{16,24},{20,28},{24,16},{28,20},{1,9},{5... | collective-permute-start | bytes 196616 | tf_op jit(solution)/shard_map/ppermute | solution.py:673
  55.6 1.2 %add_convert_fusion = bf16[32,64,128]{2,1,0:T(8,128)(2,1)S(1)} fusion(bf16[32,64,128]{2,1,0:T(8,128)(2,1)} %collective-permute-done.4, bf16[32,64,128]{2,1,0:T(8,128)(2,1)S(1)} %get-tuple-element.39), kind=kLoop, calls=%fused_computation | loop fusion | flops 1048576 | bytes 1572864 | tf_op jit(solution)/shard_map/convert_element_type | solution.py:687
  56.8 1.6 %collective-permute-start.5 = (bf16[32,64,128]{2,1,0:T(8,128)(2,1)S(1)}, bf16[32,64,128]{2,1,0:T(8,128)(2,1)S(1)}, u32[]{:S(2)}, u32[]{:S(2)}) collective-permute-start(bf16[32,64,128]{2,1,0:T(8,128)(2,1)S(1)} %add_convert_fusion), channel_id=1, source_target_pairs={{0,2},{1,3},{2,0},{3,1},{4,6},{5,7},{6,4},{7,5},{8,10},{9,11},{10,... | collective-permute-start | bytes 1572872 | tf_op jit(solution)/shard_map/ppermute | solution.py:688
  58.4 0.5 subtract_add_fusion
  58.9 2.4 %collective-permute-start.2 = (bf16[1,128,128]{2,1,0:T(8,128)(2,1)S(1)}, bf16[1,128,128]{2,1,0:T(8,128)(2,1)S(1)}, u32[]{:S(2)}, u32[]{:S(2)}) collective-permute-start(bf16[1,128,128]{2,1,0:T(8,128)(2,1)S(1)} %slice.42), channel_id=1, source_target_pairs={{0,16},{4,20},{8,24},{12,28},{16,0},{20,4},{24,8},{28,12},{1,17},{... | collective-permute-start | bytes 98312 | tf_op jit(solution)/shard_map/ppermute | solution.py:673
  61.4 2.4 %collective-permute-done.2 = bf16[1,128,128]{2,1,0:T(8,128)(2,1)S(1)} collective-permute-done((bf16[1,128,128]{2,1,0:T(8,128)(2,1)S(1)}, bf16[1,128,128]{2,1,0:T(8,128)(2,1)S(1)}, u32[]{:S(2)}, u32[]{:S(2)}) %collective-permute-start.2) | collective-permute-done | bytes 32800 | tf_op jit(solution)/shard_map/ppermute | solution.py:673
  63.8 0.8 %finish_queries.1 = bf16[128,128]{1,0:T(8,128)(2,1)} custom-call(bf16[128,128]{1,0:T(8,128)(2,1)S(1)} %bitcast.8, f32[128,128]{1,0:T(8,128)S(1)} %slice_bitcast_fusion.refs_0_, bf16[128,128]{1,0:T(8,128)(2,1)S(1)} %bitcast.9), custom_call_target="tpu_custom_call" | custom-call | tf_op jit(solution)/shard_map/finish_queries/pallas_call | solution.py:638
  64.6 5.5 %collective-permute-done.5.refs_2_ = bf16[32,64,128]{2,1,0:T(8,128)(2,1)S(1)} collective-permute-done((bf16[32,64,128]{2,1,0:T(8,128)(2,1)S(1)}, bf16[32,64,128]{2,1,0:T(8,128)(2,1)S(1)}, u32[]{:S(2)}, u32[]{:S(2)}) %collective-permute-start.5) | collective-permute-done | bytes 524320 | tf_op jit(solution)/shard_map/ppermute | solution.py:688
  70.1 2.0 %finish.1 = bf16[32,64,128]{2,1,0:T(8,128)(2,1)} custom-call(bf16[32,64,128]{2,1,0:T(8,128)(2,1)S(1)} %get-tuple-element.34.raw_ref, bf16[32,64,128]{2,1,0:T(8,128)(2,1)S(1)} %get-tuple-element.37.refs_0_, bf16[32,64,128]{2,1,0:T(8,128)(2,1)S(1)} %collective-permute-done.3.refs_1_, bf16[32,64,128]{2,1,0:T(8,128)(2,1)S(1)} %collective-permute-done.5.refs_2_), custom_call_target="tpu_custom_call" | custom-call | tf_op jit(solution)/shard_map/finish/pallas_call | solution.py:626
  (20 shorter events, 0.5 us)
Async XLA Ops:
  2.2 16.9 %all-to-all-start = ((bf16[8,144,128]{2,1,0:T(8,128)(2,1)}), bf16[8,144,128]{2,1,0:T(8,128)(2,1)S(1)}, u32[]{:S(2)}, u32[]{:S(2)}) async-start(bf16[8,144,128]{2,1,0:T(8,128)(2,1)} %pack.1), calls=%async_computation | async-start | bytes 589824 | tf_op jit(solution)/shard_map/all_to_all | solution.py:656
  13.2 1.3 %copy-start = (bf16[32,128,256]{2,1,0:T(8,128)(2,1)}, bf16[32,128,256]{2,1,0:T(8,128)(2,1)S(1)}, u32[]{:S(2)}) copy-start(bf16[32,128,256]{2,1,0:T(8,128)(2,1)S(1)} %get-tuple-element.27.refs_0_) | copy-start | bytes 6291460
  14.5 1.3 %copy-start.2 = (bf16[32,256,128]{2,1,0:T(8,128)(2,1)}, bf16[32,256,128]{2,1,0:T(8,128)(2,1)S(1)}, u32[]{:S(2)}) copy-start(bf16[32,256,128]{2,1,0:T(8,128)(2,1)S(1)} %get-tuple-element.22.refs_1_) | copy-start | bytes 6291460
  28.9 12.1 %all-to-all-start.1 = ((f32[8,32,128]{2,1,0:T(8,128)}), f32[8,32,128]{2,1,0:T(8,128)S(1)}, u32[]{:S(2)}, u32[]{:S(2)}) async-start(f32[8,32,128]{2,1,0:T(8,128)} %get-tuple-element.23), calls=%async_computation.1 | async-start | bytes 262144 | tf_op jit(solution)/shard_map/all_to_all | solution.py:667
  41.1 6.3 %copy-start.3 = (f32[4,32]{1,0:T(4,128)S(1)}, f32[4,32]{1,0:T(4,128)}, u32[]{:S(2)}) copy-start(f32[4,32]{1,0:T(4,128)} %refs_2_.1) | copy-start | bytes 1540
  47.3 16.5 %copy-start.1 = (bf16[4,32,128]{2,1,0:T(8,128)(2,1)S(1)}, bf16[4,32,128]{2,1,0:T(8,128)(2,1)}, u32[]{:S(2)}) copy-start(bf16[4,32,128]{2,1,0:T(8,128)(2,1)} %param.4) | copy-start | bytes 98308
  47.3 8.3 %collective-permute-start.4 = (bf16[32,64,128]{2,1,0:T(8,128)(2,1)S(1)}, bf16[32,64,128]{2,1,0:T(8,128)(2,1)}, u32[]{:S(2)}, u32[]{:S(2)}) collective-permute-start(bf16[32,64,128]{2,1,0:T(8,128)(2,1)S(1)} %get-tuple-element.40), channel_id=1, source_target_pairs={{0,1},{1,0},{2,3},{3,2},{4,5},{5,4},{6,7},{7,6},{8,9},{9,8},{10,11... | collective-permute-start | bytes 1572872 | tf_op jit(solution)/shard_map/ppermute | solution.py:686
  47.5 6.2 %collective-permute-start = (bf16[4,128,128]{2,1,0:T(8,128)(2,1)S(1)}, bf16[4,128,128]{2,1,0:T(8,128)(2,1)S(1)}, u32[]{:S(2)}, u32[]{:S(2)}) collective-permute-start(bf16[4,128,128]{2,1,0:T(8,128)(2,1)S(1)} %get-tuple-element.33), channel_id=1, source_target_pairs={{0,4},{4,0},{8,12},{12,8},{16,20},{20,16},{24,28},{28,24},{1,5},{5... | collective-permute-start | bytes 393224 | tf_op jit(solution)/shard_map/ppermute | solution.py:673
  49.8 14.8 %collective-permute-start.3 = (bf16[32,64,128]{2,1,0:T(8,128)(2,1)S(1)}, bf16[32,64,128]{2,1,0:T(8,128)(2,1)S(1)}, u32[]{:S(2)}, u32[]{:S(2)}) collective-permute-start(bf16[32,64,128]{2,1,0:T(8,128)(2,1)S(1)} %get-tuple-element.38), channel_id=1, source_target_pairs={{0,1},{1,0},{2,3},{3,2},{4,5},{5,4},{6,7},{7,6},{8,9},{9,8},{10,11... | collective-permute-start | bytes 1572872 | tf_op jit(solution)/shard_map/ppermute | solution.py:689
  53.8 5.1 %collective-permute-start.1 = (bf16[2,128,128]{2,1,0:T(8,128)(2,1)S(1)}, bf16[2,128,128]{2,1,0:T(8,128)(2,1)S(1)}, u32[]{:S(2)}, u32[]{:S(2)}) collective-permute-start(bf16[2,128,128]{2,1,0:T(8,128)(2,1)S(1)} %slice.41), channel_id=1, source_target_pairs={{0,8},{4,12},{8,0},{12,4},{16,24},{20,28},{24,16},{28,20},{1,9},{5... | collective-permute-start | bytes 196616 | tf_op jit(solution)/shard_map/ppermute | solution.py:673
  56.8 13.3 %collective-permute-start.5 = (bf16[32,64,128]{2,1,0:T(8,128)(2,1)S(1)}, bf16[32,64,128]{2,1,0:T(8,128)(2,1)S(1)}, u32[]{:S(2)}, u32[]{:S(2)}) collective-permute-start(bf16[32,64,128]{2,1,0:T(8,128)(2,1)S(1)} %add_convert_fusion), channel_id=1, source_target_pairs={{0,2},{1,3},{2,0},{3,1},{4,6},{5,7},{6,4},{7,5},{8,10},{9,11},{10,... | collective-permute-start | bytes 1572872 | tf_op jit(solution)/shard_map/ppermute | solution.py:688
  58.9 4.9 %collective-permute-start.2 = (bf16[1,128,128]{2,1,0:T(8,128)(2,1)S(1)}, bf16[1,128,128]{2,1,0:T(8,128)(2,1)S(1)}, u32[]{:S(2)}, u32[]{:S(2)}) collective-permute-start(bf16[1,128,128]{2,1,0:T(8,128)(2,1)S(1)} %slice.42), channel_id=1, source_target_pairs={{0,16},{4,20},{8,24},{12,28},{16,0},{20,4},{24,8},{28,12},{1,17},{... | collective-permute-start | bytes 98312 | tf_op jit(solution)/shard_map/ppermute | solution.py:673

commit v3 on v2

--- a/solution.py
+++ b/solution.py
@@ -9,13 +9,16 @@
 
 epsilon = 1e-06
 softness_scale = 0.05
-block_pairs = 16
+chunk_pairs = 8
 vmem_bytes = 44 << 20
 row_pad = 8
 
 VMEM = pl.BlockSpec(memory_space=pltpu.VMEM)
 HBM = pl.BlockSpec(memory_space=pltpu.HBM)
-unroll = 4
+chunk_unroll = 8
+passage_unroll = 4
+copy_parts = 8
+meta_rows = 8
 
 
 def in_hbm(array):
@@ -121,9 +124,9 @@
             pl.BlockSpec((step, share, width), lambda i: (i, 0, 0)),
         ],
         out_shape=[
-            jax.ShapeDtypeStruct((count, tokens, width), jnp.bfloat16),
-            jax.ShapeDtypeStruct((count, width, tokens), jnp.bfloat16),
-            jax.ShapeDtypeStruct((count, share, width), jnp.bfloat16),
+            pltpu.HBM((count, tokens, width), jnp.bfloat16),
+            pltpu.HBM((count, width, tokens), jnp.bfloat16),
+            pltpu.HBM((count, share, width), jnp.bfloat16),
         ],
         compiler_params=params(),
         cost_estimate=pl.CostEstimate(flops=1 << 24, bytes_accessed=6 << 20, transcendentals=0),
@@ -131,20 +134,33 @@
     )(in_hbm(passages))
 
 
-def each_extra(pass_count, list_smem, count_row, visit):
-    def passage_step(p, used):
-        pairs = list_smem[count_row, p]
-        blocks = (pairs + block_pairs - 1) // block_pairs
-        extra = jnp.maximum(blocks - 1, 0)
-
-        def step(b, carry):
-            visit(p, (b + 1) * block_pairs, pass_count + used + b)
-            return carry
-
-        lax.fori_loop(0, extra, step, 0)
-        return used + extra
-
-    return lax.fori_loop(0, pass_count, passage_step, jnp.int32(0))
+def list_layout(group):
+    empty = -(-group // chunk_pairs) * chunk_pairs
+    return empty, empty + chunk_pairs
+
+
+def slot_total(pass_count, pairs):
+    worst = (pairs + pass_count * (chunk_pairs - 1)) // chunk_pairs
+    return -(-(worst + 1) // chunk_unroll) * chunk_unroll
+
+
+def steps_of(list_smem, tables):
+    total = list_smem[tables + 4, 0]
+    return jnp.maximum((total + chunk_unroll - 1) // chunk_unroll, 1)
+
+
+def part_copies(source, target, sems):
+    size = source.shape[0] // copy_parts
+    return [
+        pltpu.make_async_copy(
+            source.at[pl.ds(i * size, size)], target.at[pl.ds(i * size, size)], sems.at[i]
+        )
+        for i in range(copy_parts)
+    ]
+
+
+def query_places(ids, query_tokens):
+    return [pl.ds(pl.multiple_of(n * query_tokens, query_tokens), query_tokens) for n in ids]
 
 
 def forward_kernel(
@@ -170,14 +186,15 @@
     norm_sem,
     soft_sems,
 ):
-    norm_copy = pltpu.make_async_copy(norm_hbm, norm_ref, norm_sem)
-    norm_copy.start()
+    norm_copies = part_copies(norm_hbm, norm_ref, norm_sem)
+    for copy in norm_copies:
+        copy.start()
     sources = recv_ref.shape[0]
     pass_count, tokens, width = norm_ref.shape
     group = sources * query_count
     rows = query_count * query_tokens
     stride = group + row_pad
-    count_row = list_ref.shape[0] - row_pad
+    empty, tables = list_layout(group)
     owner = lax.axis_index("psg").astype(jnp.float32)
     for s in range(sources):
         packed = recv_ref[s, rows : rows + 16, :].astype(jnp.float32)
@@ -218,59 +235,69 @@
     rank = jnp.dot(lower, active_value.astype(jnp.bfloat16), preferred_element_type=jnp.float32)
     rank = jnp.where(active, rank, -1.0)
     less = lax.broadcasted_iota(jnp.int32, main.shape, 0).astype(jnp.float32) - group
-    for k in range(count_row):
+    for k in range(empty):
         found = jnp.sum(jnp.where(rank == k, less, 0.0), 0, keepdims=True) + group
         list_ref[k : k + 1, :] = found.astype(jnp.int32)
-    total = jnp.sum(active_value, 0, keepdims=True).astype(jnp.int32)
-    list_ref[count_row:, :] = jnp.broadcast_to(total, (row_pad, 128))
+    list_ref[empty:tables, :] = jnp.full((tables - empty, 128), group, jnp.int32)
+    square = (128, 128)
+    first_id = lax.broadcasted_iota(jnp.int32, square, 0)
+    second_id = lax.broadcasted_iota(jnp.int32, square, 1)
+    counts = lax.dot_general(
+        active_value, jnp.ones((group, 128), jnp.float32), (((0,), (0,)), ((), ())),
+        preferred_element_type=jnp.float32,
+    )
+    chunks = jnp.floor((counts + (chunk_pairs - 1)) * (1.0 / chunk_pairs))
+    ends = jnp.dot(
+        (first_id >= second_id).astype(jnp.bfloat16),
+        chunks.astype(jnp.bfloat16),
+        preferred_element_type=jnp.float32,
+    )
+    past = ends <= second_id.astype(jnp.float32)
+    passage_of = jnp.sum(jnp.where(past, 1.0, 0.0), 0, keepdims=True)
+    start_of = jnp.sum(jnp.where(past, chunks, 0.0), 0, keepdims=True)
+    chunk_id = lax.broadcasted_iota(jnp.int32, (1, 128), 1).astype(jnp.float32)
+    beyond = passage_of > pass_count - 0.5
+    passage_of = jnp.where(beyond, 0.0, passage_of)
+    first_of = jnp.where(beyond, float(empty), (chunk_id - start_of) * chunk_pairs)
+    flat = jnp.sum(active_value, 0, keepdims=True)
+    starts = jnp.sum(jnp.where(first_id == second_id, ends - chunks, 0.0), 0, keepdims=True)
+    total = jnp.sum(jnp.where(first_id == 127, ends, 0.0), 0, keepdims=True)
+    for row, value in enumerate((passage_of, first_of, starts, flat, total)):
+        list_ref[tables + row : tables + row + 1, :] = value.astype(jnp.int32)
     copy = pltpu.make_async_copy(list_ref, list_smem, sem)
     copy.start()
-    norm_copy.wait()
+    for other in norm_copies:
+        other.wait()
     copy.wait()
-
-    half = block_pairs // 2
 
     def soft_copy(slot):
         return pltpu.make_async_copy(soft_ref.at[slot], soft_hbm.at[slot], soft_sems.at[slot])
 
-    def block(p, first, slot):
-        passage = norm_ref[p]
-        for h in range(2):
-            ids = [list_smem[first + h * half + r, p] for r in range(half)]
-            tile = jnp.concatenate(
-                [
-                    qn_ref[pl.ds(pl.multiple_of(n * query_tokens, query_tokens), query_tokens), :]
-                    for n in ids
-                ],
-                0,
-            )
-            dots = lax.dot_general(
-                passage, tile, (((1,), (1,)), ((), ())), preferred_element_type=jnp.float32
-            )
-            power = jnp.exp2(dots * (math.log2(math.e) / softness_scale))
-            sums = jnp.sum(power, 0, keepdims=True)
-            span = half * query_tokens
-            soft_ref[slot, :, h * span : (h + 1) * span] = (power * (1.0 / sums)).astype(
-                jnp.bfloat16
-            )
-            for r in range(half):
-                sums_ref[pl.ds(p * stride + ids[r], 1), :query_tokens] = sums[
-                    :, r * query_tokens : (r + 1) * query_tokens
-                ]
-
-    def step(p, carry):
-        for u in range(unroll):
-            block(unroll * p + u, 0, unroll * p + u)
-        for u in range(unroll):
-            soft_copy(unroll * p + u).start()
+    def chunk(slot):
+        p = list_smem[tables, slot]
+        first = list_smem[tables + 1, slot]
+        ids = [list_smem[first + r, p] for r in range(chunk_pairs)]
+        tile = jnp.concatenate([qn_ref[place, :] for place in query_places(ids, query_tokens)], 0)
+        dots = lax.dot_general(
+            norm_ref[p], tile, (((1,), (1,)), ((), ())), preferred_element_type=jnp.float32
+        )
+        power = jnp.exp2(dots * (math.log2(math.e) / softness_scale))
+        sums = jnp.sum(power, 0, keepdims=True)
+        soft_ref[slot] = (power * (1.0 / sums)).astype(jnp.bfloat16)
+        for r, n in enumerate(ids):
+            sums_ref[pl.ds(p * stride + n, 1), :query_tokens] = sums[
+                :, r * query_tokens : (r + 1) * query_tokens
+            ]
+
+    def step(i, carry):
+        for u in range(chunk_unroll):
+            chunk(i * chunk_unroll + u)
+        for u in range(chunk_unroll):
+            soft_copy(i * chunk_unroll + u).start()
         return carry
 
-    def extra(p, first, slot):
-        block(p, first, slot)
-        soft_copy(slot).start()
-
-    lax.fori_loop(0, pass_count // unroll, step, 0)
-    used = each_extra(pass_count, list_smem, count_row, extra)
+    steps = steps_of(list_smem, tables)
+    lax.fori_loop(0, steps, step, 0)
 
     scores = jnp.zeros(main.shape, jnp.float32)
     for p in range(pass_count):
@@ -291,7 +318,7 @@
         soft_copy(slot).wait()
         return carry
 
-    lax.fori_loop(0, pass_count + used, drain, 0)
+    lax.fori_loop(0, steps * chunk_unroll, drain, 0)
 
 
 def forward(received, norm, cand_count, query_count, query_tokens):
@@ -299,11 +326,11 @@
     pass_count, tokens, width = norm.shape
     group = sources * query_count
     capacity = max(2, -(-5 * query_count * cand_count // (2 * sources)))
-    blocks = pass_count + sources * capacity // block_pairs
-    list_rows = -(-group // block_pairs) * block_pairs + row_pad
+    slots = slot_total(pass_count, sources * capacity)
+    list_rows = list_layout(group)[1] + meta_rows
     rows = query_count * query_tokens
-    soft_shape = (blocks, tokens, block_pairs * query_tokens)
-    flops = 2 * pass_count * block_pairs * query_tokens * tokens * width
+    soft_shape = (slots, tokens, chunk_pairs * query_tokens)
+    flops = 2 * slots * chunk_pairs * query_tokens * tokens * width
     return pl.pallas_call(
         lambda *refs: forward_kernel(cand_count, query_count, query_tokens, *refs),
         in_specs=[VMEM, HBM],
@@ -325,8 +352,8 @@
             pltpu.VMEM((pass_count * (group + row_pad), 128), jnp.float32),
             pltpu.SMEM((list_rows, 128), jnp.int32),
             pltpu.SemaphoreType.DMA,
-            pltpu.SemaphoreType.DMA,
-            pltpu.SemaphoreType.DMA((blocks,)),
+            pltpu.SemaphoreType.DMA((copy_parts,)),
+            pltpu.SemaphoreType.DMA((slots,)),
         ],
         compiler_params=params(),
         cost_estimate=pl.CostEstimate(flops=flops, bytes_accessed=12 << 20, transcendentals=1 << 22),
@@ -334,11 +361,11 @@
     )(received, in_hbm(norm))
 
 
-def spread(ref, values, pass_count, stride):
+def spread(ref, values, pass_count, stride, start=0):
     group = values.shape[0]
     for p in range(pass_count):
         ref[p * stride : p * stride + group, :] = jnp.broadcast_to(
-            values[:, p : p + 1], (group, 128)
+            values[:, start + p : start + p + 1], (group, 128)
         )
         ref[p * stride + group : (p + 1) * stride, :] = jnp.zeros((stride - group, 128), jnp.float32)
 
@@ -369,8 +396,8 @@
     stride = group + row_pad
     list_copy = pltpu.make_async_copy(list_ref, list_smem, sem)
     list_copy.start()
-    flip_copy = pltpu.make_async_copy(flip_hbm, flip_ref, flip_sem)
-    flip_copy.start()
+    flip_copies = part_copies(flip_hbm, flip_ref, flip_sem)
+    empty, tables = list_layout(group)
 
     def soft_copy(slot):
         return pltpu.make_async_copy(soft_hbm.at[slot], soft_ref.at[slot], soft_sems.at[slot])
@@ -379,19 +406,26 @@
         soft_copy(slot).start()
         return carry
 
-    lax.fori_loop(0, pass_count, fetch, 0)
+    list_copy.wait()
+    steps = steps_of(list_smem, tables)
+    lax.fori_loop(0, chunk_unroll, fetch, 0)
+    for copy in flip_copies:
+        copy.start()
+    lax.fori_loop(chunk_unroll, steps * chunk_unroll, fetch, 0)
     spread(raised_rows, many_ref[...] * jnp.exp(score_ref[...]), pass_count, stride)
     spread(wanted_rows, target_ref[...], pass_count, stride)
     raised_sum[...] = jnp.zeros(raised_sum.shape, jnp.float32)
     wanted_sum[...] = jnp.zeros(wanted_sum.shape, jnp.float32)
-    list_copy.wait()
-    flip_copy.wait()
-
-    def block(p, first, slot):
+    for copy in flip_copies:
+        copy.wait()
+
+    def chunk(slot):
+        p = list_smem[tables, slot]
+        first = list_smem[tables + 1, slot]
+        ids = [list_smem[first + r, p] for r in range(chunk_pairs)]
+        places = query_places(ids, query_tokens)
         mixed = jnp.dot(flip_ref[p], soft_ref[slot], preferred_element_type=jnp.float32)
         mixed = jnp.transpose(mixed, (1, 0))
-        ids = [list_smem[first + r, p] for r in range(block_pairs)]
-        places = [pl.ds(pl.multiple_of(n * query_tokens, query_tokens), query_tokens) for n in ids]
         for total, rows in ((raised_sum, raised_rows), (wanted_sum, wanted_rows)):
             added = [
                 total[place, :]
@@ -402,29 +436,23 @@
             for place, value in zip(places, added):
                 total[place, :] = value
 
-    def step(p, carry):
-        for u in range(unroll):
-            soft_copy(unroll * p + u).wait()
-        for u in range(unroll):
-            block(unroll * p + u, 0, unroll * p + u)
+    def step(i, carry):
+        for u in range(chunk_unroll):
+            soft_copy(i * chunk_unroll + u).wait()
+        for u in range(chunk_unroll):
+            chunk(i * chunk_unroll + u)
         return carry
 
-    def extra(p, first, slot):
-        soft_copy(slot).start()
-        soft_copy(slot).wait()
-        block(p, first, slot)
-
-    lax.fori_loop(0, pass_count // unroll, step, 0)
-    each_extra(pass_count, list_smem, list_ref.shape[0] - row_pad, extra)
+    lax.fori_loop(0, steps, step, 0)
     raised_ref[...] = raised_sum[: group * query_tokens, :]
     wanted_ref[...] = wanted_sum[: group * query_tokens, :]
 
 
 def attend(flip, soft, ids, score, many, target, query_tokens):
-    blocks, tokens, columns = soft.shape
+    slots, tokens, columns = soft.shape
     pass_count, width, _ = flip.shape
     group = score.shape[0]
-    flops = 2 * pass_count * columns * tokens * width
+    flops = 2 * slots * columns * tokens * width
     total = jax.ShapeDtypeStruct((group * query_tokens, width), jnp.float32)
     rows = pltpu.VMEM((pass_count * (group + row_pad), 128), jnp.float32)
     padded = pltpu.VMEM(((group + 1) * query_tokens, width), jnp.float32)
@@ -442,8 +470,8 @@
             padded,
             pltpu.SMEM(ids.shape, jnp.int32),
             pltpu.SemaphoreType.DMA,
-            pltpu.SemaphoreType.DMA,
-            pltpu.SemaphoreType.DMA((blocks,)),
+            pltpu.SemaphoreType.DMA((copy_parts,)),
+            pltpu.SemaphoreType.DMA((slots,)),
         ],
         compiler_params=params(),
         cost_estimate=pl.CostEstimate(flops=flops, bytes_accessed=12 << 20, transcendentals=0),
@@ -518,6 +546,7 @@
 
 def passage_kernel(
     query_tokens,
+    start,
     list_ref,
     grads_ref,
     qn_ref,
@@ -535,8 +564,9 @@
     list_copy = pltpu.make_async_copy(list_ref, list_smem, sem)
     list_copy.start()
     pass_count, share, width = own_ref.shape
-    stride = grads_ref.shape[0] + row_pad
-    count_row = list_ref.shape[0] - row_pad
+    group = grads_ref.shape[0]
+    stride = group + row_pad
+    empty, tables = list_layout(group)
 
     def soft_copy(slot):
         return pltpu.make_async_copy(soft_hbm.at[slot], soft_ref.at[slot], soft_sems.at[slot])
@@ -545,56 +575,81 @@
         soft_copy(slot).start()
         return carry
 
-    lax.fori_loop(0, pass_count, fetch, 0)
-    spread(grad_ref, grads_ref[...], pass_count, stride)
+    def drain(slot, carry):
+        soft_copy(slot).wait()
+        return carry
+
     list_copy.wait()
-
-    def product(p, first, slot):
-        ids = [list_smem[first + r, p] for r in range(block_pairs)]
-        tile = jnp.concatenate(
-            [
-                (
-                    qn_ref[
-                        pl.ds(pl.multiple_of(n * query_tokens, query_tokens), query_tokens), :
-                    ].astype(jnp.float32)
-                    * grad_ref[pl.ds(p * stride + n, 1), :]
-                ).astype(jnp.bfloat16)
-                for n in ids
-            ],
-            0,
-        )
-        return jnp.dot(soft_ref[slot], tile, preferred_element_type=jnp.float32)
+    low = list_smem[tables + 2, start]
+    high = jnp.maximum(list_smem[tables + 2, start + pass_count], low + 1)
+    lax.fori_loop(low, high, fetch, 0)
+    spread(grad_ref, grads_ref[...], pass_count, stride, start)
+
+    def tile(p, first):
+        ids = [list_smem[first + r, start + p] for r in range(chunk_pairs)]
+        return [
+            (qn_ref[place, :].astype(jnp.float32) * grad_ref[pl.ds(p * stride + n, 1), :]).astype(
+                jnp.bfloat16
+            )
+            for n, place in zip(ids, query_places(ids, query_tokens))
+        ]
 
     outs = (own_ref, core_ref, far_ref, cross_ref)
 
-    def step(p, carry):
-        for u in range(unroll):
-            soft_copy(unroll * p + u).wait()
-        for u in range(unroll):
-            value = product(unroll * p + u, 0, unroll * p + u).astype(jnp.bfloat16)
+    def passage(p):
+        pairs = list_smem[tables + 3, start + p]
+        slot = list_smem[tables + 2, start + p]
+        tiles, softs = [], []
+        for h in range(2):
+            some = pairs > h * chunk_pairs
+            tiles += tile(p, jnp.where(some, h * chunk_pairs, empty))
+            softs.append(soft_ref[jnp.where(some, slot + h, low)])
+        value = jnp.dot(
+            jnp.concatenate(softs, 1),
+            jnp.concatenate(tiles, 0),
+            preferred_element_type=jnp.float32,
+        ).astype(jnp.bfloat16)
+        for place, ref in enumerate(outs):
+            ref[p] = value[place * share : (place + 1) * share]
+
+    def step(i, ready):
+        last = (i + 1) * passage_unroll
+        needed = jnp.maximum(list_smem[tables + 2, start + last], low + 1)
+        lax.fori_loop(ready, needed, drain, 0)
+        for u in range(passage_unroll):
+            passage(i * passage_unroll + u)
+        return needed
+
+    lax.fori_loop(0, pass_count // passage_unroll, step, low)
+
+    def rest(p, carry):
+        chunks = (list_smem[tables + 3, start + p] + chunk_pairs - 1) // chunk_pairs
+        slot = list_smem[tables + 2, start + p]
+
+        def add(b, inner):
+            value = jnp.dot(
+                soft_ref[slot + b],
+                jnp.concatenate(tile(p, b * chunk_pairs), 0),
+                preferred_element_type=jnp.float32,
+            )
             for place, ref in enumerate(outs):
-                ref[unroll * p + u] = value[place * share : (place + 1) * share]
+                piece = value[place * share : (place + 1) * share]
+                ref[p] = (ref[p].astype(jnp.float32) + piece).astype(jnp.bfloat16)
+            return inner
+
+        lax.fori_loop(2, chunks, add, 0)
         return carry
 
-    def extra(p, first, slot):
-        soft_copy(slot).start()
-        soft_copy(slot).wait()
-        value = product(p, first, slot)
-        for place, ref in enumerate(outs):
-            piece = value[place * share : (place + 1) * share]
-            ref[p] = (ref[p].astype(jnp.float32) + piece).astype(jnp.bfloat16)
-
-    lax.fori_loop(0, pass_count // unroll, step, 0)
-    each_extra(pass_count, list_smem, count_row, extra)
-
-
-def passage_backward(ids, grads, qn, soft, pass_count, query_tokens, slices):
-    tokens = soft.shape[1]
+    lax.fori_loop(0, pass_count, rest, 0)
+
+
+def passage_backward(ids, grads, qn, soft, start, pass_count, query_tokens, slices):
+    slots, tokens, columns = soft.shape
     width = qn.shape[1]
     piece = jax.ShapeDtypeStruct((pass_count, tokens // slices, width), jnp.bfloat16)
-    flops = 2 * pass_count * soft.shape[2] * tokens * width
+    flops = 4 * pass_count * columns * tokens * width
     return pl.pallas_call(
-        lambda *refs: passage_kernel(query_tokens, *refs),
+        lambda *refs: passage_kernel(query_tokens, start, *refs),
         in_specs=[VMEM] * 3 + [HBM],
         out_specs=[VMEM] * 4,
         out_shape=[piece] * 4,
@@ -603,10 +658,10 @@
             pltpu.VMEM((pass_count * (grads.shape[0] + row_pad), 128), jnp.float32),
             pltpu.SMEM(ids.shape, jnp.int32),
             pltpu.SemaphoreType.DMA,
-            pltpu.SemaphoreType.DMA((soft.shape[0],)),
+            pltpu.SemaphoreType.DMA((slots,)),
         ],
         compiler_params=params(),
-        cost_estimate=pl.CostEstimate(flops=flops, bytes_accessed=12 << 20, transcendentals=0),
+        cost_estimate=pl.CostEstimate(flops=flops, bytes_accessed=6 << 20, transcendentals=0),
         name="passage_backward",
     )(ids, grads, qn, in_hbm(soft))
 
@@ -620,15 +675,11 @@
 
 
 def finish(raw, parts):
-    shape = raw.shape
-    step = math.gcd(shape[0], 8)
-    spec = pl.BlockSpec((step,) + shape[1:], lambda i: (i, 0, 0))
     return pl.pallas_call(
         finish_kernel,
-        grid=(shape[0] // step,),
-        in_specs=[spec] * (1 + len(parts)),
-        out_specs=spec,
-        out_shape=jax.ShapeDtypeStruct(shape, jnp.bfloat16),
+        in_specs=[VMEM] * (1 + len(parts)),
+        out_specs=VMEM,
+        out_shape=jax.ShapeDtypeStruct(raw.shape, jnp.bfloat16),
         compiler_params=params(),
         name="finish",
     )(raw, *parts)
@@ -667,6 +718,16 @@
     zw = lax.all_to_all(zw, "psg", split_axis=0, concat_axis=0, tiled=True)
     raised_sum, wanted_sum = attend(flip, soft, ids, score, many, target, query_tokens)
     keep, send, grads = query_backward(zw, score, many, target, raised_sum, wanted_sum)
+    near = [(k, k ^ 1) for k in range(slices)]
+    away = [(k, k ^ 2) for k in range(slices)]
+    own, core, far, cross = passage_backward(
+        ids, grads, qn, soft, 0, pass_count, query_tokens, slices
+    )
+    cross = lax.ppermute(cross, "qry", near)
+    far = (far.astype(jnp.float32) + cross.astype(jnp.float32)).astype(jnp.bfloat16)
+    far, send = lax.optimization_barrier((far, send))
+    far = lax.ppermute(far, "qry", away)
+    core = lax.ppermute(core, "qry", near)
     bit = 1
     while bit < sources:
         swap = [(i, i ^ bit) for i in range(sources)]
@@ -678,15 +739,6 @@
         bit *= 2
     grad_queries = finish_queries(queries.reshape(rows, width), [keep[0], send[0]])
 
-    own, core, far, cross = passage_backward(
-        ids, grads, qn, soft, pass_count, query_tokens, slices
-    )
-    near = [(k, k ^ 1) for k in range(slices)]
-    away = [(k, k ^ 2) for k in range(slices)]
-    cross = lax.ppermute(cross, "qry", near)
-    far = (far.astype(jnp.float32) + cross.astype(jnp.float32)).astype(jnp.bfloat16)
-    far = lax.ppermute(far, "qry", away)
-    core = lax.ppermute(core, "qry", near)
     grad_passages = finish(own_raw, [own, core, far])
 
     raised = jnp.exp(teacher)

time: 72.7 us -> 65.9 us (0.906); the launches traced: 72.2 us -> 66.3 us
  local copies, waits for them, and re-layouts: 2.83 us -> 0.23 us
  Pallas kernels: 32.6 us -> 30.9 us
  other arithmetic: 2.1 us -> 1.06 us
  starting transfers between devices: 19.1 us -> 18.1 us
    ppermute x1, waiting for transfers between devices: 5.53 us -> 0.01 us  [shards(): far = lax.ppermute(far, 'qry', away)]
    unnamed x8 -> x6, local copies, waits for them, and re-layouts: 2.62 us -> 0.02 us
    ppermute x3, waiting for transfers between devices: 5.93 us -> 8.15 us  [shards(): send = lax.ppermute(send, 'psg', swap)]
    pallas_call x1, Pallas kernels: 9.73 us -> 7.71 us  [forward(): pl.pallas_call(lambda *refs: forward_kernel(cand_count, query_count, quer...]
    ppermute x1, waiting for transfers between devices: 0.01 us -> 1.76 us  [shards(): cross = lax.ppermute(cross, 'qry', near)]
    pallas_call x1, Pallas kernels: 8.44 us -> 6.8 us  [attend(): pl.pallas_call(lambda *refs: attend_kernel(query_tokens, *refs), in_specs...]
    all_to_all x1, waiting for transfers between devices: 3.33 us -> 4.69 us  [shards(): lax.all_to_all(pack(queries.reshape(rows, width), candidates, teacher, so...]
    pallas_call x1, Pallas kernels: 3.67 us -> 4.93 us  [prepare_passages(): pl.pallas_call(lambda *refs: passages_kernel(slices, *refs), grid=(count...]
  transfers between devices with their start and end apart: 8 -> 8, of which waited for: 4 -> 6; matrix products, arithmetic and copies ran while one was open for 3% -> 2% of each run, Pallas kernels for 18% -> 19%
where the time goes in v3:
time: 65.9 us; the launch traced here: 66.3 us
  Pallas kernels  30.9 us (47%)
  starting transfers between devices  18.1 us (27%)
  waiting for transfers between devices  15.1 us (23%)
  other arithmetic  1.06 us (2%)
  between operations  0.77 us (1%)
    ppermute x3, waiting for transfers between devices, shards(): send = lax.ppermute(send, 'psg', swap)  8.15 us
    pallas_call x1, Pallas kernels, forward(): pl.pallas_call(lambda *refs: forward_kernel(cand_count, query_count, quer...  7.71 us
    pallas_call x1, Pallas kernels, passage_backward(): pl.pallas_call(lambda *refs: passage_kernel(query_tokens, start, *refs),...  7.49 us
    all_to_all x1, starting transfers between devices, shards(): lax.all_to_all(pack(queries.reshape(rows, width), candidates, teacher, so...  7.29 us
    pallas_call x1, Pallas kernels, attend(): pl.pallas_call(lambda *refs: attend_kernel(query_tokens, *refs), in_specs...  6.8 us
    ppermute x3, starting transfers between devices, shards(): send = lax.ppermute(send, 'psg', swap)  6.11 us
    pallas_call x1, Pallas kernels, prepare_passages(): pl.pallas_call(lambda *refs: passages_kernel(slices, *refs), grid=(count...  4.93 us
    all_to_all x1, waiting for transfers between devices, shards(): lax.all_to_all(pack(queries.reshape(rows, width), candidates, teacher, so...  4.69 us
  transfers between devices with their start and end apart: 8, of which 6 were waited for; matrix products, arithmetic and copies ran while one was open for 2% of the time, Pallas kernels for 19%

profile of v3, /device:TPU:0, one launch (start us, length us, event | category | flops | bytes accessed | tf_op | source)
XLA Modules:
  0.0 66.3 jit_solution(13468685069743835932)
XLA Ops:
  0.6 1.6 %pack.1 = bf16[8,144,128]{2,1,0:T(8,128)(2,1)} custom-call(bf16[128,128]{1,0:T(8,128)(2,1)} %bitcast.7, s32[4,32]{1,0:T(4,128)} %refs_1_.1, f32[4,32]{1,0:T(4,128)} %refs_2_.1), custom_call_target="tpu_custom_call" | custom-call | tf_op jit(solution)/shard_map/pack/pallas_call | solution.py:72
  2.2 7.3 %all-to-all-start = ((bf16[8,144,128]{2,1,0:T(8,128)(2,1)}), bf16[8,144,128]{2,1,0:T(8,128)(2,1)S(1)}, u32[]{:S(2)}, u32[]{:S(2)}) async-start(bf16[8,144,128]{2,1,0:T(8,128)(2,1)} %pack.1), calls=%async_computation | async-start | bytes 589824 | tf_op jit(solution)/shard_map/all_to_all | solution.py:707
  9.5 4.9 %prepare_passages.1 = (bf16[32,256,128]{2,1,0:T(8,128)(2,1)}, bf16[32,128,256]{2,1,0:T(8,128)(2,1)}, bf16[32,64,128]{2,1,0:T(8,128)(2,1)}) custom-call(bf16[32,256,128]{2,1,0:T(8,128)(2,1)} %refs_0_.1), custom_call_target="tpu_custom_call" | custom-call | flops 16777216 | bytes 6291456 | tf_op jit(solution)/shard_map/prepare_passages/pallas_call | solution.py:117
  14.4 4.7 %all-to-all-done.refs_0_ = bf16[8,144,128]{2,1,0:T(8,128)(2,1)S(1)} async-done(((bf16[8,144,128]{2,1,0:T(8,128)(2,1)}), bf16[8,144,128]{2,1,0:T(8,128)(2,1)S(1)}, u32[]{:S(2)}, u32[]{:S(2)}) %all-to-all-start) | async-done | bytes 294944 | tf_op jit(solution)/shard_map/all_to_all | solution.py:707
  19.1 7.7 %forward.1 = (bf16[72,256,256]{2,1,0:T(8,128)(2,1)}, bf16[1056,128]{1,0:T(8,128)(2,1)S(1)}, f32[32,128]{1,0:T(8,128)S(1)}, f32[32,128]{1,0:T(8,128)S(1)}, f32[32...) custom-call(bf16[8,144,128]{2,1,0:T(8,128)(2,1)S(1)} %all-to-all-done.refs_0_, ...), custom_call_target="tpu_custom_call" | custom-call | flops 1207959552 | bytes 12582912 | tf_op jit(solution)/shard_map/forward/pallas_call | solution.py:334
  26.8 3.7 %all-to-all-start.1 = ((f32[8,32,128]{2,1,0:T(8,128)}), f32[8,32,128]{2,1,0:T(8,128)S(1)}, u32[]{:S(2)}, u32[]{:S(2)}) async-start(f32[8,32,128]{2,1,0:T(8,128)} %get-tuple-element.25), calls=%async_computation.1 | async-start | bytes 262144 | tf_op jit(solution)/shard_map/all_to_all | solution.py:718
  30.6 6.8 %attend.1 = (f32[1024,128]{1,0:T(8,128)S(1)}, f32[1024,128]{1,0:T(8,128)S(1)}) custom-call(bf16[32,128,256]{2,1,0:T(8,128)(2,1)} %get-tuple-element.29.refs_0_, bf16[72,256,256]{2,1,0:T(8,128)(2,1)} %get-tuple-element.30.refs_1_.refs_3_, s32[48,128]{1,0:T(8,128)S(1)} %get-tuple-element.31.refs_2_.refs_0_, f32[32,128]{1,0:T(8,128)S(1)} %get-tuple-element.26.refs_3_.refs_1_, ...), custom_call_target="tpu_custom_call" | custom-call | flops 1207959552 | bytes 12582912 | tf_op jit(solution)/shard_map/attend/pallas_call | solution.py:459
  37.4 0.5 all-to-all-done.1.refs_0_
  37.9 0.2 query_backward.1
  38.1 7.5 %passage_backward.1 = (bf16[32,64,128]{2,1,0:T(8,128)(2,1)S(1)}, bf16[32,64,128]{2,1,0:T(8,128)(2,1)S(1)}, bf16[32,64,128]{2,1,0:T(8,128)(2,1)S(1)}, bf16[32,64,128]{2,1,0:T(8,128)(2,1)S(1)}) custom-call(s32[48,128]{1,0:T(8,128)S(1)} %get-tuple-element.31.refs_2_.refs_0_, f32[32,128]{1,0:T(8,128)S(1)} %get-tuple-element.35.refs_1_, ...), custom_call_target="tpu_custom_call" | custom-call | flops 1073741824 | bytes 6291456 | tf_op jit(solution)/shard_map/passage_backward/pallas_call | solution.py:651
  45.8 1.8 %collective-permute-done = bf16[32,64,128]{2,1,0:T(8,128)(2,1)S(1)} collective-permute-done((bf16[32,64,128]{2,1,0:T(8,128)(2,1)S(1)}, bf16[32,64,128]{2,1,0:T(8,128)(2,1)S(1)}, u32[]{:S(2)}, u32[]{:S(2)}) %collective-permute-start) | collective-permute-done | bytes 524320 | tf_op jit(solution)/shard_map/ppermute | solution.py:726
  47.6 0.2 add_convert_fusion
  47.8 0.9 %collective-permute-start.1 = (bf16[4,128,128]{2,1,0:T(8,128)(2,1)S(1)}, bf16[4,128,128]{2,1,0:T(8,128)(2,1)S(1)}, u32[]{:S(2)}, u32[]{:S(2)}) collective-permute-start(bf16[4,128,128]{2,1,0:T(8,128)(2,1)S(1)} %get-tuple-element.40), channel_id=1, source_target_pairs={{0,4},{4,0},{8,12},{12,8},{16,20},{20,16},{24,28},{28,24},{1,5},{5... | collective-permute-start | bytes 393224 | tf_op jit(solution)/shard_map/ppermute | solution.py:734
  48.7 0.2 fusion
  49.0 0.2 slice_reduce_fusion
  49.1 0.9 %collective-permute-start.5 = (bf16[32,64,128]{2,1,0:T(8,128)(2,1)S(1)}, bf16[32,64,128]{2,1,0:T(8,128)(2,1)S(1)}, u32[]{:S(2)}, u32[]{:S(2)}) collective-permute-start(bf16[32,64,128]{2,1,0:T(8,128)(2,1)S(1)} %add_convert_fusion), channel_id=1, source_target_pairs={{0,2},{1,3},{2,0},{3,1},{4,6},{5,7},{6,4},{7,5},{8,10},{9,11},{10,... | collective-permute-start | bytes 1572872 | tf_op jit(solution)/shard_map/ppermute | solution.py:729
  50.0 3.3 %collective-permute-done.1 = bf16[4,128,128]{2,1,0:T(8,128)(2,1)S(1)} collective-permute-done((bf16[4,128,128]{2,1,0:T(8,128)(2,1)S(1)}, bf16[4,128,128]{2,1,0:T(8,128)(2,1)S(1)}, u32[]{:S(2)}, u32[]{:S(2)}) %collective-permute-start.1) | collective-permute-done | bytes 131104 | tf_op jit(solution)/shard_map/ppermute | solution.py:734
  53.4 0.9 %collective-permute-start.2 = (bf16[2,128,128]{2,1,0:T(8,128)(2,1)S(1)}, bf16[2,128,128]{2,1,0:T(8,128)(2,1)S(1)}, u32[]{:S(2)}, u32[]{:S(2)}) collective-permute-start(bf16[2,128,128]{2,1,0:T(8,128)(2,1)S(1)} %slice.41), channel_id=1, source_target_pairs={{0,8},{4,12},{8,0},{12,4},{16,24},{20,28},{24,16},{28,20},{1,9},{5... | collective-permute-start | bytes 196616 | tf_op jit(solution)/shard_map/ppermute | solution.py:734
  54.3 0.5 subtract_add_fusion
  54.8 2.9 %collective-permute-done.2 = bf16[2,128,128]{2,1,0:T(8,128)(2,1)S(1)} collective-permute-done((bf16[2,128,128]{2,1,0:T(8,128)(2,1)S(1)}, bf16[2,128,128]{2,1,0:T(8,128)(2,1)S(1)}, u32[]{:S(2)}, u32[]{:S(2)}) %collective-permute-start.2) | collective-permute-done | bytes 65568 | tf_op jit(solution)/shard_map/ppermute | solution.py:734
  57.8 4.3 %collective-permute-start.3 = (bf16[1,128,128]{2,1,0:T(8,128)(2,1)S(1)}, bf16[1,128,128]{2,1,0:T(8,128)(2,1)S(1)}, u32[]{:S(2)}, u32[]{:S(2)}) collective-permute-start(bf16[1,128,128]{2,1,0:T(8,128)(2,1)S(1)} %slice.42), channel_id=1, source_target_pairs={{0,16},{4,20},{8,24},{12,28},{16,0},{20,4},{24,8},{28,12},{1,17},{... | collective-permute-start | bytes 98312 | tf_op jit(solution)/shard_map/ppermute | solution.py:734
  62.1 1.9 %collective-permute-done.3 = bf16[1,128,128]{2,1,0:T(8,128)(2,1)S(1)} collective-permute-done((bf16[1,128,128]{2,1,0:T(8,128)(2,1)S(1)}, bf16[1,128,128]{2,1,0:T(8,128)(2,1)S(1)}, u32[]{:S(2)}, u32[]{:S(2)}) %collective-permute-start.3) | collective-permute-done | bytes 32800 | tf_op jit(solution)/shard_map/ppermute | solution.py:734
  64.0 0.8 %finish_queries.1 = bf16[128,128]{1,0:T(8,128)(2,1)} custom-call(bf16[128,128]{1,0:T(8,128)(2,1)S(1)} %bitcast.8, f32[128,128]{1,0:T(8,128)S(1)} %slice_bitcast_fusion.refs_0_, bf16[128,128]{1,0:T(8,128)(2,1)S(1)} %bitcast.9), custom_call_target="tpu_custom_call" | custom-call | tf_op jit(solution)/shard_map/finish_queries/pallas_call | solution.py:689
  64.8 1.5 %finish.1 = bf16[32,64,128]{2,1,0:T(8,128)(2,1)} custom-call(bf16[32,64,128]{2,1,0:T(8,128)(2,1)S(1)} %copy-done, bf16[32,64,128]{2,1,0:T(8,128)(2,1)S(1)} %get-tuple-element.42.refs_0_, bf16[32,64,128]{2,1,0:T(8,128)(2,1)S(1)} %collective-permute-done.4.refs_1_, bf16[32,64,128]{2,1,0:T(8,128)(2,1)S(1)} %collective-permute-done.5.refs_2_), custom_call_target="tpu_custom_call" | custom-call | tf_op jit(solution)/shard_map/finish/pallas_call | solution.py:678
  (18 shorter events, 0.4 us)
Async XLA Ops:
  2.2 16.9 %all-to-all-start = ((bf16[8,144,128]{2,1,0:T(8,128)(2,1)}), bf16[8,144,128]{2,1,0:T(8,128)(2,1)S(1)}, u32[]{:S(2)}, u32[]{:S(2)}) async-start(bf16[8,144,128]{2,1,0:T(8,128)(2,1)} %pack.1), calls=%async_computation | async-start | bytes 589824 | tf_op jit(solution)/shard_map/all_to_all | solution.py:707
  26.8 11.1 %all-to-all-start.1 = ((f32[8,32,128]{2,1,0:T(8,128)}), f32[8,32,128]{2,1,0:T(8,128)S(1)}, u32[]{:S(2)}, u32[]{:S(2)}) async-start(f32[8,32,128]{2,1,0:T(8,128)} %get-tuple-element.25), calls=%async_computation.1 | async-start | bytes 262144 | tf_op jit(solution)/shard_map/all_to_all | solution.py:718
  38.1 7.6 %copy-start.2 = (f32[4,32]{1,0:T(4,128)S(1)}, f32[4,32]{1,0:T(4,128)}, u32[]{:S(2)}) copy-start(f32[4,32]{1,0:T(4,128)} %refs_2_.1) | copy-start | bytes 1540
  45.6 18.4 %copy-start.1 = (bf16[4,32,128]{2,1,0:T(8,128)(2,1)S(1)}, bf16[4,32,128]{2,1,0:T(8,128)(2,1)}, u32[]{:S(2)}) copy-start(bf16[4,32,128]{2,1,0:T(8,128)(2,1)} %param.4) | copy-start | bytes 98308
  45.6 19.2 %copy-start = (bf16[32,64,128]{2,1,0:T(8,128)(2,1)S(1)}, bf16[32,64,128]{2,1,0:T(8,128)(2,1)}, u32[]{:S(2)}) copy-start(bf16[32,64,128]{2,1,0:T(8,128)(2,1)} %get-tuple-element.41.raw_ref) | copy-start | bytes 1572868
  45.6 2.0 %collective-permute-start = (bf16[32,64,128]{2,1,0:T(8,128)(2,1)S(1)}, bf16[32,64,128]{2,1,0:T(8,128)(2,1)S(1)}, u32[]{:S(2)}, u32[]{:S(2)}) collective-permute-start(bf16[32,64,128]{2,1,0:T(8,128)(2,1)S(1)} %get-tuple-element.38), channel_id=1, source_target_pairs={{0,1},{1,0},{2,3},{3,2},{4,5},{5,4},{6,7},{7,6},{8,9},{9,8},{10,11... | collective-permute-start | bytes 1572872 | tf_op jit(solution)/shard_map/ppermute | solution.py:726
  47.8 5.6 %collective-permute-start.1 = (bf16[4,128,128]{2,1,0:T(8,128)(2,1)S(1)}, bf16[4,128,128]{2,1,0:T(8,128)(2,1)S(1)}, u32[]{:S(2)}, u32[]{:S(2)}) collective-permute-start(bf16[4,128,128]{2,1,0:T(8,128)(2,1)S(1)} %get-tuple-element.40), channel_id=1, source_target_pairs={{0,4},{4,0},{8,12},{12,8},{16,20},{20,16},{24,28},{28,24},{1,5},{5... | collective-permute-start | bytes 393224 | tf_op jit(solution)/shard_map/ppermute | solution.py:734
  48.9 15.9 %collective-permute-start.4 = (bf16[32,64,128]{2,1,0:T(8,128)(2,1)S(1)}, bf16[32,64,128]{2,1,0:T(8,128)(2,1)S(1)}, u32[]{:S(2)}, u32[]{:S(2)}) collective-permute-start(bf16[32,64,128]{2,1,0:T(8,128)(2,1)S(1)} %get-tuple-element.43), channel_id=1, source_target_pairs={{0,1},{1,0},{2,3},{3,2},{4,5},{5,4},{6,7},{7,6},{8,9},{9,8},{10,11... | collective-permute-start | bytes 1572872 | tf_op jit(solution)/shard_map/ppermute | solution.py:730
  49.1 15.7 %collective-permute-start.5 = (bf16[32,64,128]{2,1,0:T(8,128)(2,1)S(1)}, bf16[32,64,128]{2,1,0:T(8,128)(2,1)S(1)}, u32[]{:S(2)}, u32[]{:S(2)}) collective-permute-start(bf16[32,64,128]{2,1,0:T(8,128)(2,1)S(1)} %add_convert_fusion), channel_id=1, source_target_pairs={{0,2},{1,3},{2,0},{3,1},{4,6},{5,7},{6,4},{7,5},{8,10},{9,11},{10,... | collective-permute-start | bytes 1572872 | tf_op jit(solution)/shard_map/ppermute | solution.py:729
  53.4 4.3 %collective-permute-start.2 = (bf16[2,128,128]{2,1,0:T(8,128)(2,1)S(1)}, bf16[2,128,128]{2,1,0:T(8,128)(2,1)S(1)}, u32[]{:S(2)}, u32[]{:S(2)}) collective-permute-start(bf16[2,128,128]{2,1,0:T(8,128)(2,1)S(1)} %slice.41), channel_id=1, source_target_pairs={{0,8},{4,12},{8,0},{12,4},{16,24},{20,28},{24,16},{28,20},{1,9},{5... | collective-permute-start | bytes 196616 | tf_op jit(solution)/shard_map/ppermute | solution.py:734
  57.8 6.2 %collective-permute-start.3 = (bf16[1,128,128]{2,1,0:T(8,128)(2,1)S(1)}, bf16[1,128,128]{2,1,0:T(8,128)(2,1)S(1)}, u32[]{:S(2)}, u32[]{:S(2)}) collective-permute-start(bf16[1,128,128]{2,1,0:T(8,128)(2,1)S(1)} %slice.42), channel_id=1, source_target_pairs={{0,16},{4,20},{8,24},{12,28},{16,0},{20,4},{24,8},{28,12},{1,17},{... | collective-permute-start | bytes 98312 | tf_op jit(solution)/shard_map/ppermute | solution.py:734

commit v4 on v3

--- a/solution.py
+++ b/solution.py
@@ -16,7 +16,9 @@
 VMEM = pl.BlockSpec(memory_space=pltpu.VMEM)
 HBM = pl.BlockSpec(memory_space=pltpu.HBM)
 chunk_unroll = 8
-passage_unroll = 4
+chunk_tail = 4
+passage_unroll = 8
+early_slots = 24
 copy_parts = 8
 meta_rows = 8
 
@@ -135,18 +137,41 @@
 
 
 def list_layout(group):
-    empty = -(-group // chunk_pairs) * chunk_pairs
-    return empty, empty + chunk_pairs
+    empty = -(-group // chunk_pairs) * chunk_pairs // 4
+    return empty, empty + chunk_pairs // 4
 
 
 def slot_total(pass_count, pairs):
     worst = (pairs + pass_count * (chunk_pairs - 1)) // chunk_pairs
-    return -(-(worst + 1) // chunk_unroll) * chunk_unroll
-
-
-def steps_of(list_smem, tables):
-    total = list_smem[tables + 4, 0]
-    return jnp.maximum((total + chunk_unroll - 1) // chunk_unroll, 1)
+    return -(-max(worst, early_slots) // chunk_unroll) * chunk_unroll
+
+
+def list_ids(list_smem, row, p):
+    words = [list_smem[row + w, p] for w in range(chunk_pairs // 4)]
+    return [(words[r // 4] >> (8 * (r % 4))) & 255 for r in range(chunk_pairs)]
+
+
+def each_chunk(list_smem, tables, visit):
+    total = jnp.maximum(list_smem[tables + 4, 0], 1)
+    full = total // chunk_unroll
+    tail = (total - full * chunk_unroll + chunk_tail - 1) // chunk_tail
+
+    def step(i, carry):
+        visit(i * chunk_unroll, chunk_unroll)
+        return carry
+
+    def tail_step(i, carry):
+        visit(full * chunk_unroll + i * chunk_tail, chunk_tail)
+        return carry
+
+    lax.fori_loop(0, full, step, 0)
+    lax.fori_loop(0, tail, tail_step, 0)
+    return full * chunk_unroll + tail * chunk_tail
+
+
+def slots_used(list_smem, tables):
+    total = jnp.maximum(list_smem[tables + 4, 0], 1)
+    return (total + chunk_tail - 1) // chunk_tail * chunk_tail
 
 
 def part_copies(source, target, sems):
@@ -176,6 +201,7 @@
     target_ref,
     list_ref,
     zw_ref,
+    inverse_ref,
     norm_ref,
     soft_ref,
     ext_ref,
@@ -235,34 +261,53 @@
     rank = jnp.dot(lower, active_value.astype(jnp.bfloat16), preferred_element_type=jnp.float32)
     rank = jnp.where(active, rank, -1.0)
     less = lax.broadcasted_iota(jnp.int32, main.shape, 0).astype(jnp.float32) - group
-    for k in range(empty):
-        found = jnp.sum(jnp.where(rank == k, less, 0.0), 0, keepdims=True) + group
-        list_ref[k : k + 1, :] = found.astype(jnp.int32)
-    list_ref[empty:tables, :] = jnp.full((tables - empty, 128), group, jnp.int32)
+    for w in range(empty):
+        word = jnp.zeros((1, 128), jnp.int32)
+        for b in range(4):
+            found = jnp.sum(jnp.where(rank == 4 * w + b, less, 0.0), 0, keepdims=True) + group
+            word = word | (found.astype(jnp.int32) << (8 * b))
+        list_ref[w : w + 1, :] = word
+    blank = jnp.full((tables - empty, 128), group, jnp.int32)
+    list_ref[empty:tables, :] = blank | (blank << 8) | (blank << 16) | (blank << 24)
     square = (128, 128)
     first_id = lax.broadcasted_iota(jnp.int32, square, 0)
     second_id = lax.broadcasted_iota(jnp.int32, square, 1)
     counts = lax.dot_general(
-        active_value, jnp.ones((group, 128), jnp.float32), (((0,), (0,)), ((), ())),
+        active_value.astype(jnp.bfloat16),
+        jnp.ones((group, 128), jnp.bfloat16),
+        (((0,), (0,)), ((), ())),
         preferred_element_type=jnp.float32,
     )
     chunks = jnp.floor((counts + (chunk_pairs - 1)) * (1.0 / chunk_pairs))
-    ends = jnp.dot(
-        (first_id >= second_id).astype(jnp.bfloat16),
-        chunks.astype(jnp.bfloat16),
-        preferred_element_type=jnp.float32,
-    )
-    past = ends <= second_id.astype(jnp.float32)
-    passage_of = jnp.sum(jnp.where(past, 1.0, 0.0), 0, keepdims=True)
-    start_of = jnp.sum(jnp.where(past, chunks, 0.0), 0, keepdims=True)
+    more = jnp.maximum(chunks - 2.0, 0.0)
+    lower_square = (first_id >= second_id).astype(jnp.bfloat16)
+    ends = jnp.dot(lower_square, chunks.astype(jnp.bfloat16), preferred_element_type=jnp.float32)
+    more_ends = jnp.dot(lower_square, more.astype(jnp.bfloat16), preferred_element_type=jnp.float32)
     chunk_id = lax.broadcasted_iota(jnp.int32, (1, 128), 1).astype(jnp.float32)
+
+    def places_of(chunk_ends, chunk_counts):
+        past = chunk_ends <= second_id.astype(jnp.float32)
+        passage_of = jnp.sum(jnp.where(past, 1.0, 0.0), 0, keepdims=True)
+        start_of = jnp.sum(jnp.where(past, chunk_counts, 0.0), 0, keepdims=True)
+        return passage_of, chunk_id - start_of
+
+    def last_row(values):
+        return jnp.sum(jnp.where(first_id == 127, values, 0.0), 0, keepdims=True)
+
+    passage_of, chunk_of = places_of(ends, chunks)
+    more_passage, more_chunk = places_of(more_ends, more)
     beyond = passage_of > pass_count - 0.5
-    passage_of = jnp.where(beyond, 0.0, passage_of)
-    first_of = jnp.where(beyond, float(empty), (chunk_id - start_of) * chunk_pairs)
-    flat = jnp.sum(active_value, 0, keepdims=True)
-    starts = jnp.sum(jnp.where(first_id == second_id, ends - chunks, 0.0), 0, keepdims=True)
-    total = jnp.sum(jnp.where(first_id == 127, ends, 0.0), 0, keepdims=True)
-    for row, value in enumerate((passage_of, first_of, starts, flat, total)):
+    rows_of = (
+        jnp.where(beyond, 0.0, passage_of),
+        jnp.where(beyond, float(empty), chunk_of * (chunk_pairs // 4)),
+        jnp.sum(jnp.where(first_id == second_id, ends - chunks, 0.0), 0, keepdims=True),
+        jnp.sum(active_value, 0, keepdims=True),
+        last_row(ends),
+        more_passage,
+        more_chunk + 2.0,
+        last_row(more_ends),
+    )
+    for row, value in enumerate(rows_of):
         list_ref[tables + row : tables + row + 1, :] = value.astype(jnp.int32)
     copy = pltpu.make_async_copy(list_ref, list_smem, sem)
     copy.start()
@@ -275,29 +320,27 @@
 
     def chunk(slot):
         p = list_smem[tables, slot]
-        first = list_smem[tables + 1, slot]
-        ids = [list_smem[first + r, p] for r in range(chunk_pairs)]
+        ids = list_ids(list_smem, list_smem[tables + 1, slot], p)
         tile = jnp.concatenate([qn_ref[place, :] for place in query_places(ids, query_tokens)], 0)
         dots = lax.dot_general(
             norm_ref[p], tile, (((1,), (1,)), ((), ())), preferred_element_type=jnp.float32
         )
         power = jnp.exp2(dots * (math.log2(math.e) / softness_scale))
         sums = jnp.sum(power, 0, keepdims=True)
-        soft_ref[slot] = (power * (1.0 / sums)).astype(jnp.bfloat16)
+        soft_ref[slot] = power.astype(jnp.bfloat16)
+        inverse_ref[pl.ds(slot, 1), :] = 1.0 / sums
         for r, n in enumerate(ids):
             sums_ref[pl.ds(p * stride + n, 1), :query_tokens] = sums[
                 :, r * query_tokens : (r + 1) * query_tokens
             ]
 
-    def step(i, carry):
-        for u in range(chunk_unroll):
-            chunk(i * chunk_unroll + u)
-        for u in range(chunk_unroll):
-            soft_copy(i * chunk_unroll + u).start()
-        return carry
-
-    steps = steps_of(list_smem, tables)
-    lax.fori_loop(0, steps, step, 0)
+    def visit(first, count):
+        for u in range(count):
+            chunk(first + u)
+        for u in range(count):
+            soft_copy(first + u).start()
+
+    used = each_chunk(list_smem, tables, visit)
 
     scores = jnp.zeros(main.shape, jnp.float32)
     for p in range(pass_count):
@@ -318,7 +361,7 @@
         soft_copy(slot).wait()
         return carry
 
-    lax.fori_loop(0, steps * chunk_unroll, drain, 0)
+    lax.fori_loop(0, used, drain, 0)
 
 
 def forward(received, norm, cand_count, query_count, query_tokens):
@@ -327,14 +370,14 @@
     group = sources * query_count
     capacity = max(2, -(-5 * query_count * cand_count // (2 * sources)))
     slots = slot_total(pass_count, sources * capacity)
-    list_rows = list_layout(group)[1] + meta_rows
+    list_rows = -(-(list_layout(group)[1] + meta_rows) // 8) * 8
     rows = query_count * query_tokens
     soft_shape = (slots, tokens, chunk_pairs * query_tokens)
     flops = 2 * slots * chunk_pairs * query_tokens * tokens * width
     return pl.pallas_call(
         lambda *refs: forward_kernel(cand_count, query_count, query_tokens, *refs),
         in_specs=[VMEM, HBM],
-        out_specs=[HBM] + [VMEM] * 6,
+        out_specs=[HBM] + [VMEM] * 7,
         out_shape=[
             pltpu.HBM(soft_shape, jnp.bfloat16),
             jax.ShapeDtypeStruct((sources * rows + query_tokens, width), jnp.bfloat16),
@@ -343,6 +386,7 @@
             jax.ShapeDtypeStruct((group, 128), jnp.float32),
             jax.ShapeDtypeStruct((list_rows, 128), jnp.int32),
             jax.ShapeDtypeStruct((sources, group, 128), jnp.float32),
+            jax.ShapeDtypeStruct((slots, chunk_pairs * query_tokens), jnp.float32),
         ],
         scratch_shapes=[
             pltpu.VMEM(norm.shape, jnp.bfloat16),
@@ -378,6 +422,7 @@
     score_ref,
     many_ref,
     target_ref,
+    inverse_ref,
     raised_ref,
     wanted_ref,
     flip_ref,
@@ -406,12 +451,13 @@
         soft_copy(slot).start()
         return carry
 
-    list_copy.wait()
-    steps = steps_of(list_smem, tables)
     lax.fori_loop(0, chunk_unroll, fetch, 0)
     for copy in flip_copies:
         copy.start()
-    lax.fori_loop(chunk_unroll, steps * chunk_unroll, fetch, 0)
+    lax.fori_loop(chunk_unroll, early_slots, fetch, 0)
+    list_copy.wait()
+    used = slots_used(list_smem, tables)
+    lax.fori_loop(early_slots, used, fetch, 0)
     spread(raised_rows, many_ref[...] * jnp.exp(score_ref[...]), pass_count, stride)
     spread(wanted_rows, target_ref[...], pass_count, stride)
     raised_sum[...] = jnp.zeros(raised_sum.shape, jnp.float32)
@@ -421,11 +467,10 @@
 
     def chunk(slot):
         p = list_smem[tables, slot]
-        first = list_smem[tables + 1, slot]
-        ids = [list_smem[first + r, p] for r in range(chunk_pairs)]
+        ids = list_ids(list_smem, list_smem[tables + 1, slot], p)
         places = query_places(ids, query_tokens)
         mixed = jnp.dot(flip_ref[p], soft_ref[slot], preferred_element_type=jnp.float32)
-        mixed = jnp.transpose(mixed, (1, 0))
+        mixed = jnp.transpose(mixed * inverse_ref[pl.ds(slot, 1), :], (1, 0))
         for total, rows in ((raised_sum, raised_rows), (wanted_sum, wanted_rows)):
             added = [
                 total[place, :]
@@ -436,19 +481,24 @@
             for place, value in zip(places, added):
                 total[place, :] = value
 
-    def step(i, carry):
-        for u in range(chunk_unroll):
-            soft_copy(i * chunk_unroll + u).wait()
-        for u in range(chunk_unroll):
-            chunk(i * chunk_unroll + u)
+    def visit(first, count):
+        for u in range(count):
+            soft_copy(first + u).wait()
+        for u in range(count):
+            chunk(first + u)
+
+    each_chunk(list_smem, tables, visit)
+
+    def drain(slot, carry):
+        soft_copy(slot).wait()
         return carry
 
-    lax.fori_loop(0, steps, step, 0)
+    lax.fori_loop(used, early_slots, drain, 0)
     raised_ref[...] = raised_sum[: group * query_tokens, :]
     wanted_ref[...] = wanted_sum[: group * query_tokens, :]
 
 
-def attend(flip, soft, ids, score, many, target, query_tokens):
+def attend(flip, soft, ids, score, many, target, inverse, query_tokens):
     slots, tokens, columns = soft.shape
     pass_count, width, _ = flip.shape
     group = score.shape[0]
@@ -458,7 +508,7 @@
     padded = pltpu.VMEM(((group + 1) * query_tokens, width), jnp.float32)
     return pl.pallas_call(
         lambda *refs: attend_kernel(query_tokens, *refs),
-        in_specs=[HBM, HBM] + [VMEM] * 4,
+        in_specs=[HBM, HBM] + [VMEM] * 5,
         out_specs=[VMEM] * 2,
         out_shape=[total, total],
         scratch_shapes=[
@@ -476,7 +526,7 @@
         compiler_params=params(),
         cost_estimate=pl.CostEstimate(flops=flops, bytes_accessed=12 << 20, transcendentals=0),
         name="attend",
-    )(in_hbm(flip), in_hbm(soft), ids, score, many, target)
+    )(in_hbm(flip), in_hbm(soft), ids, score, many, target, inverse)
 
 
 def halving_order(count):
@@ -546,10 +596,10 @@
 
 def passage_kernel(
     query_tokens,
-    start,
     list_ref,
     grads_ref,
     qn_ref,
+    inverse_ref,
     soft_hbm,
     own_ref,
     core_ref,
@@ -579,14 +629,14 @@
         soft_copy(slot).wait()
         return carry
 
+    lax.fori_loop(0, early_slots, fetch, 0)
+    spread(grad_ref, grads_ref[...], pass_count, stride)
     list_copy.wait()
-    low = list_smem[tables + 2, start]
-    high = jnp.maximum(list_smem[tables + 2, start + pass_count], low + 1)
-    lax.fori_loop(low, high, fetch, 0)
-    spread(grad_ref, grads_ref[...], pass_count, stride, start)
-
-    def tile(p, first):
-        ids = [list_smem[first + r, start + p] for r in range(chunk_pairs)]
+    total = list_smem[tables + 4, 0]
+    lax.fori_loop(early_slots, total, fetch, 0)
+
+    def tile(p, row):
+        ids = list_ids(list_smem, row, p)
         return [
             (qn_ref[place, :].astype(jnp.float32) * grad_ref[pl.ds(p * stride + n, 1), :]).astype(
                 jnp.bfloat16
@@ -594,16 +644,22 @@
             for n, place in zip(ids, query_places(ids, query_tokens))
         ]
 
+    def weights(slot):
+        value = soft_ref[slot]
+        tokens, columns = value.shape
+        scale = jnp.broadcast_to(inverse_ref[pl.ds(slot, 1), :], (16, columns)).astype(jnp.bfloat16)
+        return (value.reshape(tokens // 16, 16, columns) * scale[None]).reshape(tokens, columns)
+
     outs = (own_ref, core_ref, far_ref, cross_ref)
 
     def passage(p):
-        pairs = list_smem[tables + 3, start + p]
-        slot = list_smem[tables + 2, start + p]
+        pairs = list_smem[tables + 3, p]
+        slot = list_smem[tables + 2, p]
         tiles, softs = [], []
         for h in range(2):
             some = pairs > h * chunk_pairs
-            tiles += tile(p, jnp.where(some, h * chunk_pairs, empty))
-            softs.append(soft_ref[jnp.where(some, slot + h, low)])
+            tiles += tile(p, jnp.where(some, h * (chunk_pairs // 4), empty))
+            softs.append(weights(jnp.where(some, slot + h, 0)))
         value = jnp.dot(
             jnp.concatenate(softs, 1),
             jnp.concatenate(tiles, 0),
@@ -613,44 +669,39 @@
             ref[p] = value[place * share : (place + 1) * share]
 
     def step(i, ready):
-        last = (i + 1) * passage_unroll
-        needed = jnp.maximum(list_smem[tables + 2, start + last], low + 1)
+        needed = jnp.maximum(list_smem[tables + 2, (i + 1) * passage_unroll], 1)
         lax.fori_loop(ready, needed, drain, 0)
         for u in range(passage_unroll):
             passage(i * passage_unroll + u)
         return needed
 
-    lax.fori_loop(0, pass_count // passage_unroll, step, low)
-
-    def rest(p, carry):
-        chunks = (list_smem[tables + 3, start + p] + chunk_pairs - 1) // chunk_pairs
-        slot = list_smem[tables + 2, start + p]
-
-        def add(b, inner):
-            value = jnp.dot(
-                soft_ref[slot + b],
-                jnp.concatenate(tile(p, b * chunk_pairs), 0),
-                preferred_element_type=jnp.float32,
-            )
-            for place, ref in enumerate(outs):
-                piece = value[place * share : (place + 1) * share]
-                ref[p] = (ref[p].astype(jnp.float32) + piece).astype(jnp.bfloat16)
-            return inner
-
-        lax.fori_loop(2, chunks, add, 0)
+    ready = lax.fori_loop(0, pass_count // passage_unroll, step, jnp.int32(0))
+    lax.fori_loop(ready, early_slots, drain, 0)
+
+    def rest(i, carry):
+        p = list_smem[tables + 5, i]
+        b = list_smem[tables + 6, i]
+        value = jnp.dot(
+            weights(list_smem[tables + 2, p] + b),
+            jnp.concatenate(tile(p, b * (chunk_pairs // 4)), 0),
+            preferred_element_type=jnp.float32,
+        )
+        for place, ref in enumerate(outs):
+            piece = value[place * share : (place + 1) * share]
+            ref[p] = (ref[p].astype(jnp.float32) + piece).astype(jnp.bfloat16)
         return carry
 
-    lax.fori_loop(0, pass_count, rest, 0)
-
-
-def passage_backward(ids, grads, qn, soft, start, pass_count, query_tokens, slices):
+    lax.fori_loop(0, list_smem[tables + 7, 0], rest, 0)
+
+
+def passage_backward(ids, grads, qn, inverse, soft, pass_count, query_tokens, slices):
     slots, tokens, columns = soft.shape
     width = qn.shape[1]
     piece = jax.ShapeDtypeStruct((pass_count, tokens // slices, width), jnp.bfloat16)
     flops = 4 * pass_count * columns * tokens * width
     return pl.pallas_call(
-        lambda *refs: passage_kernel(query_tokens, start, *refs),
-        in_specs=[VMEM] * 3 + [HBM],
+        lambda *refs: passage_kernel(query_tokens, *refs),
+        in_specs=[VMEM] * 4 + [HBM],
         out_specs=[VMEM] * 4,
         out_shape=[piece] * 4,
         scratch_shapes=[
@@ -663,7 +714,7 @@
         compiler_params=params(),
         cost_estimate=pl.CostEstimate(flops=flops, bytes_accessed=6 << 20, transcendentals=0),
         name="passage_backward",
-    )(ids, grads, qn, in_hbm(soft))
+    )(ids, grads, qn, inverse, in_hbm(soft))
 
 
 def finish_kernel(raw_ref, *refs):
@@ -712,32 +763,39 @@
         tiled=True,
     )
     norm, flip, own_raw = prepare_passages(passages, slices)
-    soft, qn, score, many, target, ids, zw = forward(
+    soft, qn, score, many, target, ids, zw, inverse = forward(
         received, norm, cand_count, query_count, query_tokens
     )
     zw = lax.all_to_all(zw, "psg", split_axis=0, concat_axis=0, tiled=True)
-    raised_sum, wanted_sum = attend(flip, soft, ids, score, many, target, query_tokens)
+    raised_sum, wanted_sum = attend(
+        flip, soft, ids, score, many, target, inverse, query_tokens
+    )
     keep, send, grads = query_backward(zw, score, many, target, raised_sum, wanted_sum)
     near = [(k, k ^ 1) for k in range(slices)]
     away = [(k, k ^ 2) for k in range(slices)]
     own, core, far, cross = passage_backward(
-        ids, grads, qn, soft, 0, pass_count, query_tokens, slices
+        ids, grads, qn, inverse, soft, pass_count, query_tokens, slices
     )
     cross = lax.ppermute(cross, "qry", near)
     far = (far.astype(jnp.float32) + cross.astype(jnp.float32)).astype(jnp.bfloat16)
-    far, send = lax.optimization_barrier((far, send))
+    far, send, core = lax.optimization_barrier((far, send, core))
     far = lax.ppermute(far, "qry", away)
     core = lax.ppermute(core, "qry", near)
     bit = 1
-    while bit < sources:
-        swap = [(i, i ^ bit) for i in range(sources)]
-        send = lax.ppermute(send, "psg", swap)
-        if bit * 2 < sources:
-            total = keep.astype(jnp.float32) + send.astype(jnp.float32)
-            half = total.shape[0] // 2
+    while sources // bit > 4:
+        send = lax.ppermute(send, "psg", [(i, i ^ bit) for i in range(sources)])
+        send, zw = lax.optimization_barrier((send, zw))
+        total = keep.astype(jnp.float32) + send.astype(jnp.float32)
+        half = total.shape[0] // 2
+        bit *= 2
+        if sources // bit > 4:
             keep, send = total[:half], total[half:].astype(jnp.bfloat16)
-        bit *= 2
-    grad_queries = finish_queries(queries.reshape(rows, width), [keep[0], send[0]])
+    query_parts = [total[0]]
+    for place, d in enumerate(halving_order(sources)[: total.shape[0]]):
+        if place:
+            piece = total[place].astype(jnp.bfloat16)
+            query_parts.append(lax.ppermute(piece, "psg", [(i, i ^ d) for i in range(sources)]))
+    grad_queries = finish_queries(queries.reshape(rows, width), query_parts)
 
     grad_passages = finish(own_raw, [own, core, far])
 

time: 65.9 us -> 61.5 us (0.933)
  Pallas kernels: 30.9 us -> 28.6 us
  waiting for transfers between devices: 15.1 us -> 13.8 us
  starting transfers between devices: 18.1 us -> 17 us
    pallas_call x1, Pallas kernels: 7.49 us -> 5.36 us  [passage_backward(): pl.pallas_call(lambda *refs: passage_kernel(query_tokens, *refs), in_spec...]
    ppermute x3 -> x4, waiting for transfers between devices: 8.15 us -> 6.08 us  [the longest x1 3.51 us: shards(): send = lax.ppermute(send, 'psg', [(i, i ^ bit) for i in range(sources)])]
    ppermute x3 -> x4, starting transfers between devices: 6.11 us -> 4.53 us  [the longest x3 4.45 us: shards(): lax.ppermute(piece, 'psg', [(i, i ^ d) for i in range(sources)])]
  transfers between devices with their start and end apart: 8 -> 9, of which waited for: 6 -> 6; matrix products, arithmetic and copies ran while one was open for 2% -> 2% of each run, Pallas kernels for 19% -> 20%
where the time goes in v4:
time: 61.5 us; the launch traced here: 61.4 us
  Pallas kernels  28.6 us (47%)
  starting transfers between devices  17 us (28%)
  waiting for transfers between devices  13.8 us (22%)
  other arithmetic  1.06 us (2%)
  between operations  0.76 us (1%)
    pallas_call x1, Pallas kernels, forward(): pl.pallas_call(lambda *refs: forward_kernel(cand_count, query_count, quer...  7.61 us
    all_to_all x1, starting transfers between devices, shards(): lax.all_to_all(pack(queries.reshape(rows, width), candidates, teacher, so...  7.29 us
    pallas_call x1, Pallas kernels, attend(): pl.pallas_call(lambda *refs: attend_kernel(query_tokens, *refs), in_specs...  6.73 us
    pallas_call x1, Pallas kernels, passage_backward(): pl.pallas_call(lambda *refs: passage_kernel(query_tokens, *refs), in_spec...  5.36 us
    pallas_call x1, Pallas kernels, prepare_passages(): pl.pallas_call(lambda *refs: passages_kernel(slices, *refs), grid=(count...  4.93 us
    all_to_all x1, waiting for transfers between devices, shards(): lax.all_to_all(pack(queries.reshape(rows, width), candidates, teacher, so...  4.69 us
    ppermute x3, starting transfers between devices, shards(): lax.ppermute(piece, 'psg', [(i, i ^ d) for i in range(sources)])  4.45 us
    ppermute x1, waiting for transfers between devices, shards(): send = lax.ppermute(send, 'psg', [(i, i ^ bit) for i in range(sources)])  3.51 us
  transfers between devices with their start and end apart: 9, of which 6 were waited for; matrix products, arithmetic and copies ran while one was open for 2% of the time, Pallas kernels for 20%

profile of v4, /device:TPU:0, one launch (start us, length us, event | category | flops | bytes accessed | tf_op | source)
XLA Modules:
  0.0 61.4 jit_solution(95264528597466968)
XLA Ops:
  0.6 1.6 %pack.1 = bf16[8,144,128]{2,1,0:T(8,128)(2,1)} custom-call(bf16[128,128]{1,0:T(8,128)(2,1)} %bitcast.12, s32[4,32]{1,0:T(4,128)} %refs_1_.1, f32[4,32]{1,0:T(4,128)} %refs_2_.1), custom_call_target="tpu_custom_call" | custom-call | tf_op jit(solution)/shard_map/pack/pallas_call | solution.py:74
  2.2 7.3 %all-to-all-start = ((bf16[8,144,128]{2,1,0:T(8,128)(2,1)}), bf16[8,144,128]{2,1,0:T(8,128)(2,1)S(1)}, u32[]{:S(2)}, u32[]{:S(2)}) async-start(bf16[8,144,128]{2,1,0:T(8,128)(2,1)} %pack.1), calls=%async_computation | async-start | bytes 589824 | tf_op jit(solution)/shard_map/all_to_all | solution.py:758
  9.5 4.9 %prepare_passages.1 = (bf16[32,256,128]{2,1,0:T(8,128)(2,1)}, bf16[32,128,256]{2,1,0:T(8,128)(2,1)}, bf16[32,64,128]{2,1,0:T(8,128)(2,1)}) custom-call(bf16[32,256,128]{2,1,0:T(8,128)(2,1)} %refs_0_.1), custom_call_target="tpu_custom_call" | custom-call | flops 16777216 | bytes 6291456 | tf_op jit(solution)/shard_map/prepare_passages/pallas_call | solution.py:119
  14.4 4.7 %all-to-all-done.refs_0_ = bf16[8,144,128]{2,1,0:T(8,128)(2,1)S(1)} async-done(((bf16[8,144,128]{2,1,0:T(8,128)(2,1)}), bf16[8,144,128]{2,1,0:T(8,128)(2,1)S(1)}, u32[]{:S(2)}, u32[]{:S(2)}) %all-to-all-start) | async-done | bytes 294944 | tf_op jit(solution)/shard_map/all_to_all | solution.py:758
  19.1 7.6 %forward.1 = (bf16[72,256,256]{2,1,0:T(8,128)(2,1)}, bf16[1056,128]{1,0:T(8,128)(2,1)S(1)}, f32[32,128]{1,0:T(8,128)S(1)}, f32[32,128]{1,0:T(8,128)S(1)}, f32[32...) custom-call(bf16[8,144,128]{2,1,0:T(8,128)(2,1)S(1)} %all-to-all-done.refs_0_, ...), custom_call_target="tpu_custom_call" | custom-call | flops 1207959552 | bytes 12582912 | tf_op jit(solution)/shard_map/forward/pallas_call | solution.py:377
  26.7 3.4 %all-to-all-start.1 = ((f32[8,32,128]{2,1,0:T(8,128)}), f32[8,32,128]{2,1,0:T(8,128)S(1)}, u32[]{:S(2)}, u32[]{:S(2)}) async-start(f32[8,32,128]{2,1,0:T(8,128)} %get-tuple-element.30), calls=%async_computation.1 | async-start | bytes 262144 | tf_op jit(solution)/shard_map/all_to_all | solution.py:769
  30.1 6.7 %attend.1 = (f32[1024,128]{1,0:T(8,128)S(1)}, f32[1024,128]{1,0:T(8,128)S(1)}) custom-call(bf16[32,128,256]{2,1,0:T(8,128)(2,1)} %get-tuple-element.34.refs_0_, bf16[72,256,256]{2,1,0:T(8,128)(2,1)} %get-tuple-element.35.refs_1_.refs_4_, s32[24,128]{1,0:T(8,128)S(1)} %get-tuple-element.29.refs_2_.refs_0_, f32[32,128]{1,0:T(8,128)S(1)} %get-tuple-element.31.refs_3_.refs_1_, ...), custom_call_target="tpu_custom_call" | custom-call | flops 1207959552 | bytes 12582912 | tf_op jit(solution)/shard_map/attend/pallas_call | solution.py:509
  36.9 0.5 all-to-all-done.1.refs_0_
  37.6 5.4 %passage_backward.1 = (bf16[32,64,128]{2,1,0:T(8,128)(2,1)S(1)}, bf16[32,64,128]{2,1,0:T(8,128)(2,1)S(1)}, bf16[32,64,128]{2,1,0:T(8,128)(2,1)S(1)}, bf16[32,64,128]{2,1,0:T(8,128)(2,1)S(1)}) custom-call(s32[24,128]{1,0:T(8,128)S(1)} %get-tuple-element.29.refs_2_.refs_0_, f32[32,128]{1,0:T(8,128)S(1)} %get-tuple-element.39.refs_1_, ...), custom_call_target="tpu_custom_call" | custom-call | flops 1073741824 | bytes 6291456 | tf_op jit(solution)/shard_map/passage_backward/pallas_call | solution.py:702
  43.1 1.9 %collective-permute-done = bf16[32,64,128]{2,1,0:T(8,128)(2,1)S(1)} collective-permute-done((bf16[32,64,128]{2,1,0:T(8,128)(2,1)S(1)}, bf16[32,64,128]{2,1,0:T(8,128)(2,1)S(1)}, u32[]{:S(2)}, u32[]{:S(2)}) %collective-permute-start) | collective-permute-done | bytes 524320 | tf_op jit(solution)/shard_map/ppermute | solution.py:779
  45.0 0.2 add_convert_fusion
  45.4 0.2 fusion
  45.6 0.2 collective-permute-start.5
  45.8 1.5 %collective-permute-start.6 = (bf16[32,64,128]{2,1,0:T(8,128)(2,1)S(1)}, bf16[32,64,128]{2,1,0:T(8,128)(2,1)S(1)}, u32[]{:S(2)}, u32[]{:S(2)}) collective-permute-start(bf16[32,64,128]{2,1,0:T(8,128)(2,1)S(1)} %add_convert_fusion), channel_id=1, source_target_pairs={{0,2},{1,3},{2,0},{3,1},{4,6},{5,7},{6,4},{7,5},{8,10},{9,11},{10,... | collective-permute-start | bytes 1572872 | tf_op jit(solution)/shard_map/ppermute | solution.py:782
  47.2 3.5 %collective-permute-done.1 = bf16[4,128,128]{2,1,0:T(8,128)(2,1)S(1)} collective-permute-done((bf16[4,128,128]{2,1,0:T(8,128)(2,1)S(1)}, bf16[4,128,128]{2,1,0:T(8,128)(2,1)S(1)}, u32[]{:S(2)}, u32[]{:S(2)}) %collective-permute-start.1) | collective-permute-done | bytes 131104 | tf_op jit(solution)/shard_map/ppermute | solution.py:786
  50.8 0.7 %collective-permute-start.2 = (bf16[128,128]{1,0:T(8,128)(2,1)S(1)}, bf16[128,128]{1,0:T(8,128)(2,1)S(1)}, u32[]{:S(2)}, u32[]{:S(2)}) collective-permute-start(bf16[128,128]{1,0:T(8,128)(2,1)S(1)} %get-tuple-element.59), channel_id=1, source_target_pairs={{0,16},{4,20},{8,24},{12,28},{16,0},{20,4},{24,8},{28,12},{1,17},{... | collective-permute-start | bytes 98312 | tf_op jit(solution)/shard_map/ppermute | solution.py:797
  51.5 1.3 %collective-permute-start.3 = (bf16[128,128]{1,0:T(8,128)(2,1)S(1)}, bf16[128,128]{1,0:T(8,128)(2,1)S(1)}, u32[]{:S(2)}, u32[]{:S(2)}) collective-permute-start(bf16[128,128]{1,0:T(8,128)(2,1)S(1)} %get-tuple-element.58), channel_id=1, source_target_pairs={{0,8},{4,12},{8,0},{12,4},{16,24},{20,28},{24,16},{28,20},{1,9},{5... | collective-permute-start | bytes 98312 | tf_op jit(solution)/shard_map/ppermute | solution.py:797
  52.9 2.4 %collective-permute-start.4 = (bf16[128,128]{1,0:T(8,128)(2,1)S(1)}, bf16[128,128]{1,0:T(8,128)(2,1)S(1)}, u32[]{:S(2)}, u32[]{:S(2)}) collective-permute-start(bf16[128,128]{1,0:T(8,128)(2,1)S(1)} %get-tuple-element.57), channel_id=1, source_target_pairs={{0,24},{4,28},{8,16},{12,20},{16,8},{20,12},{24,0},{28,4},{1,25},{... | collective-permute-start | bytes 98312 | tf_op jit(solution)/shard_map/ppermute | solution.py:797
  55.3 0.2 slice_reduce_fusion
  55.5 0.5 subtract_add_fusion
  56.0 2.6 %collective-permute-done.4.refs_3_ = bf16[128,128]{1,0:T(8,128)(2,1)S(1)} collective-permute-done((bf16[128,128]{1,0:T(8,128)(2,1)S(1)}, bf16[128,128]{1,0:T(8,128)(2,1)S(1)}, u32[]{:S(2)}, u32[]{:S(2)}) %collective-permute-start.4) | collective-permute-done | bytes 32800 | tf_op jit(solution)/shard_map/ppermute | solution.py:797
  58.6 0.8 %finish_queries.1 = bf16[128,128]{1,0:T(8,128)(2,1)} custom-call(bf16[128,128]{1,0:T(8,128)(2,1)S(1)} %bitcast.13, f32[128,128]{1,0:T(8,128)S(1)} %slice_bitcast_fusion.refs_0_, bf16[128,128]{1,0:T(8,128)(2,1)S(1)} %collective-permute-done.2.refs_1_, bf16[128,128]{1,0:T(8,128)(2,1)S(1)} %collective-permute-done.3.refs_2_, ...), custom_call_target="tpu_custom_call" | custom-call | tf_op jit(solution)/shard_map/finish_queries/pallas_call | solution.py:740
  59.4 0.6 collective-permute-done.6.refs_2_
  60.0 1.5 %finish.1 = bf16[32,64,128]{2,1,0:T(8,128)(2,1)} custom-call(bf16[32,64,128]{2,1,0:T(8,128)(2,1)S(1)} %copy-done, bf16[32,64,128]{2,1,0:T(8,128)(2,1)S(1)} %get-tuple-element.50.refs_0_, bf16[32,64,128]{2,1,0:T(8,128)(2,1)S(1)} %collective-permute-done.5.refs_1_, bf16[32,64,128]{2,1,0:T(8,128)(2,1)S(1)} %collective-permute-done.6.refs_2_), custom_call_target="tpu_custom_call" | custom-call | tf_op jit(solution)/shard_map/finish/pallas_call | solution.py:729
  (18 shorter events, 0.5 us)
Async XLA Ops:
  2.2 16.9 %all-to-all-start = ((bf16[8,144,128]{2,1,0:T(8,128)(2,1)}), bf16[8,144,128]{2,1,0:T(8,128)(2,1)S(1)}, u32[]{:S(2)}, u32[]{:S(2)}) async-start(bf16[8,144,128]{2,1,0:T(8,128)(2,1)} %pack.1), calls=%async_computation | async-start | bytes 589824 | tf_op jit(solution)/shard_map/all_to_all | solution.py:758
  26.7 10.7 %all-to-all-start.1 = ((f32[8,32,128]{2,1,0:T(8,128)}), f32[8,32,128]{2,1,0:T(8,128)S(1)}, u32[]{:S(2)}, u32[]{:S(2)}) async-start(f32[8,32,128]{2,1,0:T(8,128)} %get-tuple-element.30), calls=%async_computation.1 | async-start | bytes 262144 | tf_op jit(solution)/shard_map/all_to_all | solution.py:769
  37.6 7.7 %copy-start.2 = (f32[4,32]{1,0:T(4,128)S(1)}, f32[4,32]{1,0:T(4,128)}, u32[]{:S(2)}) copy-start(f32[4,32]{1,0:T(4,128)} %refs_2_.1) | copy-start | bytes 1540
  43.0 15.6 %copy-start.1 = (bf16[4,32,128]{2,1,0:T(8,128)(2,1)S(1)}, bf16[4,32,128]{2,1,0:T(8,128)(2,1)}, u32[]{:S(2)}) copy-start(bf16[4,32,128]{2,1,0:T(8,128)(2,1)} %param.4) | copy-start | bytes 98308
  43.0 17.0 %copy-start = (bf16[32,64,128]{2,1,0:T(8,128)(2,1)S(1)}, bf16[32,64,128]{2,1,0:T(8,128)(2,1)}, u32[]{:S(2)}) copy-start(bf16[32,64,128]{2,1,0:T(8,128)(2,1)} %get-tuple-element.49.raw_ref) | copy-start | bytes 1572868
  43.0 2.0 %collective-permute-start = (bf16[32,64,128]{2,1,0:T(8,128)(2,1)S(1)}, bf16[32,64,128]{2,1,0:T(8,128)(2,1)S(1)}, u32[]{:S(2)}, u32[]{:S(2)}) collective-permute-start(bf16[32,64,128]{2,1,0:T(8,128)(2,1)S(1)} %get-tuple-element.42), channel_id=1, source_target_pairs={{0,1},{1,0},{2,3},{3,2},{4,5},{5,4},{6,7},{7,6},{8,9},{9,8},{10,11... | collective-permute-start | bytes 1572872 | tf_op jit(solution)/shard_map/ppermute | solution.py:779
  45.1 5.6 %collective-permute-start.1 = (bf16[4,128,128]{2,1,0:T(8,128)(2,1)S(1)}, bf16[4,128,128]{2,1,0:T(8,128)(2,1)S(1)}, u32[]{:S(2)}, u32[]{:S(2)}) collective-permute-start(bf16[4,128,128]{2,1,0:T(8,128)(2,1)S(1)} %get-tuple-element.45), channel_id=1, source_target_pairs={{0,4},{4,0},{8,12},{12,8},{16,20},{20,16},{24,28},{28,24},{1,5},{5... | collective-permute-start | bytes 393224 | tf_op jit(solution)/shard_map/ppermute | solution.py:786
  45.6 13.8 %collective-permute-start.5 = (bf16[32,64,128]{2,1,0:T(8,128)(2,1)S(1)}, bf16[32,64,128]{2,1,0:T(8,128)(2,1)S(1)}, u32[]{:S(2)}, u32[]{:S(2)}) collective-permute-start(bf16[32,64,128]{2,1,0:T(8,128)(2,1)S(1)} %get-tuple-element.51), channel_id=1, source_target_pairs={{0,1},{1,0},{2,3},{3,2},{4,5},{5,4},{6,7},{7,6},{8,9},{9,8},{10,11... | collective-permute-start | bytes 1572872 | tf_op jit(solution)/shard_map/ppermute | solution.py:783
  45.8 14.2 %collective-permute-start.6 = (bf16[32,64,128]{2,1,0:T(8,128)(2,1)S(1)}, bf16[32,64,128]{2,1,0:T(8,128)(2,1)S(1)}, u32[]{:S(2)}, u32[]{:S(2)}) collective-permute-start(bf16[32,64,128]{2,1,0:T(8,128)(2,1)S(1)} %add_convert_fusion), channel_id=1, source_target_pairs={{0,2},{1,3},{2,0},{3,1},{4,6},{5,7},{6,4},{7,5},{8,10},{9,11},{10,... | collective-permute-start | bytes 1572872 | tf_op jit(solution)/shard_map/ppermute | solution.py:782
  50.8 5.2 %collective-permute-start.2 = (bf16[128,128]{1,0:T(8,128)(2,1)S(1)}, bf16[128,128]{1,0:T(8,128)(2,1)S(1)}, u32[]{:S(2)}, u32[]{:S(2)}) collective-permute-start(bf16[128,128]{1,0:T(8,128)(2,1)S(1)} %get-tuple-element.59), channel_id=1, source_target_pairs={{0,16},{4,20},{8,24},{12,28},{16,0},{20,4},{24,8},{28,12},{1,17},{... | collective-permute-start | bytes 98312 | tf_op jit(solution)/shard_map/ppermute | solution.py:797
  51.5 4.5 %collective-permute-start.3 = (bf16[128,128]{1,0:T(8,128)(2,1)S(1)}, bf16[128,128]{1,0:T(8,128)(2,1)S(1)}, u32[]{:S(2)}, u32[]{:S(2)}) collective-permute-start(bf16[128,128]{1,0:T(8,128)(2,1)S(1)} %get-tuple-element.58), channel_id=1, source_target_pairs={{0,8},{4,12},{8,0},{12,4},{16,24},{20,28},{24,16},{28,20},{1,9},{5... | collective-permute-start | bytes 98312 | tf_op jit(solution)/shard_map/ppermute | solution.py:797
  52.9 5.7 %collective-permute-start.4 = (bf16[128,128]{1,0:T(8,128)(2,1)S(1)}, bf16[128,128]{1,0:T(8,128)(2,1)S(1)}, u32[]{:S(2)}, u32[]{:S(2)}) collective-permute-start(bf16[128,128]{1,0:T(8,128)(2,1)S(1)} %get-tuple-element.57), channel_id=1, source_target_pairs={{0,24},{4,28},{8,16},{12,20},{16,8},{20,12},{24,0},{28,4},{1,25},{... | collective-permute-start | bytes 98312 | tf_op jit(solution)/shard_map/ppermute | solution.py:797

commit v5 on v4

--- a/solution.py
+++ b/solution.py
@@ -64,18 +64,17 @@
     low = jnp.concatenate([low, jnp.zeros((query_count, 128 - cand_count), jnp.float32)], 1)
     extra = jnp.concatenate([main, blank, low, blank], 0).astype(jnp.bfloat16)
     rows = queries_ref.shape[0]
-    for d in range(out_ref.shape[0]):
-        out_ref[d, :rows, :] = queries_ref[...]
-        out_ref[d, rows:, :] = extra
-
-
-def pack(queries, candidates, teacher, sources, pass_count):
+    out_ref[:rows, :] = queries_ref[...]
+    out_ref[rows:, :] = extra
+
+
+def pack(queries, candidates, teacher, pass_count):
     rows, width = queries.shape
     return pl.pallas_call(
         lambda *refs: pack_kernel(pass_count, *refs),
         in_specs=[HBM] * 3,
         out_specs=VMEM,
-        out_shape=jax.ShapeDtypeStruct((sources, rows + 16, width), jnp.bfloat16),
+        out_shape=jax.ShapeDtypeStruct((rows + 16, width), jnp.bfloat16),
         scratch_shapes=[
             pltpu.VMEM(queries.shape, queries.dtype),
             pltpu.VMEM(candidates.shape, candidates.dtype),
@@ -96,39 +95,60 @@
     return inverse * (grad - unit * jnp.sum(unit * grad, -1, keepdims=True))
 
 
-def passages_kernel(slices, in_ref, norm_ref, flip_ref, own_ref):
-    count, tokens, _ = in_ref.shape
+def passages_kernel(
+    slices, in_hbm_ref, norm_ref, flip_hbm, own_ref, in_ref, flip_ref, in_sems, flip_sems
+):
+    total, tokens, _ = norm_ref.shape
+    parts = in_sems.shape[0]
+    count = total // parts
     share = tokens // slices
     me = lax.axis_index("qry")
-    for item in range(count):
-        for place in range(slices):
-            start = pl.multiple_of((me ^ place) * share, share)
-            raw = in_ref[item, pl.ds(start, share), :]
-            if place == 0:
-                own_ref[item] = raw
-            norm_ref[item, pl.ds(place * share, share), :] = unit_rows(raw)[0].astype(
-                jnp.bfloat16
-            )
-        flip_ref[item] = jnp.transpose(norm_ref[item], (1, 0))
+
+    def in_copy(part):
+        place = pl.ds(part * count, count)
+        return pltpu.make_async_copy(in_hbm_ref.at[place], in_ref.at[place], in_sems.at[part])
+
+    def flip_copy(part):
+        place = pl.ds(part * count, count)
+        return pltpu.make_async_copy(flip_ref.at[place], flip_hbm.at[place], flip_sems.at[part])
+
+    for part in range(parts):
+        in_copy(part).start()
+    for part in range(parts):
+        in_copy(part).wait()
+        for item in range(part * count, (part + 1) * count):
+            for place in range(slices):
+                start = pl.multiple_of((me ^ place) * share, share)
+                raw = in_ref[item, pl.ds(start, share), :]
+                if place == 0:
+                    own_ref[item] = raw
+                norm_ref[item, pl.ds(place * share, share), :] = unit_rows(raw)[0].astype(
+                    jnp.bfloat16
+                )
+            flip_ref[item] = jnp.transpose(norm_ref[item], (1, 0))
+        flip_copy(part).start()
+    for part in range(parts):
+        flip_copy(part).wait()
 
 
 def prepare_passages(passages, slices):
     count, tokens, width = passages.shape
-    step = math.gcd(count, 8)
+    parts = math.gcd(count, 4)
     share = tokens // slices
     return pl.pallas_call(
         lambda *refs: passages_kernel(slices, *refs),
-        grid=(count // step,),
-        in_specs=[pl.BlockSpec((step, tokens, width), lambda i: (i, 0, 0))],
-        out_specs=[
-            pl.BlockSpec((step, tokens, width), lambda i: (i, 0, 0)),
-            pl.BlockSpec((step, width, tokens), lambda i: (i, 0, 0)),
-            pl.BlockSpec((step, share, width), lambda i: (i, 0, 0)),
+        in_specs=[HBM],
+        out_specs=[VMEM, HBM, VMEM],
+        out_shape=[
+            jax.ShapeDtypeStruct((count, tokens, width), jnp.bfloat16),
+            pltpu.HBM((count, width, tokens), jnp.bfloat16),
+            jax.ShapeDtypeStruct((count, share, width), jnp.bfloat16),
         ],
-        out_shape=[
-            pltpu.HBM((count, tokens, width), jnp.bfloat16),
-            pltpu.HBM((count, width, tokens), jnp.bfloat16),
-            pltpu.HBM((count, share, width), jnp.bfloat16),
+        scratch_shapes=[
+            pltpu.VMEM((count, tokens, width), jnp.bfloat16),
+            pltpu.VMEM((count, width, tokens), jnp.bfloat16),
+            pltpu.SemaphoreType.DMA((parts,)),
+            pltpu.SemaphoreType.DMA((parts,)),
         ],
         compiler_params=params(),
         cost_estimate=pl.CostEstimate(flops=1 << 24, bytes_accessed=6 << 20, transcendentals=0),
@@ -192,8 +212,8 @@
     cand_count,
     query_count,
     query_tokens,
-    recv_ref,
-    norm_hbm,
+    recv_refs,
+    norm_ref,
     soft_hbm,
     qn_ref,
     score_ref,
@@ -202,33 +222,33 @@
     list_ref,
     zw_ref,
     inverse_ref,
-    norm_ref,
     soft_ref,
     ext_ref,
     low_ref,
     sums_ref,
     list_smem,
     sem,
-    norm_sem,
     soft_sems,
 ):
-    norm_copies = part_copies(norm_hbm, norm_ref, norm_sem)
-    for copy in norm_copies:
-        copy.start()
-    sources = recv_ref.shape[0]
+    near = recv_refs[0].shape[0]
+    sources = near * len(recv_refs)
     pass_count, tokens, width = norm_ref.shape
     group = sources * query_count
     rows = query_count * query_tokens
     stride = group + row_pad
     empty, tables = list_layout(group)
-    owner = lax.axis_index("psg").astype(jnp.float32)
-    for s in range(sources):
-        packed = recv_ref[s, rows : rows + 16, :].astype(jnp.float32)
-        ext_ref[s * query_count : (s + 1) * query_count, :] = packed[:query_count]
-        low_ref[s * query_count : (s + 1) * query_count, :] = packed[8 : 8 + query_count]
-        qn_ref[s * rows : (s + 1) * rows, :] = unit_rows(recv_ref[s, :rows, :])[0].astype(
-            jnp.bfloat16
-        )
+    me = lax.axis_index("psg")
+    owner = me.astype(jnp.float32)
+    for d in range(sources):
+        recv_ref = recv_refs[d // near].at[d % near]
+        source = me ^ d
+        packed = recv_ref[rows : rows + 16, :].astype(jnp.float32)
+        place = pl.ds(pl.multiple_of(source * query_count, query_count), query_count)
+        ext_ref[place, :] = packed[:query_count]
+        low_ref[place, :] = packed[8 : 8 + query_count]
+        qn_ref[pl.ds(pl.multiple_of(source * rows, rows), rows), :] = unit_rows(
+            recv_ref[:rows, :]
+        )[0].astype(jnp.bfloat16)
     qn_ref[sources * rows :, :] = jnp.zeros((query_tokens, width), jnp.bfloat16)
 
     main = ext_ref[...]
@@ -311,8 +331,6 @@
         list_ref[tables + row : tables + row + 1, :] = value.astype(jnp.int32)
     copy = pltpu.make_async_copy(list_ref, list_smem, sem)
     copy.start()
-    for other in norm_copies:
-        other.wait()
     copy.wait()
 
     def soft_copy(slot):
@@ -353,7 +371,14 @@
     score_ref[...] = scores
     mass = jnp.sum(many * jnp.exp(scores), -1, keepdims=True)
     agreed = jnp.sum(wanted * scores, -1, keepdims=True)
-    message = jnp.where(lanes == 0, mass, jnp.where(lanes == 1, agreed, 0.0))
+    same_id = lax.broadcasted_iota(jnp.int32, main.shape, 0) == lanes
+    message = jnp.concatenate(
+        [
+            jnp.sum(jnp.where(same_id, value, 0.0), 0, keepdims=True) for value in (mass, agreed)
+        ]
+        + [jnp.zeros((6, 128), jnp.float32)],
+        0,
+    )
     for s in range(sources):
         zw_ref[s] = message
 
@@ -365,7 +390,7 @@
 
 
 def forward(received, norm, cand_count, query_count, query_tokens):
-    sources = received.shape[0]
+    sources = received[0].shape[0] * len(received)
     pass_count, tokens, width = norm.shape
     group = sources * query_count
     capacity = max(2, -(-5 * query_count * cand_count // (2 * sources)))
@@ -375,8 +400,10 @@
     soft_shape = (slots, tokens, chunk_pairs * query_tokens)
     flops = 2 * slots * chunk_pairs * query_tokens * tokens * width
     return pl.pallas_call(
-        lambda *refs: forward_kernel(cand_count, query_count, query_tokens, *refs),
-        in_specs=[VMEM, HBM],
+        lambda *refs: forward_kernel(
+            cand_count, query_count, query_tokens, refs[: len(received)], *refs[len(received) :]
+        ),
+        in_specs=[VMEM] * (len(received) + 1),
         out_specs=[HBM] + [VMEM] * 7,
         out_shape=[
             pltpu.HBM(soft_shape, jnp.bfloat16),
@@ -385,24 +412,22 @@
             jax.ShapeDtypeStruct((group, 128), jnp.float32),
             jax.ShapeDtypeStruct((group, 128), jnp.float32),
             jax.ShapeDtypeStruct((list_rows, 128), jnp.int32),
-            jax.ShapeDtypeStruct((sources, group, 128), jnp.float32),
+            jax.ShapeDtypeStruct((sources, 8, 128), jnp.float32),
             jax.ShapeDtypeStruct((slots, chunk_pairs * query_tokens), jnp.float32),
         ],
         scratch_shapes=[
-            pltpu.VMEM(norm.shape, jnp.bfloat16),
             pltpu.VMEM(soft_shape, jnp.bfloat16),
             pltpu.VMEM((group, 128), jnp.float32),
             pltpu.VMEM((group, 128), jnp.float32),
             pltpu.VMEM((pass_count * (group + row_pad), 128), jnp.float32),
             pltpu.SMEM((list_rows, 128), jnp.int32),
             pltpu.SemaphoreType.DMA,
-            pltpu.SemaphoreType.DMA((copy_parts,)),
             pltpu.SemaphoreType.DMA((slots,)),
         ],
         compiler_params=params(),
         cost_estimate=pl.CostEstimate(flops=flops, bytes_accessed=12 << 20, transcendentals=1 << 22),
         name="forward",
-    )(received, in_hbm(norm))
+    )(*received, norm)
 
 
 def spread(ref, values, pass_count, stride, start=0):
@@ -470,7 +495,8 @@
         ids = list_ids(list_smem, list_smem[tables + 1, slot], p)
         places = query_places(ids, query_tokens)
         mixed = jnp.dot(flip_ref[p], soft_ref[slot], preferred_element_type=jnp.float32)
-        mixed = jnp.transpose(mixed * inverse_ref[pl.ds(slot, 1), :], (1, 0))
+        mixed = (mixed * inverse_ref[pl.ds(slot, 1), :]).astype(jnp.bfloat16)
+        mixed = jnp.transpose(mixed, (1, 0)).astype(jnp.float32)
         for total, rows in ((raised_sum, raised_rows), (wanted_sum, wanted_rows)):
             added = [
                 total[place, :]
@@ -552,11 +578,13 @@
     scale_ref,
     query_ref,
 ):
-    sources, group, _ = zw_ref.shape
+    sources, group = zw_ref.shape[0], score_ref.shape[0]
     sums = zw_ref[0]
     for s in range(1, sources):
         sums = sums + zw_ref[s]
-    inverse = 1.0 / sums[:, :1]
+    lanes = lane_ids((group, 128))
+    same_id = lax.broadcasted_iota(jnp.int32, (group, 128), 0) == lanes
+    inverse = 1.0 / jnp.sum(jnp.where(same_id, sums[:1], 0.0), -1, keepdims=True)
     grads_ref[...] = many_ref[...] * jnp.exp(score_ref[...]) * inverse - target_ref[...]
     scale_ref[...] = jnp.broadcast_to(inverse, scale_ref.shape)
     for n in range(group):
@@ -577,7 +605,7 @@
 
 
 def query_backward(zw, score, many, target, raised, wanted):
-    sources, group, _ = zw.shape
+    sources, group = zw.shape[0], score.shape[0]
     rows, width = raised.shape
     part = jax.ShapeDtypeStruct((sources // 2, rows // sources, width), jnp.bfloat16)
     return pl.pallas_call(
@@ -755,13 +783,16 @@
     slices = lax.axis_size("qry")
     rows = query_count * query_tokens
 
-    received = lax.all_to_all(
-        pack(queries.reshape(rows, width), candidates, teacher, sources, pass_count),
-        "psg",
-        split_axis=0,
-        concat_axis=0,
-        tiled=True,
-    )
+    received = pack(queries.reshape(rows, width), candidates, teacher, pass_count)[None]
+    while received.shape[0] * 4 < sources:
+        bit = received.shape[0]
+        swap = [(i, i ^ bit) for i in range(sources)]
+        received = jnp.concatenate([received, lax.ppermute(received, "psg", swap)], 0)
+    stride = received.shape[0]
+    received = [received] + [
+        lax.ppermute(received, "psg", [(i, i ^ d) for i in range(sources)])
+        for d in range(stride, sources, stride)
+    ]
     norm, flip, own_raw = prepare_passages(passages, slices)
     soft, qn, score, many, target, ids, zw, inverse = forward(
         received, norm, cand_count, query_count, query_tokens
@@ -804,10 +835,9 @@
     log_target = teacher - jnp.log(raised_sum)
     known = jnp.sum(raised / raised_sum * log_target, -1)
     mine = lax.dynamic_slice_in_dim(
-        zw[:, :, :2], lax.axis_index("psg") * query_count, query_count, 1
-    )
-    mine = jnp.sum(mine, 0)
-    pair_loss = known - mine[:, 1] + jnp.log(mine[:, 0])
+        jnp.sum(zw[:, :2], 0), lax.axis_index("psg") * query_count, query_count, 1
+    )
+    pair_loss = known - mine[1] + jnp.log(mine[0])
     return (pair_loss, grad_queries.reshape(queries.shape), grad_passages)
 
 

time: 61.5 us -> 60.8 us (0.989); the launches traced: 61.4 us -> 60 us
  Pallas kernels: 28.6 us -> 23.7 us
  waiting for transfers between devices: 13.8 us -> 15.7 us
  starting transfers between devices: 17 us -> 18.7 us
    ppermute x0 -> x4, starting transfers between devices: none -> 7.77 us  [the longest x3 4.73 us: shards(): lax.ppermute(received, 'psg', [(i, i ^ d) for i in range(sources)])]
    all_to_all x1 -> x0, starting transfers between devices: 7.29 us -> none  [shards(): lax.all_to_all(pack(queries.reshape(rows, width), candidates, teacher, so...]
    all_to_all x1 -> x0, waiting for transfers between devices: 4.69 us -> none  [shards(): lax.all_to_all(pack(queries.reshape(rows, width), candidates, teacher, so...]
    ppermute x0 -> x4, waiting for transfers between devices: none -> 4.15 us  [the longest x3 2.22 us: shards(): lax.ppermute(received, 'psg', [(i, i ^ d) for i in range(sources)])]
    ppermute x3, waiting for transfers between devices: 2.58 us -> 5.04 us  [shards(): lax.ppermute(piece, 'psg', [(i, i ^ d) for i in range(sources)])]
    pallas_call x1, Pallas kernels: 6.73 us -> 5.14 us  [attend(): pl.pallas_call(lambda *refs: attend_kernel(query_tokens, *refs), in_specs...]
    pallas_call x1, Pallas kernels: 7.61 us -> 6.18 us  [forward(): pl.pallas_call(lambda *refs: forward_kernel(cand_count, query_count, quer...]
    pallas_call x1, Pallas kernels: 4.93 us -> 3.91 us  [prepare_passages(): pl.pallas_call(lambda *refs: passages_kernel(slices, *refs), in_specs=[HB...]
  transfers between devices with their start and end apart: 9 -> 12, of which waited for: 6 -> 8; matrix products, arithmetic and copies ran while one was open for 2% -> 2% of each run, Pallas kernels for 20% -> 16%
where the time goes in v5:
time: 60.8 us; the launch traced here: 60 us
  Pallas kernels  23.7 us (39%)
  starting transfers between devices  18.7 us (31%)
  waiting for transfers between devices  15.7 us (26%)
  other arithmetic  1.07 us (2%)
  between operations  0.76 us (1%)
    pallas_call x1, Pallas kernels, forward(): pl.pallas_call(lambda *refs: forward_kernel(cand_count, query_count, quer...  6.18 us
    pallas_call x1, Pallas kernels, passage_backward(): pl.pallas_call(lambda *refs: passage_kernel(query_tokens, *refs), in_spec...  5.17 us
    pallas_call x1, Pallas kernels, attend(): pl.pallas_call(lambda *refs: attend_kernel(query_tokens, *refs), in_specs...  5.14 us
    ppermute x3, waiting for transfers between devices, shards(): lax.ppermute(piece, 'psg', [(i, i ^ d) for i in range(sources)])  5.04 us
    ppermute x3, starting transfers between devices, shards(): lax.ppermute(received, 'psg', [(i, i ^ d) for i in range(sources)])  4.73 us
    ppermute x3, starting transfers between devices, shards(): lax.ppermute(piece, 'psg', [(i, i ^ d) for i in range(sources)])  4.45 us
    all_to_all x1, starting transfers between devices, shards(): zw = lax.all_to_all(zw, 'psg', split_axis=0, concat_axis=0, tiled=True)  4.12 us
    pallas_call x1, Pallas kernels, prepare_passages(): pl.pallas_call(lambda *refs: passages_kernel(slices, *refs), in_specs=[HB...  3.91 us
  transfers between devices with their start and end apart: 12, of which 8 were waited for; matrix products, arithmetic and copies ran while one was open for 2% of the time, Pallas kernels for 16%

profile of v5, /device:TPU:0, one launch (start us, length us, event | category | flops | bytes accessed | tf_op | source)
XLA Modules:
  0.0 60.0 jit_solution(1333651775861043060)
XLA Ops:
  0.6 0.9 %pack.1 = bf16[144,128]{1,0:T(8,128)(2,1)S(1)} custom-call(bf16[128,128]{1,0:T(8,128)(2,1)} %bitcast.19, s32[4,32]{1,0:T(4,128)} %refs_1_.1, f32[4,32]{1,0:T(4,128)} %refs_2_.1), custom_call_target="tpu_custom_call" | custom-call | tf_op jit(solution)/shard_map/pack/pallas_call | solution.py:73
  1.5 3.0 %collective-permute-start = (bf16[1,144,128]{2,1,0:T(8,128)(2,1)S(1)}, bf16[1,144,128]{2,1,0:T(8,128)(2,1)S(1)}, u32[]{:S(2)}, u32[]{:S(2)}) collective-permute-start(bf16[1,144,128]{2,1,0:T(8,128)(2,1)S(1)} %bitcast.17), channel_id=1, source_target_pairs={{0,4},{4,0},{8,12},{12,8},{16,20},{20,16},{24,28},{28,24},{1,5},{5... | collective-permute-start | bytes 110600 | tf_op jit(solution)/shard_map/ppermute | solution.py:790
  4.5 1.9 %collective-permute-done = bf16[1,144,128]{2,1,0:T(8,128)(2,1)S(1)} collective-permute-done((bf16[1,144,128]{2,1,0:T(8,128)(2,1)S(1)}, bf16[1,144,128]{2,1,0:T(8,128)(2,1)S(1)}, u32[]{:S(2)}, u32[]{:S(2)}) %collective-permute-start) | collective-permute-done | bytes 36896 | tf_op jit(solution)/shard_map/ppermute | solution.py:790
  6.5 2.1 %collective-permute-start.1 = (bf16[2,144,128]{2,1,0:T(8,128)(2,1)S(1)}, bf16[2,144,128]{2,1,0:T(8,128)(2,1)S(1)}, u32[]{:S(2)}, u32[]{:S(2)}) collective-permute-start(bf16[2,144,128]{2,1,0:T(8,128)(2,1)S(1)} %pad_maximum_fusion.refs_0_), channel_id=1, source_target_pairs={{0,8},{4,12},{8,0},{12,4},{16,24},{20,28},{24,16},{28,20},{1,9},{5... | collective-permute-start | bytes 221192 | tf_op jit(solution)/shard_map/ppermute | solution.py:793
  8.6 2.6 %collective-permute-start.2 = (bf16[2,144,128]{2,1,0:T(8,128)(2,1)S(1)}, bf16[2,144,128]{2,1,0:T(8,128)(2,1)S(1)}, u32[]{:S(2)}, u32[]{:S(2)}) collective-permute-start(bf16[2,144,128]{2,1,0:T(8,128)(2,1)S(1)} %pad_maximum_fusion.refs_0_), channel_id=1, source_target_pairs={{0,16},{4,20},{8,24},{12,28},{16,0},{20,4},{24,8},{28,12},{1,17},{... | collective-permute-start | bytes 221192 | tf_op jit(solution)/shard_map/ppermute | solution.py:793
  11.2 3.9 %prepare_passages.1 = (bf16[32,256,128]{2,1,0:T(8,128)(2,1)S(1)}, bf16[32,128,256]{2,1,0:T(8,128)(2,1)}, bf16[32,64,128]{2,1,0:T(8,128)(2,1)S(1)}) custom-call(bf16[32,256,128]{2,1,0:T(8,128)(2,1)} %refs_0_.1), custom_call_target="tpu_custom_call" | custom-call | flops 16777216 | bytes 6291456 | tf_op jit(solution)/shard_map/prepare_passages/pallas_call | solution.py:138
  15.2 0.3 collective-permute-done.2.refs_2_
  15.5 1.9 %collective-permute-done.3.refs_3_ = bf16[2,144,128]{2,1,0:T(8,128)(2,1)S(1)} collective-permute-done((bf16[2,144,128]{2,1,0:T(8,128)(2,1)S(1)}, bf16[2,144,128]{2,1,0:T(8,128)(2,1)S(1)}, u32[]{:S(2)}, u32[]{:S(2)}) %collective-permute-start.3) | collective-permute-done | bytes 73760 | tf_op jit(solution)/shard_map/ppermute | solution.py:793
  17.4 6.2 %forward.1 = (bf16[72,256,256]{2,1,0:T(8,128)(2,1)}, bf16[1056,128]{1,0:T(8,128)(2,1)S(1)}, f32[32,128]{1,0:T(8,128)S(1)}, f32[32,128]{1,0:T(8,128)S(1)}, f32[32...) custom-call(bf16[2,144,128]{2,1,0:T(8,128)(2,1)S(1)} %pad_maximum_fusion.refs_0_, ...), custom_call_target="tpu_custom_call" | custom-call | flops 1207959552 | bytes 12582912 | tf_op jit(solution)/shard_map/forward/pallas_call | solution.py:402
  23.6 4.1 %all-to-all-start = ((f32[8,8,128]{2,1,0:T(8,128)}), f32[8,8,128]{2,1,0:T(8,128)S(1)}, u32[]{:S(2)}, u32[]{:S(2)}) async-start(f32[8,8,128]{2,1,0:T(8,128)} %get-tuple-element.30), calls=%async_computation | async-start | bytes 65536 | tf_op jit(solution)/shard_map/all_to_all | solution.py:800
  27.7 5.1 %attend.1 = (f32[1024,128]{1,0:T(8,128)S(1)}, f32[1024,128]{1,0:T(8,128)S(1)}) custom-call(bf16[32,128,256]{2,1,0:T(8,128)(2,1)} %get-tuple-element.34.refs_0_, bf16[72,256,256]{2,1,0:T(8,128)(2,1)} %get-tuple-element.35.refs_1_.refs_4_, s32[24,128]{1,0:T(8,128)S(1)} %get-tuple-element.29.refs_2_.refs_0_, f32[32,128]{1,0:T(8,128)S(1)} %get-tuple-element.31.refs_3_.refs_1_, ...), custom_call_target="tpu_custom_call" | custom-call | flops 1207959552 | bytes 12582912 | tf_op jit(solution)/shard_map/attend/pallas_call | solution.py:535
  32.8 1.5 %all-to-all-done.refs_0_ = f32[8,8,128]{2,1,0:T(8,128)S(1)} async-done(((f32[8,8,128]{2,1,0:T(8,128)}), f32[8,8,128]{2,1,0:T(8,128)S(1)}, u32[]{:S(2)}, u32[]{:S(2)}) %all-to-all-start) | async-done | bytes 32800 | tf_op jit(solution)/shard_map/all_to_all | solution.py:800
  34.6 5.2 %passage_backward.1 = (bf16[32,64,128]{2,1,0:T(8,128)(2,1)S(1)}, bf16[32,64,128]{2,1,0:T(8,128)(2,1)S(1)}, bf16[32,64,128]{2,1,0:T(8,128)(2,1)S(1)}, bf16[32,64,128]{2,1,0:T(8,128)(2,1)S(1)}) custom-call(s32[24,128]{1,0:T(8,128)S(1)} %get-tuple-element.29.refs_2_.refs_0_, f32[32,128]{1,0:T(8,128)S(1)} %get-tuple-element.39.refs_1_, ...), custom_call_target="tpu_custom_call" | custom-call | flops 1073741824 | bytes 6291456 | tf_op jit(solution)/shard_map/passage_backward/pallas_call | solution.py:730
  39.8 1.9 %collective-permute-done.4 = bf16[32,64,128]{2,1,0:T(8,128)(2,1)S(1)} collective-permute-done((bf16[32,64,128]{2,1,0:T(8,128)(2,1)S(1)}, bf16[32,64,128]{2,1,0:T(8,128)(2,1)S(1)}, u32[]{:S(2)}, u32[]{:S(2)}) %collective-permute-start.4) | collective-permute-done | bytes 524320 | tf_op jit(solution)/shard_map/ppermute | solution.py:810
  41.9 0.9 %collective-permute-start.5 = (bf16[4,128,128]{2,1,0:T(8,128)(2,1)S(1)}, bf16[4,128,128]{2,1,0:T(8,128)(2,1)S(1)}, u32[]{:S(2)}, u32[]{:S(2)}) collective-permute-start(bf16[4,128,128]{2,1,0:T(8,128)(2,1)S(1)} %get-tuple-element.45), channel_id=1, source_target_pairs={{0,4},{4,0},{8,12},{12,8},{16,20},{20,16},{24,28},{28,24},{1,5},{5... | collective-permute-start | bytes 393224 | tf_op jit(solution)/shard_map/ppermute | solution.py:817
  43.2 1.3 %collective-permute-start.10 = (bf16[32,64,128]{2,1,0:T(8,128)(2,1)S(1)}, bf16[32,64,128]{2,1,0:T(8,128)(2,1)S(1)}, u32[]{:S(2)}, u32[]{:S(2)}) collective-permute-start(bf16[32,64,128]{2,1,0:T(8,128)(2,1)S(1)} %add_convert_fusion), channel_id=1, source_target_pairs={{0,2},{1,3},{2,0},{3,1},{4,6},{5,7},{6,4},{7,5},{8,10},{9,11},{10,... | collective-permute-start | bytes 1572872 | tf_op jit(solution)/shard_map/ppermute | solution.py:813
  44.5 3.0 %collective-permute-done.5 = bf16[4,128,128]{2,1,0:T(8,128)(2,1)S(1)} collective-permute-done((bf16[4,128,128]{2,1,0:T(8,128)(2,1)S(1)}, bf16[4,128,128]{2,1,0:T(8,128)(2,1)S(1)}, u32[]{:S(2)}, u32[]{:S(2)}) %collective-permute-start.5) | collective-permute-done | bytes 131104 | tf_op jit(solution)/shard_map/ppermute | solution.py:817
  47.6 1.4 %collective-permute-start.6 = (bf16[128,128]{1,0:T(8,128)(2,1)S(1)}, bf16[128,128]{1,0:T(8,128)(2,1)S(1)}, u32[]{:S(2)}, u32[]{:S(2)}) collective-permute-start(bf16[128,128]{1,0:T(8,128)(2,1)S(1)} %get-tuple-element.57), channel_id=1, source_target_pairs={{0,16},{4,20},{8,24},{12,28},{16,0},{20,4},{24,8},{28,12},{1,17},{... | collective-permute-start | bytes 98312 | tf_op jit(solution)/shard_map/ppermute | solution.py:828
  49.0 3.0 %collective-permute-start.7 = (bf16[128,128]{1,0:T(8,128)(2,1)S(1)}, bf16[128,128]{1,0:T(8,128)(2,1)S(1)}, u32[]{:S(2)}, u32[]{:S(2)}) collective-permute-start(bf16[128,128]{1,0:T(8,128)(2,1)S(1)} %get-tuple-element.56), channel_id=1, source_target_pairs={{0,8},{4,12},{8,0},{12,4},{16,24},{20,28},{24,16},{28,20},{1,9},{5... | collective-permute-start | bytes 98312 | tf_op jit(solution)/shard_map/ppermute | solution.py:828
  52.1 0.5 bitcast_add_fusion
  52.6 1.2 %collective-permute-done.7.refs_2_ = bf16[128,128]{1,0:T(8,128)(2,1)S(1)} collective-permute-done((bf16[128,128]{1,0:T(8,128)(2,1)S(1)}, bf16[128,128]{1,0:T(8,128)(2,1)S(1)}, u32[]{:S(2)}, u32[]{:S(2)}) %collective-permute-start.7) | collective-permute-done | bytes 32800 | tf_op jit(solution)/shard_map/ppermute | solution.py:828
  53.9 3.8 %collective-permute-done.8.refs_3_ = bf16[128,128]{1,0:T(8,128)(2,1)S(1)} collective-permute-done((bf16[128,128]{1,0:T(8,128)(2,1)S(1)}, bf16[128,128]{1,0:T(8,128)(2,1)S(1)}, u32[]{:S(2)}, u32[]{:S(2)}) %collective-permute-start.8) | collective-permute-done | bytes 32800 | tf_op jit(solution)/shard_map/ppermute | solution.py:828
  57.7 0.8 %finish_queries.1 = bf16[128,128]{1,0:T(8,128)(2,1)} custom-call(bf16[128,128]{1,0:T(8,128)(2,1)S(1)} %bitcast.20, f32[128,128]{1,0:T(8,128)S(1)} %slice_bitcast_fusion.refs_0_, bf16[128,128]{1,0:T(8,128)(2,1)S(1)} %collective-permute-done.6.refs_1_, bf16[128,128]{1,0:T(8,128)(2,1)S(1)} %collective-permute-done.7.refs_2_, ...), custom_call_target="tpu_custom_call" | custom-call | tf_op jit(solution)/shard_map/finish_queries/pallas_call | solution.py:768
  58.5 1.5 %finish.1 = bf16[32,64,128]{2,1,0:T(8,128)(2,1)} custom-call(bf16[32,64,128]{2,1,0:T(8,128)(2,1)S(1)} %get-tuple-element.49.raw_ref, bf16[32,64,128]{2,1,0:T(8,128)(2,1)S(1)} %get-tuple-element.50.refs_0_, bf16[32,64,128]{2,1,0:T(8,128)(2,1)S(1)} %collective-permute-done.9.refs_1_, bf16[32,64,128]{2,1,0:T(8,128)(2,1)S(1)} %collective-permute-done.10.refs_2_), custom_call_target="tpu_custom_call" | custom-call | tf_op jit(solution)/shard_map/finish/pallas_call | solution.py:757
  (23 shorter events, 1.0 us)
Async XLA Ops:
  1.5 5.0 %collective-permute-start = (bf16[1,144,128]{2,1,0:T(8,128)(2,1)S(1)}, bf16[1,144,128]{2,1,0:T(8,128)(2,1)S(1)}, u32[]{:S(2)}, u32[]{:S(2)}) collective-permute-start(bf16[1,144,128]{2,1,0:T(8,128)(2,1)S(1)} %bitcast.17), channel_id=1, source_target_pairs={{0,4},{4,0},{8,12},{12,8},{16,20},{20,16},{24,28},{28,24},{1,5},{5... | collective-permute-start | bytes 110600 | tf_op jit(solution)/shard_map/ppermute | solution.py:790
  6.5 8.7 %collective-permute-start.1 = (bf16[2,144,128]{2,1,0:T(8,128)(2,1)S(1)}, bf16[2,144,128]{2,1,0:T(8,128)(2,1)S(1)}, u32[]{:S(2)}, u32[]{:S(2)}) collective-permute-start(bf16[2,144,128]{2,1,0:T(8,128)(2,1)S(1)} %pad_maximum_fusion.refs_0_), channel_id=1, source_target_pairs={{0,8},{4,12},{8,0},{12,4},{16,24},{20,28},{24,16},{28,20},{1,9},{5... | collective-permute-start | bytes 221192 | tf_op jit(solution)/shard_map/ppermute | solution.py:793
  8.6 6.8 %collective-permute-start.2 = (bf16[2,144,128]{2,1,0:T(8,128)(2,1)S(1)}, bf16[2,144,128]{2,1,0:T(8,128)(2,1)S(1)}, u32[]{:S(2)}, u32[]{:S(2)}) collective-permute-start(bf16[2,144,128]{2,1,0:T(8,128)(2,1)S(1)} %pad_maximum_fusion.refs_0_), channel_id=1, source_target_pairs={{0,16},{4,20},{8,24},{12,28},{16,0},{20,4},{24,8},{28,12},{1,17},{... | collective-permute-start | bytes 221192 | tf_op jit(solution)/shard_map/ppermute | solution.py:793
  11.2 6.2 %collective-permute-start.3 = (bf16[2,144,128]{2,1,0:T(8,128)(2,1)S(1)}, bf16[2,144,128]{2,1,0:T(8,128)(2,1)S(1)}, u32[]{:S(2)}, u32[]{:S(2)}) collective-permute-start(bf16[2,144,128]{2,1,0:T(8,128)(2,1)S(1)} %pad_maximum_fusion.refs_0_), channel_id=1, source_target_pairs={{0,24},{4,28},{8,16},{12,20},{16,8},{20,12},{24,0},{28,4},{1,25},{... | collective-permute-start | bytes 221192 | tf_op jit(solution)/shard_map/ppermute | solution.py:793
  23.6 10.8 %all-to-all-start = ((f32[8,8,128]{2,1,0:T(8,128)}), f32[8,8,128]{2,1,0:T(8,128)S(1)}, u32[]{:S(2)}, u32[]{:S(2)}) async-start(f32[8,8,128]{2,1,0:T(8,128)} %get-tuple-element.30), calls=%async_computation | async-start | bytes 65536 | tf_op jit(solution)/shard_map/all_to_all | solution.py:800
  34.5 8.3 %copy-start.1 = (f32[4,32]{1,0:T(4,128)S(1)}, f32[4,32]{1,0:T(4,128)}, u32[]{:S(2)}) copy-start(f32[4,32]{1,0:T(4,128)} %refs_2_.1) | copy-start | bytes 1540
  39.7 18.0 %copy-start = (bf16[4,32,128]{2,1,0:T(8,128)(2,1)S(1)}, bf16[4,32,128]{2,1,0:T(8,128)(2,1)}, u32[]{:S(2)}) copy-start(bf16[4,32,128]{2,1,0:T(8,128)(2,1)} %param.4) | copy-start | bytes 98308
  39.7 2.0 %collective-permute-start.4 = (bf16[32,64,128]{2,1,0:T(8,128)(2,1)S(1)}, bf16[32,64,128]{2,1,0:T(8,128)(2,1)S(1)}, u32[]{:S(2)}, u32[]{:S(2)}) collective-permute-start(bf16[32,64,128]{2,1,0:T(8,128)(2,1)S(1)} %get-tuple-element.42), channel_id=1, source_target_pairs={{0,1},{1,0},{2,3},{3,2},{4,5},{5,4},{6,7},{7,6},{8,9},{9,8},{10,11... | collective-permute-start | bytes 1572872 | tf_op jit(solution)/shard_map/ppermute | solution.py:810
  41.9 5.6 %collective-permute-start.5 = (bf16[4,128,128]{2,1,0:T(8,128)(2,1)S(1)}, bf16[4,128,128]{2,1,0:T(8,128)(2,1)S(1)}, u32[]{:S(2)}, u32[]{:S(2)}) collective-permute-start(bf16[4,128,128]{2,1,0:T(8,128)(2,1)S(1)} %get-tuple-element.45), channel_id=1, source_target_pairs={{0,4},{4,0},{8,12},{12,8},{16,20},{20,16},{24,28},{28,24},{1,5},{5... | collective-permute-start | bytes 393224 | tf_op jit(solution)/shard_map/ppermute | solution.py:817
  43.2 15.3 %collective-permute-start.10 = (bf16[32,64,128]{2,1,0:T(8,128)(2,1)S(1)}, bf16[32,64,128]{2,1,0:T(8,128)(2,1)S(1)}, u32[]{:S(2)}, u32[]{:S(2)}) collective-permute-start(bf16[32,64,128]{2,1,0:T(8,128)(2,1)S(1)} %add_convert_fusion), channel_id=1, source_target_pairs={{0,2},{1,3},{2,0},{3,1},{4,6},{5,7},{6,4},{7,5},{8,10},{9,11},{10,... | collective-permute-start | bytes 1572872 | tf_op jit(solution)/shard_map/ppermute | solution.py:813
  44.5 14.0 %collective-permute-start.9 = (bf16[32,64,128]{2,1,0:T(8,128)(2,1)S(1)}, bf16[32,64,128]{2,1,0:T(8,128)(2,1)S(1)}, u32[]{:S(2)}, u32[]{:S(2)}) collective-permute-start(bf16[32,64,128]{2,1,0:T(8,128)(2,1)S(1)} %get-tuple-element.51), channel_id=1, source_target_pairs={{0,1},{1,0},{2,3},{3,2},{4,5},{5,4},{6,7},{7,6},{8,9},{9,8},{10,11... | collective-permute-start | bytes 1572872 | tf_op jit(solution)/shard_map/ppermute | solution.py:814
  47.6 5.1 %collective-permute-start.6 = (bf16[128,128]{1,0:T(8,128)(2,1)S(1)}, bf16[128,128]{1,0:T(8,128)(2,1)S(1)}, u32[]{:S(2)}, u32[]{:S(2)}) collective-permute-start(bf16[128,128]{1,0:T(8,128)(2,1)S(1)} %get-tuple-element.57), channel_id=1, source_target_pairs={{0,16},{4,20},{8,24},{12,28},{16,0},{20,4},{24,8},{28,12},{1,17},{... | collective-permute-start | bytes 98312 | tf_op jit(solution)/shard_map/ppermute | solution.py:828
  49.0 4.9 %collective-permute-start.7 = (bf16[128,128]{1,0:T(8,128)(2,1)S(1)}, bf16[128,128]{1,0:T(8,128)(2,1)S(1)}, u32[]{:S(2)}, u32[]{:S(2)}) collective-permute-start(bf16[128,128]{1,0:T(8,128)(2,1)S(1)} %get-tuple-element.56), channel_id=1, source_target_pairs={{0,8},{4,12},{8,0},{12,4},{16,24},{20,28},{24,16},{28,20},{1,9},{5... | collective-permute-start | bytes 98312 | tf_op jit(solution)/shard_map/ppermute | solution.py:828
  52.0 5.7 %collective-permute-start.8 = (bf16[128,128]{1,0:T(8,128)(2,1)S(1)}, bf16[128,128]{1,0:T(8,128)(2,1)S(1)}, u32[]{:S(2)}, u32[]{:S(2)}) collective-permute-start(bf16[128,128]{1,0:T(8,128)(2,1)S(1)} %get-tuple-element.55), channel_id=1, source_target_pairs={{0,24},{4,28},{8,16},{12,20},{16,8},{20,12},{24,0},{28,4},{1,25},{... | collective-permute-start | bytes 98312 | tf_op jit(solution)/shard_map/ppermute | solution.py:828

commit v6 on v5

--- a/solution.py
+++ b/solution.py
@@ -10,7 +10,7 @@
 epsilon = 1e-06
 softness_scale = 0.05
 chunk_pairs = 8
-vmem_bytes = 44 << 20
+vmem_bytes = 20 << 20
 row_pad = 8
 
 VMEM = pl.BlockSpec(memory_space=pltpu.VMEM)
@@ -18,8 +18,6 @@
 chunk_unroll = 8
 chunk_tail = 4
 passage_unroll = 8
-early_slots = 24
-copy_parts = 8
 meta_rows = 8
 
 
@@ -96,7 +94,7 @@
 
 
 def passages_kernel(
-    slices, in_hbm_ref, norm_ref, flip_hbm, own_ref, in_ref, flip_ref, in_sems, flip_sems
+    slices, in_hbm_ref, norm_ref, flip_ref, own_ref, in_ref, in_sems
 ):
     total, tokens, _ = norm_ref.shape
     parts = in_sems.shape[0]
@@ -107,10 +105,6 @@
     def in_copy(part):
         place = pl.ds(part * count, count)
         return pltpu.make_async_copy(in_hbm_ref.at[place], in_ref.at[place], in_sems.at[part])
-
-    def flip_copy(part):
-        place = pl.ds(part * count, count)
-        return pltpu.make_async_copy(flip_ref.at[place], flip_hbm.at[place], flip_sems.at[part])
 
     for part in range(parts):
         in_copy(part).start()
@@ -126,9 +120,6 @@
                     jnp.bfloat16
                 )
             flip_ref[item] = jnp.transpose(norm_ref[item], (1, 0))
-        flip_copy(part).start()
-    for part in range(parts):
-        flip_copy(part).wait()
 
 
 def prepare_passages(passages, slices):
@@ -138,16 +129,14 @@
     return pl.pallas_call(
         lambda *refs: passages_kernel(slices, *refs),
         in_specs=[HBM],
-        out_specs=[VMEM, HBM, VMEM],
+        out_specs=[VMEM] * 3,
         out_shape=[
             jax.ShapeDtypeStruct((count, tokens, width), jnp.bfloat16),
-            pltpu.HBM((count, width, tokens), jnp.bfloat16),
+            jax.ShapeDtypeStruct((count, width, tokens), jnp.bfloat16),
             jax.ShapeDtypeStruct((count, share, width), jnp.bfloat16),
         ],
         scratch_shapes=[
             pltpu.VMEM((count, tokens, width), jnp.bfloat16),
-            pltpu.VMEM((count, width, tokens), jnp.bfloat16),
-            pltpu.SemaphoreType.DMA((parts,)),
             pltpu.SemaphoreType.DMA((parts,)),
         ],
         compiler_params=params(),
@@ -163,7 +152,7 @@
 
 def slot_total(pass_count, pairs):
     worst = (pairs + pass_count * (chunk_pairs - 1)) // chunk_pairs
-    return -(-max(worst, early_slots) // chunk_unroll) * chunk_unroll
+    return -(-worst // chunk_unroll) * chunk_unroll
 
 
 def list_ids(list_smem, row, p):
@@ -186,22 +175,6 @@
 
     lax.fori_loop(0, full, step, 0)
     lax.fori_loop(0, tail, tail_step, 0)
-    return full * chunk_unroll + tail * chunk_tail
-
-
-def slots_used(list_smem, tables):
-    total = jnp.maximum(list_smem[tables + 4, 0], 1)
-    return (total + chunk_tail - 1) // chunk_tail * chunk_tail
-
-
-def part_copies(source, target, sems):
-    size = source.shape[0] // copy_parts
-    return [
-        pltpu.make_async_copy(
-            source.at[pl.ds(i * size, size)], target.at[pl.ds(i * size, size)], sems.at[i]
-        )
-        for i in range(copy_parts)
-    ]
 
 
 def query_places(ids, query_tokens):
@@ -214,7 +187,7 @@
     query_tokens,
     recv_refs,
     norm_ref,
-    soft_hbm,
+    soft_ref,
     qn_ref,
     score_ref,
     many_ref,
@@ -222,13 +195,11 @@
     list_ref,
     zw_ref,
     inverse_ref,
-    soft_ref,
     ext_ref,
     low_ref,
     sums_ref,
     list_smem,
     sem,
-    soft_sems,
 ):
     near = recv_refs[0].shape[0]
     sources = near * len(recv_refs)
@@ -246,10 +217,6 @@
         place = pl.ds(pl.multiple_of(source * query_count, query_count), query_count)
         ext_ref[place, :] = packed[:query_count]
         low_ref[place, :] = packed[8 : 8 + query_count]
-        qn_ref[pl.ds(pl.multiple_of(source * rows, rows), rows), :] = unit_rows(
-            recv_ref[:rows, :]
-        )[0].astype(jnp.bfloat16)
-    qn_ref[sources * rows :, :] = jnp.zeros((query_tokens, width), jnp.bfloat16)
 
     main = ext_ref[...]
     lanes = lane_ids(main.shape)
@@ -331,10 +298,12 @@
         list_ref[tables + row : tables + row + 1, :] = value.astype(jnp.int32)
     copy = pltpu.make_async_copy(list_ref, list_smem, sem)
     copy.start()
+    for d in range(sources):
+        recv_ref = recv_refs[d // near].at[d % near]
+        place = pl.ds(pl.multiple_of((me ^ d) * rows, rows), rows)
+        qn_ref[place, :] = unit_rows(recv_ref[:rows, :])[0].astype(jnp.bfloat16)
+    qn_ref[sources * rows :, :] = jnp.zeros((query_tokens, width), jnp.bfloat16)
     copy.wait()
-
-    def soft_copy(slot):
-        return pltpu.make_async_copy(soft_ref.at[slot], soft_hbm.at[slot], soft_sems.at[slot])
 
     def chunk(slot):
         p = list_smem[tables, slot]
@@ -355,10 +324,8 @@
     def visit(first, count):
         for u in range(count):
             chunk(first + u)
-        for u in range(count):
-            soft_copy(first + u).start()
-
-    used = each_chunk(list_smem, tables, visit)
+
+    each_chunk(list_smem, tables, visit)
 
     scores = jnp.zeros(main.shape, jnp.float32)
     for p in range(pass_count):
@@ -379,14 +346,7 @@
         + [jnp.zeros((6, 128), jnp.float32)],
         0,
     )
-    for s in range(sources):
-        zw_ref[s] = message
-
-    def drain(slot, carry):
-        soft_copy(slot).wait()
-        return carry
-
-    lax.fori_loop(0, used, drain, 0)
+    zw_ref[...] = message
 
 
 def forward(received, norm, cand_count, query_count, query_tokens):
@@ -404,25 +364,23 @@
             cand_count, query_count, query_tokens, refs[: len(received)], *refs[len(received) :]
         ),
         in_specs=[VMEM] * (len(received) + 1),
-        out_specs=[HBM] + [VMEM] * 7,
+        out_specs=[VMEM] * 8,
         out_shape=[
-            pltpu.HBM(soft_shape, jnp.bfloat16),
+            jax.ShapeDtypeStruct(soft_shape, jnp.bfloat16),
             jax.ShapeDtypeStruct((sources * rows + query_tokens, width), jnp.bfloat16),
             jax.ShapeDtypeStruct((group, 128), jnp.float32),
             jax.ShapeDtypeStruct((group, 128), jnp.float32),
             jax.ShapeDtypeStruct((group, 128), jnp.float32),
             jax.ShapeDtypeStruct((list_rows, 128), jnp.int32),
-            jax.ShapeDtypeStruct((sources, 8, 128), jnp.float32),
+            jax.ShapeDtypeStruct((8, 128), jnp.float32),
             jax.ShapeDtypeStruct((slots, chunk_pairs * query_tokens), jnp.float32),
         ],
         scratch_shapes=[
-            pltpu.VMEM(soft_shape, jnp.bfloat16),
             pltpu.VMEM((group, 128), jnp.float32),
             pltpu.VMEM((group, 128), jnp.float32),
             pltpu.VMEM((pass_count * (group + row_pad), 128), jnp.float32),
             pltpu.SMEM((list_rows, 128), jnp.int32),
             pltpu.SemaphoreType.DMA,
-            pltpu.SemaphoreType.DMA((slots,)),
         ],
         compiler_params=params(),
         cost_estimate=pl.CostEstimate(flops=flops, bytes_accessed=12 << 20, transcendentals=1 << 22),
@@ -441,8 +399,8 @@
 
 def attend_kernel(
     query_tokens,
-    flip_hbm,
-    soft_hbm,
+    flip_ref,
+    soft_ref,
     list_ref,
     score_ref,
     many_ref,
@@ -450,45 +408,23 @@
     inverse_ref,
     raised_ref,
     wanted_ref,
-    flip_ref,
-    soft_ref,
     raised_rows,
     wanted_rows,
-    raised_sum,
-    wanted_sum,
     list_smem,
     sem,
-    flip_sem,
-    soft_sems,
 ):
     pass_count = flip_ref.shape[0]
     group = score_ref.shape[0]
     stride = group + row_pad
     list_copy = pltpu.make_async_copy(list_ref, list_smem, sem)
     list_copy.start()
-    flip_copies = part_copies(flip_hbm, flip_ref, flip_sem)
     empty, tables = list_layout(group)
 
-    def soft_copy(slot):
-        return pltpu.make_async_copy(soft_hbm.at[slot], soft_ref.at[slot], soft_sems.at[slot])
-
-    def fetch(slot, carry):
-        soft_copy(slot).start()
-        return carry
-
-    lax.fori_loop(0, chunk_unroll, fetch, 0)
-    for copy in flip_copies:
-        copy.start()
-    lax.fori_loop(chunk_unroll, early_slots, fetch, 0)
-    list_copy.wait()
-    used = slots_used(list_smem, tables)
-    lax.fori_loop(early_slots, used, fetch, 0)
     spread(raised_rows, many_ref[...] * jnp.exp(score_ref[...]), pass_count, stride)
     spread(wanted_rows, target_ref[...], pass_count, stride)
-    raised_sum[...] = jnp.zeros(raised_sum.shape, jnp.float32)
-    wanted_sum[...] = jnp.zeros(wanted_sum.shape, jnp.float32)
-    for copy in flip_copies:
-        copy.wait()
+    raised_ref[...] = jnp.zeros(raised_ref.shape, jnp.float32)
+    wanted_ref[...] = jnp.zeros(wanted_ref.shape, jnp.float32)
+    list_copy.wait()
 
     def chunk(slot):
         p = list_smem[tables, slot]
@@ -497,7 +433,7 @@
         mixed = jnp.dot(flip_ref[p], soft_ref[slot], preferred_element_type=jnp.float32)
         mixed = (mixed * inverse_ref[pl.ds(slot, 1), :]).astype(jnp.bfloat16)
         mixed = jnp.transpose(mixed, (1, 0)).astype(jnp.float32)
-        for total, rows in ((raised_sum, raised_rows), (wanted_sum, wanted_rows)):
+        for total, rows in ((raised_ref, raised_rows), (wanted_ref, wanted_rows)):
             added = [
                 total[place, :]
                 + mixed[r * query_tokens : (r + 1) * query_tokens]
@@ -509,19 +445,9 @@
 
     def visit(first, count):
         for u in range(count):
-            soft_copy(first + u).wait()
-        for u in range(count):
             chunk(first + u)
 
     each_chunk(list_smem, tables, visit)
-
-    def drain(slot, carry):
-        soft_copy(slot).wait()
-        return carry
-
-    lax.fori_loop(used, early_slots, drain, 0)
-    raised_ref[...] = raised_sum[: group * query_tokens, :]
-    wanted_ref[...] = wanted_sum[: group * query_tokens, :]
 
 
 def attend(flip, soft, ids, score, many, target, inverse, query_tokens):
@@ -529,30 +455,23 @@
     pass_count, width, _ = flip.shape
     group = score.shape[0]
     flops = 2 * slots * columns * tokens * width
-    total = jax.ShapeDtypeStruct((group * query_tokens, width), jnp.float32)
+    total = jax.ShapeDtypeStruct(((group + 1) * query_tokens, width), jnp.float32)
     rows = pltpu.VMEM((pass_count * (group + row_pad), 128), jnp.float32)
-    padded = pltpu.VMEM(((group + 1) * query_tokens, width), jnp.float32)
     return pl.pallas_call(
         lambda *refs: attend_kernel(query_tokens, *refs),
-        in_specs=[HBM, HBM] + [VMEM] * 5,
+        in_specs=[VMEM] * 7,
         out_specs=[VMEM] * 2,
         out_shape=[total, total],
         scratch_shapes=[
-            pltpu.VMEM(flip.shape, jnp.bfloat16),
-            pltpu.VMEM(soft.shape, jnp.bfloat16),
             rows,
             rows,
-            padded,
-            padded,
             pltpu.SMEM(ids.shape, jnp.int32),
             pltpu.SemaphoreType.DMA,
-            pltpu.SemaphoreType.DMA((copy_parts,)),
-            pltpu.SemaphoreType.DMA((slots,)),
         ],
         compiler_params=params(),
         cost_estimate=pl.CostEstimate(flops=flops, bytes_accessed=12 << 20, transcendentals=0),
         name="attend",
-    )(in_hbm(flip), in_hbm(soft), ids, score, many, target, inverse)
+    )(flip, soft, ids, score, many, target, inverse)
 
 
 def halving_order(count):
@@ -566,7 +485,8 @@
 
 def query_kernel(
     query_tokens,
-    zw_ref,
+    sources,
+    zw_refs,
     score_ref,
     many_ref,
     target_ref,
@@ -578,10 +498,8 @@
     scale_ref,
     query_ref,
 ):
-    sources, group = zw_ref.shape[0], score_ref.shape[0]
-    sums = zw_ref[0]
-    for s in range(1, sources):
-        sums = sums + zw_ref[s]
+    group = score_ref.shape[0]
+    sums = sum(ref[...] for ref in zw_refs)
     lanes = lane_ids((group, 128))
     same_id = lax.broadcasted_iota(jnp.int32, (group, 128), 0) == lanes
     inverse = 1.0 / jnp.sum(jnp.where(same_id, sums[:1], 0.0), -1, keepdims=True)
@@ -604,13 +522,16 @@
             send_ref[place - half] = value
 
 
-def query_backward(zw, score, many, target, raised, wanted):
-    sources, group = zw.shape[0], score.shape[0]
-    rows, width = raised.shape
+def query_backward(zw, score, many, target, raised, wanted, sources):
+    group = score.shape[0]
+    width = raised.shape[1]
+    rows = raised.shape[0] // (group + 1) * group
     part = jax.ShapeDtypeStruct((sources // 2, rows // sources, width), jnp.bfloat16)
     return pl.pallas_call(
-        lambda *refs: query_kernel(rows // group, *refs),
-        in_specs=[VMEM] * 6,
+        lambda *refs: query_kernel(
+            rows // group, sources, refs[: len(zw)], *refs[len(zw) :]
+        ),
+        in_specs=[VMEM] * (len(zw) + 5),
         out_specs=[VMEM] * 3,
         out_shape=[part, part, jax.ShapeDtypeStruct((group, 128), jnp.float32)],
         scratch_shapes=[
@@ -619,7 +540,7 @@
         ],
         compiler_params=params(),
         name="query_backward",
-    )(zw, score, many, target, raised, wanted)
+    )(*zw, score, many, target, raised, wanted)
 
 
 def passage_kernel(
@@ -628,16 +549,14 @@
     grads_ref,
     qn_ref,
     inverse_ref,
-    soft_hbm,
+    soft_ref,
     own_ref,
     core_ref,
     far_ref,
     cross_ref,
-    soft_ref,
     grad_ref,
     list_smem,
     sem,
-    soft_sems,
 ):
     list_copy = pltpu.make_async_copy(list_ref, list_smem, sem)
     list_copy.start()
@@ -645,23 +564,8 @@
     group = grads_ref.shape[0]
     stride = group + row_pad
     empty, tables = list_layout(group)
-
-    def soft_copy(slot):
-        return pltpu.make_async_copy(soft_hbm.at[slot], soft_ref.at[slot], soft_sems.at[slot])
-
-    def fetch(slot, carry):
-        soft_copy(slot).start()
-        return carry
-
-    def drain(slot, carry):
-        soft_copy(slot).wait()
-        return carry
-
-    lax.fori_loop(0, early_slots, fetch, 0)
     spread(grad_ref, grads_ref[...], pass_count, stride)
     list_copy.wait()
-    total = list_smem[tables + 4, 0]
-    lax.fori_loop(early_slots, total, fetch, 0)
 
     def tile(p, row):
         ids = list_ids(list_smem, row, p)
@@ -696,15 +600,12 @@
         for place, ref in enumerate(outs):
             ref[p] = value[place * share : (place + 1) * share]
 
-    def step(i, ready):
-        needed = jnp.maximum(list_smem[tables + 2, (i + 1) * passage_unroll], 1)
-        lax.fori_loop(ready, needed, drain, 0)
+    def step(i, carry):
         for u in range(passage_unroll):
             passage(i * passage_unroll + u)
-        return needed
-
-    ready = lax.fori_loop(0, pass_count // passage_unroll, step, jnp.int32(0))
-    lax.fori_loop(ready, early_slots, drain, 0)
+        return carry
+
+    lax.fori_loop(0, pass_count // passage_unroll, step, 0)
 
     def rest(i, carry):
         p = list_smem[tables + 5, i]
@@ -723,56 +624,48 @@
 
 
 def passage_backward(ids, grads, qn, inverse, soft, pass_count, query_tokens, slices):
-    slots, tokens, columns = soft.shape
+    _, tokens, columns = soft.shape
     width = qn.shape[1]
     piece = jax.ShapeDtypeStruct((pass_count, tokens // slices, width), jnp.bfloat16)
     flops = 4 * pass_count * columns * tokens * width
     return pl.pallas_call(
         lambda *refs: passage_kernel(query_tokens, *refs),
-        in_specs=[VMEM] * 4 + [HBM],
+        in_specs=[VMEM] * 5,
         out_specs=[VMEM] * 4,
         out_shape=[piece] * 4,
         scratch_shapes=[
-            pltpu.VMEM(soft.shape, jnp.bfloat16),
             pltpu.VMEM((pass_count * (grads.shape[0] + row_pad), 128), jnp.float32),
             pltpu.SMEM(ids.shape, jnp.int32),
             pltpu.SemaphoreType.DMA,
-            pltpu.SemaphoreType.DMA((slots,)),
         ],
         compiler_params=params(),
         cost_estimate=pl.CostEstimate(flops=flops, bytes_accessed=6 << 20, transcendentals=0),
         name="passage_backward",
-    )(ids, grads, qn, inverse, in_hbm(soft))
-
-
-def finish_kernel(raw_ref, *refs):
-    out_ref = refs[-1]
-    grad = refs[0][...].astype(jnp.float32)
-    for ref in refs[1:-1]:
-        grad = grad + ref[...].astype(jnp.float32)
-    out_ref[...] = tangent(raw_ref[...], grad).astype(jnp.bfloat16)
-
-
-def finish(raw, parts):
+    )(ids, grads, qn, inverse, soft)
+
+
+def finish_kernel(query_parts, *refs):
+    raw_query, raw_passage = refs[:2]
+    query_out, passage_out = refs[-2:]
+    queries, passages = refs[2 : 2 + query_parts], refs[2 + query_parts : -2]
+    for raw, parts, out in ((raw_query, queries, query_out), (raw_passage, passages, passage_out)):
+        grad = sum(ref[...].astype(jnp.float32) for ref in parts)
+        out[...] = tangent(raw[...], grad).astype(jnp.bfloat16)
+
+
+def finish(raw_query, raw_passage, query_parts, passage_parts):
+    count = 2 + len(query_parts) + len(passage_parts)
     return pl.pallas_call(
-        finish_kernel,
-        in_specs=[VMEM] * (1 + len(parts)),
-        out_specs=VMEM,
-        out_shape=jax.ShapeDtypeStruct(raw.shape, jnp.bfloat16),
+        lambda *refs: finish_kernel(len(query_parts), *refs),
+        in_specs=[VMEM] * count,
+        out_specs=[VMEM] * 2,
+        out_shape=[
+            jax.ShapeDtypeStruct(raw_query.shape, jnp.bfloat16),
+            jax.ShapeDtypeStruct(raw_passage.shape, jnp.bfloat16),
+        ],
         compiler_params=params(),
         name="finish",
-    )(raw, *parts)
-
-
-def finish_queries(raw, parts):
-    return pl.pallas_call(
-        finish_kernel,
-        in_specs=[VMEM] * (1 + len(parts)),
-        out_specs=VMEM,
-        out_shape=jax.ShapeDtypeStruct(raw.shape, jnp.bfloat16),
-        compiler_params=params(),
-        name="finish_queries",
-    )(raw, *parts)
+    )(raw_query, raw_passage, *query_parts, *passage_parts)
 
 
 def shards(queries, passages, candidates, teacher):
@@ -786,8 +679,8 @@
     received = pack(queries.reshape(rows, width), candidates, teacher, pass_count)[None]
     while received.shape[0] * 4 < sources:
         bit = received.shape[0]
-        swap = [(i, i ^ bit) for i in range(sources)]
-        received = jnp.concatenate([received, lax.ppermute(received, "psg", swap)], 0)
+        pairs = [(i, i ^ bit) for i in range(sources)]
+        received = jnp.concatenate([received, lax.ppermute(received, "psg", pairs)], 0)
     stride = received.shape[0]
     received = [received] + [
         lax.ppermute(received, "psg", [(i, i ^ d) for i in range(sources)])
@@ -797,11 +690,22 @@
     soft, qn, score, many, target, ids, zw, inverse = forward(
         received, norm, cand_count, query_count, query_tokens
     )
-    zw = lax.all_to_all(zw, "psg", split_axis=0, concat_axis=0, tiled=True)
+
+    def swap(values, bit):
+        return lax.ppermute(values, "psg", [(i, i ^ bit) for i in range(sources)])
+
+    bit = 1
+    while sources // bit > 4:
+        zw = zw + swap(zw, bit)
+        bit *= 2
     raised_sum, wanted_sum = attend(
         flip, soft, ids, score, many, target, inverse, query_tokens
     )
-    keep, send, grads = query_backward(zw, score, many, target, raised_sum, wanted_sum)
+    zw, raised_sum = lax.optimization_barrier((zw, raised_sum))
+    zw = [zw] + [swap(zw, d) for d in range(bit, sources, bit)]
+    keep, send, grads = query_backward(
+        zw, score, many, target, raised_sum, wanted_sum, sources
+    )
     near = [(k, k ^ 1) for k in range(slices)]
     away = [(k, k ^ 2) for k in range(slices)]
     own, core, far, cross = passage_backward(
@@ -809,9 +713,9 @@
     )
     cross = lax.ppermute(cross, "qry", near)
     far = (far.astype(jnp.float32) + cross.astype(jnp.float32)).astype(jnp.bfloat16)
-    far, send, core = lax.optimization_barrier((far, send, core))
+    far, core, send = lax.optimization_barrier((far, core, send))
+    core = lax.ppermute(core, "qry", near)
     far = lax.ppermute(far, "qry", away)
-    core = lax.ppermute(core, "qry", near)
     bit = 1
     while sources // bit > 4:
         send = lax.ppermute(send, "psg", [(i, i ^ bit) for i in range(sources)])
@@ -826,16 +730,16 @@
         if place:
             piece = total[place].astype(jnp.bfloat16)
             query_parts.append(lax.ppermute(piece, "psg", [(i, i ^ d) for i in range(sources)]))
-    grad_queries = finish_queries(queries.reshape(rows, width), query_parts)
-
-    grad_passages = finish(own_raw, [own, core, far])
+    grad_queries, grad_passages = finish(
+        queries.reshape(rows, width), own_raw, query_parts, [own, core, far]
+    )
 
     raised = jnp.exp(teacher)
     raised_sum = jnp.sum(raised, -1, keepdims=True)
     log_target = teacher - jnp.log(raised_sum)
     known = jnp.sum(raised / raised_sum * log_target, -1)
     mine = lax.dynamic_slice_in_dim(
-        jnp.sum(zw[:, :2], 0), lax.axis_index("psg") * query_count, query_count, 1
+        sum(zw)[:2], lax.axis_index("psg") * query_count, query_count, 1
     )
     pair_loss = known - mine[1] + jnp.log(mine[0])
     return (pair_loss, grad_queries.reshape(queries.shape), grad_passages)

time: 60.8 us -> 57.7 us (0.949)
  Pallas kernels: 23.7 us -> 16.7 us
  starting transfers between devices: 18.7 us -> 20.6 us
  waiting for transfers between devices: 15.7 us -> 17.3 us
    ppermute x1 -> x5, starting transfers between devices: 3.03 us -> 8.93 us  [the longest x4 5.89 us: swap(): return lax.ppermute(values, 'psg', [(i, i ^ bit) for i in range(sources)])]
    all_to_all x1 -> x0, starting transfers between devices: 4.12 us -> none  [shards(): zw = lax.all_to_all(zw, 'psg', split_axis=0, concat_axis=0, tiled=True)]
    ppermute x1 -> x5, waiting for transfers between devices: 1.94 us -> 4.94 us  [the longest x4 3 us: swap(): return lax.ppermute(values, 'psg', [(i, i ^ bit) for i in range(sources)])]
    pallas_call x1, Pallas kernels: 5.14 us -> 3.08 us  [attend(): pl.pallas_call(lambda *refs: attend_kernel(query_tokens, *refs), in_specs...]
    pallas_call x1, Pallas kernels: 6.18 us -> 4.23 us  [forward(): pl.pallas_call(lambda *refs: forward_kernel(cand_count, query_count, quer...]
    all_to_all x1 -> x0, waiting for transfers between devices: 1.54 us -> none  [shards(): zw = lax.all_to_all(zw, 'psg', split_axis=0, concat_axis=0, tiled=True)]
    pallas_call x1, Pallas kernels: 5.17 us -> 3.79 us  [passage_backward(): pl.pallas_call(lambda *refs: passage_kernel(query_tokens, *refs), in_spec...]
    ppermute x3, waiting for transfers between devices: 5.04 us -> 3.68 us  [shards(): lax.ppermute(piece, 'psg', [(i, i ^ d) for i in range(sources)])]
  transfers between devices with their start and end apart: 12 -> 15, of which waited for: 8 -> 10; matrix products, arithmetic and copies ran while one was open for 2% -> 2% of each run, Pallas kernels for 16% -> 11%
where the time goes in v6:
time: 57.7 us; the launch traced here: 56.6 us
  starting transfers between devices  20.6 us (36%)
  waiting for transfers between devices  17.3 us (30%)
  Pallas kernels  16.7 us (29%)
  other arithmetic  1.06 us (2%)
  between operations  0.79 us (1%)
    ppermute x4, starting transfers between devices, swap(): return lax.ppermute(values, 'psg', [(i, i ^ bit) for i in range(sources)])  5.89 us
    ppermute x3, starting transfers between devices, shards(): lax.ppermute(received, 'psg', [(i, i ^ d) for i in range(sources)])  4.73 us
    ppermute x3, starting transfers between devices, shards(): lax.ppermute(piece, 'psg', [(i, i ^ d) for i in range(sources)])  4.45 us
    pallas_call x1, Pallas kernels, forward(): pl.pallas_call(lambda *refs: forward_kernel(cand_count, query_count, quer...  4.23 us
    pallas_call x1, Pallas kernels, passage_backward(): pl.pallas_call(lambda *refs: passage_kernel(query_tokens, *refs), in_spec...  3.79 us
    ppermute x3, waiting for transfers between devices, shards(): lax.ppermute(piece, 'psg', [(i, i ^ d) for i in range(sources)])  3.68 us
    pallas_call x1, Pallas kernels, prepare_passages(): pl.pallas_call(lambda *refs: passages_kernel(slices, *refs), in_specs=[HB...  3.09 us
    pallas_call x1, Pallas kernels, attend(): pl.pallas_call(lambda *refs: attend_kernel(query_tokens, *refs), in_specs...  3.08 us
  transfers between devices with their start and end apart: 15, of which 10 were waited for; matrix products, arithmetic and copies ran while one was open for 2% of the time, Pallas kernels for 11%

profile of v6, /device:TPU:0, one launch (start us, length us, event | category | flops | bytes accessed | tf_op | source)
XLA Modules:
  0.0 56.6 jit_solution(13496452944501347583)
XLA Ops:
  1.5 3.0 %collective-permute-start = (bf16[1,144,128]{2,1,0:T(8,128)(2,1)S(1)}, bf16[1,144,128]{2,1,0:T(8,128)(2,1)S(1)}, u32[]{:S(2)}, u32[]{:S(2)}) collective-permute-start(bf16[1,144,128]{2,1,0:T(8,128)(2,1)S(1)} %bitcast.17), channel_id=1, source_target_pairs={{0,4},{4,0},{8,12},{12,8},{16,20},{20,16},{24,28},{28,24},{1,5},{5... | collective-permute-start | bytes 110600 | tf_op jit(solution)/shard_map/ppermute | solution.py:683
  4.5 1.9 %collective-permute-done = bf16[1,144,128]{2,1,0:T(8,128)(2,1)S(1)} collective-permute-done((bf16[1,144,128]{2,1,0:T(8,128)(2,1)S(1)}, bf16[1,144,128]{2,1,0:T(8,128)(2,1)S(1)}, u32[]{:S(2)}, u32[]{:S(2)}) %collective-permute-start) | collective-permute-done | bytes 36896 | tf_op jit(solution)/shard_map/ppermute | solution.py:683
  6.5 2.1 %collective-permute-start.1 = (bf16[2,144,128]{2,1,0:T(8,128)(2,1)S(1)}, bf16[2,144,128]{2,1,0:T(8,128)(2,1)S(1)}, u32[]{:S(2)}, u32[]{:S(2)}) collective-permute-start(bf16[2,144,128]{2,1,0:T(8,128)(2,1)S(1)} %pad_maximum_fusion.refs_0_), channel_id=1, source_target_pairs={{0,8},{4,12},{8,0},{12,4},{16,24},{20,28},{24,16},{28,20},{1,9},{5... | collective-permute-start | bytes 221192 | tf_op jit(solution)/shard_map/ppermute | solution.py:686
  8.6 2.6 %collective-permute-start.2 = (bf16[2,144,128]{2,1,0:T(8,128)(2,1)S(1)}, bf16[2,144,128]{2,1,0:T(8,128)(2,1)S(1)}, u32[]{:S(2)}, u32[]{:S(2)}) collective-permute-start(bf16[2,144,128]{2,1,0:T(8,128)(2,1)S(1)} %pad_maximum_fusion.refs_0_), channel_id=1, source_target_pairs={{0,16},{4,20},{8,24},{12,28},{16,0},{20,4},{24,8},{28,12},{1,17},{... | collective-permute-start | bytes 221192 | tf_op jit(solution)/shard_map/ppermute | solution.py:686
  11.2 3.1 %prepare_passages.1 = (bf16[32,256,128]{2,1,0:T(8,128)(2,1)S(1)}, bf16[32,128,256]{2,1,0:T(8,128)(2,1)S(1)}, bf16[32,64,128]{2,1,0:T(8,128)(2,1)S(1)}) custom-call(bf16[32,256,128]{2,1,0:T(8,128)(2,1)} %refs_0_.1), custom_call_target="tpu_custom_call" | custom-call | flops 16777216 | bytes 6291456 | tf_op jit(solution)/shard_map/prepare_passages/pallas_call | solution.py:129
  14.3 1.1 %collective-permute-done.2.refs_2_ = bf16[2,144,128]{2,1,0:T(8,128)(2,1)S(1)} collective-permute-done((bf16[2,144,128]{2,1,0:T(8,128)(2,1)S(1)}, bf16[2,144,128]{2,1,0:T(8,128)(2,1)S(1)}, u32[]{:S(2)}, u32[]{:S(2)}) %collective-permute-start.2) | collective-permute-done | bytes 73760 | tf_op jit(solution)/shard_map/ppermute | solution.py:686
  15.5 1.9 %collective-permute-done.3.refs_3_ = bf16[2,144,128]{2,1,0:T(8,128)(2,1)S(1)} collective-permute-done((bf16[2,144,128]{2,1,0:T(8,128)(2,1)S(1)}, bf16[2,144,128]{2,1,0:T(8,128)(2,1)S(1)}, u32[]{:S(2)}, u32[]{:S(2)}) %collective-permute-start.3) | collective-permute-done | bytes 73760 | tf_op jit(solution)/shard_map/ppermute | solution.py:686
  17.4 4.2 %forward.1 = (bf16[72,256,256]{2,1,0:T(8,128)(2,1)S(1)}, bf16[1056,128]{1,0:T(8,128)(2,1)S(1)}, f32[32,128]{1,0:T(8,128)S(1)}, f32[32,128]{1,0:T(8,128)S(1)}, f3...) custom-call(bf16[2,144,128]{2,1,0:T(8,128)(2,1)S(1)} %pad_maximum_fusion.refs_0_, ...), custom_call_target="tpu_custom_call" | custom-call | flops 1207959552 | bytes 12582912 | tf_op jit(solution)/shard_map/forward/pallas_call | solution.py:362
  21.6 1.4 %collective-permute-start.4 = (f32[8,128]{1,0:T(8,128)S(1)}, f32[8,128]{1,0:T(8,128)S(1)}, u32[]{:S(2)}, u32[]{:S(2)}) collective-permute-start(f32[8,128]{1,0:T(8,128)S(1)} %get-tuple-element.37), channel_id=1, source_target_pairs={{0,4},{4,0},{8,12},{12,8},{16,20},{20,16},{24,28},{28,24},{1,5},{5... | collective-permute-start | bytes 12296 | tf_op jit(solution)/shard_map/ppermute | solution.py:695
  23.1 3.1 %attend.1 = (f32[1056,128]{1,0:T(8,128)S(1)}, f32[1056,128]{1,0:T(8,128)S(1)}) custom-call(bf16[32,128,256]{2,1,0:T(8,128)(2,1)S(1)} %get-tuple-element.38.refs_0_, bf16[72,256,256]{2,1,0:T(8,128)(2,1)S(1)} %get-tuple-element.39.refs_1_.refs_4_, s32[24,128]{1,0:T(8,128)S(1)} %get-tuple-element.36.refs_2_.refs_0_, ...), custom_call_target="tpu_custom_call" | custom-call | flops 1207959552 | bytes 12582912 | tf_op jit(solution)/shard_map/attend/pallas_call | solution.py:460
  26.2 1.0 %collective-permute-start.5 = (f32[8,128]{1,0:T(8,128)S(1)}, f32[8,128]{1,0:T(8,128)S(1)}, u32[]{:S(2)}, u32[]{:S(2)}) collective-permute-start(f32[8,128]{1,0:T(8,128)S(1)} %add.24.refs_0_), channel_id=1, source_target_pairs={{0,8},{4,12},{8,0},{12,4},{16,24},{20,28},{24,16},{28,20},{1,9},{5... | collective-permute-start | bytes 12296 | tf_op jit(solution)/shard_map/ppermute | solution.py:695
  27.2 1.0 %collective-permute-start.6 = (f32[8,128]{1,0:T(8,128)S(1)}, f32[8,128]{1,0:T(8,128)S(1)}, u32[]{:S(2)}, u32[]{:S(2)}) collective-permute-start(f32[8,128]{1,0:T(8,128)S(1)} %add.24.refs_0_), channel_id=1, source_target_pairs={{0,16},{4,20},{8,24},{12,28},{16,0},{20,4},{24,8},{28,12},{1,17},{... | collective-permute-start | bytes 12296 | tf_op jit(solution)/shard_map/ppermute | solution.py:695
  28.2 2.4 %collective-permute-start.7 = (f32[8,128]{1,0:T(8,128)S(1)}, f32[8,128]{1,0:T(8,128)S(1)}, u32[]{:S(2)}, u32[]{:S(2)}) collective-permute-start(f32[8,128]{1,0:T(8,128)S(1)} %add.24.refs_0_), channel_id=1, source_target_pairs={{0,24},{4,28},{8,16},{12,20},{16,8},{20,12},{24,0},{28,4},{1,25},{... | collective-permute-start | bytes 12296 | tf_op jit(solution)/shard_map/ppermute | solution.py:695
  30.6 1.1 %collective-permute-done.6.refs_2_ = f32[8,128]{1,0:T(8,128)S(1)} collective-permute-done((f32[8,128]{1,0:T(8,128)S(1)}, f32[8,128]{1,0:T(8,128)S(1)}, u32[]{:S(2)}, u32[]{:S(2)}) %collective-permute-start.6) | collective-permute-done | bytes 4128 | tf_op jit(solution)/shard_map/ppermute | solution.py:695
  31.7 1.9 %collective-permute-done.7.refs_3_ = f32[8,128]{1,0:T(8,128)S(1)} collective-permute-done((f32[8,128]{1,0:T(8,128)S(1)}, f32[8,128]{1,0:T(8,128)S(1)}, u32[]{:S(2)}, u32[]{:S(2)}) %collective-permute-start.7) | collective-permute-done | bytes 4128 | tf_op jit(solution)/shard_map/ppermute | solution.py:695
  33.8 3.8 %passage_backward.1 = (bf16[32,64,128]{2,1,0:T(8,128)(2,1)S(1)}, bf16[32,64,128]{2,1,0:T(8,128)(2,1)S(1)}, bf16[32,64,128]{2,1,0:T(8,128)(2,1)S(1)}, bf16[32,64,128]{2,1,0:T(8,128)(2,1)S(1)}) custom-call(s32[24,128]{1,0:T(8,128)S(1)} %get-tuple-element.36.refs_2_.refs_0_, f32[32,128]{1,0:T(8,128)S(1)} %get-tuple-element.48.refs_1_, ...), custom_call_target="tpu_custom_call" | custom-call | flops 1073741824 | bytes 6291456 | tf_op jit(solution)/shard_map/passage_backward/pallas_call | solution.py:631
  37.7 1.9 %collective-permute-done.8 = bf16[32,64,128]{2,1,0:T(8,128)(2,1)S(1)} collective-permute-done((bf16[32,64,128]{2,1,0:T(8,128)(2,1)S(1)}, bf16[32,64,128]{2,1,0:T(8,128)(2,1)S(1)}, u32[]{:S(2)}, u32[]{:S(2)}) %collective-permute-start.8) | collective-permute-done | bytes 524320 | tf_op jit(solution)/shard_map/ppermute | solution.py:714
  40.8 1.8 %collective-permute-start.14 = (bf16[32,64,128]{2,1,0:T(8,128)(2,1)S(1)}, bf16[32,64,128]{2,1,0:T(8,128)(2,1)S(1)}, u32[]{:S(2)}, u32[]{:S(2)}) collective-permute-start(bf16[32,64,128]{2,1,0:T(8,128)(2,1)S(1)} %add_convert_fusion), channel_id=1, source_target_pairs={{0,2},{1,3},{2,0},{3,1},{4,6},{5,7},{6,4},{7,5},{8,10},{9,11},{10,... | collective-permute-start | bytes 1572872 | tf_op jit(solution)/shard_map/ppermute | solution.py:718
  42.5 2.9 %collective-permute-done.9 = bf16[4,128,128]{2,1,0:T(8,128)(2,1)S(1)} collective-permute-done((bf16[4,128,128]{2,1,0:T(8,128)(2,1)S(1)}, bf16[4,128,128]{2,1,0:T(8,128)(2,1)S(1)}, u32[]{:S(2)}, u32[]{:S(2)}) %collective-permute-start.9) | collective-permute-done | bytes 131104 | tf_op jit(solution)/shard_map/ppermute | solution.py:721
  45.6 2.9 %collective-permute-start.11 = (bf16[128,128]{1,0:T(8,128)(2,1)S(1)}, bf16[128,128]{1,0:T(8,128)(2,1)S(1)}, u32[]{:S(2)}, u32[]{:S(2)}) collective-permute-start(bf16[128,128]{1,0:T(8,128)(2,1)S(1)} %get-tuple-element.70), channel_id=1, source_target_pairs={{0,8},{4,12},{8,0},{12,4},{16,24},{20,28},{24,16},{28,20},{1,9},{5... | collective-permute-start | bytes 98312 | tf_op jit(solution)/shard_map/ppermute | solution.py:732
  48.5 1.4 %collective-permute-start.12 = (bf16[128,128]{1,0:T(8,128)(2,1)S(1)}, bf16[128,128]{1,0:T(8,128)(2,1)S(1)}, u32[]{:S(2)}, u32[]{:S(2)}) collective-permute-start(bf16[128,128]{1,0:T(8,128)(2,1)S(1)} %get-tuple-element.69), channel_id=1, source_target_pairs={{0,24},{4,28},{8,16},{12,20},{16,8},{20,12},{24,0},{28,4},{1,25},{... | collective-permute-start | bytes 98312 | tf_op jit(solution)/shard_map/ppermute | solution.py:732
  50.7 3.5 %collective-permute-done.12.refs_5_ = bf16[128,128]{1,0:T(8,128)(2,1)S(1)} collective-permute-done((bf16[128,128]{1,0:T(8,128)(2,1)S(1)}, bf16[128,128]{1,0:T(8,128)(2,1)S(1)}, u32[]{:S(2)}, u32[]{:S(2)}) %collective-permute-start.12) | collective-permute-done | bytes 32800 | tf_op jit(solution)/shard_map/ppermute | solution.py:732
  54.2 0.9 %collective-permute-done.14.refs_8_ = bf16[32,64,128]{2,1,0:T(8,128)(2,1)S(1)} collective-permute-done((bf16[32,64,128]{2,1,0:T(8,128)(2,1)S(1)}, bf16[32,64,128]{2,1,0:T(8,128)(2,1)S(1)}, u32[]{:S(2)}, u32[]{:S(2)}) %collective-permute-start.14) | collective-permute-done | bytes 524320 | tf_op jit(solution)/shard_map/ppermute | solution.py:718
  55.1 1.5 %finish.1 = (bf16[128,128]{1,0:T(8,128)(2,1)}, bf16[32,64,128]{2,1,0:T(8,128)(2,1)}) custom-call(bf16[128,128]{1,0:T(8,128)(2,1)S(1)} %bitcast.20, bf16[32,64,128]{2,1,0:T(8,128)(2,1)S(1)} %get-tuple-element.59.refs_1_, f32[128,128]{1,0:T(8,128)S(1)} %slice_bitcast_fusion.refs_2_, bf16[128,128]{1,0:T(8,128)(2,1)S(1)} %collective-permute-done.10.refs_3_, ...), custom_call_target="tpu_custom_call" | custom-call | tf_op jit(solution)/shard_map/finish/pallas_call | solution.py:658
  (30 shorter events, 3.3 us)
Async XLA Ops:
  1.5 5.0 %collective-permute-start = (bf16[1,144,128]{2,1,0:T(8,128)(2,1)S(1)}, bf16[1,144,128]{2,1,0:T(8,128)(2,1)S(1)}, u32[]{:S(2)}, u32[]{:S(2)}) collective-permute-start(bf16[1,144,128]{2,1,0:T(8,128)(2,1)S(1)} %bitcast.17), channel_id=1, source_target_pairs={{0,4},{4,0},{8,12},{12,8},{16,20},{20,16},{24,28},{28,24},{1,5},{5... | collective-permute-start | bytes 110600 | tf_op jit(solution)/shard_map/ppermute | solution.py:683
  6.5 7.8 %collective-permute-start.1 = (bf16[2,144,128]{2,1,0:T(8,128)(2,1)S(1)}, bf16[2,144,128]{2,1,0:T(8,128)(2,1)S(1)}, u32[]{:S(2)}, u32[]{:S(2)}) collective-permute-start(bf16[2,144,128]{2,1,0:T(8,128)(2,1)S(1)} %pad_maximum_fusion.refs_0_), channel_id=1, source_target_pairs={{0,8},{4,12},{8,0},{12,4},{16,24},{20,28},{24,16},{28,20},{1,9},{5... | collective-permute-start | bytes 221192 | tf_op jit(solution)/shard_map/ppermute | solution.py:686
  8.6 6.8 %collective-permute-start.2 = (bf16[2,144,128]{2,1,0:T(8,128)(2,1)S(1)}, bf16[2,144,128]{2,1,0:T(8,128)(2,1)S(1)}, u32[]{:S(2)}, u32[]{:S(2)}) collective-permute-start(bf16[2,144,128]{2,1,0:T(8,128)(2,1)S(1)} %pad_maximum_fusion.refs_0_), channel_id=1, source_target_pairs={{0,16},{4,20},{8,24},{12,28},{16,0},{20,4},{24,8},{28,12},{1,17},{... | collective-permute-start | bytes 221192 | tf_op jit(solution)/shard_map/ppermute | solution.py:686
  11.2 6.2 %collective-permute-start.3 = (bf16[2,144,128]{2,1,0:T(8,128)(2,1)S(1)}, bf16[2,144,128]{2,1,0:T(8,128)(2,1)S(1)}, u32[]{:S(2)}, u32[]{:S(2)}) collective-permute-start(bf16[2,144,128]{2,1,0:T(8,128)(2,1)S(1)} %pad_maximum_fusion.refs_0_), channel_id=1, source_target_pairs={{0,24},{4,28},{8,16},{12,20},{16,8},{20,12},{24,0},{28,4},{1,25},{... | collective-permute-start | bytes 221192 | tf_op jit(solution)/shard_map/ppermute | solution.py:686
  21.6 4.5 %collective-permute-start.4 = (f32[8,128]{1,0:T(8,128)S(1)}, f32[8,128]{1,0:T(8,128)S(1)}, u32[]{:S(2)}, u32[]{:S(2)}) collective-permute-start(f32[8,128]{1,0:T(8,128)S(1)} %get-tuple-element.37), channel_id=1, source_target_pairs={{0,4},{4,0},{8,12},{12,8},{16,20},{20,16},{24,28},{28,24},{1,5},{5... | collective-permute-start | bytes 12296 | tf_op jit(solution)/shard_map/ppermute | solution.py:695
  26.2 4.5 %collective-permute-start.5 = (f32[8,128]{1,0:T(8,128)S(1)}, f32[8,128]{1,0:T(8,128)S(1)}, u32[]{:S(2)}, u32[]{:S(2)}) collective-permute-start(f32[8,128]{1,0:T(8,128)S(1)} %add.24.refs_0_), channel_id=1, source_target_pairs={{0,8},{4,12},{8,0},{12,4},{16,24},{20,28},{24,16},{28,20},{1,9},{5... | collective-permute-start | bytes 12296 | tf_op jit(solution)/shard_map/ppermute | solution.py:695
  27.2 4.5 %collective-permute-start.6 = (f32[8,128]{1,0:T(8,128)S(1)}, f32[8,128]{1,0:T(8,128)S(1)}, u32[]{:S(2)}, u32[]{:S(2)}) collective-permute-start(f32[8,128]{1,0:T(8,128)S(1)} %add.24.refs_0_), channel_id=1, source_target_pairs={{0,16},{4,20},{8,24},{12,28},{16,0},{20,4},{24,8},{28,12},{1,17},{... | collective-permute-start | bytes 12296 | tf_op jit(solution)/shard_map/ppermute | solution.py:695
  28.2 5.4 %collective-permute-start.7 = (f32[8,128]{1,0:T(8,128)S(1)}, f32[8,128]{1,0:T(8,128)S(1)}, u32[]{:S(2)}, u32[]{:S(2)}) collective-permute-start(f32[8,128]{1,0:T(8,128)S(1)} %add.24.refs_0_), channel_id=1, source_target_pairs={{0,24},{4,28},{8,16},{12,20},{16,8},{20,12},{24,0},{28,4},{1,25},{... | collective-permute-start | bytes 12296 | tf_op jit(solution)/shard_map/ppermute | solution.py:695
  33.8 6.6 %copy-start.1 = (f32[4,32]{1,0:T(4,128)S(1)}, f32[4,32]{1,0:T(4,128)}, u32[]{:S(2)}) copy-start(f32[4,32]{1,0:T(4,128)} %refs_2_.1) | copy-start | bytes 1540
  37.6 17.5 %copy-start = (bf16[4,32,128]{2,1,0:T(8,128)(2,1)S(1)}, bf16[4,32,128]{2,1,0:T(8,128)(2,1)}, u32[]{:S(2)}) copy-start(bf16[4,32,128]{2,1,0:T(8,128)(2,1)} %param.4) | copy-start | bytes 98308
  37.6 2.0 %collective-permute-start.8 = (bf16[32,64,128]{2,1,0:T(8,128)(2,1)S(1)}, bf16[32,64,128]{2,1,0:T(8,128)(2,1)S(1)}, u32[]{:S(2)}, u32[]{:S(2)}) collective-permute-start(bf16[32,64,128]{2,1,0:T(8,128)(2,1)S(1)} %get-tuple-element.51), channel_id=1, source_target_pairs={{0,1},{1,0},{2,3},{3,2},{4,5},{5,4},{6,7},{7,6},{8,9},{9,8},{10,11... | collective-permute-start | bytes 1572872 | tf_op jit(solution)/shard_map/ppermute | solution.py:714
  39.8 5.6 %collective-permute-start.9 = (bf16[4,128,128]{2,1,0:T(8,128)(2,1)S(1)}, bf16[4,128,128]{2,1,0:T(8,128)(2,1)S(1)}, u32[]{:S(2)}, u32[]{:S(2)}) collective-permute-start(bf16[4,128,128]{2,1,0:T(8,128)(2,1)S(1)} %get-tuple-element.54), channel_id=1, source_target_pairs={{0,4},{4,0},{8,12},{12,8},{16,20},{20,16},{24,28},{28,24},{1,5},{5... | collective-permute-start | bytes 393224 | tf_op jit(solution)/shard_map/ppermute | solution.py:721
  40.7 13.5 %collective-permute-start.13 = (bf16[32,64,128]{2,1,0:T(8,128)(2,1)S(1)}, bf16[32,64,128]{2,1,0:T(8,128)(2,1)S(1)}, u32[]{:S(2)}, u32[]{:S(2)}) collective-permute-start(bf16[32,64,128]{2,1,0:T(8,128)(2,1)S(1)} %get-tuple-element.63), channel_id=1, source_target_pairs={{0,1},{1,0},{2,3},{3,2},{4,5},{5,4},{6,7},{7,6},{8,9},{9,8},{10,11... | collective-permute-start | bytes 1572872 | tf_op jit(solution)/shard_map/ppermute | solution.py:717
  40.8 14.3 %collective-permute-start.14 = (bf16[32,64,128]{2,1,0:T(8,128)(2,1)S(1)}, bf16[32,64,128]{2,1,0:T(8,128)(2,1)S(1)}, u32[]{:S(2)}, u32[]{:S(2)}) collective-permute-start(bf16[32,64,128]{2,1,0:T(8,128)(2,1)S(1)} %add_convert_fusion), channel_id=1, source_target_pairs={{0,2},{1,3},{2,0},{3,1},{4,6},{5,7},{6,4},{7,5},{8,10},{9,11},{10,... | collective-permute-start | bytes 1572872 | tf_op jit(solution)/shard_map/ppermute | solution.py:718
  45.4 5.3 %collective-permute-start.10 = (bf16[128,128]{1,0:T(8,128)(2,1)S(1)}, bf16[128,128]{1,0:T(8,128)(2,1)S(1)}, u32[]{:S(2)}, u32[]{:S(2)}) collective-permute-start(bf16[128,128]{1,0:T(8,128)(2,1)S(1)} %get-tuple-element.71), channel_id=1, source_target_pairs={{0,16},{4,20},{8,24},{12,28},{16,0},{20,4},{24,8},{28,12},{1,17},{... | collective-permute-start | bytes 98312 | tf_op jit(solution)/shard_map/ppermute | solution.py:732
  45.6 5.1 %collective-permute-start.11 = (bf16[128,128]{1,0:T(8,128)(2,1)S(1)}, bf16[128,128]{1,0:T(8,128)(2,1)S(1)}, u32[]{:S(2)}, u32[]{:S(2)}) collective-permute-start(bf16[128,128]{1,0:T(8,128)(2,1)S(1)} %get-tuple-element.70), channel_id=1, source_target_pairs={{0,8},{4,12},{8,0},{12,4},{16,24},{20,28},{24,16},{28,20},{1,9},{5... | collective-permute-start | bytes 98312 | tf_op jit(solution)/shard_map/ppermute | solution.py:732
  48.5 5.7 %collective-permute-start.12 = (bf16[128,128]{1,0:T(8,128)(2,1)S(1)}, bf16[128,128]{1,0:T(8,128)(2,1)S(1)}, u32[]{:S(2)}, u32[]{:S(2)}) collective-permute-start(bf16[128,128]{1,0:T(8,128)(2,1)S(1)} %get-tuple-element.69), channel_id=1, source_target_pairs={{0,24},{4,28},{8,16},{12,20},{16,8},{20,12},{24,0},{28,4},{1,25},{... | collective-permute-start | bytes 98312 | tf_op jit(solution)/shard_map/ppermute | solution.py:732

commit v7 on v6

--- a/solution.py
+++ b/solution.py
@@ -647,17 +647,17 @@
 def finish_kernel(query_parts, *refs):
     raw_query, raw_passage = refs[:2]
     query_out, passage_out = refs[-2:]
-    queries, passages = refs[2 : 2 + query_parts], refs[2 + query_parts : -2]
+    queries, passages = refs[2 : 2 + query_parts], refs[2 + query_parts : -3]
     for raw, parts, out in ((raw_query, queries, query_out), (raw_passage, passages, passage_out)):
         grad = sum(ref[...].astype(jnp.float32) for ref in parts)
         out[...] = tangent(raw[...], grad).astype(jnp.bfloat16)
 
 
-def finish(raw_query, raw_passage, query_parts, passage_parts):
+def finish(raw_query, raw_passage, query_parts, passage_parts, ready):
     count = 2 + len(query_parts) + len(passage_parts)
     return pl.pallas_call(
         lambda *refs: finish_kernel(len(query_parts), *refs),
-        in_specs=[VMEM] * count,
+        in_specs=[VMEM] * count + [pl.BlockSpec(memory_space=pl.ANY)],
         out_specs=[VMEM] * 2,
         out_shape=[
             jax.ShapeDtypeStruct(raw_query.shape, jnp.bfloat16),
@@ -665,7 +665,7 @@
         ],
         compiler_params=params(),
         name="finish",
-    )(raw_query, raw_passage, *query_parts, *passage_parts)
+    )(raw_query, raw_passage, *query_parts, *passage_parts, ready)
 
 
 def shards(queries, passages, candidates, teacher):
@@ -713,25 +713,23 @@
     )
     cross = lax.ppermute(cross, "qry", near)
     far = (far.astype(jnp.float32) + cross.astype(jnp.float32)).astype(jnp.bfloat16)
-    far, core, send = lax.optimization_barrier((far, core, send))
+    send, own = lax.optimization_barrier((send, own))
+    ready = far
+    far = lax.ppermute(far, "qry", away)
     core = lax.ppermute(core, "qry", near)
-    far = lax.ppermute(far, "qry", away)
     bit = 1
-    while sources // bit > 4:
+    while bit < sources:
         send = lax.ppermute(send, "psg", [(i, i ^ bit) for i in range(sources)])
-        send, zw = lax.optimization_barrier((send, zw))
-        total = keep.astype(jnp.float32) + send.astype(jnp.float32)
-        half = total.shape[0] // 2
+        if bit == 1:
+            send, zw, ready = lax.optimization_barrier((send, zw, ready))
         bit *= 2
-        if sources // bit > 4:
+        if bit < sources:
+            total = keep.astype(jnp.float32) + send.astype(jnp.float32)
+            half = total.shape[0] // 2
             keep, send = total[:half], total[half:].astype(jnp.bfloat16)
-    query_parts = [total[0]]
-    for place, d in enumerate(halving_order(sources)[: total.shape[0]]):
-        if place:
-            piece = total[place].astype(jnp.bfloat16)
-            query_parts.append(lax.ppermute(piece, "psg", [(i, i ^ d) for i in range(sources)]))
+    query_parts = [keep[0], send[0]]
     grad_queries, grad_passages = finish(
-        queries.reshape(rows, width), own_raw, query_parts, [own, core, far]
+        queries.reshape(rows, width), own_raw, query_parts, [own, core, far], ready
     )
 
     raised = jnp.exp(teacher)

time: 57.7 us -> 55.9 us (0.969); the launches traced: 56.6 us -> 55.8 us
  Pallas kernels: 16.7 us -> 19 us
  starting transfers between devices: 20.6 us -> 18.7 us
  waiting for transfers between devices: 17.3 us -> 16.1 us
    ppermute x1 -> x3, waiting for transfers between devices: 2.85 us -> 7.62 us  [shards(): send = lax.ppermute(send, 'psg', [(i, i ^ bit) for i in range(sources)])]
    ppermute x3 -> x0, starting transfers between devices: 4.45 us -> none  [shards(): lax.ppermute(piece, 'psg', [(i, i ^ d) for i in range(sources)])]
    ppermute x3 -> x0, waiting for transfers between devices: 3.68 us -> none  [shards(): lax.ppermute(piece, 'psg', [(i, i ^ d) for i in range(sources)])]
    ppermute x1 -> x3, starting transfers between devices: 0.59 us -> 3.44 us  [shards(): send = lax.ppermute(send, 'psg', [(i, i ^ bit) for i in range(sources)])]
    ppermute x4, waiting for transfers between devices: 3 us -> 1.71 us  [swap(): return lax.ppermute(values, 'psg', [(i, i ^ bit) for i in range(sources)])]
    pallas_call x1, Pallas kernels: 3.08 us -> 4.24 us  [attend(): pl.pallas_call(lambda *refs: attend_kernel(query_tokens, *refs), in_specs...]
    ppermute x1, waiting for transfers between devices: 1.9 us -> 0.76 us  [shards(): cross = lax.ppermute(cross, 'qry', near)]
    pallas_call x1, Pallas kernels: 4.23 us -> 5.36 us  [forward(): pl.pallas_call(lambda *refs: forward_kernel(cand_count, query_count, quer...]
  transfers between devices with their start and end apart: 15 -> 14, of which waited for: 10 -> 10; matrix products, arithmetic and copies ran while one was open for 2% -> 2% of each run, Pallas kernels for 11% -> 13%
where the time goes in v7:
time: 55.9 us; the launch traced here: 55.8 us
  Pallas kernels  19 us (34%)
  starting transfers between devices  18.7 us (33%)
  waiting for transfers between devices  16.1 us (29%)
  other arithmetic  1.07 us (2%)
  between operations  0.81 us (1%)
    ppermute x3, waiting for transfers between devices, shards(): send = lax.ppermute(send, 'psg', [(i, i ^ bit) for i in range(sources)])  7.62 us
    pallas_call x1, Pallas kernels, forward(): pl.pallas_call(lambda *refs: forward_kernel(cand_count, query_count, quer...  5.36 us
    ppermute x4, starting transfers between devices, swap(): return lax.ppermute(values, 'psg', [(i, i ^ bit) for i in range(sources)])  4.9 us
    ppermute x3, starting transfers between devices, shards(): lax.ppermute(received, 'psg', [(i, i ^ d) for i in range(sources)])  4.73 us
    pallas_call x1, Pallas kernels, attend(): pl.pallas_call(lambda *refs: attend_kernel(query_tokens, *refs), in_specs...  4.24 us
    pallas_call x1, Pallas kernels, passage_backward(): pl.pallas_call(lambda *refs: passage_kernel(query_tokens, *refs), in_spec...  3.78 us
    ppermute x3, starting transfers between devices, shards(): send = lax.ppermute(send, 'psg', [(i, i ^ bit) for i in range(sources)])  3.44 us
    pallas_call x1, Pallas kernels, prepare_passages(): pl.pallas_call(lambda *refs: passages_kernel(slices, *refs), in_specs=[HB...  3.09 us
  transfers between devices with their start and end apart: 14, of which 10 were waited for; matrix products, arithmetic and copies ran while one was open for 2% of the time, Pallas kernels for 13%

profile of v7, /device:TPU:0, one launch (start us, length us, event | category | flops | bytes accessed | tf_op | source)
XLA Modules:
  0.0 55.8 jit_solution(7190884918777120472)
XLA Ops:
  0.6 0.9 %pack.1 = bf16[144,128]{1,0:T(8,128)(2,1)S(1)} custom-call(bf16[128,128]{1,0:T(8,128)(2,1)} %bitcast.14, s32[4,32]{1,0:T(4,128)} %refs_1_.1, f32[4,32]{1,0:T(4,128)} %refs_2_.1), custom_call_target="tpu_custom_call" | custom-call | tf_op jit(solution)/shard_map/pack/pallas_call | solution.py:71
  1.5 3.0 %collective-permute-start = (bf16[1,144,128]{2,1,0:T(8,128)(2,1)S(1)}, bf16[1,144,128]{2,1,0:T(8,128)(2,1)S(1)}, u32[]{:S(2)}, u32[]{:S(2)}) collective-permute-start(bf16[1,144,128]{2,1,0:T(8,128)(2,1)S(1)} %bitcast.12), channel_id=1, source_target_pairs={{0,4},{4,0},{8,12},{12,8},{16,20},{20,16},{24,28},{28,24},{1,5},{5... | collective-permute-start | bytes 110600 | tf_op jit(solution)/shard_map/ppermute | solution.py:683
  4.5 1.9 %collective-permute-done = bf16[1,144,128]{2,1,0:T(8,128)(2,1)S(1)} collective-permute-done((bf16[1,144,128]{2,1,0:T(8,128)(2,1)S(1)}, bf16[1,144,128]{2,1,0:T(8,128)(2,1)S(1)}, u32[]{:S(2)}, u32[]{:S(2)}) %collective-permute-start) | collective-permute-done | bytes 36896 | tf_op jit(solution)/shard_map/ppermute | solution.py:683
  6.5 2.1 %collective-permute-start.1 = (bf16[2,144,128]{2,1,0:T(8,128)(2,1)S(1)}, bf16[2,144,128]{2,1,0:T(8,128)(2,1)S(1)}, u32[]{:S(2)}, u32[]{:S(2)}) collective-permute-start(bf16[2,144,128]{2,1,0:T(8,128)(2,1)S(1)} %pad_maximum_fusion.refs_0_), channel_id=1, source_target_pairs={{0,8},{4,12},{8,0},{12,4},{16,24},{20,28},{24,16},{28,20},{1,9},{5... | collective-permute-start | bytes 221192 | tf_op jit(solution)/shard_map/ppermute | solution.py:686
  8.6 2.6 %collective-permute-start.2 = (bf16[2,144,128]{2,1,0:T(8,128)(2,1)S(1)}, bf16[2,144,128]{2,1,0:T(8,128)(2,1)S(1)}, u32[]{:S(2)}, u32[]{:S(2)}) collective-permute-start(bf16[2,144,128]{2,1,0:T(8,128)(2,1)S(1)} %pad_maximum_fusion.refs_0_), channel_id=1, source_target_pairs={{0,16},{4,20},{8,24},{12,28},{16,0},{20,4},{24,8},{28,12},{1,17},{... | collective-permute-start | bytes 221192 | tf_op jit(solution)/shard_map/ppermute | solution.py:686
  11.2 3.1 %prepare_passages.1 = (bf16[32,256,128]{2,1,0:T(8,128)(2,1)S(1)}, bf16[32,128,256]{2,1,0:T(8,128)(2,1)S(1)}, bf16[32,64,128]{2,1,0:T(8,128)(2,1)S(1)}) custom-call(bf16[32,256,128]{2,1,0:T(8,128)(2,1)} %refs_0_.1), custom_call_target="tpu_custom_call" | custom-call | flops 16777216 | bytes 6291456 | tf_op jit(solution)/shard_map/prepare_passages/pallas_call | solution.py:129
  14.3 1.1 %collective-permute-done.2.refs_2_ = bf16[2,144,128]{2,1,0:T(8,128)(2,1)S(1)} collective-permute-done((bf16[2,144,128]{2,1,0:T(8,128)(2,1)S(1)}, bf16[2,144,128]{2,1,0:T(8,128)(2,1)S(1)}, u32[]{:S(2)}, u32[]{:S(2)}) %collective-permute-start.2) | collective-permute-done | bytes 73760 | tf_op jit(solution)/shard_map/ppermute | solution.py:686
  15.5 1.9 %collective-permute-done.3.refs_3_ = bf16[2,144,128]{2,1,0:T(8,128)(2,1)S(1)} collective-permute-done((bf16[2,144,128]{2,1,0:T(8,128)(2,1)S(1)}, bf16[2,144,128]{2,1,0:T(8,128)(2,1)S(1)}, u32[]{:S(2)}, u32[]{:S(2)}) %collective-permute-start.3) | collective-permute-done | bytes 73760 | tf_op jit(solution)/shard_map/ppermute | solution.py:686
  17.4 5.4 %forward.1 = (bf16[72,256,256]{2,1,0:T(8,128)(2,1)S(1)}, bf16[1056,128]{1,0:T(8,128)(2,1)S(1)}, f32[32,128]{1,0:T(8,128)S(1)}, f32[32,128]{1,0:T(8,128)S(1)}, f3...) custom-call(bf16[2,144,128]{2,1,0:T(8,128)(2,1)S(1)} %pad_maximum_fusion.refs_0_, ...), custom_call_target="tpu_custom_call" | custom-call | flops 1207959552 | bytes 12582912 | tf_op jit(solution)/shard_map/forward/pallas_call | solution.py:362
  23.2 4.2 %attend.1 = (f32[1056,128]{1,0:T(8,128)S(1)}, f32[1056,128]{1,0:T(8,128)S(1)}) custom-call(bf16[32,128,256]{2,1,0:T(8,128)(2,1)S(1)} %get-tuple-element.37.refs_0_, bf16[72,256,256]{2,1,0:T(8,128)(2,1)S(1)} %get-tuple-element.38.refs_1_.refs_4_, s32[24,128]{1,0:T(8,128)S(1)} %get-tuple-element.39.refs_2_.refs_0_, ...), custom_call_target="tpu_custom_call" | custom-call | flops 1207959552 | bytes 12582912 | tf_op jit(solution)/shard_map/attend/pallas_call | solution.py:460
  27.5 0.7 %collective-permute-start.6 = (f32[8,128]{1,0:T(8,128)S(1)}, f32[8,128]{1,0:T(8,128)S(1)}, u32[]{:S(2)}, u32[]{:S(2)}) collective-permute-start(f32[8,128]{1,0:T(8,128)S(1)} %add.27.refs_0_), channel_id=1, source_target_pairs={{0,16},{4,20},{8,24},{12,28},{16,0},{20,4},{24,8},{28,12},{1,17},{... | collective-permute-start | bytes 12296 | tf_op jit(solution)/shard_map/ppermute | solution.py:695
  28.2 3.7 %collective-permute-start.7 = (f32[8,128]{1,0:T(8,128)S(1)}, f32[8,128]{1,0:T(8,128)S(1)}, u32[]{:S(2)}, u32[]{:S(2)}) collective-permute-start(f32[8,128]{1,0:T(8,128)S(1)} %add.27.refs_0_), channel_id=1, source_target_pairs={{0,24},{4,28},{8,16},{12,20},{16,8},{20,12},{24,0},{28,4},{1,25},{... | collective-permute-start | bytes 12296 | tf_op jit(solution)/shard_map/ppermute | solution.py:695
  32.1 1.5 %collective-permute-done.7.refs_3_ = f32[8,128]{1,0:T(8,128)S(1)} collective-permute-done((f32[8,128]{1,0:T(8,128)S(1)}, f32[8,128]{1,0:T(8,128)S(1)}, u32[]{:S(2)}, u32[]{:S(2)}) %collective-permute-start.7) | collective-permute-done | bytes 4128 | tf_op jit(solution)/shard_map/ppermute | solution.py:695
  33.8 3.8 %passage_backward.1 = (bf16[32,64,128]{2,1,0:T(8,128)(2,1)S(1)}, bf16[32,64,128]{2,1,0:T(8,128)(2,1)S(1)}, bf16[32,64,128]{2,1,0:T(8,128)(2,1)S(1)}, bf16[32,64,128]{2,1,0:T(8,128)(2,1)S(1)}) custom-call(s32[24,128]{1,0:T(8,128)S(1)} %get-tuple-element.39.refs_2_.refs_0_, f32[32,128]{1,0:T(8,128)S(1)} %get-tuple-element.49.refs_1_, ...), custom_call_target="tpu_custom_call" | custom-call | flops 1073741824 | bytes 6291456 | tf_op jit(solution)/shard_map/passage_backward/pallas_call | solution.py:631
  38.0 0.6 %collective-permute-start.8 = (bf16[4,128,128]{2,1,0:T(8,128)(2,1)S(1)}, bf16[4,128,128]{2,1,0:T(8,128)(2,1)S(1)}, u32[]{:S(2)}, u32[]{:S(2)}) collective-permute-start(bf16[4,128,128]{2,1,0:T(8,128)(2,1)S(1)} %get-tuple-element.52), channel_id=1, source_target_pairs={{0,4},{4,0},{8,12},{12,8},{16,20},{20,16},{24,28},{28,24},{1,5},{5... | collective-permute-start | bytes 393224 | tf_op jit(solution)/shard_map/ppermute | solution.py:722
  38.8 0.8 %collective-permute-done.9 = bf16[32,64,128]{2,1,0:T(8,128)(2,1)S(1)} collective-permute-done((bf16[32,64,128]{2,1,0:T(8,128)(2,1)S(1)}, bf16[32,64,128]{2,1,0:T(8,128)(2,1)S(1)}, u32[]{:S(2)}, u32[]{:S(2)}) %collective-permute-start.9) | collective-permute-done | bytes 524320 | tf_op jit(solution)/shard_map/ppermute | solution.py:714
  39.8 2.3 %collective-permute-start.13 = (bf16[32,64,128]{2,1,0:T(8,128)(2,1)S(1)}, bf16[32,64,128]{2,1,0:T(8,128)(2,1)S(1)}, u32[]{:S(2)}, u32[]{:S(2)}) collective-permute-start(bf16[32,64,128]{2,1,0:T(8,128)(2,1)S(1)} %add_convert_fusion.refs_7_), channel_id=1, source_target_pairs={{0,2},{1,3},{2,0},{3,1},{4,6},{5,7},{6,4},{7,5},{8,10},{9,11},{10,... | collective-permute-start | bytes 1572872 | tf_op jit(solution)/shard_map/ppermute | solution.py:718
  42.1 1.9 %collective-permute-done.8 = bf16[4,128,128]{2,1,0:T(8,128)(2,1)S(1)} collective-permute-done((bf16[4,128,128]{2,1,0:T(8,128)(2,1)S(1)}, bf16[4,128,128]{2,1,0:T(8,128)(2,1)S(1)}, u32[]{:S(2)}, u32[]{:S(2)}) %collective-permute-start.8) | collective-permute-done | bytes 131104 | tf_op jit(solution)/shard_map/ppermute | solution.py:722
  44.6 0.5 bitcast_add_fusion
  45.1 3.2 %collective-permute-done.10 = bf16[2,128,128]{2,1,0:T(8,128)(2,1)S(1)} collective-permute-done((bf16[2,128,128]{2,1,0:T(8,128)(2,1)S(1)}, bf16[2,128,128]{2,1,0:T(8,128)(2,1)S(1)}, u32[]{:S(2)}, u32[]{:S(2)}) %collective-permute-start.10) | collective-permute-done | bytes 65568 | tf_op jit(solution)/shard_map/ppermute | solution.py:722
  48.4 2.3 %collective-permute-start.11 = (bf16[1,128,128]{2,1,0:T(8,128)(2,1)S(1)}, bf16[1,128,128]{2,1,0:T(8,128)(2,1)S(1)}, u32[]{:S(2)}, u32[]{:S(2)}) collective-permute-start(bf16[1,128,128]{2,1,0:T(8,128)(2,1)S(1)} %slice.41), channel_id=1, source_target_pairs={{0,16},{4,20},{8,24},{12,28},{16,0},{20,4},{24,8},{28,12},{1,17},{... | collective-permute-start | bytes 98312 | tf_op jit(solution)/shard_map/ppermute | solution.py:722
  50.7 2.5 %collective-permute-done.11 = bf16[1,128,128]{2,1,0:T(8,128)(2,1)S(1)} collective-permute-done((bf16[1,128,128]{2,1,0:T(8,128)(2,1)S(1)}, bf16[1,128,128]{2,1,0:T(8,128)(2,1)S(1)}, u32[]{:S(2)}, u32[]{:S(2)}) %collective-permute-start.11) | collective-permute-done | bytes 32800 | tf_op jit(solution)/shard_map/ppermute | solution.py:722
  53.3 1.1 %collective-permute-done.13.refs_6_ = bf16[32,64,128]{2,1,0:T(8,128)(2,1)S(1)} collective-permute-done((bf16[32,64,128]{2,1,0:T(8,128)(2,1)S(1)}, bf16[32,64,128]{2,1,0:T(8,128)(2,1)S(1)}, u32[]{:S(2)}, u32[]{:S(2)}) %collective-permute-start.13) | collective-permute-done | bytes 524320 | tf_op jit(solution)/shard_map/ppermute | solution.py:718
  54.3 1.5 %finish.1 = (bf16[128,128]{1,0:T(8,128)(2,1)}, bf16[32,64,128]{2,1,0:T(8,128)(2,1)}) custom-call(bf16[128,128]{1,0:T(8,128)(2,1)S(1)} %bitcast.15, bf16[32,64,128]{2,1,0:T(8,128)(2,1)S(1)} %get-tuple-element.59.refs_1_, f32[128,128]{1,0:T(8,128)S(1)} %slice_bitcast_fusion.refs_2_, bf16[128,128]{1,0:T(8,128)(2,1)S(1)} %bitcast.16, ...), custom_call_target="tpu_custom_call" | custom-call | tf_op jit(solution)/shard_map/finish/pallas_call | solution.py:658
  (30 shorter events, 2.4 us)
Async XLA Ops:
  1.5 5.0 %collective-permute-start = (bf16[1,144,128]{2,1,0:T(8,128)(2,1)S(1)}, bf16[1,144,128]{2,1,0:T(8,128)(2,1)S(1)}, u32[]{:S(2)}, u32[]{:S(2)}) collective-permute-start(bf16[1,144,128]{2,1,0:T(8,128)(2,1)S(1)} %bitcast.12), channel_id=1, source_target_pairs={{0,4},{4,0},{8,12},{12,8},{16,20},{20,16},{24,28},{28,24},{1,5},{5... | collective-permute-start | bytes 110600 | tf_op jit(solution)/shard_map/ppermute | solution.py:683
  6.5 7.8 %collective-permute-start.1 = (bf16[2,144,128]{2,1,0:T(8,128)(2,1)S(1)}, bf16[2,144,128]{2,1,0:T(8,128)(2,1)S(1)}, u32[]{:S(2)}, u32[]{:S(2)}) collective-permute-start(bf16[2,144,128]{2,1,0:T(8,128)(2,1)S(1)} %pad_maximum_fusion.refs_0_), channel_id=1, source_target_pairs={{0,8},{4,12},{8,0},{12,4},{16,24},{20,28},{24,16},{28,20},{1,9},{5... | collective-permute-start | bytes 221192 | tf_op jit(solution)/shard_map/ppermute | solution.py:686
  8.6 6.8 %collective-permute-start.2 = (bf16[2,144,128]{2,1,0:T(8,128)(2,1)S(1)}, bf16[2,144,128]{2,1,0:T(8,128)(2,1)S(1)}, u32[]{:S(2)}, u32[]{:S(2)}) collective-permute-start(bf16[2,144,128]{2,1,0:T(8,128)(2,1)S(1)} %pad_maximum_fusion.refs_0_), channel_id=1, source_target_pairs={{0,16},{4,20},{8,24},{12,28},{16,0},{20,4},{24,8},{28,12},{1,17},{... | collective-permute-start | bytes 221192 | tf_op jit(solution)/shard_map/ppermute | solution.py:686
  11.2 6.2 %collective-permute-start.3 = (bf16[2,144,128]{2,1,0:T(8,128)(2,1)S(1)}, bf16[2,144,128]{2,1,0:T(8,128)(2,1)S(1)}, u32[]{:S(2)}, u32[]{:S(2)}) collective-permute-start(bf16[2,144,128]{2,1,0:T(8,128)(2,1)S(1)} %pad_maximum_fusion.refs_0_), channel_id=1, source_target_pairs={{0,24},{4,28},{8,16},{12,20},{16,8},{20,12},{24,0},{28,4},{1,25},{... | collective-permute-start | bytes 221192 | tf_op jit(solution)/shard_map/ppermute | solution.py:686
  22.7 4.7 %collective-permute-start.4 = (f32[8,128]{1,0:T(8,128)S(1)}, f32[8,128]{1,0:T(8,128)S(1)}, u32[]{:S(2)}, u32[]{:S(2)}) collective-permute-start(f32[8,128]{1,0:T(8,128)S(1)} %get-tuple-element.36), channel_id=1, source_target_pairs={{0,4},{4,0},{8,12},{12,8},{16,20},{20,16},{24,28},{28,24},{1,5},{5... | collective-permute-start | bytes 12296 | tf_op jit(solution)/shard_map/ppermute | solution.py:695
  27.5 4.5 %collective-permute-start.5 = (f32[8,128]{1,0:T(8,128)S(1)}, f32[8,128]{1,0:T(8,128)S(1)}, u32[]{:S(2)}, u32[]{:S(2)}) collective-permute-start(f32[8,128]{1,0:T(8,128)S(1)} %add.27.refs_0_), channel_id=1, source_target_pairs={{0,8},{4,12},{8,0},{12,4},{16,24},{20,28},{24,16},{28,20},{1,9},{5... | collective-permute-start | bytes 12296 | tf_op jit(solution)/shard_map/ppermute | solution.py:695
  27.5 4.6 %collective-permute-start.6 = (f32[8,128]{1,0:T(8,128)S(1)}, f32[8,128]{1,0:T(8,128)S(1)}, u32[]{:S(2)}, u32[]{:S(2)}) collective-permute-start(f32[8,128]{1,0:T(8,128)S(1)} %add.27.refs_0_), channel_id=1, source_target_pairs={{0,16},{4,20},{8,24},{12,28},{16,0},{20,4},{24,8},{28,12},{1,17},{... | collective-permute-start | bytes 12296 | tf_op jit(solution)/shard_map/ppermute | solution.py:695
  28.2 5.4 %collective-permute-start.7 = (f32[8,128]{1,0:T(8,128)S(1)}, f32[8,128]{1,0:T(8,128)S(1)}, u32[]{:S(2)}, u32[]{:S(2)}) collective-permute-start(f32[8,128]{1,0:T(8,128)S(1)} %add.27.refs_0_), channel_id=1, source_target_pairs={{0,24},{4,28},{8,16},{12,20},{16,8},{20,12},{24,0},{28,4},{1,25},{... | collective-permute-start | bytes 12296 | tf_op jit(solution)/shard_map/ppermute | solution.py:695
  33.8 3.9 %copy-start.1 = (f32[4,32]{1,0:T(4,128)S(1)}, f32[4,32]{1,0:T(4,128)}, u32[]{:S(2)}) copy-start(f32[4,32]{1,0:T(4,128)} %refs_2_.1) | copy-start | bytes 1540
  37.6 16.7 %copy-start = (bf16[4,32,128]{2,1,0:T(8,128)(2,1)S(1)}, bf16[4,32,128]{2,1,0:T(8,128)(2,1)}, u32[]{:S(2)}) copy-start(bf16[4,32,128]{2,1,0:T(8,128)(2,1)} %param.4) | copy-start | bytes 98308
  37.6 2.0 %collective-permute-start.9 = (bf16[32,64,128]{2,1,0:T(8,128)(2,1)S(1)}, bf16[32,64,128]{2,1,0:T(8,128)(2,1)S(1)}, u32[]{:S(2)}, u32[]{:S(2)}) collective-permute-start(bf16[32,64,128]{2,1,0:T(8,128)(2,1)S(1)} %get-tuple-element.54), channel_id=1, source_target_pairs={{0,1},{1,0},{2,3},{3,2},{4,5},{5,4},{6,7},{7,6},{8,9},{9,8},{10,11... | collective-permute-start | bytes 1572872 | tf_op jit(solution)/shard_map/ppermute | solution.py:714
  38.0 6.0 %collective-permute-start.8 = (bf16[4,128,128]{2,1,0:T(8,128)(2,1)S(1)}, bf16[4,128,128]{2,1,0:T(8,128)(2,1)S(1)}, u32[]{:S(2)}, u32[]{:S(2)}) collective-permute-start(bf16[4,128,128]{2,1,0:T(8,128)(2,1)S(1)} %get-tuple-element.52), channel_id=1, source_target_pairs={{0,4},{4,0},{8,12},{12,8},{16,20},{20,16},{24,28},{28,24},{1,5},{5... | collective-permute-start | bytes 393224 | tf_op jit(solution)/shard_map/ppermute | solution.py:722
  38.6 12.1 %collective-permute-start.12 = (bf16[32,64,128]{2,1,0:T(8,128)(2,1)S(1)}, bf16[32,64,128]{2,1,0:T(8,128)(2,1)S(1)}, u32[]{:S(2)}, u32[]{:S(2)}) collective-permute-start(bf16[32,64,128]{2,1,0:T(8,128)(2,1)S(1)} %get-tuple-element.63), channel_id=1, source_target_pairs={{0,1},{1,0},{2,3},{3,2},{4,5},{5,4},{6,7},{7,6},{8,9},{9,8},{10,11... | collective-permute-start | bytes 1572872 | tf_op jit(solution)/shard_map/ppermute | solution.py:719
  39.8 14.5 %collective-permute-start.13 = (bf16[32,64,128]{2,1,0:T(8,128)(2,1)S(1)}, bf16[32,64,128]{2,1,0:T(8,128)(2,1)S(1)}, u32[]{:S(2)}, u32[]{:S(2)}) collective-permute-start(bf16[32,64,128]{2,1,0:T(8,128)(2,1)S(1)} %add_convert_fusion.refs_7_), channel_id=1, source_target_pairs={{0,2},{1,3},{2,0},{3,1},{4,6},{5,7},{6,4},{7,5},{8,10},{9,11},{10,... | collective-permute-start | bytes 1572872 | tf_op jit(solution)/shard_map/ppermute | solution.py:718
  44.0 4.3 %collective-permute-start.10 = (bf16[2,128,128]{2,1,0:T(8,128)(2,1)S(1)}, bf16[2,128,128]{2,1,0:T(8,128)(2,1)S(1)}, u32[]{:S(2)}, u32[]{:S(2)}) collective-permute-start(bf16[2,128,128]{2,1,0:T(8,128)(2,1)S(1)} %slice.40), channel_id=1, source_target_pairs={{0,8},{4,12},{8,0},{12,4},{16,24},{20,28},{24,16},{28,20},{1,9},{5... | collective-permute-start | bytes 196616 | tf_op jit(solution)/shard_map/ppermute | solution.py:722
  48.4 4.9 %collective-permute-start.11 = (bf16[1,128,128]{2,1,0:T(8,128)(2,1)S(1)}, bf16[1,128,128]{2,1,0:T(8,128)(2,1)S(1)}, u32[]{:S(2)}, u32[]{:S(2)}) collective-permute-start(bf16[1,128,128]{2,1,0:T(8,128)(2,1)S(1)} %slice.41), channel_id=1, source_target_pairs={{0,16},{4,20},{8,24},{12,28},{16,0},{20,4},{24,8},{28,12},{1,17},{... | collective-permute-start | bytes 98312 | tf_op jit(solution)/shard_map/ppermute | solution.py:722

commit v8 on v7

--- a/solution.py
+++ b/solution.py
@@ -15,7 +15,7 @@
 
 VMEM = pl.BlockSpec(memory_space=pltpu.VMEM)
 HBM = pl.BlockSpec(memory_space=pltpu.HBM)
-chunk_unroll = 8
+chunk_unroll = 16
 chunk_tail = 4
 passage_unroll = 8
 meta_rows = 8
@@ -152,7 +152,7 @@
 
 def slot_total(pass_count, pairs):
     worst = (pairs + pass_count * (chunk_pairs - 1)) // chunk_pairs
-    return -(-worst // chunk_unroll) * chunk_unroll
+    return -(-worst // chunk_tail) * chunk_tail
 
 
 def list_ids(list_smem, row, p):

time: 55.9 us -> 55.9 us (level)
  waiting for transfers between devices: 16.1 us -> 19.8 us
  starting transfers between devices: 18.7 us -> 15.5 us
    ppermute x3, waiting for transfers between devices: 7.62 us -> 10.6 us  [shards(): send = lax.ppermute(send, 'psg', [(i, i ^ bit) for i in range(sources)])]
    ppermute x3, starting transfers between devices: 3.44 us -> 1.75 us  [shards(): send = lax.ppermute(send, 'psg', [(i, i ^ bit) for i in range(sources)])]
    ppermute x1, starting transfers between devices: 2.32 us -> 0.99 us  [shards(): far = lax.ppermute(far, 'qry', away)]
    ppermute x4, waiting for transfers between devices: 1.71 us -> 2.91 us  [swap(): return lax.ppermute(values, 'psg', [(i, i ^ bit) for i in range(sources)])]
where the time goes in v8:
time: 55.9 us; the launch traced here: 56 us
  waiting for transfers between devices  19.8 us (35%)
  Pallas kernels  18.7 us (33%)
  starting transfers between devices  15.5 us (28%)
  other arithmetic  1.07 us (2%)
  between operations  0.83 us (1%)
    ppermute x3, waiting for transfers between devices, shards(): send = lax.ppermute(send, 'psg', [(i, i ^ bit) for i in range(sources)])  10.6 us
    pallas_call x1, Pallas kernels, forward(): pl.pallas_call(lambda *refs: forward_kernel(cand_count, query_count, quer...  5.02 us
    ppermute x3, starting transfers between devices, shards(): lax.ppermute(received, 'psg', [(i, i ^ d) for i in range(sources)])  4.73 us
    ppermute x4, starting transfers between devices, swap(): return lax.ppermute(values, 'psg', [(i, i ^ bit) for i in range(sources)])  4.73 us
    pallas_call x1, Pallas kernels, attend(): pl.pallas_call(lambda *refs: attend_kernel(query_tokens, *refs), in_specs...  4.26 us
    pallas_call x1, Pallas kernels, passage_backward(): pl.pallas_call(lambda *refs: passage_kernel(query_tokens, *refs), in_spec...  3.79 us
    pallas_call x1, Pallas kernels, prepare_passages(): pl.pallas_call(lambda *refs: passages_kernel(slices, *refs), in_specs=[HB...  3.09 us
    ppermute x3, waiting for transfers between devices, shards(): lax.ppermute(received, 'psg', [(i, i ^ d) for i in range(sources)])  3.04 us
  transfers between devices with their start and end apart: 14, of which 10 were waited for; matrix products, arithmetic and copies ran while one was open for 2% of the time, Pallas kernels for 13%

profile of v8, /device:TPU:0, one launch (start us, length us, event | category | flops | bytes accessed | tf_op | source)
XLA Modules:
  0.0 56.0 jit_solution(3568692299130018242)
XLA Ops:
  0.6 0.9 %pack.1 = bf16[144,128]{1,0:T(8,128)(2,1)S(1)} custom-call(bf16[128,128]{1,0:T(8,128)(2,1)} %bitcast.14, s32[4,32]{1,0:T(4,128)} %refs_1_.1, f32[4,32]{1,0:T(4,128)} %refs_2_.1), custom_call_target="tpu_custom_call" | custom-call | tf_op jit(solution)/shard_map/pack/pallas_call | solution.py:71
  1.5 3.0 %collective-permute-start = (bf16[1,144,128]{2,1,0:T(8,128)(2,1)S(1)}, bf16[1,144,128]{2,1,0:T(8,128)(2,1)S(1)}, u32[]{:S(2)}, u32[]{:S(2)}) collective-permute-start(bf16[1,144,128]{2,1,0:T(8,128)(2,1)S(1)} %bitcast.12), channel_id=1, source_target_pairs={{0,4},{4,0},{8,12},{12,8},{16,20},{20,16},{24,28},{28,24},{1,5},{5... | collective-permute-start | bytes 110600 | tf_op jit(solution)/shard_map/ppermute | solution.py:683
  4.5 1.9 %collective-permute-done = bf16[1,144,128]{2,1,0:T(8,128)(2,1)S(1)} collective-permute-done((bf16[1,144,128]{2,1,0:T(8,128)(2,1)S(1)}, bf16[1,144,128]{2,1,0:T(8,128)(2,1)S(1)}, u32[]{:S(2)}, u32[]{:S(2)}) %collective-permute-start) | collective-permute-done | bytes 36896 | tf_op jit(solution)/shard_map/ppermute | solution.py:683
  6.5 2.1 %collective-permute-start.1 = (bf16[2,144,128]{2,1,0:T(8,128)(2,1)S(1)}, bf16[2,144,128]{2,1,0:T(8,128)(2,1)S(1)}, u32[]{:S(2)}, u32[]{:S(2)}) collective-permute-start(bf16[2,144,128]{2,1,0:T(8,128)(2,1)S(1)} %pad_maximum_fusion.refs_0_), channel_id=1, source_target_pairs={{0,8},{4,12},{8,0},{12,4},{16,24},{20,28},{24,16},{28,20},{1,9},{5... | collective-permute-start | bytes 221192 | tf_op jit(solution)/shard_map/ppermute | solution.py:686
  8.6 2.6 %collective-permute-start.2 = (bf16[2,144,128]{2,1,0:T(8,128)(2,1)S(1)}, bf16[2,144,128]{2,1,0:T(8,128)(2,1)S(1)}, u32[]{:S(2)}, u32[]{:S(2)}) collective-permute-start(bf16[2,144,128]{2,1,0:T(8,128)(2,1)S(1)} %pad_maximum_fusion.refs_0_), channel_id=1, source_target_pairs={{0,16},{4,20},{8,24},{12,28},{16,0},{20,4},{24,8},{28,12},{1,17},{... | collective-permute-start | bytes 221192 | tf_op jit(solution)/shard_map/ppermute | solution.py:686
  11.2 3.1 %prepare_passages.1 = (bf16[32,256,128]{2,1,0:T(8,128)(2,1)S(1)}, bf16[32,128,256]{2,1,0:T(8,128)(2,1)S(1)}, bf16[32,64,128]{2,1,0:T(8,128)(2,1)S(1)}) custom-call(bf16[32,256,128]{2,1,0:T(8,128)(2,1)} %refs_0_.1), custom_call_target="tpu_custom_call" | custom-call | flops 16777216 | bytes 6291456 | tf_op jit(solution)/shard_map/prepare_passages/pallas_call | solution.py:129
  14.3 1.1 %collective-permute-done.2.refs_2_ = bf16[2,144,128]{2,1,0:T(8,128)(2,1)S(1)} collective-permute-done((bf16[2,144,128]{2,1,0:T(8,128)(2,1)S(1)}, bf16[2,144,128]{2,1,0:T(8,128)(2,1)S(1)}, u32[]{:S(2)}, u32[]{:S(2)}) %collective-permute-start.2) | collective-permute-done | bytes 73760 | tf_op jit(solution)/shard_map/ppermute | solution.py:686
  15.5 1.9 %collective-permute-done.3.refs_3_ = bf16[2,144,128]{2,1,0:T(8,128)(2,1)S(1)} collective-permute-done((bf16[2,144,128]{2,1,0:T(8,128)(2,1)S(1)}, bf16[2,144,128]{2,1,0:T(8,128)(2,1)S(1)}, u32[]{:S(2)}, u32[]{:S(2)}) %collective-permute-start.3) | collective-permute-done | bytes 73760 | tf_op jit(solution)/shard_map/ppermute | solution.py:686
  17.4 5.0 %forward.1 = (bf16[68,256,256]{2,1,0:T(8,128)(2,1)S(1)}, bf16[1056,128]{1,0:T(8,128)(2,1)S(1)}, f32[32,128]{1,0:T(8,128)S(1)}, f32[32,128]{1,0:T(8,128)S(1)}, f3...) custom-call(bf16[2,144,128]{2,1,0:T(8,128)(2,1)S(1)} %pad_maximum_fusion.refs_0_, ...), custom_call_target="tpu_custom_call" | custom-call | flops 1140850688 | bytes 12582912 | tf_op jit(solution)/shard_map/forward/pallas_call | solution.py:362
  22.7 4.3 %attend.1 = (f32[1056,128]{1,0:T(8,128)S(1)}, f32[1056,128]{1,0:T(8,128)S(1)}) custom-call(bf16[32,128,256]{2,1,0:T(8,128)(2,1)S(1)} %get-tuple-element.37.refs_0_, bf16[68,256,256]{2,1,0:T(8,128)(2,1)S(1)} %get-tuple-element.38.refs_1_.refs_4_, s32[24,128]{1,0:T(8,128)S(1)} %get-tuple-element.39.refs_2_.refs_0_, ...), custom_call_target="tpu_custom_call" | custom-call | flops 1140850688 | bytes 12582912 | tf_op jit(solution)/shard_map/attend/pallas_call | solution.py:460
  27.1 1.9 %collective-permute-start.6 = (f32[8,128]{1,0:T(8,128)S(1)}, f32[8,128]{1,0:T(8,128)S(1)}, u32[]{:S(2)}, u32[]{:S(2)}) collective-permute-start(f32[8,128]{1,0:T(8,128)S(1)} %add.27.refs_0_), channel_id=1, source_target_pairs={{0,16},{4,20},{8,24},{12,28},{16,0},{20,4},{24,8},{28,12},{1,17},{... | collective-permute-start | bytes 12296 | tf_op jit(solution)/shard_map/ppermute | solution.py:695
  28.9 2.5 %collective-permute-start.7 = (f32[8,128]{1,0:T(8,128)S(1)}, f32[8,128]{1,0:T(8,128)S(1)}, u32[]{:S(2)}, u32[]{:S(2)}) collective-permute-start(f32[8,128]{1,0:T(8,128)S(1)} %add.27.refs_0_), channel_id=1, source_target_pairs={{0,24},{4,28},{8,16},{12,20},{16,8},{20,12},{24,0},{28,4},{1,25},{... | collective-permute-start | bytes 12296 | tf_op jit(solution)/shard_map/ppermute | solution.py:695
  31.6 2.7 %collective-permute-done.7.refs_3_ = f32[8,128]{1,0:T(8,128)S(1)} collective-permute-done((f32[8,128]{1,0:T(8,128)S(1)}, f32[8,128]{1,0:T(8,128)S(1)}, u32[]{:S(2)}, u32[]{:S(2)}) %collective-permute-start.7) | collective-permute-done | bytes 4128 | tf_op jit(solution)/shard_map/ppermute | solution.py:695
  34.5 3.8 %passage_backward.1 = (bf16[32,64,128]{2,1,0:T(8,128)(2,1)S(1)}, bf16[32,64,128]{2,1,0:T(8,128)(2,1)S(1)}, bf16[32,64,128]{2,1,0:T(8,128)(2,1)S(1)}, bf16[32,64,128]{2,1,0:T(8,128)(2,1)S(1)}) custom-call(s32[24,128]{1,0:T(8,128)S(1)} %get-tuple-element.39.refs_2_.refs_0_, f32[32,128]{1,0:T(8,128)S(1)} %get-tuple-element.49.refs_1_, ...), custom_call_target="tpu_custom_call" | custom-call | flops 1073741824 | bytes 6291456 | tf_op jit(solution)/shard_map/passage_backward/pallas_call | solution.py:631
  38.7 0.6 %collective-permute-start.8 = (bf16[4,128,128]{2,1,0:T(8,128)(2,1)S(1)}, bf16[4,128,128]{2,1,0:T(8,128)(2,1)S(1)}, u32[]{:S(2)}, u32[]{:S(2)}) collective-permute-start(bf16[4,128,128]{2,1,0:T(8,128)(2,1)S(1)} %get-tuple-element.52), channel_id=1, source_target_pairs={{0,4},{4,0},{8,12},{12,8},{16,20},{20,16},{24,28},{28,24},{1,5},{5... | collective-permute-start | bytes 393224 | tf_op jit(solution)/shard_map/ppermute | solution.py:722
  39.5 0.8 %collective-permute-done.9 = bf16[32,64,128]{2,1,0:T(8,128)(2,1)S(1)} collective-permute-done((bf16[32,64,128]{2,1,0:T(8,128)(2,1)S(1)}, bf16[32,64,128]{2,1,0:T(8,128)(2,1)S(1)}, u32[]{:S(2)}, u32[]{:S(2)}) %collective-permute-start.9) | collective-permute-done | bytes 524320 | tf_op jit(solution)/shard_map/ppermute | solution.py:714
  40.5 1.0 %collective-permute-start.13 = (bf16[32,64,128]{2,1,0:T(8,128)(2,1)S(1)}, bf16[32,64,128]{2,1,0:T(8,128)(2,1)S(1)}, u32[]{:S(2)}, u32[]{:S(2)}) collective-permute-start(bf16[32,64,128]{2,1,0:T(8,128)(2,1)S(1)} %add_convert_fusion.refs_7_), channel_id=1, source_target_pairs={{0,2},{1,3},{2,0},{3,1},{4,6},{5,7},{6,4},{7,5},{8,10},{9,11},{10,... | collective-permute-start | bytes 1572872 | tf_op jit(solution)/shard_map/ppermute | solution.py:718
  41.5 3.2 %collective-permute-done.8 = bf16[4,128,128]{2,1,0:T(8,128)(2,1)S(1)} collective-permute-done((bf16[4,128,128]{2,1,0:T(8,128)(2,1)S(1)}, bf16[4,128,128]{2,1,0:T(8,128)(2,1)S(1)}, u32[]{:S(2)}, u32[]{:S(2)}) %collective-permute-start.8) | collective-permute-done | bytes 131104 | tf_op jit(solution)/shard_map/ppermute | solution.py:722
  44.9 0.5 bitcast_add_fusion
  45.4 3.6 %collective-permute-done.10 = bf16[2,128,128]{2,1,0:T(8,128)(2,1)S(1)} collective-permute-done((bf16[2,128,128]{2,1,0:T(8,128)(2,1)S(1)}, bf16[2,128,128]{2,1,0:T(8,128)(2,1)S(1)}, u32[]{:S(2)}, u32[]{:S(2)}) %collective-permute-start.10) | collective-permute-done | bytes 65568 | tf_op jit(solution)/shard_map/ppermute | solution.py:722
  49.1 1.1 %collective-permute-start.11 = (bf16[1,128,128]{2,1,0:T(8,128)(2,1)S(1)}, bf16[1,128,128]{2,1,0:T(8,128)(2,1)S(1)}, u32[]{:S(2)}, u32[]{:S(2)}) collective-permute-start(bf16[1,128,128]{2,1,0:T(8,128)(2,1)S(1)} %slice.41), channel_id=1, source_target_pairs={{0,16},{4,20},{8,24},{12,28},{16,0},{20,4},{24,8},{28,12},{1,17},{... | collective-permute-start | bytes 98312 | tf_op jit(solution)/shard_map/ppermute | solution.py:722
  50.2 3.8 %collective-permute-done.11 = bf16[1,128,128]{2,1,0:T(8,128)(2,1)S(1)} collective-permute-done((bf16[1,128,128]{2,1,0:T(8,128)(2,1)S(1)}, bf16[1,128,128]{2,1,0:T(8,128)(2,1)S(1)}, u32[]{:S(2)}, u32[]{:S(2)}) %collective-permute-start.11) | collective-permute-done | bytes 32800 | tf_op jit(solution)/shard_map/ppermute | solution.py:722
  54.0 0.5 collective-permute-done.13.refs_6_
  54.5 1.5 %finish.1 = (bf16[128,128]{1,0:T(8,128)(2,1)}, bf16[32,64,128]{2,1,0:T(8,128)(2,1)}) custom-call(bf16[128,128]{1,0:T(8,128)(2,1)S(1)} %bitcast.15, bf16[32,64,128]{2,1,0:T(8,128)(2,1)S(1)} %get-tuple-element.59.refs_1_, f32[128,128]{1,0:T(8,128)S(1)} %slice_bitcast_fusion.refs_2_, bf16[128,128]{1,0:T(8,128)(2,1)S(1)} %bitcast.16, ...), custom_call_target="tpu_custom_call" | custom-call | tf_op jit(solution)/shard_map/finish/pallas_call | solution.py:658
  (30 shorter events, 1.7 us)
Async XLA Ops:
  1.5 5.0 %collective-permute-start = (bf16[1,144,128]{2,1,0:T(8,128)(2,1)S(1)}, bf16[1,144,128]{2,1,0:T(8,128)(2,1)S(1)}, u32[]{:S(2)}, u32[]{:S(2)}) collective-permute-start(bf16[1,144,128]{2,1,0:T(8,128)(2,1)S(1)} %bitcast.12), channel_id=1, source_target_pairs={{0,4},{4,0},{8,12},{12,8},{16,20},{20,16},{24,28},{28,24},{1,5},{5... | collective-permute-start | bytes 110600 | tf_op jit(solution)/shard_map/ppermute | solution.py:683
  6.5 7.8 %collective-permute-start.1 = (bf16[2,144,128]{2,1,0:T(8,128)(2,1)S(1)}, bf16[2,144,128]{2,1,0:T(8,128)(2,1)S(1)}, u32[]{:S(2)}, u32[]{:S(2)}) collective-permute-start(bf16[2,144,128]{2,1,0:T(8,128)(2,1)S(1)} %pad_maximum_fusion.refs_0_), channel_id=1, source_target_pairs={{0,8},{4,12},{8,0},{12,4},{16,24},{20,28},{24,16},{28,20},{1,9},{5... | collective-permute-start | bytes 221192 | tf_op jit(solution)/shard_map/ppermute | solution.py:686
  8.6 6.8 %collective-permute-start.2 = (bf16[2,144,128]{2,1,0:T(8,128)(2,1)S(1)}, bf16[2,144,128]{2,1,0:T(8,128)(2,1)S(1)}, u32[]{:S(2)}, u32[]{:S(2)}) collective-permute-start(bf16[2,144,128]{2,1,0:T(8,128)(2,1)S(1)} %pad_maximum_fusion.refs_0_), channel_id=1, source_target_pairs={{0,16},{4,20},{8,24},{12,28},{16,0},{20,4},{24,8},{28,12},{1,17},{... | collective-permute-start | bytes 221192 | tf_op jit(solution)/shard_map/ppermute | solution.py:686
  11.2 6.2 %collective-permute-start.3 = (bf16[2,144,128]{2,1,0:T(8,128)(2,1)S(1)}, bf16[2,144,128]{2,1,0:T(8,128)(2,1)S(1)}, u32[]{:S(2)}, u32[]{:S(2)}) collective-permute-start(bf16[2,144,128]{2,1,0:T(8,128)(2,1)S(1)} %pad_maximum_fusion.refs_0_), channel_id=1, source_target_pairs={{0,24},{4,28},{8,16},{12,20},{16,8},{20,12},{24,0},{28,4},{1,25},{... | collective-permute-start | bytes 221192 | tf_op jit(solution)/shard_map/ppermute | solution.py:686
  22.4 4.6 %collective-permute-start.4 = (f32[8,128]{1,0:T(8,128)S(1)}, f32[8,128]{1,0:T(8,128)S(1)}, u32[]{:S(2)}, u32[]{:S(2)}) collective-permute-start(f32[8,128]{1,0:T(8,128)S(1)} %get-tuple-element.36), channel_id=1, source_target_pairs={{0,4},{4,0},{8,12},{12,8},{16,20},{20,16},{24,28},{28,24},{1,5},{5... | collective-permute-start | bytes 12296 | tf_op jit(solution)/shard_map/ppermute | solution.py:695
  27.0 4.5 %collective-permute-start.5 = (f32[8,128]{1,0:T(8,128)S(1)}, f32[8,128]{1,0:T(8,128)S(1)}, u32[]{:S(2)}, u32[]{:S(2)}) collective-permute-start(f32[8,128]{1,0:T(8,128)S(1)} %add.27.refs_0_), channel_id=1, source_target_pairs={{0,8},{4,12},{8,0},{12,4},{16,24},{20,28},{24,16},{28,20},{1,9},{5... | collective-permute-start | bytes 12296 | tf_op jit(solution)/shard_map/ppermute | solution.py:695
  27.1 4.6 %collective-permute-start.6 = (f32[8,128]{1,0:T(8,128)S(1)}, f32[8,128]{1,0:T(8,128)S(1)}, u32[]{:S(2)}, u32[]{:S(2)}) collective-permute-start(f32[8,128]{1,0:T(8,128)S(1)} %add.27.refs_0_), channel_id=1, source_target_pairs={{0,16},{4,20},{8,24},{12,28},{16,0},{20,4},{24,8},{28,12},{1,17},{... | collective-permute-start | bytes 12296 | tf_op jit(solution)/shard_map/ppermute | solution.py:695
  28.9 5.4 %collective-permute-start.7 = (f32[8,128]{1,0:T(8,128)S(1)}, f32[8,128]{1,0:T(8,128)S(1)}, u32[]{:S(2)}, u32[]{:S(2)}) collective-permute-start(f32[8,128]{1,0:T(8,128)S(1)} %add.27.refs_0_), channel_id=1, source_target_pairs={{0,24},{4,28},{8,16},{12,20},{16,8},{20,12},{24,0},{28,4},{1,25},{... | collective-permute-start | bytes 12296 | tf_op jit(solution)/shard_map/ppermute | solution.py:695
  34.5 3.9 %copy-start.1 = (f32[4,32]{1,0:T(4,128)S(1)}, f32[4,32]{1,0:T(4,128)}, u32[]{:S(2)}) copy-start(f32[4,32]{1,0:T(4,128)} %refs_2_.1) | copy-start | bytes 1540
  38.3 16.2 %copy-start = (bf16[4,32,128]{2,1,0:T(8,128)(2,1)S(1)}, bf16[4,32,128]{2,1,0:T(8,128)(2,1)}, u32[]{:S(2)}) copy-start(bf16[4,32,128]{2,1,0:T(8,128)(2,1)} %param.4) | copy-start | bytes 98308
  38.3 2.0 %collective-permute-start.9 = (bf16[32,64,128]{2,1,0:T(8,128)(2,1)S(1)}, bf16[32,64,128]{2,1,0:T(8,128)(2,1)S(1)}, u32[]{:S(2)}, u32[]{:S(2)}) collective-permute-start(bf16[32,64,128]{2,1,0:T(8,128)(2,1)S(1)} %get-tuple-element.54), channel_id=1, source_target_pairs={{0,1},{1,0},{2,3},{3,2},{4,5},{5,4},{6,7},{7,6},{8,9},{9,8},{10,11... | collective-permute-start | bytes 1572872 | tf_op jit(solution)/shard_map/ppermute | solution.py:714
  38.7 6.0 %collective-permute-start.8 = (bf16[4,128,128]{2,1,0:T(8,128)(2,1)S(1)}, bf16[4,128,128]{2,1,0:T(8,128)(2,1)S(1)}, u32[]{:S(2)}, u32[]{:S(2)}) collective-permute-start(bf16[4,128,128]{2,1,0:T(8,128)(2,1)S(1)} %get-tuple-element.52), channel_id=1, source_target_pairs={{0,4},{4,0},{8,12},{12,8},{16,20},{20,16},{24,28},{28,24},{1,5},{5... | collective-permute-start | bytes 393224 | tf_op jit(solution)/shard_map/ppermute | solution.py:722
  39.3 10.9 %collective-permute-start.12 = (bf16[32,64,128]{2,1,0:T(8,128)(2,1)S(1)}, bf16[32,64,128]{2,1,0:T(8,128)(2,1)S(1)}, u32[]{:S(2)}, u32[]{:S(2)}) collective-permute-start(bf16[32,64,128]{2,1,0:T(8,128)(2,1)S(1)} %get-tuple-element.63), channel_id=1, source_target_pairs={{0,1},{1,0},{2,3},{3,2},{4,5},{5,4},{6,7},{7,6},{8,9},{9,8},{10,11... | collective-permute-start | bytes 1572872 | tf_op jit(solution)/shard_map/ppermute | solution.py:719
  40.5 14.0 %collective-permute-start.13 = (bf16[32,64,128]{2,1,0:T(8,128)(2,1)S(1)}, bf16[32,64,128]{2,1,0:T(8,128)(2,1)S(1)}, u32[]{:S(2)}, u32[]{:S(2)}) collective-permute-start(bf16[32,64,128]{2,1,0:T(8,128)(2,1)S(1)} %add_convert_fusion.refs_7_), channel_id=1, source_target_pairs={{0,2},{1,3},{2,0},{3,1},{4,6},{5,7},{6,4},{7,5},{8,10},{9,11},{10,... | collective-permute-start | bytes 1572872 | tf_op jit(solution)/shard_map/ppermute | solution.py:718
  44.7 4.3 %collective-permute-start.10 = (bf16[2,128,128]{2,1,0:T(8,128)(2,1)S(1)}, bf16[2,128,128]{2,1,0:T(8,128)(2,1)S(1)}, u32[]{:S(2)}, u32[]{:S(2)}) collective-permute-start(bf16[2,128,128]{2,1,0:T(8,128)(2,1)S(1)} %slice.40), channel_id=1, source_target_pairs={{0,8},{4,12},{8,0},{12,4},{16,24},{20,28},{24,16},{28,20},{1,9},{5... | collective-permute-start | bytes 196616 | tf_op jit(solution)/shard_map/ppermute | solution.py:722
  49.1 4.9 %collective-permute-start.11 = (bf16[1,128,128]{2,1,0:T(8,128)(2,1)S(1)}, bf16[1,128,128]{2,1,0:T(8,128)(2,1)S(1)}, u32[]{:S(2)}, u32[]{:S(2)}) collective-permute-start(bf16[1,128,128]{2,1,0:T(8,128)(2,1)S(1)} %slice.41), channel_id=1, source_target_pairs={{0,16},{4,20},{8,24},{12,28},{16,0},{20,4},{24,8},{28,12},{1,17},{... | collective-permute-start | bytes 98312 | tf_op jit(solution)/shard_map/ppermute | solution.py:722

commit v9 on v8

--- a/solution.py
+++ b/solution.py
@@ -644,28 +644,55 @@
     )(ids, grads, qn, inverse, soft)
 
 
-def finish_kernel(query_parts, *refs):
-    raw_query, raw_passage = refs[:2]
-    query_out, passage_out = refs[-2:]
-    queries, passages = refs[2 : 2 + query_parts], refs[2 + query_parts : -3]
-    for raw, parts, out in ((raw_query, queries, query_out), (raw_passage, passages, passage_out)):
-        grad = sum(ref[...].astype(jnp.float32) for ref in parts)
-        out[...] = tangent(raw[...], grad).astype(jnp.bfloat16)
-
-
-def finish(raw_query, raw_passage, query_parts, passage_parts, ready):
-    count = 2 + len(query_parts) + len(passage_parts)
+def add_parts(refs, place=slice(None)):
+    return sum(ref[place].astype(jnp.float32) for ref in refs)
+
+
+def finish_first_kernel(raw_ref, own_ref, core_ref, far_ref, out_ref):
+    place = pl.ds(0, far_ref.shape[0])
+    grad = add_parts((own_ref, core_ref), place) + add_parts((far_ref,))
+    out_ref[...] = tangent(raw_ref[place], grad).astype(jnp.bfloat16)
+
+
+def finish_last_kernel(raw_ref, own_ref, core_ref, far_ref, raw_query, *refs):
+    parts, (query_out, out_ref) = refs[:-4], refs[-2:]
+    query_out[...] = tangent(raw_query[...], add_parts(parts)).astype(jnp.bfloat16)
+    count = far_ref.shape[0]
+    place = pl.ds(count, count)
+    grad = add_parts((own_ref, core_ref), place) + add_parts((far_ref,))
+    out_ref[...] = tangent(raw_ref[place], grad).astype(jnp.bfloat16)
+
+
+def finish_first(raw, own, core, far):
     return pl.pallas_call(
-        lambda *refs: finish_kernel(len(query_parts), *refs),
-        in_specs=[VMEM] * count + [pl.BlockSpec(memory_space=pl.ANY)],
-        out_specs=[VMEM] * 2,
+        finish_first_kernel,
+        grid=(1,),
+        in_specs=[VMEM] * 4,
+        out_specs=pl.BlockSpec(far.shape, lambda i: (0, 0, 0)),
+        out_shape=jax.ShapeDtypeStruct(raw.shape, jnp.bfloat16),
+        compiler_params=params(),
+        name="finish_first",
+    )(raw, own, core, far)
+
+
+def finish_last(raw, own, core, far, raw_query, query_parts, ready, before):
+    count = 5 + len(query_parts)
+    return pl.pallas_call(
+        finish_last_kernel,
+        grid=(1,),
+        in_specs=[VMEM] * count + [pl.BlockSpec(memory_space=pl.ANY)] * 2,
+        out_specs=[
+            pl.BlockSpec(raw_query.shape, lambda i: (0, 0)),
+            pl.BlockSpec(far.shape, lambda i: (1, 0, 0)),
+        ],
         out_shape=[
             jax.ShapeDtypeStruct(raw_query.shape, jnp.bfloat16),
-            jax.ShapeDtypeStruct(raw_passage.shape, jnp.bfloat16),
-        ],
+            jax.ShapeDtypeStruct(raw.shape, jnp.bfloat16),
+        ],
+        input_output_aliases={count + 1: 1},
         compiler_params=params(),
-        name="finish",
-    )(raw_query, raw_passage, *query_parts, *passage_parts, ready)
+        name="finish_last",
+    )(raw, own, core, far, raw_query, *query_parts, ready, before)
 
 
 def shards(queries, passages, candidates, teacher):
@@ -712,10 +739,14 @@
         ids, grads, qn, inverse, soft, pass_count, query_tokens, slices
     )
     cross = lax.ppermute(cross, "qry", near)
-    far = (far.astype(jnp.float32) + cross.astype(jnp.float32)).astype(jnp.bfloat16)
+    half = pass_count // 2
+    far = [
+        (far[part].astype(jnp.float32) + cross[part].astype(jnp.float32)).astype(jnp.bfloat16)
+        for part in (slice(0, half), slice(half, pass_count))
+    ]
     send, own = lax.optimization_barrier((send, own))
-    ready = far
-    far = lax.ppermute(far, "qry", away)
+    ready = far[1]
+    far = [lax.ppermute(piece, "qry", away) for piece in far]
     core = lax.ppermute(core, "qry", near)
     bit = 1
     while bit < sources:
@@ -728,8 +759,16 @@
             half = total.shape[0] // 2
             keep, send = total[:half], total[half:].astype(jnp.bfloat16)
     query_parts = [keep[0], send[0]]
-    grad_queries, grad_passages = finish(
-        queries.reshape(rows, width), own_raw, query_parts, [own, core, far], ready
+    grad_passages = finish_first(own_raw, own, core, far[0])
+    grad_queries, grad_passages = finish_last(
+        own_raw,
+        own,
+        core,
+        far[1],
+        queries.reshape(rows, width),
+        query_parts,
+        ready,
+        grad_passages,
     )
 
     raised = jnp.exp(teacher)

time: 55.9 us -> 56.2 us (level)
  starting transfers between devices: 15.5 us -> 17.7 us
  waiting for transfers between devices: 19.8 us -> 18.2 us
  Pallas kernels: 18.7 us -> 18 us
    ppermute x3, waiting for transfers between devices: 10.6 us -> 8.95 us  [shards(): send = lax.ppermute(send, 'psg', [(i, i ^ bit) for i in range(sources)])]
    ppermute x1 -> x2, starting transfers between devices: 0.99 us -> 2.09 us  [shards(): far = [lax.ppermute(piece, 'qry', away) for piece in far]]
    ppermute x4, starting transfers between devices: 4.73 us -> 5.61 us  [swap(): return lax.ppermute(values, 'psg', [(i, i ^ bit) for i in range(sources)])]
    pallas_call x1, Pallas kernels: 4.26 us -> 3.4 us  [attend(): pl.pallas_call(lambda *refs: attend_kernel(query_tokens, *refs), in_specs...]
    ppermute x1, waiting for transfers between devices: 0.78 us -> 0.01 us  [shards(): cross = lax.ppermute(cross, 'qry', near)]
    ppermute x4, waiting for transfers between devices: 2.91 us -> 3.66 us  [swap(): return lax.ppermute(values, 'psg', [(i, i ^ bit) for i in range(sources)])]
    pallas_call x1 -> x2, Pallas kernels: 1.51 us -> 2.16 us  [the longest x1 1.11 us: finish_last(): pl.pallas_call(finish_last_kernel, grid=(1,), in_specs=[VMEM] * count + [...]
  transfers between devices with their start and end apart: 14 -> 15, of which waited for: 10 -> 10; matrix products, arithmetic and copies ran while one was open for 2% -> 2% of each run, Pallas kernels for 13% -> 14%
where the time goes in v9:
time: 56.2 us; the launch traced here: 55.9 us
  waiting for transfers between devices  18.2 us (32%)
  Pallas kernels  18 us (32%)
  starting transfers between devices  17.7 us (31%)
  other arithmetic  1.07 us (2%)
  between operations  0.81 us (1%)
    ppermute x3, waiting for transfers between devices, shards(): send = lax.ppermute(send, 'psg', [(i, i ^ bit) for i in range(sources)])  8.95 us
    ppermute x4, starting transfers between devices, swap(): return lax.ppermute(values, 'psg', [(i, i ^ bit) for i in range(sources)])  5.61 us
    ppermute x3, starting transfers between devices, shards(): lax.ppermute(received, 'psg', [(i, i ^ d) for i in range(sources)])  4.73 us
    pallas_call x1, Pallas kernels, forward(): pl.pallas_call(lambda *refs: forward_kernel(cand_count, query_count, quer...  4.53 us
    pallas_call x1, Pallas kernels, passage_backward(): pl.pallas_call(lambda *refs: passage_kernel(query_tokens, *refs), in_spec...  3.79 us
    ppermute x4, waiting for transfers between devices, swap(): return lax.ppermute(values, 'psg', [(i, i ^ bit) for i in range(sources)])  3.66 us
    pallas_call x1, Pallas kernels, attend(): pl.pallas_call(lambda *refs: attend_kernel(query_tokens, *refs), in_specs...  3.4 us
    pallas_call x1, Pallas kernels, prepare_passages(): pl.pallas_call(lambda *refs: passages_kernel(slices, *refs), in_specs=[HB...  3.09 us
  transfers between devices with their start and end apart: 15, of which 10 were waited for; matrix products, arithmetic and copies ran while one was open for 2% of the time, Pallas kernels for 14%

profile of v9, /device:TPU:0, one launch (start us, length us, event | category | flops | bytes accessed | tf_op | source)
XLA Modules:
  0.0 55.9 jit_solution(8039773285460524798)
XLA Ops:
  0.6 0.9 %pack.1 = bf16[144,128]{1,0:T(8,128)(2,1)S(1)} custom-call(bf16[128,128]{1,0:T(8,128)(2,1)} %bitcast.14, s32[4,32]{1,0:T(4,128)} %refs_1_.1, f32[4,32]{1,0:T(4,128)} %refs_2_.1), custom_call_target="tpu_custom_call" | custom-call | tf_op jit(solution)/shard_map/pack/pallas_call | solution.py:71
  1.5 3.0 %collective-permute-start = (bf16[1,144,128]{2,1,0:T(8,128)(2,1)S(1)}, bf16[1,144,128]{2,1,0:T(8,128)(2,1)S(1)}, u32[]{:S(2)}, u32[]{:S(2)}) collective-permute-start(bf16[1,144,128]{2,1,0:T(8,128)(2,1)S(1)} %bitcast.12), channel_id=1, source_target_pairs={{0,4},{4,0},{8,12},{12,8},{16,20},{20,16},{24,28},{28,24},{1,5},{5... | collective-permute-start | bytes 110600 | tf_op jit(solution)/shard_map/ppermute | solution.py:710
  4.5 1.9 %collective-permute-done = bf16[1,144,128]{2,1,0:T(8,128)(2,1)S(1)} collective-permute-done((bf16[1,144,128]{2,1,0:T(8,128)(2,1)S(1)}, bf16[1,144,128]{2,1,0:T(8,128)(2,1)S(1)}, u32[]{:S(2)}, u32[]{:S(2)}) %collective-permute-start) | collective-permute-done | bytes 36896 | tf_op jit(solution)/shard_map/ppermute | solution.py:710
  6.5 2.1 %collective-permute-start.1 = (bf16[2,144,128]{2,1,0:T(8,128)(2,1)S(1)}, bf16[2,144,128]{2,1,0:T(8,128)(2,1)S(1)}, u32[]{:S(2)}, u32[]{:S(2)}) collective-permute-start(bf16[2,144,128]{2,1,0:T(8,128)(2,1)S(1)} %pad_maximum_fusion.refs_0_), channel_id=1, source_target_pairs={{0,8},{4,12},{8,0},{12,4},{16,24},{20,28},{24,16},{28,20},{1,9},{5... | collective-permute-start | bytes 221192 | tf_op jit(solution)/shard_map/ppermute | solution.py:713
  8.6 2.6 %collective-permute-start.2 = (bf16[2,144,128]{2,1,0:T(8,128)(2,1)S(1)}, bf16[2,144,128]{2,1,0:T(8,128)(2,1)S(1)}, u32[]{:S(2)}, u32[]{:S(2)}) collective-permute-start(bf16[2,144,128]{2,1,0:T(8,128)(2,1)S(1)} %pad_maximum_fusion.refs_0_), channel_id=1, source_target_pairs={{0,16},{4,20},{8,24},{12,28},{16,0},{20,4},{24,8},{28,12},{1,17},{... | collective-permute-start | bytes 221192 | tf_op jit(solution)/shard_map/ppermute | solution.py:713
  11.2 3.1 %prepare_passages.1 = (bf16[32,256,128]{2,1,0:T(8,128)(2,1)S(1)}, bf16[32,128,256]{2,1,0:T(8,128)(2,1)S(1)}, bf16[32,64,128]{2,1,0:T(8,128)(2,1)S(1)}) custom-call(bf16[32,256,128]{2,1,0:T(8,128)(2,1)} %refs_0_.1), custom_call_target="tpu_custom_call" | custom-call | flops 16777216 | bytes 6291456 | tf_op jit(solution)/shard_map/prepare_passages/pallas_call | solution.py:129
  14.3 1.1 %collective-permute-done.2.refs_2_ = bf16[2,144,128]{2,1,0:T(8,128)(2,1)S(1)} collective-permute-done((bf16[2,144,128]{2,1,0:T(8,128)(2,1)S(1)}, bf16[2,144,128]{2,1,0:T(8,128)(2,1)S(1)}, u32[]{:S(2)}, u32[]{:S(2)}) %collective-permute-start.2) | collective-permute-done | bytes 73760 | tf_op jit(solution)/shard_map/ppermute | solution.py:713
  15.5 1.9 %collective-permute-done.3.refs_3_ = bf16[2,144,128]{2,1,0:T(8,128)(2,1)S(1)} collective-permute-done((bf16[2,144,128]{2,1,0:T(8,128)(2,1)S(1)}, bf16[2,144,128]{2,1,0:T(8,128)(2,1)S(1)}, u32[]{:S(2)}, u32[]{:S(2)}) %collective-permute-start.3) | collective-permute-done | bytes 73760 | tf_op jit(solution)/shard_map/ppermute | solution.py:713
  17.4 4.5 %forward.1 = (bf16[68,256,256]{2,1,0:T(8,128)(2,1)S(1)}, bf16[1056,128]{1,0:T(8,128)(2,1)S(1)}, f32[32,128]{1,0:T(8,128)S(1)}, f32[32,128]{1,0:T(8,128)S(1)}, f3...) custom-call(bf16[2,144,128]{2,1,0:T(8,128)(2,1)S(1)} %pad_maximum_fusion.refs_0_, ...), custom_call_target="tpu_custom_call" | custom-call | flops 1140850688 | bytes 12582912 | tf_op jit(solution)/shard_map/forward/pallas_call | solution.py:362
  21.9 1.2 %collective-permute-start.4 = (f32[8,128]{1,0:T(8,128)S(1)}, f32[8,128]{1,0:T(8,128)S(1)}, u32[]{:S(2)}, u32[]{:S(2)}) collective-permute-start(f32[8,128]{1,0:T(8,128)S(1)} %get-tuple-element.36), channel_id=1, source_target_pairs={{0,4},{4,0},{8,12},{12,8},{16,20},{20,16},{24,28},{28,24},{1,5},{5... | collective-permute-start | bytes 12296 | tf_op jit(solution)/shard_map/ppermute | solution.py:722
  23.1 3.4 %attend.1 = (f32[1056,128]{1,0:T(8,128)S(1)}, f32[1056,128]{1,0:T(8,128)S(1)}) custom-call(bf16[32,128,256]{2,1,0:T(8,128)(2,1)S(1)} %get-tuple-element.37.refs_0_, bf16[68,256,256]{2,1,0:T(8,128)(2,1)S(1)} %get-tuple-element.38.refs_1_.refs_4_, s32[24,128]{1,0:T(8,128)S(1)} %get-tuple-element.39.refs_2_.refs_0_, ...), custom_call_target="tpu_custom_call" | custom-call | flops 1140850688 | bytes 12582912 | tf_op jit(solution)/shard_map/attend/pallas_call | solution.py:460
  26.6 2.6 %collective-permute-start.6 = (f32[8,128]{1,0:T(8,128)S(1)}, f32[8,128]{1,0:T(8,128)S(1)}, u32[]{:S(2)}, u32[]{:S(2)}) collective-permute-start(f32[8,128]{1,0:T(8,128)S(1)} %add.30.refs_0_), channel_id=1, source_target_pairs={{0,16},{4,20},{8,24},{12,28},{16,0},{20,4},{24,8},{28,12},{1,17},{... | collective-permute-start | bytes 12296 | tf_op jit(solution)/shard_map/ppermute | solution.py:722
  29.2 1.8 %collective-permute-start.7 = (f32[8,128]{1,0:T(8,128)S(1)}, f32[8,128]{1,0:T(8,128)S(1)}, u32[]{:S(2)}, u32[]{:S(2)}) collective-permute-start(f32[8,128]{1,0:T(8,128)S(1)} %add.30.refs_0_), channel_id=1, source_target_pairs={{0,24},{4,28},{8,16},{12,20},{16,8},{20,12},{24,0},{28,4},{1,25},{... | collective-permute-start | bytes 12296 | tf_op jit(solution)/shard_map/ppermute | solution.py:722
  31.2 3.5 %collective-permute-done.7.refs_3_ = f32[8,128]{1,0:T(8,128)S(1)} collective-permute-done((f32[8,128]{1,0:T(8,128)S(1)}, f32[8,128]{1,0:T(8,128)S(1)}, u32[]{:S(2)}, u32[]{:S(2)}) %collective-permute-start.7) | collective-permute-done | bytes 4128 | tf_op jit(solution)/shard_map/ppermute | solution.py:722
  34.8 3.8 %passage_backward.1 = (bf16[32,64,128]{2,1,0:T(8,128)(2,1)S(1)}, bf16[32,64,128]{2,1,0:T(8,128)(2,1)S(1)}, bf16[32,64,128]{2,1,0:T(8,128)(2,1)S(1)}, bf16[32,64,128]{2,1,0:T(8,128)(2,1)S(1)}) custom-call(s32[24,128]{1,0:T(8,128)S(1)} %get-tuple-element.39.refs_2_.refs_0_, f32[32,128]{1,0:T(8,128)S(1)} %get-tuple-element.49.refs_1_, ...), custom_call_target="tpu_custom_call" | custom-call | flops 1073741824 | bytes 6291456 | tf_op jit(solution)/shard_map/passage_backward/pallas_call | solution.py:631
  39.0 0.5 collective-permute-start.10
  39.6 1.0 %collective-permute-start.8 = (bf16[4,128,128]{2,1,0:T(8,128)(2,1)S(1)}, bf16[4,128,128]{2,1,0:T(8,128)(2,1)S(1)}, u32[]{:S(2)}, u32[]{:S(2)}) collective-permute-start(bf16[4,128,128]{2,1,0:T(8,128)(2,1)S(1)} %get-tuple-element.52), channel_id=1, source_target_pairs={{0,4},{4,0},{8,12},{12,8},{16,20},{20,16},{24,28},{28,24},{1,5},{5... | collective-permute-start | bytes 393224 | tf_op jit(solution)/shard_map/ppermute | solution.py:753
  40.8 0.7 %collective-permute-start.14 = (bf16[16,64,128]{2,1,0:T(8,128)(2,1)S(1)}, bf16[16,64,128]{2,1,0:T(8,128)(2,1)S(1)}, u32[]{:S(2)}, u32[]{:S(2)}) collective-permute-start(bf16[16,64,128]{2,1,0:T(8,128)(2,1)S(1)} %get-tuple-element.67), channel_id=1, source_target_pairs={{0,2},{1,3},{2,0},{3,1},{4,6},{5,7},{6,4},{7,5},{8,10},{9,11},{10,... | collective-permute-start | bytes 786440 | tf_op jit(solution)/shard_map/ppermute | solution.py:749
  41.5 1.4 %collective-permute-start.11 = (bf16[16,64,128]{2,1,0:T(8,128)(2,1)S(1)}, bf16[16,64,128]{2,1,0:T(8,128)(2,1)S(1)}, u32[]{:S(2)}, u32[]{:S(2)}) collective-permute-start(bf16[16,64,128]{2,1,0:T(8,128)(2,1)S(1)} %get-tuple-element.64.refs_2_), channel_id=1, source_target_pairs={{0,2},{1,3},{2,0},{3,1},{4,6},{5,7},{6,4},{7,5},{8,10},{9,11},{10,... | collective-permute-start | bytes 786440 | tf_op jit(solution)/shard_map/ppermute | solution.py:749
  42.9 2.2 %collective-permute-done.8 = bf16[4,128,128]{2,1,0:T(8,128)(2,1)S(1)} collective-permute-done((bf16[4,128,128]{2,1,0:T(8,128)(2,1)S(1)}, bf16[4,128,128]{2,1,0:T(8,128)(2,1)S(1)}, u32[]{:S(2)}, u32[]{:S(2)}) %collective-permute-start.8) | collective-permute-done | bytes 131104 | tf_op jit(solution)/shard_map/ppermute | solution.py:753
  45.9 3.5 %collective-permute-done.12 = bf16[2,128,128]{2,1,0:T(8,128)(2,1)S(1)} collective-permute-done((bf16[2,128,128]{2,1,0:T(8,128)(2,1)S(1)}, bf16[2,128,128]{2,1,0:T(8,128)(2,1)S(1)}, u32[]{:S(2)}, u32[]{:S(2)}) %collective-permute-start.12) | collective-permute-done | bytes 65568 | tf_op jit(solution)/shard_map/ppermute | solution.py:753
  50.0 1.1 %finish_first.1.refs_3_ = bf16[32,64,128]{2,1,0:T(8,128)(2,1)} custom-call(bf16[32,64,128]{2,1,0:T(8,128)(2,1)S(1)} %get-tuple-element.59.raw_ref, bf16[32,64,128]{2,1,0:T(8,128)(2,1)S(1)} %get-tuple-element.60.own_ref, bf16[32,64,128]{2,1,0:T(8,128)(2,1)S(1)} %collective-permute-done.10.core_ref, bf16[16,64,128]{2,1,0:T(8,128)(2,1)S(1)} %collective-permute-done.14.far_ref), custom_call_target="tpu_custom_call" | custom-call | tf_op jit(solution)/shard_map/finish_first/pallas_call | solution.py:667
  51.1 3.3 %collective-permute-done.13 = bf16[1,128,128]{2,1,0:T(8,128)(2,1)S(1)} collective-permute-done((bf16[1,128,128]{2,1,0:T(8,128)(2,1)S(1)}, bf16[1,128,128]{2,1,0:T(8,128)(2,1)S(1)}, u32[]{:S(2)}, u32[]{:S(2)}) %collective-permute-start.13) | collective-permute-done | bytes 32800 | tf_op jit(solution)/shard_map/ppermute | solution.py:753
  54.8 1.1 %finish_last.1 = (bf16[128,128]{1,0:T(8,128)(2,1)}, bf16[32,64,128]{2,1,0:T(8,128)(2,1)}) custom-call(bf16[32,64,128]{2,1,0:T(8,128)(2,1)S(1)} %get-tuple-element.59.raw_ref, bf16[32,64,128]{2,1,0:T(8,128)(2,1)S(1)} %get-tuple-element.60.own_ref, bf16[32,64,128]{2,1,0:T(8,128)(2,1)S(1)} %collective-permute-done.10.core_ref, ...), custom_call_target="tpu_custom_call", output_to_operand_aliasing={{1}: (8, {})} | custom-call | tf_op jit(solution)/shard_map/finish_last/pallas_call | solution.py:680
  (33 shorter events, 2.9 us)
Async XLA Ops:
  1.5 5.0 %collective-permute-start = (bf16[1,144,128]{2,1,0:T(8,128)(2,1)S(1)}, bf16[1,144,128]{2,1,0:T(8,128)(2,1)S(1)}, u32[]{:S(2)}, u32[]{:S(2)}) collective-permute-start(bf16[1,144,128]{2,1,0:T(8,128)(2,1)S(1)} %bitcast.12), channel_id=1, source_target_pairs={{0,4},{4,0},{8,12},{12,8},{16,20},{20,16},{24,28},{28,24},{1,5},{5... | collective-permute-start | bytes 110600 | tf_op jit(solution)/shard_map/ppermute | solution.py:710
  6.5 7.8 %collective-permute-start.1 = (bf16[2,144,128]{2,1,0:T(8,128)(2,1)S(1)}, bf16[2,144,128]{2,1,0:T(8,128)(2,1)S(1)}, u32[]{:S(2)}, u32[]{:S(2)}) collective-permute-start(bf16[2,144,128]{2,1,0:T(8,128)(2,1)S(1)} %pad_maximum_fusion.refs_0_), channel_id=1, source_target_pairs={{0,8},{4,12},{8,0},{12,4},{16,24},{20,28},{24,16},{28,20},{1,9},{5... | collective-permute-start | bytes 221192 | tf_op jit(solution)/shard_map/ppermute | solution.py:713
  8.6 6.8 %collective-permute-start.2 = (bf16[2,144,128]{2,1,0:T(8,128)(2,1)S(1)}, bf16[2,144,128]{2,1,0:T(8,128)(2,1)S(1)}, u32[]{:S(2)}, u32[]{:S(2)}) collective-permute-start(bf16[2,144,128]{2,1,0:T(8,128)(2,1)S(1)} %pad_maximum_fusion.refs_0_), channel_id=1, source_target_pairs={{0,16},{4,20},{8,24},{12,28},{16,0},{20,4},{24,8},{28,12},{1,17},{... | collective-permute-start | bytes 221192 | tf_op jit(solution)/shard_map/ppermute | solution.py:713
  11.2 6.2 %collective-permute-start.3 = (bf16[2,144,128]{2,1,0:T(8,128)(2,1)S(1)}, bf16[2,144,128]{2,1,0:T(8,128)(2,1)S(1)}, u32[]{:S(2)}, u32[]{:S(2)}) collective-permute-start(bf16[2,144,128]{2,1,0:T(8,128)(2,1)S(1)} %pad_maximum_fusion.refs_0_), channel_id=1, source_target_pairs={{0,24},{4,28},{8,16},{12,20},{16,8},{20,12},{24,0},{28,4},{1,25},{... | collective-permute-start | bytes 221192 | tf_op jit(solution)/shard_map/ppermute | solution.py:713
  21.9 4.6 %collective-permute-start.4 = (f32[8,128]{1,0:T(8,128)S(1)}, f32[8,128]{1,0:T(8,128)S(1)}, u32[]{:S(2)}, u32[]{:S(2)}) collective-permute-start(f32[8,128]{1,0:T(8,128)S(1)} %get-tuple-element.36), channel_id=1, source_target_pairs={{0,4},{4,0},{8,12},{12,8},{16,20},{20,16},{24,28},{28,24},{1,5},{5... | collective-permute-start | bytes 12296 | tf_op jit(solution)/shard_map/ppermute | solution.py:722
  26.5 4.5 %collective-permute-start.5 = (f32[8,128]{1,0:T(8,128)S(1)}, f32[8,128]{1,0:T(8,128)S(1)}, u32[]{:S(2)}, u32[]{:S(2)}) collective-permute-start(f32[8,128]{1,0:T(8,128)S(1)} %add.30.refs_0_), channel_id=1, source_target_pairs={{0,8},{4,12},{8,0},{12,4},{16,24},{20,28},{24,16},{28,20},{1,9},{5... | collective-permute-start | bytes 12296 | tf_op jit(solution)/shard_map/ppermute | solution.py:722
  26.6 4.6 %collective-permute-start.6 = (f32[8,128]{1,0:T(8,128)S(1)}, f32[8,128]{1,0:T(8,128)S(1)}, u32[]{:S(2)}, u32[]{:S(2)}) collective-permute-start(f32[8,128]{1,0:T(8,128)S(1)} %add.30.refs_0_), channel_id=1, source_target_pairs={{0,16},{4,20},{8,24},{12,28},{16,0},{20,4},{24,8},{28,12},{1,17},{... | collective-permute-start | bytes 12296 | tf_op jit(solution)/shard_map/ppermute | solution.py:722
  29.2 5.4 %collective-permute-start.7 = (f32[8,128]{1,0:T(8,128)S(1)}, f32[8,128]{1,0:T(8,128)S(1)}, u32[]{:S(2)}, u32[]{:S(2)}) collective-permute-start(f32[8,128]{1,0:T(8,128)S(1)} %add.30.refs_0_), channel_id=1, source_target_pairs={{0,24},{4,28},{8,16},{12,20},{16,8},{20,12},{24,0},{28,4},{1,25},{... | collective-permute-start | bytes 12296 | tf_op jit(solution)/shard_map/ppermute | solution.py:722
  34.8 3.9 %copy-start.1 = (f32[4,32]{1,0:T(4,128)S(1)}, f32[4,32]{1,0:T(4,128)}, u32[]{:S(2)}) copy-start(f32[4,32]{1,0:T(4,128)} %refs_2_.1) | copy-start | bytes 1540
  38.6 2.0 %collective-permute-start.9 = (bf16[32,64,128]{2,1,0:T(8,128)(2,1)S(1)}, bf16[32,64,128]{2,1,0:T(8,128)(2,1)S(1)}, u32[]{:S(2)}, u32[]{:S(2)}) collective-permute-start(bf16[32,64,128]{2,1,0:T(8,128)(2,1)S(1)} %get-tuple-element.54), channel_id=1, source_target_pairs={{0,1},{1,0},{2,3},{3,2},{4,5},{5,4},{6,7},{7,6},{8,9},{9,8},{10,11... | collective-permute-start | bytes 1572872 | tf_op jit(solution)/shard_map/ppermute | solution.py:741
  39.0 10.8 %collective-permute-start.10 = (bf16[32,64,128]{2,1,0:T(8,128)(2,1)S(1)}, bf16[32,64,128]{2,1,0:T(8,128)(2,1)S(1)}, u32[]{:S(2)}, u32[]{:S(2)}) collective-permute-start(bf16[32,64,128]{2,1,0:T(8,128)(2,1)S(1)} %get-tuple-element.61), channel_id=1, source_target_pairs={{0,1},{1,0},{2,3},{3,2},{4,5},{5,4},{6,7},{7,6},{8,9},{9,8},{10,11... | collective-permute-start | bytes 1572872 | tf_op jit(solution)/shard_map/ppermute | solution.py:750
  39.6 5.5 %collective-permute-start.8 = (bf16[4,128,128]{2,1,0:T(8,128)(2,1)S(1)}, bf16[4,128,128]{2,1,0:T(8,128)(2,1)S(1)}, u32[]{:S(2)}, u32[]{:S(2)}) collective-permute-start(bf16[4,128,128]{2,1,0:T(8,128)(2,1)S(1)} %get-tuple-element.52), channel_id=1, source_target_pairs={{0,4},{4,0},{8,12},{12,8},{16,20},{20,16},{24,28},{28,24},{1,5},{5... | collective-permute-start | bytes 393224 | tf_op jit(solution)/shard_map/ppermute | solution.py:753
  40.8 14.0 %copy-start = (bf16[4,32,128]{2,1,0:T(8,128)(2,1)S(1)}, bf16[4,32,128]{2,1,0:T(8,128)(2,1)}, u32[]{:S(2)}) copy-start(bf16[4,32,128]{2,1,0:T(8,128)(2,1)} %param.4) | copy-start | bytes 98308
  40.8 9.2 %collective-permute-start.14 = (bf16[16,64,128]{2,1,0:T(8,128)(2,1)S(1)}, bf16[16,64,128]{2,1,0:T(8,128)(2,1)S(1)}, u32[]{:S(2)}, u32[]{:S(2)}) collective-permute-start(bf16[16,64,128]{2,1,0:T(8,128)(2,1)S(1)} %get-tuple-element.67), channel_id=1, source_target_pairs={{0,2},{1,3},{2,0},{3,1},{4,6},{5,7},{6,4},{7,5},{8,10},{9,11},{10,... | collective-permute-start | bytes 786440 | tf_op jit(solution)/shard_map/ppermute | solution.py:749
  41.5 13.3 %collective-permute-start.11 = (bf16[16,64,128]{2,1,0:T(8,128)(2,1)S(1)}, bf16[16,64,128]{2,1,0:T(8,128)(2,1)S(1)}, u32[]{:S(2)}, u32[]{:S(2)}) collective-permute-start(bf16[16,64,128]{2,1,0:T(8,128)(2,1)S(1)} %get-tuple-element.64.refs_2_), channel_id=1, source_target_pairs={{0,2},{1,3},{2,0},{3,1},{4,6},{5,7},{6,4},{7,5},{8,10},{9,11},{10,... | collective-permute-start | bytes 786440 | tf_op jit(solution)/shard_map/ppermute | solution.py:749
  45.1 4.3 %collective-permute-start.12 = (bf16[2,128,128]{2,1,0:T(8,128)(2,1)S(1)}, bf16[2,128,128]{2,1,0:T(8,128)(2,1)S(1)}, u32[]{:S(2)}, u32[]{:S(2)}) collective-permute-start(bf16[2,128,128]{2,1,0:T(8,128)(2,1)S(1)} %slice.62), channel_id=1, source_target_pairs={{0,8},{4,12},{8,0},{12,4},{16,24},{20,28},{24,16},{28,20},{1,9},{5... | collective-permute-start | bytes 196616 | tf_op jit(solution)/shard_map/ppermute | solution.py:753
  49.5 4.9 %collective-permute-start.13 = (bf16[1,128,128]{2,1,0:T(8,128)(2,1)S(1)}, bf16[1,128,128]{2,1,0:T(8,128)(2,1)S(1)}, u32[]{:S(2)}, u32[]{:S(2)}) collective-permute-start(bf16[1,128,128]{2,1,0:T(8,128)(2,1)S(1)} %slice.63), channel_id=1, source_target_pairs={{0,16},{4,20},{8,24},{12,28},{16,0},{20,4},{24,8},{28,12},{1,17},{... | collective-permute-start | bytes 98312 | tf_op jit(solution)/shard_map/ppermute | solution.py:753

commit v10 on v9

--- a/solution.py
+++ b/solution.py
@@ -747,12 +747,12 @@
     send, own = lax.optimization_barrier((send, own))
     ready = far[1]
     far = [lax.ppermute(piece, "qry", away) for piece in far]
-    core = lax.ppermute(core, "qry", near)
     bit = 1
     while bit < sources:
         send = lax.ppermute(send, "psg", [(i, i ^ bit) for i in range(sources)])
         if bit == 1:
-            send, zw, ready = lax.optimization_barrier((send, zw, ready))
+            send, zw, ready, core = lax.optimization_barrier((send, zw, ready, core))
+            core = lax.ppermute(core, "qry", near)
         bit *= 2
         if bit < sources:
             total = keep.astype(jnp.float32) + send.astype(jnp.float32)

time: 56.2 us -> 56.5 us (level); the launches traced: 55.9 us -> 56.9 us
  starting transfers between devices: 17.7 us -> 19.8 us
  Pallas kernels: 18 us -> 16.6 us
    ppermute x3, waiting for transfers between devices: 8.95 us -> 5.92 us  [shards(): send = lax.ppermute(send, 'psg', [(i, i ^ bit) for i in range(sources)])]
    ppermute x2, waiting for transfers between devices: 0.65 us -> 3.02 us  [shards(): far = [lax.ppermute(piece, 'qry', away) for piece in far]]
    ppermute x2, starting transfers between devices: 2.09 us -> 3.82 us  [shards(): far = [lax.ppermute(piece, 'qry', away) for piece in far]]
    ppermute x4, starting transfers between devices: 5.61 us -> 6.84 us  [swap(): return lax.ppermute(values, 'psg', [(i, i ^ bit) for i in range(sources)])]
    ppermute x1, waiting for transfers between devices: 0.01 us -> 1.13 us  [shards(): cross = lax.ppermute(cross, 'qry', near)]
    pallas_call x1, Pallas kernels: 4.53 us -> 3.72 us  [forward(): pl.pallas_call(lambda *refs: forward_kernel(cand_count, query_count, quer...]
  transfers between devices with their start and end apart: 15 -> 15, of which waited for: 10 -> 10; matrix products, arithmetic and copies ran while one was open for 2% -> 2% of each run, Pallas kernels for 14% -> 12%
where the time goes in v10:
time: 56.5 us; the launch traced here: 56.9 us
  starting transfers between devices  19.8 us (35%)
  waiting for transfers between devices  18.4 us (33%)
  Pallas kernels  16.6 us (29%)
  other arithmetic  1.07 us (2%)
  between operations  0.8 us (1%)
    ppermute x4, starting transfers between devices, swap(): return lax.ppermute(values, 'psg', [(i, i ^ bit) for i in range(sources)])  6.84 us
    ppermute x3, waiting for transfers between devices, shards(): send = lax.ppermute(send, 'psg', [(i, i ^ bit) for i in range(sources)])  5.92 us
    ppermute x3, starting transfers between devices, shards(): lax.ppermute(received, 'psg', [(i, i ^ d) for i in range(sources)])  4.73 us
    ppermute x2, starting transfers between devices, shards(): far = [lax.ppermute(piece, 'qry', away) for piece in far]  3.82 us
    pallas_call x1, Pallas kernels, passage_backward(): pl.pallas_call(lambda *refs: passage_kernel(query_tokens, *refs), in_spec...  3.79 us
    pallas_call x1, Pallas kernels, forward(): pl.pallas_call(lambda *refs: forward_kernel(cand_count, query_count, quer...  3.72 us
    ppermute x4, waiting for transfers between devices, swap(): return lax.ppermute(values, 'psg', [(i, i ^ bit) for i in range(sources)])  3.39 us
    pallas_call x1, Pallas kernels, prepare_passages(): pl.pallas_call(lambda *refs: passages_kernel(slices, *refs), in_specs=[HB...  3.09 us
  transfers between devices with their start and end apart: 15, of which 10 were waited for; matrix products, arithmetic and copies ran while one was open for 2% of the time, Pallas kernels for 12%

profile of v10, /device:TPU:0, one launch (start us, length us, event | category | flops | bytes accessed | tf_op | source)
XLA Modules:
  0.0 56.9 jit_solution(14553894215497605102)
XLA Ops:
  0.6 0.9 %pack.1 = bf16[144,128]{1,0:T(8,128)(2,1)S(1)} custom-call(bf16[128,128]{1,0:T(8,128)(2,1)} %bitcast.14, s32[4,32]{1,0:T(4,128)} %refs_1_.1, f32[4,32]{1,0:T(4,128)} %refs_2_.1), custom_call_target="tpu_custom_call" | custom-call | tf_op jit(solution)/shard_map/pack/pallas_call | solution.py:71
  1.5 3.0 %collective-permute-start = (bf16[1,144,128]{2,1,0:T(8,128)(2,1)S(1)}, bf16[1,144,128]{2,1,0:T(8,128)(2,1)S(1)}, u32[]{:S(2)}, u32[]{:S(2)}) collective-permute-start(bf16[1,144,128]{2,1,0:T(8,128)(2,1)S(1)} %bitcast.12), channel_id=1, source_target_pairs={{0,4},{4,0},{8,12},{12,8},{16,20},{20,16},{24,28},{28,24},{1,5},{5... | collective-permute-start | bytes 110600 | tf_op jit(solution)/shard_map/ppermute | solution.py:710
  4.5 1.9 %collective-permute-done = bf16[1,144,128]{2,1,0:T(8,128)(2,1)S(1)} collective-permute-done((bf16[1,144,128]{2,1,0:T(8,128)(2,1)S(1)}, bf16[1,144,128]{2,1,0:T(8,128)(2,1)S(1)}, u32[]{:S(2)}, u32[]{:S(2)}) %collective-permute-start) | collective-permute-done | bytes 36896 | tf_op jit(solution)/shard_map/ppermute | solution.py:710
  6.5 2.1 %collective-permute-start.1 = (bf16[2,144,128]{2,1,0:T(8,128)(2,1)S(1)}, bf16[2,144,128]{2,1,0:T(8,128)(2,1)S(1)}, u32[]{:S(2)}, u32[]{:S(2)}) collective-permute-start(bf16[2,144,128]{2,1,0:T(8,128)(2,1)S(1)} %pad_maximum_fusion.refs_0_), channel_id=1, source_target_pairs={{0,8},{4,12},{8,0},{12,4},{16,24},{20,28},{24,16},{28,20},{1,9},{5... | collective-permute-start | bytes 221192 | tf_op jit(solution)/shard_map/ppermute | solution.py:713
  8.6 2.6 %collective-permute-start.2 = (bf16[2,144,128]{2,1,0:T(8,128)(2,1)S(1)}, bf16[2,144,128]{2,1,0:T(8,128)(2,1)S(1)}, u32[]{:S(2)}, u32[]{:S(2)}) collective-permute-start(bf16[2,144,128]{2,1,0:T(8,128)(2,1)S(1)} %pad_maximum_fusion.refs_0_), channel_id=1, source_target_pairs={{0,16},{4,20},{8,24},{12,28},{16,0},{20,4},{24,8},{28,12},{1,17},{... | collective-permute-start | bytes 221192 | tf_op jit(solution)/shard_map/ppermute | solution.py:713
  11.2 3.1 %prepare_passages.1 = (bf16[32,256,128]{2,1,0:T(8,128)(2,1)S(1)}, bf16[32,128,256]{2,1,0:T(8,128)(2,1)S(1)}, bf16[32,64,128]{2,1,0:T(8,128)(2,1)S(1)}) custom-call(bf16[32,256,128]{2,1,0:T(8,128)(2,1)} %refs_0_.1), custom_call_target="tpu_custom_call" | custom-call | flops 16777216 | bytes 6291456 | tf_op jit(solution)/shard_map/prepare_passages/pallas_call | solution.py:129
  14.3 1.1 %collective-permute-done.2.refs_2_ = bf16[2,144,128]{2,1,0:T(8,128)(2,1)S(1)} collective-permute-done((bf16[2,144,128]{2,1,0:T(8,128)(2,1)S(1)}, bf16[2,144,128]{2,1,0:T(8,128)(2,1)S(1)}, u32[]{:S(2)}, u32[]{:S(2)}) %collective-permute-start.2) | collective-permute-done | bytes 73760 | tf_op jit(solution)/shard_map/ppermute | solution.py:713
  15.5 1.9 %collective-permute-done.3.refs_3_ = bf16[2,144,128]{2,1,0:T(8,128)(2,1)S(1)} collective-permute-done((bf16[2,144,128]{2,1,0:T(8,128)(2,1)S(1)}, bf16[2,144,128]{2,1,0:T(8,128)(2,1)S(1)}, u32[]{:S(2)}, u32[]{:S(2)}) %collective-permute-start.3) | collective-permute-done | bytes 73760 | tf_op jit(solution)/shard_map/ppermute | solution.py:713
  17.4 3.7 %forward.1 = (bf16[68,256,256]{2,1,0:T(8,128)(2,1)S(1)}, bf16[1056,128]{1,0:T(8,128)(2,1)S(1)}, f32[32,128]{1,0:T(8,128)S(1)}, f32[32,128]{1,0:T(8,128)S(1)}, f3...) custom-call(bf16[2,144,128]{2,1,0:T(8,128)(2,1)S(1)} %pad_maximum_fusion.refs_0_, ...), custom_call_target="tpu_custom_call" | custom-call | flops 1140850688 | bytes 12582912 | tf_op jit(solution)/shard_map/forward/pallas_call | solution.py:362
  21.1 2.4 %collective-permute-start.4 = (f32[8,128]{1,0:T(8,128)S(1)}, f32[8,128]{1,0:T(8,128)S(1)}, u32[]{:S(2)}, u32[]{:S(2)}) collective-permute-start(f32[8,128]{1,0:T(8,128)S(1)} %get-tuple-element.37), channel_id=1, source_target_pairs={{0,4},{4,0},{8,12},{12,8},{16,20},{20,16},{24,28},{28,24},{1,5},{5... | collective-permute-start | bytes 12296 | tf_op jit(solution)/shard_map/ppermute | solution.py:722
  23.5 2.8 %attend.1 = (f32[1056,128]{1,0:T(8,128)S(1)}, f32[1056,128]{1,0:T(8,128)S(1)}) custom-call(bf16[32,128,256]{2,1,0:T(8,128)(2,1)S(1)} %get-tuple-element.38.refs_0_, bf16[68,256,256]{2,1,0:T(8,128)(2,1)S(1)} %get-tuple-element.39.refs_1_.refs_4_, s32[24,128]{1,0:T(8,128)S(1)} %get-tuple-element.40.refs_2_.refs_0_, ...), custom_call_target="tpu_custom_call" | custom-call | flops 1140850688 | bytes 12582912 | tf_op jit(solution)/shard_map/attend/pallas_call | solution.py:460
  26.4 2.4 %collective-permute-start.6 = (f32[8,128]{1,0:T(8,128)S(1)}, f32[8,128]{1,0:T(8,128)S(1)}, u32[]{:S(2)}, u32[]{:S(2)}) collective-permute-start(f32[8,128]{1,0:T(8,128)S(1)} %add.30.refs_0_), channel_id=1, source_target_pairs={{0,16},{4,20},{8,24},{12,28},{16,0},{20,4},{24,8},{28,12},{1,17},{... | collective-permute-start | bytes 12296 | tf_op jit(solution)/shard_map/ppermute | solution.py:722
  28.8 2.0 %collective-permute-start.7 = (f32[8,128]{1,0:T(8,128)S(1)}, f32[8,128]{1,0:T(8,128)S(1)}, u32[]{:S(2)}, u32[]{:S(2)}) collective-permute-start(f32[8,128]{1,0:T(8,128)S(1)} %add.30.refs_0_), channel_id=1, source_target_pairs={{0,24},{4,28},{8,16},{12,20},{16,8},{20,12},{24,0},{28,4},{1,25},{... | collective-permute-start | bytes 12296 | tf_op jit(solution)/shard_map/ppermute | solution.py:722
  31.0 3.2 %collective-permute-done.7.refs_3_ = f32[8,128]{1,0:T(8,128)S(1)} collective-permute-done((f32[8,128]{1,0:T(8,128)S(1)}, f32[8,128]{1,0:T(8,128)S(1)}, u32[]{:S(2)}, u32[]{:S(2)}) %collective-permute-start.7) | collective-permute-done | bytes 4128 | tf_op jit(solution)/shard_map/ppermute | solution.py:722
  34.4 3.8 %passage_backward.1 = (bf16[32,64,128]{2,1,0:T(8,128)(2,1)S(1)}, bf16[32,64,128]{2,1,0:T(8,128)(2,1)S(1)}, bf16[32,64,128]{2,1,0:T(8,128)(2,1)S(1)}, bf16[32,64,128]{2,1,0:T(8,128)(2,1)S(1)}) custom-call(s32[24,128]{1,0:T(8,128)S(1)} %get-tuple-element.40.refs_2_.refs_0_, f32[32,128]{1,0:T(8,128)S(1)} %get-tuple-element.50.refs_1_, ...), custom_call_target="tpu_custom_call" | custom-call | flops 1073741824 | bytes 6291456 | tf_op jit(solution)/shard_map/passage_backward/pallas_call | solution.py:631
  39.0 1.1 %collective-permute-done.9 = bf16[32,64,128]{2,1,0:T(8,128)(2,1)S(1)} collective-permute-done((bf16[32,64,128]{2,1,0:T(8,128)(2,1)S(1)}, bf16[32,64,128]{2,1,0:T(8,128)(2,1)S(1)}, u32[]{:S(2)}, u32[]{:S(2)}) %collective-permute-start.9) | collective-permute-done | bytes 524320 | tf_op jit(solution)/shard_map/ppermute | solution.py:741
  40.4 1.9 %collective-permute-start.11 = (bf16[16,64,128]{2,1,0:T(8,128)(2,1)S(1)}, bf16[16,64,128]{2,1,0:T(8,128)(2,1)S(1)}, u32[]{:S(2)}, u32[]{:S(2)}) collective-permute-start(bf16[16,64,128]{2,1,0:T(8,128)(2,1)S(1)} %get-tuple-element.66.refs_2_), channel_id=1, source_target_pairs={{0,2},{1,3},{2,0},{3,1},{4,6},{5,7},{6,4},{7,5},{8,10},{9,11},{10,... | collective-permute-start | bytes 786440 | tf_op jit(solution)/shard_map/ppermute | solution.py:749
  42.3 2.2 %collective-permute-done.8 = bf16[4,128,128]{2,1,0:T(8,128)(2,1)S(1)} collective-permute-done((bf16[4,128,128]{2,1,0:T(8,128)(2,1)S(1)}, bf16[4,128,128]{2,1,0:T(8,128)(2,1)S(1)}, u32[]{:S(2)}, u32[]{:S(2)}) %collective-permute-start.8) | collective-permute-done | bytes 131104 | tf_op jit(solution)/shard_map/ppermute | solution.py:752
  44.6 1.9 %collective-permute-start.14 = (bf16[16,64,128]{2,1,0:T(8,128)(2,1)S(1)}, bf16[16,64,128]{2,1,0:T(8,128)(2,1)S(1)}, u32[]{:S(2)}, u32[]{:S(2)}) collective-permute-start(bf16[16,64,128]{2,1,0:T(8,128)(2,1)S(1)} %get-tuple-element.69), channel_id=1, source_target_pairs={{0,2},{1,3},{2,0},{3,1},{4,6},{5,7},{6,4},{7,5},{8,10},{9,11},{10,... | collective-permute-start | bytes 786440 | tf_op jit(solution)/shard_map/ppermute | solution.py:749
  47.3 3.5 %collective-permute-done.12 = bf16[2,128,128]{2,1,0:T(8,128)(2,1)S(1)} collective-permute-done((bf16[2,128,128]{2,1,0:T(8,128)(2,1)S(1)}, bf16[2,128,128]{2,1,0:T(8,128)(2,1)S(1)}, u32[]{:S(2)}, u32[]{:S(2)}) %collective-permute-start.12) | collective-permute-done | bytes 65568 | tf_op jit(solution)/shard_map/ppermute | solution.py:752
  50.8 0.7 %collective-permute-start.13 = (bf16[1,128,128]{2,1,0:T(8,128)(2,1)S(1)}, bf16[1,128,128]{2,1,0:T(8,128)(2,1)S(1)}, u32[]{:S(2)}, u32[]{:S(2)}) collective-permute-start(bf16[1,128,128]{2,1,0:T(8,128)(2,1)S(1)} %slice.63), channel_id=1, source_target_pairs={{0,16},{4,20},{8,24},{12,28},{16,0},{20,4},{24,8},{28,12},{1,17},{... | collective-permute-start | bytes 98312 | tf_op jit(solution)/shard_map/ppermute | solution.py:752
  51.5 3.0 %collective-permute-done.14.far_ref = bf16[16,64,128]{2,1,0:T(8,128)(2,1)S(1)} collective-permute-done((bf16[16,64,128]{2,1,0:T(8,128)(2,1)S(1)}, bf16[16,64,128]{2,1,0:T(8,128)(2,1)S(1)}, u32[]{:S(2)}, u32[]{:S(2)}) %collective-permute-start.14) | collective-permute-done | bytes 262176 | tf_op jit(solution)/shard_map/ppermute | solution.py:749
  54.5 1.1 %finish_first.1.refs_3_ = bf16[32,64,128]{2,1,0:T(8,128)(2,1)} custom-call(bf16[32,64,128]{2,1,0:T(8,128)(2,1)S(1)} %get-tuple-element.61.raw_ref, bf16[32,64,128]{2,1,0:T(8,128)(2,1)S(1)} %get-tuple-element.62.own_ref, bf16[32,64,128]{2,1,0:T(8,128)(2,1)S(1)} %collective-permute-done.10.core_ref, bf16[16,64,128]{2,1,0:T(8,128)(2,1)S(1)} %collective-permute-done.14.far_ref), custom_call_target="tpu_custom_call" | custom-call | tf_op jit(solution)/shard_map/finish_first/pallas_call | solution.py:667
  55.8 1.1 %finish_last.1 = (bf16[128,128]{1,0:T(8,128)(2,1)}, bf16[32,64,128]{2,1,0:T(8,128)(2,1)}) custom-call(bf16[32,64,128]{2,1,0:T(8,128)(2,1)S(1)} %get-tuple-element.61.raw_ref, bf16[32,64,128]{2,1,0:T(8,128)(2,1)S(1)} %get-tuple-element.62.own_ref, bf16[32,64,128]{2,1,0:T(8,128)(2,1)S(1)} %collective-permute-done.10.core_ref, ...), custom_call_target="tpu_custom_call", output_to_operand_aliasing={{1}: (8, {})} | custom-call | tf_op jit(solution)/shard_map/finish_last/pallas_call | solution.py:680
  (33 shorter events, 2.5 us)
Async XLA Ops:
  1.5 5.0 %collective-permute-start = (bf16[1,144,128]{2,1,0:T(8,128)(2,1)S(1)}, bf16[1,144,128]{2,1,0:T(8,128)(2,1)S(1)}, u32[]{:S(2)}, u32[]{:S(2)}) collective-permute-start(bf16[1,144,128]{2,1,0:T(8,128)(2,1)S(1)} %bitcast.12), channel_id=1, source_target_pairs={{0,4},{4,0},{8,12},{12,8},{16,20},{20,16},{24,28},{28,24},{1,5},{5... | collective-permute-start | bytes 110600 | tf_op jit(solution)/shard_map/ppermute | solution.py:710
  6.5 7.8 %collective-permute-start.1 = (bf16[2,144,128]{2,1,0:T(8,128)(2,1)S(1)}, bf16[2,144,128]{2,1,0:T(8,128)(2,1)S(1)}, u32[]{:S(2)}, u32[]{:S(2)}) collective-permute-start(bf16[2,144,128]{2,1,0:T(8,128)(2,1)S(1)} %pad_maximum_fusion.refs_0_), channel_id=1, source_target_pairs={{0,8},{4,12},{8,0},{12,4},{16,24},{20,28},{24,16},{28,20},{1,9},{5... | collective-permute-start | bytes 221192 | tf_op jit(solution)/shard_map/ppermute | solution.py:713
  8.6 6.8 %collective-permute-start.2 = (bf16[2,144,128]{2,1,0:T(8,128)(2,1)S(1)}, bf16[2,144,128]{2,1,0:T(8,128)(2,1)S(1)}, u32[]{:S(2)}, u32[]{:S(2)}) collective-permute-start(bf16[2,144,128]{2,1,0:T(8,128)(2,1)S(1)} %pad_maximum_fusion.refs_0_), channel_id=1, source_target_pairs={{0,16},{4,20},{8,24},{12,28},{16,0},{20,4},{24,8},{28,12},{1,17},{... | collective-permute-start | bytes 221192 | tf_op jit(solution)/shard_map/ppermute | solution.py:713
  11.2 6.2 %collective-permute-start.3 = (bf16[2,144,128]{2,1,0:T(8,128)(2,1)S(1)}, bf16[2,144,128]{2,1,0:T(8,128)(2,1)S(1)}, u32[]{:S(2)}, u32[]{:S(2)}) collective-permute-start(bf16[2,144,128]{2,1,0:T(8,128)(2,1)S(1)} %pad_maximum_fusion.refs_0_), channel_id=1, source_target_pairs={{0,24},{4,28},{8,16},{12,20},{16,8},{20,12},{24,0},{28,4},{1,25},{... | collective-permute-start | bytes 221192 | tf_op jit(solution)/shard_map/ppermute | solution.py:713
  21.1 5.2 %collective-permute-start.4 = (f32[8,128]{1,0:T(8,128)S(1)}, f32[8,128]{1,0:T(8,128)S(1)}, u32[]{:S(2)}, u32[]{:S(2)}) collective-permute-start(f32[8,128]{1,0:T(8,128)S(1)} %get-tuple-element.37), channel_id=1, source_target_pairs={{0,4},{4,0},{8,12},{12,8},{16,20},{20,16},{24,28},{28,24},{1,5},{5... | collective-permute-start | bytes 12296 | tf_op jit(solution)/shard_map/ppermute | solution.py:722
  26.4 4.5 %collective-permute-start.5 = (f32[8,128]{1,0:T(8,128)S(1)}, f32[8,128]{1,0:T(8,128)S(1)}, u32[]{:S(2)}, u32[]{:S(2)}) collective-permute-start(f32[8,128]{1,0:T(8,128)S(1)} %add.30.refs_0_), channel_id=1, source_target_pairs={{0,8},{4,12},{8,0},{12,4},{16,24},{20,28},{24,16},{28,20},{1,9},{5... | collective-permute-start | bytes 12296 | tf_op jit(solution)/shard_map/ppermute | solution.py:722
  26.4 4.6 %collective-permute-start.6 = (f32[8,128]{1,0:T(8,128)S(1)}, f32[8,128]{1,0:T(8,128)S(1)}, u32[]{:S(2)}, u32[]{:S(2)}) collective-permute-start(f32[8,128]{1,0:T(8,128)S(1)} %add.30.refs_0_), channel_id=1, source_target_pairs={{0,16},{4,20},{8,24},{12,28},{16,0},{20,4},{24,8},{28,12},{1,17},{... | collective-permute-start | bytes 12296 | tf_op jit(solution)/shard_map/ppermute | solution.py:722
  28.8 5.4 %collective-permute-start.7 = (f32[8,128]{1,0:T(8,128)S(1)}, f32[8,128]{1,0:T(8,128)S(1)}, u32[]{:S(2)}, u32[]{:S(2)}) collective-permute-start(f32[8,128]{1,0:T(8,128)S(1)} %add.30.refs_0_), channel_id=1, source_target_pairs={{0,24},{4,28},{8,16},{12,20},{16,8},{20,12},{24,0},{28,4},{1,25},{... | collective-permute-start | bytes 12296 | tf_op jit(solution)/shard_map/ppermute | solution.py:722
  34.4 3.9 %copy-start.1 = (f32[4,32]{1,0:T(4,128)S(1)}, f32[4,32]{1,0:T(4,128)}, u32[]{:S(2)}) copy-start(f32[4,32]{1,0:T(4,128)} %refs_2_.1) | copy-start | bytes 1540
  38.2 2.0 %collective-permute-start.9 = (bf16[32,64,128]{2,1,0:T(8,128)(2,1)S(1)}, bf16[32,64,128]{2,1,0:T(8,128)(2,1)S(1)}, u32[]{:S(2)}, u32[]{:S(2)}) collective-permute-start(bf16[32,64,128]{2,1,0:T(8,128)(2,1)S(1)} %get-tuple-element.55), channel_id=1, source_target_pairs={{0,1},{1,0},{2,3},{3,2},{4,5},{5,4},{6,7},{7,6},{8,9},{9,8},{10,11... | collective-permute-start | bytes 1572872 | tf_op jit(solution)/shard_map/ppermute | solution.py:741
  38.6 6.0 %collective-permute-start.8 = (bf16[4,128,128]{2,1,0:T(8,128)(2,1)S(1)}, bf16[4,128,128]{2,1,0:T(8,128)(2,1)S(1)}, u32[]{:S(2)}, u32[]{:S(2)}) collective-permute-start(bf16[4,128,128]{2,1,0:T(8,128)(2,1)S(1)} %get-tuple-element.53), channel_id=1, source_target_pairs={{0,4},{4,0},{8,12},{12,8},{16,20},{20,16},{24,28},{28,24},{1,5},{5... | collective-permute-start | bytes 393224 | tf_op jit(solution)/shard_map/ppermute | solution.py:752
  40.3 15.4 %copy-start = (bf16[4,32,128]{2,1,0:T(8,128)(2,1)S(1)}, bf16[4,32,128]{2,1,0:T(8,128)(2,1)}, u32[]{:S(2)}) copy-start(bf16[4,32,128]{2,1,0:T(8,128)(2,1)} %param.4) | copy-start | bytes 98308
  40.4 15.4 %collective-permute-start.11 = (bf16[16,64,128]{2,1,0:T(8,128)(2,1)S(1)}, bf16[16,64,128]{2,1,0:T(8,128)(2,1)S(1)}, u32[]{:S(2)}, u32[]{:S(2)}) collective-permute-start(bf16[16,64,128]{2,1,0:T(8,128)(2,1)S(1)} %get-tuple-element.66.refs_2_), channel_id=1, source_target_pairs={{0,2},{1,3},{2,0},{3,1},{4,6},{5,7},{6,4},{7,5},{8,10},{9,11},{10,... | collective-permute-start | bytes 786440 | tf_op jit(solution)/shard_map/ppermute | solution.py:749
  44.5 10.0 %collective-permute-start.10 = (bf16[32,64,128]{2,1,0:T(8,128)(2,1)S(1)}, bf16[32,64,128]{2,1,0:T(8,128)(2,1)S(1)}, u32[]{:S(2)}, u32[]{:S(2)}) collective-permute-start(bf16[32,64,128]{2,1,0:T(8,128)(2,1)S(1)} %get-tuple-element.63), channel_id=1, source_target_pairs={{0,1},{1,0},{2,3},{3,2},{4,5},{5,4},{6,7},{7,6},{8,9},{9,8},{10,11... | collective-permute-start | bytes 1572872 | tf_op jit(solution)/shard_map/ppermute | solution.py:755
  44.6 10.0 %collective-permute-start.14 = (bf16[16,64,128]{2,1,0:T(8,128)(2,1)S(1)}, bf16[16,64,128]{2,1,0:T(8,128)(2,1)S(1)}, u32[]{:S(2)}, u32[]{:S(2)}) collective-permute-start(bf16[16,64,128]{2,1,0:T(8,128)(2,1)S(1)} %get-tuple-element.69), channel_id=1, source_target_pairs={{0,2},{1,3},{2,0},{3,1},{4,6},{5,7},{6,4},{7,5},{8,10},{9,11},{10,... | collective-permute-start | bytes 786440 | tf_op jit(solution)/shard_map/ppermute | solution.py:749
  46.5 4.3 %collective-permute-start.12 = (bf16[2,128,128]{2,1,0:T(8,128)(2,1)S(1)}, bf16[2,128,128]{2,1,0:T(8,128)(2,1)S(1)}, u32[]{:S(2)}, u32[]{:S(2)}) collective-permute-start(bf16[2,128,128]{2,1,0:T(8,128)(2,1)S(1)} %slice.62), channel_id=1, source_target_pairs={{0,8},{4,12},{8,0},{12,4},{16,24},{20,28},{24,16},{28,20},{1,9},{5... | collective-permute-start | bytes 196616 | tf_op jit(solution)/shard_map/ppermute | solution.py:752
  50.8 4.9 %collective-permute-start.13 = (bf16[1,128,128]{2,1,0:T(8,128)(2,1)S(1)}, bf16[1,128,128]{2,1,0:T(8,128)(2,1)S(1)}, u32[]{:S(2)}, u32[]{:S(2)}) collective-permute-start(bf16[1,128,128]{2,1,0:T(8,128)(2,1)S(1)} %slice.63), channel_id=1, source_target_pairs={{0,16},{4,20},{8,24},{12,28},{16,0},{20,4},{24,8},{28,12},{1,17},{... | collective-permute-start | bytes 98312 | tf_op jit(solution)/shard_map/ppermute | solution.py:752
